TPU v7x, 32 devices: a whole 2x2x4 slice. The times are simulated.
32 devices in a mesh: seq: 8 (over y, x, core), tp: 4 (over z).
Axes of the slice: x: 2, y: 2, z: 4, core: 2. Of those that a mesh axis runs over, the one named last changes fastest.
Arguments:
- hidden_in: bfloat16 [5120, 1152], P('seq'), may hold values from -6 to 6
- cotangent: bfloat16 [5120, 1152], P('seq'), may hold values from -6 to 6
- modulation: bfloat16 [8, 6, 1152], P('seq'), may hold values from -3 to 3
- text_states: bfloat16 [8, 300, 1152], P('seq'), may hold values from -6 to 6
- image_shapes: int32 [8, 2], replicated, may hold values from 8 to 64, as said below
- text_lengths: int32 [8], replicated, may hold values from 75 to 300
- qkv_weight: bfloat16 [1152, 3, 1152], P(None, None, 'tp'), may hold values from -0.1875 to 0.1875
- attn_out_weight: bfloat16 [1152, 1152], P(None, 'tp'), may hold values from -1.75 to 1.75
- cross_q_weight: bfloat16 [1152, 1152], P(None, 'tp'), may hold values from -0.1875 to 0.1875
- cross_kv_weight: bfloat16 [1152, 2, 1152], P(None, None, 'tp'), may hold values from -0.1875 to 0.1875
- cross_out_weight: bfloat16 [1152, 1152], P(None, 'tp'), may hold values from -1.5 to 1.5
- up_weight: bfloat16 [1152, 2, 2880], P(None, None, 'tp'), may hold values from -0.1875 to 0.1875
- conv_weight: bfloat16 [9, 2, 2880], P(None, None, 'tp'), may hold values from -2 to 2
- down_weight: bfloat16 [1152, 2880], P(None, 'tp'), may hold values from -0.3125 to 0.3125
Outputs:
- output: bfloat16 [5120, 1152], P('seq')
- input_grad: float32 [5120, 1152], P('seq')
- modulation_grad: float32 [8, 6, 1152], P('seq')
- qkv_grad: float32 [1152, 3, 1152], P('seq', None, 'tp')
- attn_out_grad: float32 [1152, 1152], P('seq', 'tp')
- cross_q_grad: float32 [1152, 1152], P('seq', 'tp')
- cross_kv_grad: float32 [1152, 2, 1152], P('seq', None, 'tp')
- cross_out_grad: float32 [1152, 1152], P('seq', 'tp')
- up_grad: float32 [1152, 2, 2880], P('seq', None, 'tp')
- conv_grad: float32 [9, 2, 2880], P(None, None, 'tp')
- down_grad: float32 [1152, 2880], P('seq', 'tp')
Inputs may be any that keep to these rules, and one draw needn't show every extreme that they name: `image_shapes`: images 2k and 2k + 1 together have exactly 1280 patches and the same width, 32 or 16; a width of 32 comes with heights of 8 to 32, a width of 16 with heights of 16 to 64.
All inputs are finite; a program needn't handle non-finite values.
Results may differ from a plain program's by a relative error of at most 0.02.
Values may be sent and summed in bfloat16 or wider, within the bound.
No kernel may reach another device: no remote copies, remote signals or barrier semaphores. Data moves between devices by JAX's collectives and lax.ppermute only.
A program may use at most 256 MiB of HBM per device.

v0:
```python
import math

import jax
import jax.numpy as jnp
from jax import lax
from jax.sharding import PartitionSpec as P

HEAD = 32
CROSS_HEAD = 72
MAXW = 32


EPSILON = 1e-06
PRECISE = lax.Precision.HIGHEST
MASKED_OUT = -1e30


def swapped(block, axis, apart):
    count = lax.axis_size(axis)
    route = []
    for low in range(count):
        high = low | 1 << apart
        if high != low and high < count:
            route += [(low, high), (high, low)]
    return lax.ppermute(block, axis, route)


def modulated_norm(inputs, shifts, scales):
    inverse = lax.rsqrt(jnp.mean(inputs * inputs, axis=-1, keepdims=True) + EPSILON)
    return inputs * inverse * (1.0 + scales) + shifts


def glu_product(value_in, gate_in):
    return value_in * jax.nn.silu(gate_in)


def times_transposed(left_side, right_side):
    return lax.dot_general(
        left_side, right_side, (((1,), (1,)), ((), ())), preferred_element_type=jnp.float32
    )


def over_tokens(left_side, right_side):
    return lax.dot_general(
        left_side, right_side, (((0,), (0,)), ((), ())), preferred_element_type=jnp.float32
    )


def sum_weights(first_grad, second_grad, third_grad, fourth_grad):
    return (
        lax.psum_scatter(first_grad, "seq", scatter_dimension=0, tiled=True),
        lax.psum_scatter(second_grad, "seq", scatter_dimension=0, tiled=True),
        lax.psum_scatter(third_grad, "seq", scatter_dimension=0, tiled=True),
        lax.psum_scatter(fourth_grad, "seq", scatter_dimension=0, tiled=True),
    )


def by_image(second, pair_values):
    return jnp.where(
        second.reshape((-1,) + (1,) * (pair_values.ndim - 2)), pair_values[1], pair_values[0]
    )


def shards(
    hidden_in,
    cotangent,
    modulation,
    text_states,
    image_shapes,
    text_lengths,
    qkv_weight,
    attn_out_weight,
    cross_q_weight,
    cross_kv_weight,
    cross_out_weight,
    up_weight,
    conv_weight,
    down_weight,
):
    tokens_here, model_width = hidden_in.shape
    context = text_states.shape[1]
    self_cols = qkv_weight.shape[2]
    cross_cols = cross_q_weight.shape[1]
    ffn_cols = up_weight.shape[2]
    self_heads = self_cols // HEAD
    cross_heads = cross_cols // CROSS_HEAD
    score_scale = 1.0 / math.sqrt(CROSS_HEAD)
    rim_depth = MAXW + 1
    seq_count = lax.axis_size("seq")
    seq_index = lax.axis_index("seq")
    first_half = seq_index % 2 == 0
    pair_index = seq_index // 2
    pair_shapes = lax.dynamic_slice_in_dim(image_shapes, 2 * pair_index, 2, 0)
    pair_lengths = lax.dynamic_slice_in_dim(text_lengths, 2 * pair_index, 2, 0)
    row_width = pair_shapes[0, 1]
    size_first = pair_shapes[0, 0] * row_width
    places = jnp.arange(tokens_here, dtype=jnp.int32) + jnp.where(first_half, 0, tokens_here)
    second = places >= size_first
    within = places - jnp.where(second, size_first, 0)
    row_index = within // row_width
    col_index = within % row_width
    height = jnp.where(second, pair_shapes[1, 0], pair_shapes[0, 0])
    length = jnp.where(second, pair_lengths[1], pair_lengths[0])
    second_float = second.astype(jnp.float32)
    image_masks = jnp.stack([1.0 - second_float, second_float])
    mask_low = image_masks.astype(jnp.bfloat16)
    mask_pair = mask_low.T

    def inside(row_step, col_step):
        return (
            (row_index + row_step >= 0)
            & (row_index + row_step < height)
            & (col_index + col_step >= 0)
            & (col_index + col_step < row_width)
        )

    text_rows = text_states[0]
    kv_own = jnp.dot(
        text_rows,
        cross_kv_weight.reshape(model_width, 2 * cross_cols),
        preferred_element_type=jnp.float32,
    ).astype(jnp.bfloat16)
    mod_own = modulation[0]
    mod_other, kv_other = swapped((mod_own, kv_own), "seq", 0)
    mod_pair = jnp.where(
        first_half, jnp.stack([mod_own, mod_other]), jnp.stack([mod_other, mod_own])
    ).astype(jnp.float32)
    kv_pair = jnp.where(first_half, jnp.stack([kv_own, kv_other]), jnp.stack([kv_other, kv_own]))

    def per_token(row_pick):
        return jnp.where(second[:, None], mod_pair[1, row_pick], mod_pair[0, row_pick])

    inputs = hidden_in.astype(jnp.float32)
    gate_attn = per_token(2)
    gate_ffn = per_token(5)
    normed, norm_back = jax.vjp(modulated_norm, inputs, per_token(0), per_token(1))
    normed_low = normed.astype(jnp.bfloat16)
    qkv_flat = qkv_weight.reshape(model_width, 3 * self_cols)
    projected = jnp.dot(normed_low, qkv_flat, preferred_element_type=jnp.float32).reshape(
        tokens_here, 3, self_heads, HEAD
    )
    self_queries = jax.nn.softplus(projected[:, 0]).astype(jnp.bfloat16)
    self_keys = jax.nn.softplus(projected[:, 1]).astype(jnp.bfloat16)
    self_values = projected[:, 2].astype(jnp.bfloat16)
    masked_keys = self_keys[None] * mask_low[:, :, None, None]
    kernel_part = jnp.einsum(
        "itzd,tze->izde", masked_keys, self_values, preferred_element_type=jnp.float32
    )
    total_part = jnp.einsum("it,tzd->izd", mask_low, self_keys, preferred_element_type=jnp.float32)
    kernel_other, total_other = swapped((kernel_part, total_part), "seq", 0)
    kernels = kernel_part + kernel_other
    key_totals = total_part + total_other
    queries_wide = self_queries.astype(jnp.float32)
    numerators = jnp.einsum("tzd,izde->itze", queries_wide, kernels, precision=PRECISE)
    denominators = jnp.einsum("tzd,izd->itz", queries_wide, key_totals, precision=PRECISE)
    numerator = by_image(second, numerators)
    denominator = by_image(second, denominators) + 1.0
    attended = numerator / denominator[:, :, None]
    attended_low = attended.reshape(tokens_here, self_cols).astype(jnp.bfloat16)
    attn_branch = lax.psum(times_transposed(attended_low, attn_out_weight), "tp")
    after_attn = inputs + gate_attn * attn_branch
    after_low = after_attn.astype(jnp.bfloat16)
    cross_queries = (
        jnp.dot(after_low, cross_q_weight, preferred_element_type=jnp.float32)
        .astype(jnp.bfloat16)
        .reshape(tokens_here, cross_heads, CROSS_HEAD)
    )
    text_keys = kv_pair[:, :, :cross_cols].reshape(2, context, cross_heads, CROSS_HEAD)
    text_values = kv_pair[:, :, cross_cols:].reshape(2, context, cross_heads, CROSS_HEAD)
    raw_scores = (
        jnp.einsum("tzd,jszd->tzjs", cross_queries, text_keys, preferred_element_type=jnp.float32)
        * score_scale
    )
    scores = jnp.where(second[:, None, None], raw_scores[:, :, 1], raw_scores[:, :, 0])
    key_live = jnp.arange(context, dtype=jnp.int32)[None, :] < length[:, None]
    masked = jnp.where(key_live[:, None, :], scores, MASKED_OUT)
    row_max = jnp.max(masked, axis=-1, keepdims=True)
    exp_scores = jnp.exp(masked - row_max)
    attn_probs = exp_scores / jnp.sum(exp_scores, axis=-1, keepdims=True)
    probs_pair = attn_probs.astype(jnp.bfloat16)[:, :, None, :] * mask_pair[:, None, :, None]
    attended_text = jnp.einsum(
        "tzjs,jszd->tzd", probs_pair, text_values, preferred_element_type=jnp.float32
    )
    text_low = attended_text.reshape(tokens_here, cross_cols).astype(jnp.bfloat16)
    cross_branch = lax.psum(times_transposed(text_low, cross_out_weight), "tp")
    after_cross = after_attn + cross_branch
    normed_two, norm_two_back = jax.vjp(modulated_norm, after_cross, per_token(3), per_token(4))
    normed_two_low = normed_two.astype(jnp.bfloat16)
    up_flat = up_weight.reshape(model_width, 2 * ffn_cols)
    up_proj = jnp.dot(normed_two_low, up_flat, preferred_element_type=jnp.float32)
    activated = jax.nn.silu(up_proj).astype(jnp.bfloat16)
    conv_taps = conv_weight.reshape(9, 2 * ffn_cols).astype(jnp.float32)
    rim_in = swapped(jnp.where(first_half, activated[-rim_depth:], activated[:rim_depth]), "seq", 0)
    zero_rim = jnp.zeros_like(rim_in)
    padded = jnp.concatenate(
        [
            jnp.where(first_half, zero_rim, rim_in),
            activated,
            jnp.where(first_half, rim_in, zero_rim),
        ],
        axis=0,
    )
    mixture = jnp.zeros_like(up_proj)
    for tap_index in range(9):
        row_step = tap_index // 3 - 1
        col_step = tap_index % 3 - 1
        offset = row_step * row_width + col_step
        shifted = lax.dynamic_slice_in_dim(padded, rim_depth + offset, tokens_here, 0)
        mixture = (
            mixture
            + jnp.where(inside(row_step, col_step)[:, None], shifted.astype(jnp.float32), 0.0)
            * conv_taps[tap_index]
        )
    hidden, gating_back = jax.vjp(glu_product, mixture[:, :ffn_cols], mixture[:, ffn_cols:])
    hidden_low = hidden.astype(jnp.bfloat16)
    ffn_branch = lax.psum(
        times_transposed(hidden_low, down_weight).astype(jnp.bfloat16), "tp"
    ).astype(jnp.float32)
    output = (after_cross + gate_ffn * ffn_branch).astype(jnp.bfloat16)
    upstream = cotangent.astype(jnp.float32)
    grad_gate_ffn = upstream * ffn_branch
    grad_ffn = (upstream * gate_ffn).astype(jnp.bfloat16)
    down_part = over_tokens(grad_ffn, hidden_low)
    grad_hidden = jnp.dot(grad_ffn, down_weight, preferred_element_type=jnp.float32)
    grad_value, grad_gating = gating_back(grad_hidden)
    grad_mixture = jnp.concatenate([grad_value, grad_gating], axis=1).astype(jnp.bfloat16)
    rim_back = swapped(
        jnp.where(first_half, grad_mixture[-rim_depth:], grad_mixture[:rim_depth]), "seq", 0
    )
    grad_padded = jnp.concatenate(
        [
            jnp.where(first_half, zero_rim, rim_back),
            grad_mixture,
            jnp.where(first_half, rim_back, zero_rim),
        ],
        axis=0,
    )
    grad_mix_wide = grad_mixture.astype(jnp.float32)
    grad_activated = jnp.zeros_like(up_proj)
    tap_grads = []
    for tap_index in range(9):
        row_step = tap_index // 3 - 1
        col_step = tap_index % 3 - 1
        offset = row_step * row_width + col_step
        source = lax.dynamic_slice_in_dim(grad_padded, rim_depth - offset, tokens_here, 0)
        grad_activated = (
            grad_activated
            + jnp.where(inside(-row_step, -col_step)[:, None], source.astype(jnp.float32), 0.0)
            * conv_taps[tap_index]
        )
        shifted = lax.dynamic_slice_in_dim(padded, rim_depth + offset, tokens_here, 0)
        tap_grads.append(
            jnp.sum(
                jnp.where(inside(row_step, col_step)[:, None], shifted.astype(jnp.float32), 0.0)
                * grad_mix_wide,
                axis=0,
            )
        )
    conv_part = jnp.stack(tap_grads)
    sigmoid_up = jax.nn.sigmoid(up_proj)
    grad_up_low = (grad_activated * sigmoid_up * (1.0 + up_proj * (1.0 - sigmoid_up))).astype(
        jnp.bfloat16
    )
    up_part = over_tokens(normed_two_low, grad_up_low).reshape(model_width, 2, ffn_cols)
    grad_norm_two = lax.psum(times_transposed(grad_up_low, up_flat), "tp")
    grad_cross_in, grad_shift_ffn, grad_scale_ffn = norm_two_back(grad_norm_two)
    grad_after_cross = upstream + grad_cross_in
    grad_cross = grad_after_cross.astype(jnp.bfloat16)
    cross_out_part = over_tokens(grad_cross, text_low)
    grad_text_low = (
        jnp.dot(grad_cross, cross_out_weight, preferred_element_type=jnp.float32)
        .astype(jnp.bfloat16)
        .reshape(tokens_here, cross_heads, CROSS_HEAD)
    )
    grad_probs_pair = jnp.einsum(
        "tzd,jszd->tzjs", grad_text_low, text_values, preferred_element_type=jnp.float32
    )
    grad_probs = jnp.where(
        second[:, None, None], grad_probs_pair[:, :, 1], grad_probs_pair[:, :, 0]
    )
    grad_values = jnp.einsum(
        "tzjs,tzd->jszd", probs_pair, grad_text_low, preferred_element_type=jnp.float32
    )
    grad_scores = attn_probs * (
        grad_probs - jnp.sum(attn_probs * grad_probs, axis=-1, keepdims=True)
    )
    grad_scores_pair = grad_scores.astype(jnp.bfloat16)[:, :, None, :] * mask_pair[:, None, :, None]
    grad_queries = (
        jnp.einsum(
            "tzjs,jszd->tzd", grad_scores_pair, text_keys, preferred_element_type=jnp.float32
        )
        * score_scale
    )
    grad_keys = (
        jnp.einsum(
            "tzjs,tzd->jszd", grad_scores_pair, cross_queries, preferred_element_type=jnp.float32
        )
        * score_scale
    )
    grad_query_low = grad_queries.reshape(tokens_here, cross_cols).astype(jnp.bfloat16)
    cross_q_part = over_tokens(after_low, grad_query_low)
    grad_kv_part = jnp.concatenate(
        [grad_keys.reshape(2, context, cross_cols), grad_values.reshape(2, context, cross_cols)],
        axis=2,
    )
    grad_after_attn = grad_after_cross + lax.psum(
        times_transposed(grad_query_low, cross_q_weight), "tp"
    )
    early_group = None
    grad_gate_attn = grad_after_attn * attn_branch
    grad_attn = (grad_after_attn * gate_attn).astype(jnp.bfloat16)
    attn_out_part = over_tokens(grad_attn, attended_low)
    grad_attended = jnp.dot(grad_attn, attn_out_weight, preferred_element_type=jnp.float32).reshape(
        tokens_here, self_heads, HEAD
    )
    grad_numer = grad_attended / denominator[:, :, None]
    grad_denom = -jnp.sum(grad_attended * attended, axis=-1) / denominator
    grad_kernel_part = jnp.einsum(
        "it,tzd,tze->izde", image_masks, queries_wide, grad_numer, precision=PRECISE
    )
    grad_total_part = jnp.einsum(
        "it,tzd,tz->izd", image_masks, queries_wide, grad_denom, precision=PRECISE
    )
    grad_kv_send = jnp.where(first_half, grad_kv_part[1], grad_kv_part[0])
    kernel_back_other, total_back_other, grad_kv_other = (
        swapped(grad_kernel_part.astype(jnp.bfloat16), "seq", 0).astype(grad_kernel_part.dtype),
        swapped(grad_total_part.astype(jnp.bfloat16), "seq", 0).astype(grad_total_part.dtype),
        swapped(grad_kv_send.astype(jnp.bfloat16), "seq", 0).astype(grad_kv_send.dtype),
    )
    grad_kernels = grad_kernel_part + kernel_back_other
    grad_totals = grad_total_part + total_back_other
    grad_q_pair = (
        jnp.einsum("tze,izde->itzd", grad_numer, kernels, precision=PRECISE)
        + grad_denom[None, :, :, None] * key_totals[:, None]
    )
    values_wide = self_values.astype(jnp.float32)
    keys_wide = self_keys.astype(jnp.float32)
    grad_k_pair = (
        jnp.einsum("tze,izde->itzd", values_wide, grad_kernels, precision=PRECISE)
        + grad_totals[:, None]
    )
    grad_v_pair = jnp.einsum("tzd,izde->itze", keys_wide, grad_kernels, precision=PRECISE)
    grad_q_self = jax.nn.sigmoid(projected[:, 0]) * by_image(second, grad_q_pair)
    grad_k_self = jax.nn.sigmoid(projected[:, 1]) * by_image(second, grad_k_pair)
    grad_v_self = by_image(second, grad_v_pair)
    grad_projected = (
        jnp.stack([grad_q_self, grad_k_self, grad_v_self], axis=1)
        .reshape(tokens_here, 3 * self_cols)
        .astype(jnp.bfloat16)
    )
    qkv_part = over_tokens(normed_low, grad_projected).reshape(model_width, 3, self_cols)
    grad_normed = lax.psum(
        times_transposed(grad_projected, qkv_flat).astype(jnp.bfloat16), "tp"
    ).astype(jnp.float32)
    grad_inputs_norm, grad_shift_attn, grad_scale_attn = norm_back(grad_normed)
    input_grad = grad_after_attn + grad_inputs_norm
    token_grads = (
        grad_shift_attn,
        grad_scale_attn,
        grad_gate_attn,
        grad_shift_ffn,
        grad_scale_ffn,
        grad_gate_ffn,
    )
    image_grads = jnp.stack(
        [jnp.dot(image_masks, member, precision=PRECISE) for member in token_grads], axis=1
    )
    mod_table = lax.dynamic_update_slice_in_dim(
        jnp.zeros((seq_count, 6, model_width), jnp.float32), image_grads, 2 * pair_index, 0
    )
    grad_kv_own = jnp.where(first_half, grad_kv_part[0], grad_kv_part[1]) + grad_kv_other
    ckv_part = over_tokens(text_rows, grad_kv_own.astype(jnp.bfloat16)).reshape(
        model_width, 2, cross_cols
    )
    conv_grad = lax.psum(conv_part, "seq").reshape(9, 2, ffn_cols)
    late_group = sum_weights(qkv_part, attn_out_part, ckv_part, mod_table)
    early_group = sum_weights(up_part, down_part, cross_out_part, cross_q_part)
    return (
        output,
        input_grad,
        late_group[3],
        late_group[0],
        late_group[1],
        early_group[3],
        late_group[2],
        early_group[2],
        early_group[0],
        conv_grad,
        early_group[1],
    )


def solution(mesh):
    placed = (
        P("seq", None),
        P("seq", None),
        P("seq", None, None),
        P("seq", None, None),
        P(),
        P(),
        P(None, None, "tp"),
        P(None, "tp"),
        P(None, "tp"),
        P(None, None, "tp"),
        P(None, "tp"),
        P(None, None, "tp"),
        P(None, None, "tp"),
        P(None, "tp"),
    )
    return jax.shard_map(
        shards,
        mesh=mesh,
        in_specs=placed,
        out_specs=(
            P("seq", None),
            P("seq", None),
            P("seq", None, None),
            P("seq", None, "tp"),
            P("seq", "tp"),
            P("seq", "tp"),
            P("seq", None, "tp"),
            P("seq", "tp"),
            P("seq", None, "tp"),
            P(None, None, "tp"),
            P("seq", "tp"),
        ),
        check_vma=False,
    )
```

profile of v0, /device:TPU:8, one launch (start us, length us, event | category | flops | bytes accessed | tf_op | source)
XLA Modules:
  0.0 1170.2 jit_solution(15831874492948904068)
XLA Ops:
  13.6 4.1 fusion.73
  26.4 2.6 fusion.206
  29.3 2.3 convolution_convert_fusion.2
  40.0 103.2 %all-reduce.12.cloned.1.call-done = f32[640,1152]{1,0:T(8,128)} async-done(((f32[640,1152]{1,0:T(8,128)}), f32[640,1152]{1,0:T(8,128)}) %all-reduce.12.cloned.1.call-update) | async-done | bytes 2949136 | tf_op jit(solution)/shard_map/psum | solution.py:160
  143.3 2.9 fusion.71
  154.3 2.6 fusion.207
  159.1 2.5 and_and_fusion.8
  161.7 2.6 and_and_fusion.5
  165.8 105.0 %all-reduce.14.cloned.1.call-done = f32[640,1152]{1,0:T(8,128)} async-done(((f32[640,1152]{1,0:T(8,128)}), f32[640,1152]{1,0:T(8,128)}) %all-reduce.14.cloned.1.call-update) | async-done | bytes 2949136 | tf_op jit(solution)/shard_map/psum | solution.py:185
  270.8 4.1 multiply_reduce_fusion.1
  275.1 5.0 multiply_convert_fusion
  301.1 3.1 pad_maximum_fusion.1
  304.5 13.0 %multiply_add_fusion = f32[640,1440]{0,1:T(8,128)S(1)} fusion(bf16[640,1440]{0,1:T(8,128)(2,1)S(1)} %copy-done.26, bf16[33,1440]{0,1:T(8,128)(2,1)S(1)} %get-tuple-element.79, bf16[33,1440]{0,1:T(8,128)(2,1)S(1)} %get-tuple-element.78, f32[1440]{0:T(1024)S(1)} %copy-done.121, f32[1440]{0:T(1024)S(1)} %copy-done.119, f32[1440]{0:T(1024)S(1)} %copy-done.117, ...), kind=kLoop, calls=%fused_computation.44 | loop fusion | flops 37785600 | bytes 16836504 | tf_op jit(solution)/shard_map/add | solution.py:210
  317.6 3.2 fusion.68
  327.2 3.2 pad_maximum_fusion.2
  330.7 16.5 %fusion.8 = bf16[640,1440]{0,1:T(8,128)(2,1)S(1)} fusion(f32[640,1440]{0,1:T(8,128)S(1)} %copy-done.46, bf16[33,1440]{0,1:T(8,128)(2,1)S(1)} %get-tuple-element.77, bf16[640,720]{0,1:T(8,128)(2,1)S(1)} %copy-done.20, bf16[640,720]{0,1:T(8,128)(2,1)S(1)} %copy-done.23, bf16[33,1440]{0,1:T(8,128)(2,1)S(1)} %get-tuple-element.76, ...), kind=kLoop, calls=%fused_computation.32 | loop fusion | flops 52531200 | bytes 18679704 | tf_op jit(solution)/shard_map/convert_element_type | solution.py:261
  348.4 4.4 fusion.208
  353.2 113.6 %all-reduce.16.cloned.1.call-done = f32[640,1152]{1,0:T(8,128)} async-done(((f32[640,1152]{1,0:T(8,128)}), f32[640,1152]{1,0:T(8,128)}) %all-reduce.16.cloned.1.call-update) | async-done | bytes 2949136 | tf_op jit(solution)/shard_map/psum | solution.py:265
  466.8 2.7 multiply_reduce_fusion
  479.3 2.6 fusion.209
  482.0 4.3 convolution_convert_fusion.1
  486.3 109.4 %all-reduce.18.cloned.1.call-done = f32[640,1152]{1,0:T(8,128)} async-done(((f32[640,1152]{1,0:T(8,128)}), f32[640,1152]{1,0:T(8,128)}) %all-reduce.18.cloned.1.call-update) | async-done | bytes 2949136 | tf_op jit(solution)/shard_map/psum | solution.py:306
  595.8 3.1 add.631
  610.2 3.0 convolution_convert_fusion
  614.2 2.8 convolution_bitcast_fusion.5
  620.5 5.4 fusion.188
  625.9 12.2 %copy.89 = f32[1152,2,720]{2,1,0:T(2,128)} copy(f32[1152,2,720]{0,2,1:T(8,128)} %bitcast.346) | data formatting | bytes 13271040 | tf_op jit(solution)/shard_map/reshape | solution.py:264
  638.1 4.2 fusion.132
  642.4 7.2 copy.88
  649.6 77.8 %all-reduce.22.cloned.1.call-done = (bf16[640,1152]{1,0:T(8,128)(2,1)}, bf16[640,1152]{1,0:T(8,128)(2,1)}) async-done(((bf16[640,1152]{1,0:T(8,128)(2,1)}, bf16[640,1152]{1,0:T(8,128)(2,1)}), (bf16[640,1152]{1,0:T(8,128)(2,1)}, bf16[640,1152]{1,0:T(8,128)(2,1)})) %all-reduce.22.cloned.1.call-update) | async-done | bytes 2949136 | tf_op jit(solution)/shard_map/psum | solution.py:216
  729.7 3.7 fusion.55
  733.4 3.7 fusion.51
  743.3 3.6 fusion.139
  751.4 3.9 fusion.210
  755.4 2.3 fusion.182
  757.9 6.8 fusion.75
  766.6 9.6 fusion.14
  776.3 13.3 %fusion.17 = (f32[1440]{0:T(1024)S(1)}, f32[1440]{0:T(1024)S(1)}, f32[1440]{0:T(1024)S(1)}, f32[1440]{0:T(1024)S(1)}, f32[1440]{0:T(1024)S(1)}, /*index=5*/f32[1440]{0:T(1024)S(1)}) fusion(pred[640]{0:T(1024)(128)(4,1)S(1)} %copy-done.153, bf16[706,1440]{0,1:T(8,128)(2,1)S(1)} %copy-done.3, s32[]{:T(128)S(6)} %select_n.472, ...), kind=kLoop, calls=%fused_computation.41 | loop fusion | flops 25796160 | bytes 12940824 | tf_op jit(solution)/shard_map/reduce_sum | solution.py:253
  789.9 26.5 %psum.55 = f32[9,2,720]{2,1,0:T(2,128)} all-reduce(f32[9,2,720]{2,1,0:T(2,128)S(1)} %reshape.422), channel_id=1, replica_groups=mesh['seq'=8,'tp'=4] {'seq'}, use_global_device_ids=true, to_apply=%region_30.31 | all-reduce | flops 12960 | bytes 103680 | tf_op jit(solution)/shard_map/psum | solution.py:375
  816.4 67.7 %all-reduce.20.cloned.1.call-done = (f32[1152,2,288]{2,1,0:T(2,128)}, f32[1152,2,720]{2,1,0:T(2,128)}) async-done(((f32[1152,2,288]{2,1,0:T(2,128)}, f32[1152,2,720]{2,1,0:T(2,128)}), (f32[1152,2,288]{2,1,0:T(2,128)}, f32[1152,2,720]{2,1,0:T(2,128)})) %all-reduce.20.cloned.1.call-update) | async-done | bytes 9289744
  886.2 2.4 constant_dynamic-slice_fusion.2
  889.6 5.4 fusion.38
  895.0 25.3 %reduce-scatter.19.cloned.1.call-done = f32[1,6,1152]{2,1,0:T(8,128)} async-done(((f32[8,6,1152]{2,1,0:T(8,128)}), f32[1,6,1152]{2,1,0:T(8,128)}) %reduce-scatter.19.cloned.1.call-update) | async-done | bytes 27664
  921.6 50.8 %reduce-scatter.17.cloned.1.call-done = f32[144,720]{1,0:T(8,128)} async-done(((f32[1152,720]{1,0:T(8,128)}), f32[144,720]{1,0:T(8,128)}) %reduce-scatter.17.cloned.1.call-update) | async-done | bytes 414736 | tf_op jit(solution)/shard_map/reduce_scatter | solution.py:52
  972.4 43.4 %reduce-scatter.15.cloned.1.call-done = f32[144,288]{1,0:T(8,128)} async-done(((f32[1152,288]{1,0:T(8,128)}), f32[144,288]{1,0:T(8,128)}) %reduce-scatter.15.cloned.1.call-update) | async-done | bytes 165904 | tf_op jit(solution)/shard_map/reduce_scatter | solution.py:53
  1015.8 43.2 %reduce-scatter.13.cloned.1.call-done = f32[144,288]{1,0:T(8,128)} async-done(((f32[1152,288]{1,0:T(8,128)}), f32[144,288]{1,0:T(8,128)}) %reduce-scatter.13.cloned.1.call-update) | async-done | bytes 165904 | tf_op jit(solution)/shard_map/reduce_scatter | solution.py:54
  1059.0 43.4 %reduce-scatter.11.cloned.1.call-done = f32[144,288]{1,0:T(8,128)} async-done(((f32[1152,288]{1,0:T(8,128)}), f32[144,288]{1,0:T(8,128)}) %reduce-scatter.11.cloned.1.call-update) | async-done | bytes 165904 | tf_op jit(solution)/shard_map/reduce_scatter | solution.py:52
  1102.4 60.8 %reduce-scatter.9.cloned.1.call-done = f32[144,3,288]{2,0,1:T(8,128)} async-done(((f32[1152,3,288]{2,0,1:T(8,128)}), f32[144,3,288]{2,0,1:T(8,128)}) %reduce-scatter.9.cloned.1.call-update) | async-done | bytes 497680 | tf_op jit(solution)/shard_map/reduce_scatter | solution.py:51
  (513 shorter events, 97.4 us)
Async XLA Ops:
  7.2 267.8 %copy-start = (bf16[1152,2,720]{0,2,1:T(8,128)(2,1)S(1)}, bf16[1152,2,720]{0,2,1:T(8,128)(2,1)}, u32[]{:S(2)}) copy-start(bf16[1152,2,720]{0,2,1:T(8,128)(2,1)} %param.25) | copy-start | bytes 9953284
  7.2 136.1 %all-reduce.12.cloned.1.call-start = ((), (), s32[]{:S(2)}) async-start(), calls=%async_computation.6 | async-start | bytes 5898240 | tf_op jit(solution)/shard_map/psum | solution.py:160
  7.2 4.7 collective-permute-start
  10.1 22.4 %copy-start.76 = (f32[1,640]{1,0:T(1,128)}, f32[1,640]{1,0:T(1,128)S(1)}, u32[]{:S(2)}) copy-start(f32[1,640]{1,0:T(1,128)S(1)} %broadcast_subtract_fusion) | copy-start | bytes 7684
  10.2 22.4 %copy-start.78 = (f32[1,640]{1,0:T(1,128)}, f32[1,640]{1,0:T(1,128)S(1)}, u32[]{:S(2)}) copy-start(f32[1,640]{1,0:T(1,128)S(1)} %compare_convert_fusion) | copy-start | bytes 7684
  12.0 13.5 %copy-start.80 = (pred[640]{0:T(1024)(128)(4,1)}, pred[640]{0:T(1024)(128)(4,1)S(1)}, u32[]{:S(2)}) copy-start(pred[640]{0:T(1024)(128)(4,1)S(1)} %fusion.165) | copy-start | bytes 1924
  19.8 1.4 collective-permute-start.2
  21.1 1.6 collective-permute-start.1
  29.1 241.8 %all-reduce.14.cloned.1.call-start = ((), (), s32[]{:S(2)}) async-start(), calls=%async_computation.7 | async-start | bytes 5898240 | tf_op jit(solution)/shard_map/psum | solution.py:185
  31.7 2.9 collective-permute-start.3
  156.9 309.9 %all-reduce.16.cloned.1.call-start = ((), (), s32[]{:S(2)}) async-start(), calls=%async_computation.8 | async-start | bytes 5898240 | tf_op jit(solution)/shard_map/psum | solution.py:265
  282.3 17.7 %collective-permute-start.4 = (bf16[33,1440]{0,1:T(8,128)(2,1)}, bf16[33,1440]{0,1:T(8,128)(2,1)}, u32[]{:S(2)}, u32[]{:S(2)}) collective-permute-start(bf16[33,1440]{0,1:T(8,128)(2,1)} %slice_select_fusion), channel_id=1, source_target_pairs={{0,4},{4,0},{8,12},{12,8},{16,20},{20,16},{24,28},{28,24},{1,5},{5... | collective-permute-start | bytes 285128 | tf_op jit(solution)/shard_map/ppermute | solution.py:25
  301.1 16.4 %copy-start.44 = (bf16[33,1440]{0,1:T(8,128)(2,1)}, bf16[33,1440]{0,1:T(8,128)(2,1)S(1)}, u32[]{:S(2)}) copy-start(bf16[33,1440]{0,1:T(8,128)(2,1)S(1)} %get-tuple-element.78) | copy-start | bytes 285124
  301.1 16.4 %copy-start.45 = (bf16[33,1440]{0,1:T(8,128)(2,1)}, bf16[33,1440]{0,1:T(8,128)(2,1)S(1)}, u32[]{:S(2)}) copy-start(bf16[33,1440]{0,1:T(8,128)(2,1)S(1)} %get-tuple-element.79) | copy-start | bytes 285124
  304.2 13.3 %copy-start.2 = (bf16[706,1440]{0,1:T(8,128)(2,1)}, bf16[706,1440]{0,1:T(8,128)(2,1)S(1)}, u32[]{:S(2)}) copy-start(bf16[706,1440]{0,1:T(8,128)(2,1)S(1)} %pad_maximum_fusion.1) | copy-start | bytes 6099844
  304.4 13.1 %copy-start.34 = (bf16[640,1152]{1,0:T(8,128)(2,1)S(1)}, bf16[640,1152]{1,0:T(8,128)(2,1)}, u32[]{:S(2)}) copy-start(bf16[640,1152]{1,0:T(8,128)(2,1)} %param.15) | copy-start | bytes 4423684
  304.4 13.1 %copy-start.83 = (pred[640]{0:T(1024)(128)(4,1)S(1)}, pred[640]{0:T(1024)(128)(4,1)}, u32[]{:S(2)}) copy-start(pred[640]{0:T(1024)(128)(4,1)} %copy-done.80) | copy-start | bytes 1924
  304.4 13.1 %copy-start.132 = (f32[1152]{0:T(1024)S(1)}, f32[1152]{0:T(1024)}, u32[]{:S(2)}) copy-start(f32[1152]{0:T(1024)} %get-tuple-element.31) | copy-start | bytes 13828
  304.5 13.1 %copy-start.134 = (f32[1152]{0:T(1024)S(1)}, f32[1152]{0:T(1024)}, u32[]{:S(2)}) copy-start(f32[1152]{0:T(1024)} %get-tuple-element.36) | copy-start | bytes 13828
  304.5 13.1 %copy-start.179 = (bf16[1152,720]{0,1:T(8,128)(2,1)S(1)}, bf16[1152,720]{0,1:T(8,128)(2,1)}, u32[]{:S(2)}) copy-start(bf16[1152,720]{0,1:T(8,128)(2,1)} %param.27) | copy-start | bytes 4976644
  322.7 3.3 collective-permute-start.5
  352.9 113.9 %copy-start.6 = (f32[640,1152]{1,0:T(8,128)S(1)}, f32[640,1152]{1,0:T(8,128)}, u32[]{:S(2)}) copy-start(f32[640,1152]{1,0:T(8,128)} %copy-done.5) | copy-start | bytes 8847364
  352.9 113.9 %copy-start.84 = (pred[640]{0:T(1024)(128)(4,1)S(1)}, pred[640]{0:T(1024)(128)(4,1)}, u32[]{:S(2)}) copy-start(pred[640]{0:T(1024)(128)(4,1)} %copy-done.80) | copy-start | bytes 1924
  352.9 116.6 %copy-start.124 = (f32[640]{0:T(1024)S(1)}, f32[640]{0:T(1024)}, u32[]{:S(2)}) copy-start(f32[640]{0:T(1024)} %copy-done.123) | copy-start | bytes 7684
  352.9 116.7 %copy-start.100 = (f32[1152]{0:T(1024)S(1)}, f32[1152]{0:T(1024)}, u32[]{:S(2)}) copy-start(f32[1152]{0:T(1024)} %get-tuple-element.34) | copy-start | bytes 13828
  352.9 116.7 %copy-start.103 = (f32[1152]{0:T(1024)S(1)}, f32[1152]{0:T(1024)}, u32[]{:S(2)}) copy-start(f32[1152]{0:T(1024)} %get-tuple-element.35) | copy-start | bytes 13828
  352.9 116.7 %copy-start.130 = (f32[640]{0:T(1024)S(1)}, f32[640]{0:T(1024)}, u32[]{:S(2)}) copy-start(f32[640]{0:T(1024)} %copy-done.129) | copy-start | bytes 7684
  352.9 242.8 %all-reduce.18.cloned.1.call-start = ((), (), s32[]{:S(2)}) async-start(), calls=%async_computation.9 | async-start | bytes 5898240 | tf_op jit(solution)/shard_map/psum | solution.py:306
  481.9 245.5 %all-reduce.22.cloned.1.call-start = ((), (), s32[]{:S(2)}) async-start(), calls=%async_computation.17 | async-start | bytes 5898240 | tf_op jit(solution)/shard_map/psum | solution.py:216
  486.3 112.5 %copy-start.86 = (pred[640]{0:T(1024)(128)(4,1)S(1)}, pred[640]{0:T(1024)(128)(4,1)}, u32[]{:S(2)}) copy-start(pred[640]{0:T(1024)(128)(4,1)} %copy-done.80) | copy-start | bytes 1924
  486.3 112.6 %copy-start.89 = (f32[1152]{0:T(1024)S(1)}, f32[1152]{0:T(1024)}, u32[]{:S(2)}) copy-start(f32[1152]{0:T(1024)} %get-tuple-element.41) | copy-start | bytes 13828
  486.3 112.6 %copy-start.90 = (f32[1152]{0:T(1024)S(1)}, f32[1152]{0:T(1024)}, u32[]{:S(2)}) copy-start(f32[1152]{0:T(1024)} %get-tuple-element.42) | copy-start | bytes 13828
  603.1 3.8 collective-permute-start.6
  604.9 1.9 collective-permute-start.7
  613.2 270.9 %all-reduce.20.cloned.1.call-start = ((), (), s32[]{:S(2)}) async-start(), calls=%async_computation.16 | async-start | bytes 21233664
  620.4 17.7 %collective-permute-start.8 = (bf16[300,576]{0,1:T(8,128)(2,1)}, bf16[300,576]{0,1:T(8,128)(2,1)}, u32[]{:S(2)}, u32[]{:S(2)}) collective-permute-start(bf16[300,576]{0,1:T(8,128)(2,1)} %fusion.135), channel_id=1, source_target_pairs={{0,4},{4,0},{8,12},{12,8},{16,20},{20,16},{24,28},{28,24},{1,5},{5... | collective-permute-start | bytes 1036808 | tf_op jit(solution)/shard_map/ppermute | solution.py:25
  649.6 80.1 %copy-start.126 = (f32[640]{0:T(1024)S(1)}, f32[640]{0:T(1024)}, u32[]{:S(2)}) copy-start(f32[640]{0:T(1024)} %copy-done.125) | copy-start | bytes 7684
  649.6 270.6 %reduce-scatter.19.cloned.1.call-start = ((), (), s32[]{:S(2)}) async-start(), calls=%async_computation.15 | async-start | bytes 331776
  743.2 229.2 %reduce-scatter.17.cloned.1.call-start = ((), (), s32[]{:S(2)}) async-start(), calls=%async_computation.14 | async-start | bytes 3981312 | tf_op jit(solution)/shard_map/reduce_scatter | solution.py:52
  746.9 268.8 %reduce-scatter.15.cloned.1.call-start = ((), (), s32[]{:S(2)}) async-start(), calls=%async_computation.13 | async-start | bytes 1990656 | tf_op jit(solution)/shard_map/reduce_scatter | solution.py:53
  751.1 307.8 %reduce-scatter.13.cloned.1.call-start = ((), (), s32[]{:S(2)}) async-start(), calls=%async_computation.12 | async-start | bytes 1990656 | tf_op jit(solution)/shard_map/reduce_scatter | solution.py:54
  755.3 347.0 %reduce-scatter.11.cloned.1.call-start = ((), (), s32[]{:S(2)}) async-start(), calls=%async_computation.11 | async-start | bytes 1990656 | tf_op jit(solution)/shard_map/reduce_scatter | solution.py:52
  757.8 405.4 %reduce-scatter.9.cloned.1.call-start = ((), (), s32[]{:S(2)}) async-start(), calls=%async_computation.10 | async-start | bytes 5971968 | tf_op jit(solution)/shard_map/reduce_scatter | solution.py:51
  764.7 11.5 copy-start.3
  789.6 99.0 %copy-start.10 = (bf16[640,1152]{1,0:T(8,128)(2,1)S(1)}, bf16[640,1152]{1,0:T(8,128)(2,1)}, u32[]{:S(2)}) copy-start(bf16[640,1152]{1,0:T(8,128)(2,1)} %param.14) | copy-start | bytes 4423684
  789.6 99.0 %copy-start.17 = (bf16[640,1152]{1,0:T(8,128)(2,1)S(1)}, bf16[640,1152]{1,0:T(8,128)(2,1)}, u32[]{:S(2)}) copy-start(bf16[640,1152]{1,0:T(8,128)(2,1)} %get-tuple-element.46) | copy-start | bytes 4423684
  789.8 99.7 %copy-start.128 = (f32[640]{0:T(1024)S(1)}, f32[640]{0:T(1024)}, u32[]{:S(2)}) copy-start(f32[640]{0:T(1024)} %copy-done.127) | copy-start | bytes 7684
  889.6 273.6 %copy-start.1 = (bf16[1152,2,720]{0,2,1:T(8,128)(2,1)S(1)}, bf16[1152,2,720]{0,2,1:T(8,128)(2,1)}, u32[]{:S(2)}) copy-start(bf16[1152,2,720]{0,2,1:T(8,128)(2,1)} %param.25) | copy-start | bytes 9953284
  (158 other events, 575.8 us)
Sparse Core Ops, SparseCore 0:
  29.2 114.0 all-reduce.11
  157.0 113.7 all-reduce.13
  353.0 113.7 all-reduce.15
  482.0 113.7 all-reduce.17
  613.3 114.0 all-reduce.21
  731.4 152.6 all-reduce.19
  887.2 32.9 reduce-scatter.18
  924.3 48.0 reduce-scatter.16
  976.3 39.3 reduce-scatter.14
  1019.5 39.4 reduce-scatter.12
  1062.9 39.4 reduce-scatter.10
  1106.2 56.9 reduce-scatter.8
where the time goes:
time: 1180 us; the launch traced here: 1170 us
  waiting for transfers between devices  845 us (72%)
  other arithmetic  101 us (9%)
  matrix products  96.4 us (8%)
  local copies, waits for them, and re-layouts  69.6 us (6%)
  between operations  27.9 us (2%)
  blocking collectives  26.5 us (2%)
    psum x1, waiting for transfers between devices, shards(): grad_norm_two = lax.psum(times_transposed(grad_up_low, up_flat), 'tp')  114 us
    psum x1, waiting for transfers between devices, shards(): lax.psum(times_transposed(grad_query_low, cross_q_weight), 'tp')  109 us
    psum x1, waiting for transfers between devices, shards(): cross_branch = lax.psum(times_transposed(text_low, cross_out_weight), 'tp')  105 us
    psum x1, waiting for transfers between devices, shards(): lax.psum(times_transposed(attended_low, attn_out_weight), 'tp')  103 us
    reduce_scatter x2, waiting for transfers between devices, sum_weights(): lax.psum_scatter(second_grad, 'seq', scatter_dimension=0, tiled=True)  94.1 us
    unnamed x14, waiting for transfers between devices  93.2 us
    psum x1, waiting for transfers between devices, shards(): lax.psum(times_transposed(hidden_low, down_weight).astype(jnp.bfloat16),...  77.8 us
    reduce_scatter x1, waiting for transfers between devices, sum_weights(): lax.psum_scatter(first_grad, 'seq', scatter_dimension=0, tiled=True)  60.8 us
  transfers between devices with their start and end apart: 21, of which 13 were waited for; matrix products, arithmetic and copies ran while one was open for 12% of the time, Pallas kernels for 0%

commit v1 on v0

v1 whole, which is shorter than its diff:
```python
import math

import jax
import jax.numpy as jnp
from jax import lax
from jax.sharding import PartitionSpec as P

HEAD = 32
CROSS_HEAD = 72
MAXW = 32


EPSILON = 1e-06
PRECISE = lax.Precision.HIGHEST
MASKED_OUT = -1e30
LOW = jnp.bfloat16
WIDE = jnp.float32


def swapped(block, axis, apart):
    count = lax.axis_size(axis)
    route = [(low, low ^ (1 << apart)) for low in range(count)]
    return lax.ppermute(block, axis, route)


def from_behind(block, step):
    count = lax.axis_size("tp")
    return lax.ppermute(block, "tp", [(k, (k + step) % count) for k in range(count)])


def from_ahead(block, step):
    count = lax.axis_size("tp")
    return lax.ppermute(block, "tp", [(k, (k - step) % count) for k in range(count)])


def bit_of(index, place):
    return (index >> place) & 1


def modulated_norm(inputs, shifts, scales):
    inverse = lax.rsqrt(jnp.mean(inputs * inputs, axis=-1, keepdims=True) + EPSILON)
    return inputs * inverse * (1.0 + scales) + shifts


def glu_product(value_in, gate_in):
    return value_in * jax.nn.silu(gate_in)


def times_transposed(left_side, right_side):
    return lax.dot_general(
        left_side, right_side, (((1,), (1,)), ((), ())), preferred_element_type=WIDE
    )


def over_tokens(left_side, right_side):
    return lax.dot_general(
        left_side, right_side, (((0,), (0,)), ((), ())), preferred_element_type=WIDE
    )


def by_image(second, pair_values):
    return jnp.where(
        second.reshape((-1,) + (1,) * (pair_values.ndim - 2)), pair_values[1], pair_values[0]
    )


def keep_and_send(grid, bit, axis):
    keep = lax.dynamic_index_in_dim(grid, bit, axis, keepdims=False)
    send = lax.dynamic_index_in_dim(grid, 1 - bit, axis, keepdims=False)
    return keep, send


def halved(grid, index, place, axis):
    keep, send = keep_and_send(grid, bit_of(index, place), axis)
    return keep + swapped(send.astype(LOW), "seq", place).astype(WIDE)


def sum_rows(grad):
    count = lax.axis_size("seq")
    index = lax.axis_index("seq")
    places = count.bit_length() - 1
    rows, columns = grad.shape
    own = rows // count
    grid = grad.reshape((2,) * places + (own, columns))
    grid = halved(grid, index, 0, places - 1)
    halves = []
    for part in range(2):
        order = list(range(1, places))
        if part:
            order = order[1:] + order[:1]
        piece = lax.slice_in_dim(
            grid, part * (own // 2), (part + 1) * (own // 2), axis=places - 1
        )
        left = list(range(places - 1, 0, -1))
        for place in order:
            piece = halved(piece, index, place, left.index(place))
            left.remove(place)
        halves.append(piece)
    return jnp.concatenate(halves, axis=0)


def gather_shards(weight, flip):
    index = lax.axis_index("seq")
    rows, columns = weight.shape
    own = rows // 8
    eighth = lax.dynamic_slice_in_dim(weight, (index % 8) * own, own, 0)
    shards = [weight]
    for step in range(1, lax.axis_size("tp")):
        piece = from_behind(eighth, step)[None]
        order = (1, 2) if (step + flip) % 2 else (2, 1)
        grid = piece.reshape(1, 1, 1, own, columns)
        for place in (*order, 0):
            axis = 2 - place
            other = swapped(grid, "seq", place)
            first = bit_of(index, place) == 0
            grid = jnp.where(
                first,
                jnp.concatenate([grid, other], axis=axis),
                jnp.concatenate([other, grid], axis=axis),
            )
        shards.append(grid.reshape(rows, columns))
    return shards


def gather_blocks(block):
    count = lax.axis_size("tp")
    place = lax.axis_index("tp")
    result = jnp.zeros((count,) + block.shape, block.dtype)
    result = lax.dynamic_update_index_in_dim(result, block, place, 0)
    for step in range(1, count):
        result = lax.dynamic_update_index_in_dim(
            result, from_behind(block, step), (place - step) % count, 0
        )
    return result.reshape((count * block.shape[0],) + block.shape[1:])


def token_block(values, place):
    count = lax.axis_size("tp")
    size = values.shape[0] // count
    return lax.dynamic_slice_in_dim(values, (place % count) * size, size, 0)


def scatter_product(left_side, right_side):
    count = lax.axis_size("tp")
    place = lax.axis_index("tp")
    sent = [
        from_behind(
            times_transposed(token_block(left_side, place + step), right_side).astype(LOW), step
        )
        for step in range(1, count)
    ]
    total = times_transposed(token_block(left_side, place), right_side)
    for piece in sent:
        total = total + piece.astype(WIDE)
    return total


def same_everywhere(block):
    pair = block + swapped(block, "tp", 0)
    return pair + swapped(pair, "tp", 1)


def shards(
    hidden_in,
    cotangent,
    modulation,
    text_states,
    image_shapes,
    text_lengths,
    qkv_weight,
    attn_out_weight,
    cross_q_weight,
    cross_kv_weight,
    cross_out_weight,
    up_weight,
    conv_weight,
    down_weight,
):
    tokens_here, model_width = hidden_in.shape
    context = text_states.shape[1]
    self_cols = qkv_weight.shape[2]
    cross_cols = cross_q_weight.shape[1]
    ffn_cols = up_weight.shape[2]
    self_heads = self_cols // HEAD
    cross_heads = cross_cols // CROSS_HEAD
    score_scale = 1.0 / math.sqrt(CROSS_HEAD)
    rim_depth = MAXW + 1
    tp_count = lax.axis_size("tp")
    tp_index = lax.axis_index("tp")
    block_size = tokens_here // tp_count
    seq_index = lax.axis_index("seq")
    first_half = seq_index % 2 == 0
    pair_index = seq_index // 2
    pair_shapes = lax.dynamic_slice_in_dim(image_shapes, 2 * pair_index, 2, 0)
    pair_lengths = lax.dynamic_slice_in_dim(text_lengths, 2 * pair_index, 2, 0)
    row_width = pair_shapes[0, 1]
    size_first = pair_shapes[0, 0] * row_width
    places = jnp.arange(tokens_here, dtype=jnp.int32) + jnp.where(first_half, 0, tokens_here)
    second = places >= size_first
    within = places - jnp.where(second, size_first, 0)
    row_index = within // row_width
    col_index = within % row_width
    height = jnp.where(second, pair_shapes[1, 0], pair_shapes[0, 0])
    second_float = second.astype(WIDE)
    image_masks = jnp.stack([1.0 - second_float, second_float])
    mask_low = image_masks.astype(LOW)
    block_second = token_block(second, tp_index)
    block_float = block_second.astype(WIDE)[:, None]

    def inside(row_step, col_step):
        return (
            (row_index + row_step >= 0)
            & (row_index + row_step < height)
            & (col_index + col_step >= 0)
            & (col_index + col_step < row_width)
        )

    text_rows = text_states[0]
    kv_own = jnp.dot(
        text_rows,
        cross_kv_weight.reshape(model_width, 2 * cross_cols),
        preferred_element_type=WIDE,
    ).astype(LOW)
    mod_own = modulation[0]
    mod_other = swapped(mod_own, "seq", 0)
    mod_pair = jnp.where(
        first_half, jnp.stack([mod_own, mod_other]), jnp.stack([mod_other, mod_own])
    ).astype(WIDE)

    out_shards = gather_shards(attn_out_weight, 0)
    query_shards = gather_shards(cross_q_weight, 1)
    kv_shards = jnp.stack([kv_own] + [from_behind(kv_own, step) for step in range(1, tp_count)])
    cross_shards = gather_shards(cross_out_weight, 0)
    kv_other = swapped(kv_shards, "seq", 0)
    kv_pair = jnp.where(
        first_half,
        jnp.stack([kv_shards, kv_other], axis=1),
        jnp.stack([kv_other, kv_shards], axis=1),
    )

    def per_token(row_pick):
        return jnp.where(second[:, None], mod_pair[1, row_pick], mod_pair[0, row_pick])

    def per_block(row_pick):
        return jnp.where(block_second[:, None], mod_pair[1, row_pick], mod_pair[0, row_pick])

    def image_sums(member):
        late = jnp.sum(member * block_float, axis=0)
        return jnp.stack([jnp.sum(member * (1.0 - block_float), axis=0), late])

    inputs = hidden_in.astype(WIDE)
    gate_ffn = per_token(5)
    normed_low = modulated_norm(inputs, per_token(0), per_token(1)).astype(LOW)
    qkv_flat = qkv_weight.reshape(model_width, 3 * self_cols)
    projected = jnp.dot(normed_low, qkv_flat, preferred_element_type=WIDE).reshape(
        tokens_here, 3, self_heads, HEAD
    )
    self_queries = jax.nn.softplus(projected[:, 0]).astype(LOW)
    self_keys = jax.nn.softplus(projected[:, 1]).astype(LOW)
    self_values = projected[:, 2].astype(LOW)
    masked_keys = self_keys[None] * mask_low[:, :, None, None]
    kernel_part = jnp.einsum(
        "itzd,tze->izde", masked_keys, self_values, preferred_element_type=WIDE
    )
    total_part = jnp.einsum("it,tzd->izd", mask_low, self_keys, preferred_element_type=WIDE)
    kernel_other, total_other = swapped((kernel_part, total_part), "seq", 0)
    kernels = kernel_part + kernel_other
    key_totals = total_part + total_other
    queries_wide = self_queries.astype(WIDE)
    numerators = jnp.einsum("tzd,izde->itze", queries_wide, kernels, precision=PRECISE)
    denominators = jnp.einsum("tzd,izd->itz", queries_wide, key_totals, precision=PRECISE)
    numerator = by_image(second, numerators)
    denominator = by_image(second, denominators) + 1.0
    attended = numerator / denominator[:, :, None]
    attended_low = attended.reshape(tokens_here, self_cols).astype(LOW)

    block_inputs = token_block(hidden_in, tp_index).astype(WIDE)
    block_upstream = token_block(cotangent, tp_index).astype(WIDE)
    attended_blocks = [token_block(attended_low, tp_index)] + [
        from_behind(token_block(attended_low, tp_index + step), step)
        for step in range(1, tp_count)
    ]
    attn_branch = sum(
        times_transposed(block, shard) for block, shard in zip(attended_blocks, out_shards)
    )
    gate_attn = per_block(2)
    after_attn = block_inputs + gate_attn * attn_branch
    after_low = after_attn.astype(LOW)
    query_low = [
        jnp.dot(after_low, shard, preferred_element_type=WIDE).astype(LOW)
        for shard in query_shards
    ]
    heads_all = tp_count * cross_heads
    cross_queries = (
        jnp.stack(query_low)
        .reshape(tp_count, block_size, cross_heads, CROSS_HEAD)
        .transpose(0, 2, 1, 3)
        .reshape(heads_all, block_size, CROSS_HEAD)
    )
    text_kv = (
        kv_pair.reshape(tp_count, 2 * context, 2, cross_heads, CROSS_HEAD)
        .transpose(2, 0, 3, 1, 4)
        .reshape(2, heads_all, 2 * context, CROSS_HEAD)
    )
    text_keys, text_values = text_kv[0], text_kv[1]
    key_place = jnp.arange(2 * context, dtype=jnp.int32)
    key_second = key_place >= context
    key_within = key_place - jnp.where(key_second, context, 0)
    key_length = jnp.where(key_second, pair_lengths[1], pair_lengths[0])
    key_live = (key_within < key_length)[None, :] & (key_second[None, :] == block_second[:, None])
    scores = (
        jnp.einsum("ztd,zsd->zts", cross_queries, text_keys, preferred_element_type=WIDE)
        * score_scale
    )
    masked = jnp.where(key_live[None], scores, MASKED_OUT)
    row_max = jnp.max(masked, axis=-1, keepdims=True)
    exp_scores = jnp.exp(masked - row_max)
    attn_probs = exp_scores / jnp.sum(exp_scores, axis=-1, keepdims=True)
    probs_low = attn_probs.astype(LOW)
    attended_text = jnp.einsum(
        "zts,zsd->ztd", probs_low, text_values, preferred_element_type=WIDE
    ).astype(LOW)

    def to_shards(heads):
        return (
            heads.reshape(tp_count, cross_heads, block_size, CROSS_HEAD)
            .transpose(0, 2, 1, 3)
            .reshape(tp_count, block_size, cross_cols)
        )

    text_low = to_shards(attended_text)
    cross_branch = sum(
        times_transposed(text_low[step], cross_shards[step]) for step in range(tp_count)
    )
    after_cross = after_attn + cross_branch
    normed_two, norm_two_back = jax.vjp(modulated_norm, after_cross, per_block(3), per_block(4))
    normed_two_low = gather_blocks(normed_two.astype(LOW))
    up_flat = up_weight.reshape(model_width, 2 * ffn_cols)
    up_proj = jnp.dot(normed_two_low, up_flat, preferred_element_type=WIDE)
    activated = jax.nn.silu(up_proj).astype(LOW)
    conv_taps = conv_weight.reshape(9, 2 * ffn_cols).astype(WIDE)
    rim_in = swapped(jnp.where(first_half, activated[-rim_depth:], activated[:rim_depth]), "seq", 0)
    zero_rim = jnp.zeros_like(rim_in)
    padded = jnp.concatenate(
        [
            jnp.where(first_half, zero_rim, rim_in),
            activated,
            jnp.where(first_half, rim_in, zero_rim),
        ],
        axis=0,
    )
    mixture = jnp.zeros_like(up_proj)
    for tap_index in range(9):
        row_step = tap_index // 3 - 1
        col_step = tap_index % 3 - 1
        offset = row_step * row_width + col_step
        shifted = lax.dynamic_slice_in_dim(padded, rim_depth + offset, tokens_here, 0)
        mixture = (
            mixture
            + jnp.where(inside(row_step, col_step)[:, None], shifted.astype(WIDE), 0.0)
            * conv_taps[tap_index]
        )
    hidden, gating_back = jax.vjp(glu_product, mixture[:, :ffn_cols], mixture[:, ffn_cols:])
    hidden_low = hidden.astype(LOW)
    upstream = cotangent.astype(WIDE)
    grad_ffn = (upstream * gate_ffn).astype(LOW)
    grad_hidden = jnp.dot(grad_ffn, down_weight, preferred_element_type=WIDE)
    grad_value, grad_gating = gating_back(grad_hidden)
    grad_mixture = jnp.concatenate([grad_value, grad_gating], axis=1).astype(LOW)
    rim_back = swapped(
        jnp.where(first_half, grad_mixture[-rim_depth:], grad_mixture[:rim_depth]), "seq", 0
    )
    ffn_branch = scatter_product(hidden_low, down_weight)
    output_block = (after_cross + per_block(5) * ffn_branch).astype(LOW)
    down_part = over_tokens(grad_ffn, hidden_low)
    grad_padded = jnp.concatenate(
        [
            jnp.where(first_half, zero_rim, rim_back),
            grad_mixture,
            jnp.where(first_half, rim_back, zero_rim),
        ],
        axis=0,
    )
    grad_mix_wide = grad_mixture.astype(WIDE)
    grad_activated = jnp.zeros_like(up_proj)
    tap_grads = []
    for tap_index in range(9):
        row_step = tap_index // 3 - 1
        col_step = tap_index % 3 - 1
        offset = row_step * row_width + col_step
        source = lax.dynamic_slice_in_dim(grad_padded, rim_depth - offset, tokens_here, 0)
        grad_activated = (
            grad_activated
            + jnp.where(inside(-row_step, -col_step)[:, None], source.astype(WIDE), 0.0)
            * conv_taps[tap_index]
        )
        shifted = lax.dynamic_slice_in_dim(padded, rim_depth + offset, tokens_here, 0)
        tap_grads.append(
            jnp.sum(
                jnp.where(inside(row_step, col_step)[:, None], shifted.astype(WIDE), 0.0)
                * grad_mix_wide,
                axis=0,
            )
        )
    conv_sum = jnp.stack(tap_grads)
    sigmoid_up = jax.nn.sigmoid(up_proj)
    grad_up_low = (grad_activated * sigmoid_up * (1.0 + up_proj * (1.0 - sigmoid_up))).astype(LOW)
    grad_norm_two = scatter_product(grad_up_low, up_flat)
    up_part = over_tokens(normed_two_low, grad_up_low)

    grad_cross_in, grad_shift_ffn, grad_scale_ffn = norm_two_back(grad_norm_two)
    grad_after_cross = block_upstream + grad_cross_in
    grad_cross = grad_after_cross.astype(LOW)
    cross_out_part = [over_tokens(grad_cross, text_low[step]) for step in range(tp_count)]
    grad_text = jnp.stack(
        [
            jnp.dot(grad_cross, shard, preferred_element_type=WIDE).astype(LOW)
            for shard in cross_shards
        ]
    )

    def to_heads(blocks):
        return (
            blocks.reshape(tp_count, block_size, cross_heads, CROSS_HEAD)
            .transpose(0, 2, 1, 3)
            .reshape(heads_all, block_size, CROSS_HEAD)
        )

    grad_text_heads = to_heads(grad_text)
    grad_probs = jnp.einsum(
        "ztd,zsd->zts", grad_text_heads, text_values, preferred_element_type=WIDE
    )
    grad_values = jnp.einsum(
        "zts,ztd->zsd", probs_low, grad_text_heads, preferred_element_type=WIDE
    )
    grad_scores = (
        attn_probs * (grad_probs - jnp.sum(attn_probs * grad_probs, axis=-1, keepdims=True))
    ).astype(LOW)
    grad_queries = (
        jnp.einsum("zts,zsd->ztd", grad_scores, text_keys, preferred_element_type=WIDE)
        * score_scale
    )
    grad_keys = (
        jnp.einsum("zts,ztd->zsd", grad_scores, cross_queries, preferred_element_type=WIDE)
        * score_scale
    )
    grad_query_low = to_shards(grad_queries.astype(LOW))
    cross_q_part = [over_tokens(after_low, grad_query_low[step]) for step in range(tp_count)]
    grad_after_attn = grad_after_cross + sum(
        times_transposed(grad_query_low[step], query_shards[step]) for step in range(tp_count)
    )

    grad_gate_attn = grad_after_attn * attn_branch
    grad_attn = (grad_after_attn * gate_attn).astype(LOW)
    grad_attended_blocks = [
        jnp.dot(grad_attn, shard, preferred_element_type=WIDE).astype(LOW) for shard in out_shards
    ]
    attn_out_part = [over_tokens(grad_attn, block) for block in attended_blocks]
    grad_attended = jnp.zeros((tp_count, block_size, self_cols), LOW)
    for step in range(tp_count):
        piece = grad_attended_blocks[step]
        if step:
            piece = from_ahead(piece, step)
        grad_attended = lax.dynamic_update_index_in_dim(
            grad_attended, piece, (tp_index + step) % tp_count, 0
        )
    grad_attended = grad_attended.reshape(tokens_here, self_heads, HEAD).astype(WIDE)
    grad_numer = grad_attended / denominator[:, :, None]
    grad_denom = -jnp.sum(grad_attended * attended, axis=-1) / denominator
    grad_kernel_part = jnp.einsum(
        "it,tzd,tze->izde", image_masks, queries_wide, grad_numer, precision=PRECISE
    )
    grad_total_part = jnp.einsum(
        "it,tzd,tz->izd", image_masks, queries_wide, grad_denom, precision=PRECISE
    )
    kernel_back_other, total_back_other = swapped((grad_kernel_part, grad_total_part), "seq", 0)
    grad_kernels = grad_kernel_part + kernel_back_other
    grad_totals = grad_total_part + total_back_other
    grad_q_pair = (
        jnp.einsum("tze,izde->itzd", grad_numer, kernels, precision=PRECISE)
        + grad_denom[None, :, :, None] * key_totals[:, None]
    )
    values_wide = self_values.astype(WIDE)
    keys_wide = self_keys.astype(WIDE)
    grad_k_pair = (
        jnp.einsum("tze,izde->itzd", values_wide, grad_kernels, precision=PRECISE)
        + grad_totals[:, None]
    )
    grad_v_pair = jnp.einsum("tzd,izde->itze", keys_wide, grad_kernels, precision=PRECISE)
    grad_q_self = jax.nn.sigmoid(projected[:, 0]) * by_image(second, grad_q_pair)
    grad_k_self = jax.nn.sigmoid(projected[:, 1]) * by_image(second, grad_k_pair)
    grad_v_self = by_image(second, grad_v_pair)
    grad_projected = (
        jnp.stack([grad_q_self, grad_k_self, grad_v_self], axis=1)
        .reshape(tokens_here, 3 * self_cols)
        .astype(LOW)
    )
    grad_normed = scatter_product(grad_projected, qkv_flat)
    qkv_part = over_tokens(normed_low, grad_projected)
    normed_unused, norm_back = jax.vjp(modulated_norm, block_inputs, per_block(0), per_block(1))
    grad_inputs_norm, grad_shift_attn, grad_scale_attn = norm_back(grad_normed)
    input_grad = gather_blocks((grad_after_attn + grad_inputs_norm).astype(LOW)).astype(WIDE)
    output = gather_blocks(output_block)

    early_sums = jnp.stack(
        [
            image_sums(member)
            for member in (
                grad_gate_attn,
                grad_shift_ffn,
                grad_scale_ffn,
                block_upstream * ffn_branch,
            )
        ],
        axis=1,
    )
    late_sums = jnp.stack(
        [image_sums(member) for member in (grad_shift_attn, grad_scale_attn)], axis=1
    )

    def image_total(pair_sums):
        own = jnp.where(first_half, pair_sums[0], pair_sums[1])
        other = jnp.where(first_half, pair_sums[1], pair_sums[0])
        return same_everywhere(own + swapped(other, "seq", 0))

    modulation_grad = jnp.concatenate([image_total(late_sums), image_total(early_sums)], axis=0)

    grad_kv = (
        jnp.stack([grad_keys, grad_values])
        .reshape(2, tp_count, cross_heads, 2, context, CROSS_HEAD)
        .transpose(3, 1, 4, 0, 2, 5)
        .reshape(2, tp_count, context, 2 * cross_cols)
    )
    grad_kv_keep = jnp.where(first_half, grad_kv[0], grad_kv[1])
    grad_kv_send = jnp.where(first_half, grad_kv[1], grad_kv[0]).astype(LOW)
    grad_kv_image = grad_kv_keep + swapped(grad_kv_send, "seq", 0).astype(WIDE)
    grad_kv_own = grad_kv_image[0] + sum(
        from_ahead(grad_kv_image[step].astype(LOW), step).astype(WIDE)
        for step in range(1, tp_count)
    )
    ckv_part = over_tokens(text_rows, grad_kv_own.astype(LOW))

    def own_columns(rows):
        total = rows[:, 0]
        for step in range(1, tp_count):
            total = total + from_ahead(rows[:, step].astype(LOW), step).astype(WIDE)
        return total

    def sum_square(parts):
        rows = sum_rows(jnp.concatenate(parts, axis=1))
        return own_columns(rows.reshape(rows.shape[0], tp_count, -1))

    for place in range(lax.axis_size("seq").bit_length() - 1):
        conv_sum = conv_sum + swapped(conv_sum, "seq", place)
    down_grad = sum_rows(down_part)
    up_grad = sum_rows(up_part)
    cross_out_grad = sum_square(cross_out_part)
    cross_q_grad = sum_square(cross_q_part)
    ckv_grad = sum_rows(ckv_part)
    attn_out_grad = sum_square(attn_out_part)
    qkv_grad = sum_rows(qkv_part)
    return (
        output,
        input_grad,
        modulation_grad[None],
        qkv_grad.reshape(-1, 3, self_cols),
        attn_out_grad,
        cross_q_grad,
        ckv_grad.reshape(-1, 2, cross_cols),
        cross_out_grad,
        up_grad.reshape(-1, 2, ffn_cols),
        conv_sum.reshape(9, 2, ffn_cols),
        down_grad,
    )


def solution(mesh):
    placed = (
        P("seq", None),
        P("seq", None),
        P("seq", None, None),
        P("seq", None, None),
        P(),
        P(),
        P(None, None, "tp"),
        P(None, "tp"),
        P(None, "tp"),
        P(None, None, "tp"),
        P(None, "tp"),
        P(None, None, "tp"),
        P(None, None, "tp"),
        P(None, "tp"),
    )
    return jax.shard_map(
        shards,
        mesh=mesh,
        in_specs=placed,
        out_specs=(
            P("seq", None),
            P("seq", None),
            P("seq", None, None),
            P("seq", None, "tp"),
            P("seq", "tp"),
            P("seq", "tp"),
            P("seq", None, "tp"),
            P("seq", "tp"),
            P("seq", None, "tp"),
            P(None, None, "tp"),
            P("seq", "tp"),
        ),
        check_vma=False,
    )
```

time: 1180 us -> 852 us (0.72)
  waiting for transfers between devices: 845 us -> 210 us
  starting transfers between devices: 3.63 us -> 142 us
  local copies, waits for them, and re-layouts: 69.6 us -> 203 us
  other arithmetic: 101 us -> 159 us
  blocking collectives: 26.5 us -> 0 us
  between operations: 27.9 us -> 14.7 us
    psum x5 -> x0, waiting for transfers between devices: 509 us -> none  [the longest x1 114 us: shards(): grad_norm_two = lax.psum(times_transposed(grad_up_low, up_flat), 'tp')]
    reduce_scatter x5 -> x0, waiting for transfers between devices: 242 us -> none  [the longest x2 94.1 us: sum_weights(): lax.psum_scatter(second_grad, 'seq', scatter_dimension=0, tiled=True)]
    ppermute x0 -> x48, waiting for transfers between devices: none -> 129 us  [the longest x33 110 us: from_behind(): lax.ppermute(block, 'tp', [(k, (k + step) % count) for k in range(count)])]
    unnamed x14 -> x0, waiting for transfers between devices: 93.2 us -> none
    ppermute x9 -> x80, waiting for transfers between devices: 1.2 us -> 81 us  [swapped(): return lax.ppermute(block, axis, route)]
    ppermute x0 -> x48, starting transfers between devices: none -> 77.2 us  [the longest x33 50.7 us: from_behind(): lax.ppermute(block, 'tp', [(k, (k + step) % count) for k in range(count)])]
    ppermute x9 -> x80, starting transfers between devices: 1.91 us -> 64.7 us  [swapped(): return lax.ppermute(block, axis, route)]
    convert_element_type x0 -> x38, local copies, waits for them, and re-layouts: none -> 35.4 us  [the longest x35 30.9 us: halved(): return keep + swapped(send.astype(LOW), 'seq', place).astype(WIDE)]
  transfers between devices with their start and end apart: 21 -> 128, of which waited for: 13 -> 53; matrix products, arithmetic and copies ran while one was open for 12% -> 40% of each run, Pallas kernels for 0% -> 0%
where the time goes in v1:
time: 852 us; the launch traced here: 837 us
  waiting for transfers between devices  210 us (25%)
  local copies, waits for them, and re-layouts  203 us (24%)
  other arithmetic  159 us (19%)
  starting transfers between devices  142 us (17%)
  matrix products  108 us (13%)
  between operations  14.7 us (2%)
    ppermute x33, waiting for transfers between devices, from_behind(): lax.ppermute(block, 'tp', [(k, (k + step) % count) for k in range(count)])  110 us
    ppermute x80, waiting for transfers between devices, swapped(): return lax.ppermute(block, axis, route)  81 us
    ppermute x80, starting transfers between devices, swapped(): return lax.ppermute(block, axis, route)  64.7 us
    ppermute x33, starting transfers between devices, from_behind(): lax.ppermute(block, 'tp', [(k, (k + step) % count) for k in range(count)])  50.7 us
    unnamed x453, local copies, waits for them, and re-layouts  33.3 us
    convert_element_type x35, local copies, waits for them, and re-layouts, halved(): return keep + swapped(send.astype(LOW), 'seq', place).astype(WIDE)  30.9 us
    dot_general x24, matrix products, times_transposed(): lax.dot_general(left_side, right_side, (((1,), (1,)), ((), ())), preferre...  26.6 us
    ppermute x15, starting transfers between devices, from_ahead(): lax.ppermute(block, 'tp', [(k, (k - step) % count) for k in range(count)])  26.4 us
  transfers between devices with their start and end apart: 128, of which 53 were waited for; matrix products, arithmetic and copies ran while one was open for 40% of the time, Pallas kernels for 0%

profile of v1, /device:TPU:8, one launch (start us, length us, event | category | flops | bytes accessed | tf_op | source)
XLA Modules:
  0.0 837.1 jit_solution(12577003215601066674)
XLA Ops:
  91.4 6.3 collective-permute-done.16
  98.5 5.2 collective-permute-done.36
  106.2 5.8 collective-permute-done.11
  154.4 9.0 %copy.346 = bf16[4,2,300,576]{2,1,3,0:T(2,128)(2,1)} copy(bf16[4,2,300,576]{3,2,0,1:T(8,128)(2,1)} %maximum_select_fusion) | data formatting | bytes 5529600 | tf_op jit(solution)/shard_map/jit(_where)/select_n | solution.py:235
  163.4 7.9 select_n.1305
  171.3 3.8 fusion.243
  175.1 6.9 fusion.262
  182.0 4.8 fusion.49
  217.9 4.3 collective-permute-start.47
  224.0 21.3 %collective-permute-done.47 = bf16[160,1152]{1,0:T(8,128)(2,1)S(1)} collective-permute-done((bf16[160,1152]{1,0:T(8,128)(2,1)}, bf16[160,1152]{1,0:T(8,128)(2,1)S(1)}, u32[]{:S(2)}, u32[]{:S(2)}) %collective-permute-start.47) | collective-permute-done | bytes 368672 | tf_op jit(solution)/shard_map/ppermute | solution.py:28
  247.1 6.2 multiply_convert_fusion.1
  256.0 3.8 copy.379
  264.1 12.6 %multiply_add_fusion = f32[640,1440]{0,1:T(8,128)S(1)} fusion(bf16[640,1440]{0,1:T(8,128)(2,1)S(1)} %copy-done.10, bf16[33,1440]{0,1:T(8,128)(2,1)S(1)} %get-tuple-element.204, bf16[33,1440]{0,1:T(8,128)(2,1)S(1)} %get-tuple-element.203, f32[1440]{0:T(1024)S(1)} %copy-done.161, f32[1440]{0:T(1024)S(1)} %copy-done.159, f32[1440]{0:T(1024)S(1)} %copy-done.157, ...), kind=kLoop, calls=%fused_computation.38 | loop fusion | flops 37785600 | bytes 16836504 | tf_op jit(solution)/shard_map/add | solution.py:359
  279.1 7.0 fusion.16
  286.1 13.8 %fusion.19 = (f32[1440]{0:T(1024)S(1)}, f32[1440]{0:T(1024)S(1)}, f32[1440]{0:T(1024)S(1)}, f32[1440]{0:T(1024)S(1)}, f32[1440]{0:T(1024)S(1)}, /*index=5*/f32[1440]{0:T(1024)S(1)}) fusion(pred[640]{0:T(1024)(128)(4,1)S(1)} %copy-done.191, bf16[706,1440]{0,1:T(8,128)(2,1)S(1)} %pad_maximum_fusion.4, s32[]{:T(128)S(6)} %select_n.1354, ...), kind=kLoop, calls=%fused_computation.37 | loop fusion | flops 25796160 | bytes 12940824 | tf_op jit(solution)/shard_map/reduce_sum | solution.py:399
  330.1 16.4 %fusion.10 = bf16[640,1440]{0,1:T(8,128)(2,1)S(1)} fusion(f32[640,1440]{0,1:T(8,128)S(1)} %copy-done.73, bf16[33,1440]{0,1:T(8,128)(2,1)S(1)} %get-tuple-element.202, bf16[640,720]{0,1:T(8,128)(2,1)S(1)} %copy-done.6, bf16[640,720]{0,1:T(8,128)(2,1)S(1)} %copy-done.8, bf16[33,1440]{0,1:T(8,128)(2,1)S(1)} %get-tuple-element.201, ...), kind=kLoop, calls=%fused_computation.28 | loop fusion | flops 52531200 | bytes 18679704 | tf_op jit(solution)/shard_map/convert_element_type | solution.py:407
  364.2 17.2 %collective-permute-done.57 = bf16[160,1152]{1,0:T(8,128)(2,1)} collective-permute-done((bf16[160,1152]{1,0:T(8,128)(2,1)}, bf16[160,1152]{1,0:T(8,128)(2,1)}, u32[]{:S(2)}, u32[]{:S(2)}) %collective-permute-start.57) | collective-permute-done | bytes 368672 | tf_op jit(solution)/shard_map/ppermute | solution.py:28
  381.4 6.4 collective-permute-done.58
  390.6 4.8 multiply_reduce_fusion.4
  405.5 5.8 fusion.37
  411.3 3.7 multiply_reduce_fusion
  415.1 5.6 stack.251
  420.7 4.3 copy.374
  433.7 5.6 stack.250
  466.9 6.9 copy.378
  479.9 5.2 pad_maximum_fusion.1
  485.1 7.0 copy.370
  499.6 6.9 copy.369
  515.4 3.9 dynamic_update_slice.58
  522.9 3.9 dynamic_update_slice.59
  526.8 3.9 dynamic_update_slice.60
  530.8 3.9 dynamic_update_slice.61
  562.4 8.7 %collective-permute-done.54 = bf16[160,1152]{1,0:T(8,128)(2,1)S(1)} collective-permute-done((bf16[160,1152]{1,0:T(8,128)(2,1)}, bf16[160,1152]{1,0:T(8,128)(2,1)S(1)}, u32[]{:S(2)}, u32[]{:S(2)}) %collective-permute-start.54) | collective-permute-done | bytes 368672 | tf_op jit(solution)/shard_map/ppermute | solution.py:28
  575.4 11.7 %collective-permute-done.55 = bf16[160,1152]{1,0:T(8,128)(2,1)S(1)} collective-permute-done((bf16[160,1152]{1,0:T(8,128)(2,1)}, bf16[160,1152]{1,0:T(8,128)(2,1)S(1)}, u32[]{:S(2)}, u32[]{:S(2)}) %collective-permute-start.55) | collective-permute-done | bytes 368672 | tf_op jit(solution)/shard_map/ppermute | solution.py:28
  587.9 6.1 collective-permute-done.65
  595.7 6.1 collective-permute-done.66
  616.8 4.8 collective-permute-done.126
  639.4 16.3 %collective-permute-done.69 = bf16[160,1152]{1,0:T(8,128)(2,1)S(1)} collective-permute-done((bf16[160,1152]{1,0:T(8,128)(2,1)S(1)}, bf16[160,1152]{1,0:T(8,128)(2,1)S(1)}, u32[]{:S(2)}, u32[]{:S(2)}) %collective-permute-start.69) | collective-permute-done | bytes 368672 | tf_op jit(solution)/shard_map/ppermute | solution.py:28
  659.2 8.0 collective-permute-done.70
  689.8 3.8 copy.376
  693.7 4.2 fusion.233
  703.8 7.1 collective-permute-done.79
  712.0 3.8 collective-permute-done.81
  729.0 4.1 collective-permute-start.100
  744.9 12.1 %collective-permute-done.100 = bf16[300,576]{0,1:T(8,128)(2,1)S(1)} collective-permute-done((bf16[300,576]{0,1:T(8,128)(2,1)S(1)}, bf16[300,576]{0,1:T(8,128)(2,1)S(1)}, u32[]{:S(2)}, u32[]{:S(2)}) %collective-permute-start.100) | collective-permute-done | bytes 345632 | tf_op jit(solution)/shard_map/ppermute | solution.py:33
  758.3 4.1 collective-permute-done.101
  783.8 3.9 collective-permute-start.113
  804.0 3.6 collective-permute-start.88
  (1058 shorter events, 483.4 us)
Async XLA Ops:
  2.6 51.5 %collective-permute-start.4 = (bf16[144,288]{1,0:T(8,128)(2,1)}, bf16[144,288]{1,0:T(8,128)(2,1)}, u32[]{:S(2)}, u32[]{:S(2)}) collective-permute-start(bf16[144,288]{1,0:T(8,128)(2,1)} %copy.416), channel_id=1, source_target_pairs={{0,1},{1,2},{2,3},{3,0},{4,5},{5,6},{6,7},{7,4},{8,9},{9,10},{10,1... | collective-permute-start | bytes 248840 | tf_op jit(solution)/shard_map/ppermute | solution.py:28
  4.2 74.6 %collective-permute-start.14 = (bf16[144,288]{1,0:T(8,128)(2,1)}, bf16[144,288]{1,0:T(8,128)(2,1)}, u32[]{:S(2)}, u32[]{:S(2)}) collective-permute-start(bf16[144,288]{1,0:T(8,128)(2,1)} %copy.416), channel_id=1, source_target_pairs={{0,3},{1,0},{2,1},{3,2},{4,7},{5,4},{6,5},{7,6},{8,11},{9,8},{10,9... | collective-permute-start | bytes 248840 | tf_op jit(solution)/shard_map/ppermute | solution.py:28
  4.7 39.8 %collective-permute-start.9 = (bf16[144,288]{1,0:T(8,128)(2,1)}, bf16[144,288]{1,0:T(8,128)(2,1)}, u32[]{:S(2)}, u32[]{:S(2)}) collective-permute-start(bf16[144,288]{1,0:T(8,128)(2,1)} %copy.416), channel_id=1, source_target_pairs={{0,2},{1,3},{2,0},{3,1},{4,6},{5,7},{6,4},{7,5},{8,10},{9,11},{10,... | collective-permute-start | bytes 248840 | tf_op jit(solution)/shard_map/ppermute | solution.py:28
  7.3 27.5 %collective-permute-start = (bf16[6,1152]{1,0:T(8,128)(2,1)}, bf16[6,1152]{1,0:T(8,128)(2,1)}, u32[]{:S(2)}, u32[]{:S(2)}) collective-permute-start(bf16[6,1152]{1,0:T(8,128)(2,1)} %bitcast.829), channel_id=1, source_target_pairs={{0,4},{4,0},{8,12},{12,8},{16,20},{20,16},{24,28},{28,24},{1,5},{5... | collective-permute-start | bytes 41480 | tf_op jit(solution)/shard_map/ppermute | solution.py:23
  9.1 42.7 %collective-permute-start.18 = (bf16[144,288]{1,0:T(8,128)(2,1)}, bf16[144,288]{1,0:T(8,128)(2,1)}, u32[]{:S(2)}, u32[]{:S(2)}) collective-permute-start(bf16[144,288]{1,0:T(8,128)(2,1)} %copy.417), channel_id=1, source_target_pairs={{0,1},{1,2},{2,3},{3,0},{4,5},{5,6},{6,7},{7,4},{8,9},{9,10},{10,1... | collective-permute-start | bytes 248840 | tf_op jit(solution)/shard_map/ppermute | solution.py:28
  54.2 26.9 %collective-permute-start.34 = (bf16[144,288]{1,0:T(8,128)(2,1)S(1)}, bf16[144,288]{1,0:T(8,128)(2,1)S(1)}, u32[]{:S(2)}, u32[]{:S(2)}) collective-permute-start(bf16[144,288]{1,0:T(8,128)(2,1)S(1)} %copy-done.150), channel_id=1, source_target_pairs={{0,1},{1,2},{2,3},{3,0},{4,5},{5,6},{6,7},{7,4},{8,9},{9,10},{10,1... | collective-permute-start | bytes 248840 | tf_op jit(solution)/shard_map/ppermute | solution.py:28
  67.9 59.7 %collective-permute-start.30 = (bf16[300,576]{1,0:T(8,128)(2,1)S(1)}, bf16[300,576]{1,0:T(8,128)(2,1)S(1)}, u32[]{:S(2)}, u32[]{:S(2)}) collective-permute-start(bf16[300,576]{1,0:T(8,128)(2,1)S(1)} %copy-done.143), channel_id=1, source_target_pairs={{0,1},{1,2},{2,3},{3,0},{4,5},{5,6},{6,7},{7,4},{8,9},{9,10},{10,1... | collective-permute-start | bytes 1036808 | tf_op jit(solution)/shard_map/ppermute | solution.py:28
  73.2 55.1 %collective-permute-start.31 = (bf16[300,576]{1,0:T(8,128)(2,1)S(1)}, bf16[300,576]{1,0:T(8,128)(2,1)S(1)}, u32[]{:S(2)}, u32[]{:S(2)}) collective-permute-start(bf16[300,576]{1,0:T(8,128)(2,1)S(1)} %copy-done.143), channel_id=1, source_target_pairs={{0,2},{1,3},{2,0},{3,1},{4,6},{5,7},{6,4},{7,5},{8,10},{9,11},{10,... | collective-permute-start | bytes 1036808 | tf_op jit(solution)/shard_map/ppermute | solution.py:28
  78.8 50.9 %collective-permute-start.32 = (bf16[300,576]{1,0:T(8,128)(2,1)S(1)}, bf16[300,576]{1,0:T(8,128)(2,1)S(1)}, u32[]{:S(2)}, u32[]{:S(2)}) collective-permute-start(bf16[300,576]{1,0:T(8,128)(2,1)S(1)} %copy-done.143), channel_id=1, source_target_pairs={{0,3},{1,0},{2,1},{3,2},{4,7},{5,4},{6,5},{7,6},{8,11},{9,8},{10,9... | collective-permute-start | bytes 1036808 | tf_op jit(solution)/shard_map/ppermute | solution.py:28
  194.5 27.8 %collective-permute-start.46 = (bf16[160,1152]{1,0:T(8,128)(2,1)}, bf16[160,1152]{1,0:T(8,128)(2,1)}, u32[]{:S(2)}, u32[]{:S(2)}) collective-permute-start(bf16[160,1152]{1,0:T(8,128)(2,1)} %get-tuple-element.142), channel_id=1, source_target_pairs={{0,1},{1,2},{2,3},{3,0},{4,5},{5,6},{6,7},{7,4},{8,9},{9,10},{10,1... | collective-permute-start | bytes 1105928 | tf_op jit(solution)/shard_map/ppermute | solution.py:28
  217.9 27.4 %collective-permute-start.47 = (bf16[160,1152]{1,0:T(8,128)(2,1)}, bf16[160,1152]{1,0:T(8,128)(2,1)S(1)}, u32[]{:S(2)}, u32[]{:S(2)}) collective-permute-start(bf16[160,1152]{1,0:T(8,128)(2,1)} %get-tuple-element.142), channel_id=1, source_target_pairs={{0,2},{1,3},{2,0},{3,1},{4,6},{5,7},{6,4},{7,5},{8,10},{9,11},{10,... | collective-permute-start | bytes 1105928 | tf_op jit(solution)/shard_map/ppermute | solution.py:28
  222.2 24.1 %collective-permute-start.48 = (bf16[160,1152]{1,0:T(8,128)(2,1)}, bf16[160,1152]{1,0:T(8,128)(2,1)S(1)}, u32[]{:S(2)}, u32[]{:S(2)}) collective-permute-start(bf16[160,1152]{1,0:T(8,128)(2,1)} %get-tuple-element.142), channel_id=1, source_target_pairs={{0,3},{1,0},{2,1},{3,2},{4,7},{5,4},{6,5},{7,6},{8,11},{9,8},{10,9... | collective-permute-start | bytes 1105928 | tf_op jit(solution)/shard_map/ppermute | solution.py:28
  318.6 40.2 %collective-permute-start.50 = (bf16[160,1152]{1,0:T(8,128)(2,1)}, bf16[160,1152]{1,0:T(8,128)(2,1)S(1)}, u32[]{:S(2)}, u32[]{:S(2)}) collective-permute-start(bf16[160,1152]{1,0:T(8,128)(2,1)} %convolution_convert_fusion.8), channel_id=1, source_target_pairs={{0,1},{1,2},{2,3},{3,0},{4,5},{5,6},{6,7},{7,4},{8,9},{9,10},{10,1... | collective-permute-start | bytes 1105928 | tf_op jit(solution)/shard_map/ppermute | solution.py:28
  318.6 45.1 %collective-permute-start.51 = (bf16[160,1152]{1,0:T(8,128)(2,1)}, bf16[160,1152]{1,0:T(8,128)(2,1)}, u32[]{:S(2)}, u32[]{:S(2)}) collective-permute-start(bf16[160,1152]{1,0:T(8,128)(2,1)} %convolution_convert_fusion.7), channel_id=1, source_target_pairs={{0,2},{1,3},{2,0},{3,1},{4,6},{5,7},{6,4},{7,5},{8,10},{9,11},{10,... | collective-permute-start | bytes 1105928 | tf_op jit(solution)/shard_map/ppermute | solution.py:28
  321.7 42.0 %collective-permute-start.52 = (bf16[160,1152]{1,0:T(8,128)(2,1)}, bf16[160,1152]{1,0:T(8,128)(2,1)}, u32[]{:S(2)}, u32[]{:S(2)}) collective-permute-start(bf16[160,1152]{1,0:T(8,128)(2,1)} %convolution_convert_fusion.6), channel_id=1, source_target_pairs={{0,3},{1,0},{2,1},{3,2},{4,7},{5,4},{6,5},{7,6},{8,11},{9,8},{10,9... | collective-permute-start | bytes 1105928 | tf_op jit(solution)/shard_map/ppermute | solution.py:28
  327.3 26.2 %collective-permute-start.121 = (f32[9,1440]{1,0:T(8,128)S(1)}, f32[9,1440]{1,0:T(8,128)S(1)}, u32[]{:S(2)}, u32[]{:S(2)}) collective-permute-start(f32[9,1440]{1,0:T(8,128)S(1)} %add.1192), channel_id=1, source_target_pairs={{0,8},{4,12},{8,0},{12,4},{16,24},{20,28},{24,16},{28,20},{1,9},{5... | collective-permute-start | bytes 155528 | tf_op jit(solution)/shard_map/ppermute | solution.py:23
  356.4 25.0 %collective-permute-start.57 = (bf16[160,1152]{1,0:T(8,128)(2,1)}, bf16[160,1152]{1,0:T(8,128)(2,1)}, u32[]{:S(2)}, u32[]{:S(2)}) collective-permute-start(bf16[160,1152]{1,0:T(8,128)(2,1)} %convolution_convert_fusion.2), channel_id=1, source_target_pairs={{0,1},{1,2},{2,3},{3,0},{4,5},{5,6},{6,7},{7,4},{8,9},{9,10},{10,1... | collective-permute-start | bytes 1105928 | tf_op jit(solution)/shard_map/ppermute | solution.py:28
  358.2 29.5 %collective-permute-start.58 = (bf16[160,1152]{1,0:T(8,128)(2,1)}, bf16[160,1152]{1,0:T(8,128)(2,1)}, u32[]{:S(2)}, u32[]{:S(2)}) collective-permute-start(bf16[160,1152]{1,0:T(8,128)(2,1)} %convolution_convert_fusion.1), channel_id=1, source_target_pairs={{0,2},{1,3},{2,0},{3,1},{4,6},{5,7},{6,4},{7,5},{8,10},{9,11},{10,... | collective-permute-start | bytes 1105928 | tf_op jit(solution)/shard_map/ppermute | solution.py:28
  358.8 31.8 %collective-permute-start.59 = (bf16[160,1152]{1,0:T(8,128)(2,1)}, bf16[160,1152]{1,0:T(8,128)(2,1)}, u32[]{:S(2)}, u32[]{:S(2)}) collective-permute-start(bf16[160,1152]{1,0:T(8,128)(2,1)} %convolution_convert_fusion), channel_id=1, source_target_pairs={{0,3},{1,0},{2,1},{3,2},{4,7},{5,4},{6,5},{7,6},{8,11},{9,8},{10,9... | collective-permute-start | bytes 1105928 | tf_op jit(solution)/shard_map/ppermute | solution.py:28
  363.7 192.5 %collective-permute-start.123 = (bf16[2,2,144,720]{3,2,1,0:T(8,128)(2,1)}, bf16[2,2,144,720]{3,2,1,0:T(8,128)(2,1)}, u32[]{:S(2)}, u32[]{:S(2)}) collective-permute-start(bf16[2,2,144,720]{3,2,1,0:T(8,128)(2,1)} %fusion.65), channel_id=1, source_target_pairs={{0,4},{4,0},{8,12},{12,8},{16,20},{20,16},{24,28},{28,24},{1,5},{5... | collective-permute-start | bytes 2488328 | tf_op jit(solution)/shard_map/ppermute | solution.py:23
  363.7 308.2 %collective-permute-start.115 = (bf16[2,2,144,1440]{3,2,1,0:T(8,128)(2,1)}, bf16[2,2,144,1440]{3,2,1,0:T(8,128)(2,1)}, u32[]{:S(2)}, u32[]{:S(2)}) collective-permute-start(bf16[2,2,144,1440]{3,2,1,0:T(8,128)(2,1)} %fusion.36), channel_id=1, source_target_pairs={{0,4},{4,0},{8,12},{12,8},{16,20},{20,16},{24,28},{28,24},{1,5},{5... | collective-permute-start | bytes 4976648 | tf_op jit(solution)/shard_map/ppermute | solution.py:23
  519.4 39.5 %collective-permute-start.53 = (bf16[160,1152]{1,0:T(8,128)(2,1)}, bf16[160,1152]{1,0:T(8,128)(2,1)}, u32[]{:S(2)}, u32[]{:S(2)}) collective-permute-start(bf16[160,1152]{1,0:T(8,128)(2,1)} %get-tuple-element.129), channel_id=1, source_target_pairs={{0,1},{1,2},{2,3},{3,0},{4,5},{5,6},{6,7},{7,4},{8,9},{9,10},{10,1... | collective-permute-start | bytes 1105928 | tf_op jit(solution)/shard_map/ppermute | solution.py:28
  543.2 28.0 %collective-permute-start.54 = (bf16[160,1152]{1,0:T(8,128)(2,1)}, bf16[160,1152]{1,0:T(8,128)(2,1)S(1)}, u32[]{:S(2)}, u32[]{:S(2)}) collective-permute-start(bf16[160,1152]{1,0:T(8,128)(2,1)} %get-tuple-element.129), channel_id=1, source_target_pairs={{0,2},{1,3},{2,0},{3,1},{4,6},{5,7},{6,4},{7,5},{8,10},{9,11},{10,... | collective-permute-start | bytes 1105928 | tf_op jit(solution)/shard_map/ppermute | solution.py:28
  546.5 40.6 %collective-permute-start.55 = (bf16[160,1152]{1,0:T(8,128)(2,1)}, bf16[160,1152]{1,0:T(8,128)(2,1)S(1)}, u32[]{:S(2)}, u32[]{:S(2)}) collective-permute-start(bf16[160,1152]{1,0:T(8,128)(2,1)} %get-tuple-element.129), channel_id=1, source_target_pairs={{0,3},{1,0},{2,1},{3,2},{4,7},{5,4},{6,5},{7,6},{8,11},{9,8},{10,9... | collective-permute-start | bytes 1105928 | tf_op jit(solution)/shard_map/ppermute | solution.py:28
  557.1 121.0 %collective-permute-start.107 = (bf16[2,2,144,1152]{3,2,1,0:T(8,128)(2,1)S(1)}, bf16[2,2,144,1152]{3,2,1,0:T(8,128)(2,1)S(1)}, u32[]{:S(2)}, u32[]{:S(2)}) collective-permute-start(bf16[2,2,144,1152]{3,2,1,0:T(8,128)(2,1)S(1)} %copy-done.125), channel_id=1, source_target_pairs={{0,4},{4,0},{8,12},{12,8},{16,20},{20,16},{24,28},{28,24},{1,5},{5... | collective-permute-start | bytes 3981320 | tf_op jit(solution)/shard_map/ppermute | solution.py:23
  558.8 35.2 %collective-permute-start.65 = (bf16[160,1152]{1,0:T(8,128)(2,1)S(1)}, bf16[160,1152]{1,0:T(8,128)(2,1)S(1)}, u32[]{:S(2)}, u32[]{:S(2)}) collective-permute-start(bf16[160,1152]{1,0:T(8,128)(2,1)S(1)} %convolution_convert_fusion.5), channel_id=1, source_target_pairs={{0,1},{1,2},{2,3},{3,0},{4,5},{5,6},{6,7},{7,4},{8,9},{9,10},{10,1... | collective-permute-start | bytes 1105928 | tf_op jit(solution)/shard_map/ppermute | solution.py:28
  571.1 30.7 %collective-permute-start.66 = (bf16[160,1152]{1,0:T(8,128)(2,1)S(1)}, bf16[160,1152]{1,0:T(8,128)(2,1)S(1)}, u32[]{:S(2)}, u32[]{:S(2)}) collective-permute-start(bf16[160,1152]{1,0:T(8,128)(2,1)S(1)} %convolution_convert_fusion.4), channel_id=1, source_target_pairs={{0,2},{1,3},{2,0},{3,1},{4,6},{5,7},{6,4},{7,5},{8,10},{9,11},{10,... | collective-permute-start | bytes 1105928 | tf_op jit(solution)/shard_map/ppermute | solution.py:28
  594.0 22.7 %collective-permute-start.124 = (bf16[2,72,720]{2,1,0:T(8,128)(2,1)S(1)}, bf16[2,72,720]{2,1,0:T(8,128)(2,1)S(1)}, u32[]{:S(2)}, u32[]{:S(2)}) collective-permute-start(bf16[2,72,720]{2,1,0:T(8,128)(2,1)S(1)} %fusion.156), channel_id=1, source_target_pairs={{0,8},{4,12},{8,0},{12,4},{16,24},{20,28},{24,16},{28,20},{1,9},{5... | collective-permute-start | bytes 622088 | tf_op jit(solution)/shard_map/ppermute | solution.py:23
  613.5 73.9 %collective-permute-start.98 = (bf16[4,300,576]{2,0,1:T(4,128)(2,1)S(1)}, bf16[4,300,576]{2,0,1:T(4,128)(2,1)S(1)}, u32[]{:S(2)}, u32[]{:S(2)}) collective-permute-start(bf16[4,300,576]{2,0,1:T(4,128)(2,1)S(1)} %copy-done.109), channel_id=1, source_target_pairs={{0,4},{4,0},{8,12},{12,8},{16,20},{20,16},{24,28},{28,24},{1,5},{5... | collective-permute-start | bytes 4147208 | tf_op jit(solution)/shard_map/ppermute | solution.py:23
  616.7 20.8 %collective-permute-start.68 = (bf16[160,1152]{1,0:T(8,128)(2,1)S(1)}, bf16[160,1152]{1,0:T(8,128)(2,1)S(1)}, u32[]{:S(2)}, u32[]{:S(2)}) collective-permute-start(bf16[160,1152]{1,0:T(8,128)(2,1)S(1)} %get-tuple-element.119), channel_id=1, source_target_pairs={{0,1},{1,2},{2,3},{3,0},{4,5},{5,6},{6,7},{7,4},{8,9},{9,10},{10,1... | collective-permute-start | bytes 1105928 | tf_op jit(solution)/shard_map/ppermute | solution.py:28
  636.7 44.8 %collective-permute-start.90 = (bf16[2,2,144,1152]{3,2,1,0:T(8,128)(2,1)S(1)}, bf16[2,2,144,1152]{3,2,1,0:T(8,128)(2,1)S(1)}, u32[]{:S(2)}, u32[]{:S(2)}) collective-permute-start(bf16[2,2,144,1152]{3,2,1,0:T(8,128)(2,1)S(1)} %copy-done.124), channel_id=1, source_target_pairs={{0,4},{4,0},{8,12},{12,8},{16,20},{20,16},{24,28},{28,24},{1,5},{5... | collective-permute-start | bytes 3981320 | tf_op jit(solution)/shard_map/ppermute | solution.py:23
  637.5 18.2 %collective-permute-start.69 = (bf16[160,1152]{1,0:T(8,128)(2,1)S(1)}, bf16[160,1152]{1,0:T(8,128)(2,1)S(1)}, u32[]{:S(2)}, u32[]{:S(2)}) collective-permute-start(bf16[160,1152]{1,0:T(8,128)(2,1)S(1)} %get-tuple-element.119), channel_id=1, source_target_pairs={{0,2},{1,3},{2,0},{3,1},{4,6},{5,7},{6,4},{7,5},{8,10},{9,11},{10,... | collective-permute-start | bytes 1105928 | tf_op jit(solution)/shard_map/ppermute | solution.py:28
  671.9 27.1 %collective-permute-start.78 = (bf16[2,72,864]{2,1,0:T(8,128)(2,1)}, bf16[2,72,864]{2,1,0:T(8,128)(2,1)}, u32[]{:S(2)}, u32[]{:S(2)}) collective-permute-start(bf16[2,72,864]{2,1,0:T(8,128)(2,1)} %fusion.151), channel_id=1, source_target_pairs={{0,8},{4,12},{8,0},{12,4},{16,24},{20,28},{24,16},{28,20},{1,9},{5... | collective-permute-start | bytes 746504 | tf_op jit(solution)/shard_map/ppermute | solution.py:23
  678.1 23.1 %collective-permute-start.80 = (bf16[2,72,864]{2,1,0:T(8,128)(2,1)}, bf16[2,72,864]{2,1,0:T(8,128)(2,1)S(1)}, u32[]{:S(2)}, u32[]{:S(2)}) collective-permute-start(bf16[2,72,864]{2,1,0:T(8,128)(2,1)} %fusion.150), channel_id=1, source_target_pairs={{0,16},{4,20},{8,24},{12,28},{16,0},{20,4},{24,8},{28,12},{1,17},{... | collective-permute-start | bytes 746504 | tf_op jit(solution)/shard_map/ppermute | solution.py:23
  681.6 57.7 %collective-permute-start.116 = (bf16[2,72,1440]{2,1,0:T(8,128)(2,1)}, bf16[2,72,1440]{2,1,0:T(8,128)(2,1)}, u32[]{:S(2)}, u32[]{:S(2)}) collective-permute-start(bf16[2,72,1440]{2,1,0:T(8,128)(2,1)} %fusion.113), channel_id=1, source_target_pairs={{0,8},{4,12},{8,0},{12,4},{16,24},{20,28},{24,16},{28,20},{1,9},{5... | collective-permute-start | bytes 1244168 | tf_op jit(solution)/shard_map/ppermute | solution.py:23
  682.4 59.4 %collective-permute-start.118 = (bf16[2,72,1440]{2,1,0:T(8,128)(2,1)}, bf16[2,72,1440]{2,1,0:T(8,128)(2,1)}, u32[]{:S(2)}, u32[]{:S(2)}) collective-permute-start(bf16[2,72,1440]{2,1,0:T(8,128)(2,1)} %fusion.112), channel_id=1, source_target_pairs={{0,16},{4,20},{8,24},{12,28},{16,0},{20,4},{24,8},{28,12},{1,17},{... | collective-permute-start | bytes 1244168 | tf_op jit(solution)/shard_map/ppermute | solution.py:23
  688.6 29.8 %collective-permute-start.108 = (bf16[2,72,1152]{2,1,0:T(8,128)(2,1)}, bf16[2,72,1152]{2,1,0:T(8,128)(2,1)}, u32[]{:S(2)}, u32[]{:S(2)}) collective-permute-start(bf16[2,72,1152]{2,1,0:T(8,128)(2,1)} %fusion.145), channel_id=1, source_target_pairs={{0,8},{4,12},{8,0},{12,4},{16,24},{20,28},{24,16},{28,20},{1,9},{5... | collective-permute-start | bytes 995336 | tf_op jit(solution)/shard_map/ppermute | solution.py:23
  699.0 21.9 %collective-permute-start.110 = (bf16[2,72,1152]{2,1,0:T(8,128)(2,1)}, bf16[2,72,1152]{2,1,0:T(8,128)(2,1)}, u32[]{:S(2)}, u32[]{:S(2)}) collective-permute-start(bf16[2,72,1152]{2,1,0:T(8,128)(2,1)} %fusion.146), channel_id=1, source_target_pairs={{0,16},{4,20},{8,24},{12,28},{16,0},{20,4},{24,8},{28,12},{1,17},{... | collective-permute-start | bytes 995336 | tf_op jit(solution)/shard_map/ppermute | solution.py:23
  729.0 28.0 %collective-permute-start.100 = (bf16[300,576]{0,1:T(8,128)(2,1)S(1)}, bf16[300,576]{0,1:T(8,128)(2,1)S(1)}, u32[]{:S(2)}, u32[]{:S(2)}) collective-permute-start(bf16[300,576]{0,1:T(8,128)(2,1)S(1)} %copy-done.142), channel_id=1, source_target_pairs={{0,2},{1,3},{2,0},{3,1},{4,6},{5,7},{6,4},{7,5},{8,10},{9,11},{10,... | collective-permute-start | bytes 1036808 | tf_op jit(solution)/shard_map/ppermute | solution.py:33
  734.7 27.8 %collective-permute-start.101 = (bf16[300,576]{0,1:T(8,128)(2,1)S(1)}, bf16[300,576]{0,1:T(8,128)(2,1)S(1)}, u32[]{:S(2)}, u32[]{:S(2)}) collective-permute-start(bf16[300,576]{0,1:T(8,128)(2,1)S(1)} %copy-done.141), channel_id=1, source_target_pairs={{0,1},{1,2},{2,3},{3,0},{4,5},{5,6},{6,7},{7,4},{8,9},{9,10},{10,1... | collective-permute-start | bytes 1036808 | tf_op jit(solution)/shard_map/ppermute | solution.py:33
  736.3 28.3 %collective-permute-start.99 = (bf16[300,576]{0,1:T(8,128)(2,1)S(1)}, bf16[300,576]{0,1:T(8,128)(2,1)S(1)}, u32[]{:S(2)}, u32[]{:S(2)}) collective-permute-start(bf16[300,576]{0,1:T(8,128)(2,1)S(1)} %copy-done.140), channel_id=1, source_target_pairs={{0,3},{1,0},{2,1},{3,2},{4,7},{5,4},{6,5},{7,6},{8,11},{9,8},{10,9... | collective-permute-start | bytes 1036808 | tf_op jit(solution)/shard_map/ppermute | solution.py:33
  739.3 33.8 %collective-permute-start.109 = (bf16[72,1152]{1,0:T(8,128)(2,1)}, bf16[72,1152]{1,0:T(8,128)(2,1)}, u32[]{:S(2)}, u32[]{:S(2)}) collective-permute-start(bf16[72,1152]{1,0:T(8,128)(2,1)} %fusion.180), channel_id=1, source_target_pairs={{0,16},{4,20},{8,24},{12,28},{16,0},{20,4},{24,8},{28,12},{1,17},{... | collective-permute-start | bytes 497672 | tf_op jit(solution)/shard_map/ppermute | solution.py:23
  741.7 32.9 %collective-permute-start.111 = (bf16[72,1152]{1,0:T(8,128)(2,1)}, bf16[72,1152]{1,0:T(8,128)(2,1)}, u32[]{:S(2)}, u32[]{:S(2)}) collective-permute-start(bf16[72,1152]{1,0:T(8,128)(2,1)} %fusion.181), channel_id=1, source_target_pairs={{0,8},{4,12},{8,0},{12,4},{16,24},{20,28},{24,16},{28,20},{1,9},{5... | collective-permute-start | bytes 497672 | tf_op jit(solution)/shard_map/ppermute | solution.py:23
  757.0 20.8 %collective-permute-start.92 = (bf16[72,1152]{1,0:T(8,128)(2,1)}, bf16[72,1152]{1,0:T(8,128)(2,1)}, u32[]{:S(2)}, u32[]{:S(2)}) collective-permute-start(bf16[72,1152]{1,0:T(8,128)(2,1)} %fusion.178), channel_id=1, source_target_pairs={{0,16},{4,20},{8,24},{12,28},{16,0},{20,4},{24,8},{28,12},{1,17},{... | collective-permute-start | bytes 497672 | tf_op jit(solution)/shard_map/ppermute | solution.py:23
  762.5 19.4 %collective-permute-start.94 = (bf16[72,1152]{1,0:T(8,128)(2,1)}, bf16[72,1152]{1,0:T(8,128)(2,1)}, u32[]{:S(2)}, u32[]{:S(2)}) collective-permute-start(bf16[72,1152]{1,0:T(8,128)(2,1)} %fusion.179), channel_id=1, source_target_pairs={{0,8},{4,12},{8,0},{12,4},{16,24},{20,28},{24,16},{28,20},{1,9},{5... | collective-permute-start | bytes 497672 | tf_op jit(solution)/shard_map/ppermute | solution.py:23
  764.6 19.3 %collective-permute-start.84 = (bf16[72,1152]{1,0:T(8,128)(2,1)S(1)}, bf16[72,1152]{1,0:T(8,128)(2,1)}, u32[]{:S(2)}, u32[]{:S(2)}) collective-permute-start(bf16[72,1152]{1,0:T(8,128)(2,1)S(1)} %fusion.176), channel_id=1, source_target_pairs={{0,16},{4,20},{8,24},{12,28},{16,0},{20,4},{24,8},{28,12},{1,17},{... | collective-permute-start | bytes 497672 | tf_op jit(solution)/shard_map/ppermute | solution.py:23
  774.7 39.1 %collective-permute-start.117 = (bf16[72,1440]{1,0:T(8,128)(2,1)}, bf16[72,1440]{1,0:T(8,128)(2,1)}, u32[]{:S(2)}, u32[]{:S(2)}) collective-permute-start(bf16[72,1440]{1,0:T(8,128)(2,1)} %fusion.153), channel_id=1, source_target_pairs={{0,16},{4,20},{8,24},{12,28},{16,0},{20,4},{24,8},{28,12},{1,17},{... | collective-permute-start | bytes 622088 | tf_op jit(solution)/shard_map/ppermute | solution.py:23
  777.8 36.9 %collective-permute-start.119 = (bf16[72,1440]{1,0:T(8,128)(2,1)}, bf16[72,1440]{1,0:T(8,128)(2,1)}, u32[]{:S(2)}, u32[]{:S(2)}) collective-permute-start(bf16[72,1440]{1,0:T(8,128)(2,1)} %fusion.154), channel_id=1, source_target_pairs={{0,8},{4,12},{8,0},{12,4},{16,24},{20,28},{24,16},{28,20},{1,9},{5... | collective-permute-start | bytes 622088 | tf_op jit(solution)/shard_map/ppermute | solution.py:23
  (302 other events, 2534.7 us)

commit v2 on v0

v2 whole, which is shorter than its diff:
```python
import functools
import math

import jax
import jax.numpy as jnp
from jax import lax
from jax.experimental import pallas as pl
from jax.experimental.pallas import tpu as pltpu
from jax.sharding import PartitionSpec as P

HEAD = 32
CROSS_HEAD = 72
MAXW = 32
LANES = 128
GRANT = 56 * 1024 * 1024

EPSILON = 1e-06
MASKED_OUT = -1e30
LOW = jnp.bfloat16
WIDE = jnp.float32

FIRST, CUT, SIDE, WIDTH, OWN_LENGTH, OTHER_LENGTH, BLOCK_FIRST, SEQ_TOKENS, TP_PLACE, ROW_PLACE = range(10)


def swapped(block, axis, apart):
    count = lax.axis_size(axis)
    route = [(low, low ^ (1 << apart)) for low in range(count)]
    return lax.ppermute(block, axis, route)


def from_behind(block, step):
    count = lax.axis_size("tp")
    return lax.ppermute(block, "tp", [(k, (k + step) % count) for k in range(count)])


def from_ahead(block, step):
    count = lax.axis_size("tp")
    return lax.ppermute(block, "tp", [(k, (k - step) % count) for k in range(count)])


def dot(left, right):
    return jnp.dot(left, right, preferred_element_type=WIDE)


def times_transposed(left, right):
    return lax.dot_general(left, right, (((1,), (1,)), ((), ())), preferred_element_type=WIDE)


def over_tokens(left, right):
    return lax.dot_general(left, right, (((0,), (0,)), ((), ())), preferred_element_type=WIDE)


def split(wide):
    high = wide.astype(LOW)
    return high, (wide - high.astype(WIDE)).astype(LOW)


def call(body, name, outs, arrays, *, grid=None, in_specs=None, out_specs=None, scratch=(), flops=0, table=None):
    shapes = tuple(jax.ShapeDtypeStruct(*out) for out in outs)
    size = sum(math.prod(a.shape) * a.dtype.itemsize for a in (*arrays, *shapes))
    whole = pl.BlockSpec(memory_space=pltpu.VMEM)
    return pl.pallas_call(
        body,
        out_shape=shapes,
        grid_spec=pltpu.PrefetchScalarGridSpec(
            num_scalar_prefetch=1,
            grid=grid or (1,),
            in_specs=in_specs or [whole] * len(arrays),
            out_specs=out_specs or [whole] * len(shapes),
            scratch_shapes=list(scratch),
        ),
        compiler_params=pltpu.CompilerParams(vmem_limit_bytes=GRANT),
        cost_estimate=pl.CostEstimate(flops=0, bytes_accessed=size // 100, transcendentals=0),
        name=name,
    )(table, *arrays)


def own_image(table, start, rows):
    place = start + lax.broadcasted_iota(jnp.int32, (rows, 1), 0)
    return (place >= table[CUT]).astype(jnp.int32) == table[SIDE]


def pick(own, own_rows, other_rows, row):
    return jnp.where(
        own, own_rows[row : row + 1, :].astype(WIDE), other_rows[row : row + 1, :].astype(WIDE)
    )


def inverse_size(wide):
    return lax.rsqrt(jnp.mean(wide * wide, axis=-1, keepdims=True) + EPSILON)


def both_sums(own, values):
    mine = jnp.sum(jnp.where(own, values, 0.0), axis=0, keepdims=True)
    return mine, jnp.sum(jnp.where(own, 0.0, values), axis=0, keepdims=True)


def same_head(rows, columns):
    row_head = lax.broadcasted_iota(jnp.int32, (rows, columns), 0) // HEAD
    return row_head == lax.broadcasted_iota(jnp.int32, (rows, columns), 1) // HEAD


def fold(square):
    size = square.shape[1]
    total = None
    for low in range(0, size, LANES):
        part = square[:, low : min(low + LANES, size)]
        if part.shape[1] < LANES:
            part = jnp.concatenate(
                [part, jnp.zeros((part.shape[0], LANES - part.shape[1]), part.dtype)], axis=1
            )
        total = part if total is None else total + part
    return total


def unfold(folded):
    size = folded.shape[0]
    parts = [folded[:, : min(LANES, size - low)] for low in range(0, size, LANES)]
    return jnp.where(same_head(size, size), jnp.concatenate(parts, axis=1), 0.0)


def packed(square, totals):
    keep = same_head(square.shape[0], square.shape[1])
    return fold(jnp.where(keep, square, 0.0)) + pltpu.roll(
        fold(jnp.where(keep, totals, 0.0)), HEAD, 1
    )


def unpacked(folded):
    return unfold(folded), unfold(pltpu.roll(folded, LANES - HEAD, 1))


def log_exp(wide):
    return jnp.maximum(wide, 0.0) + jnp.log1p(jnp.exp(-jnp.abs(wide)))


def logistic(wide):
    return 1.0 / (1.0 + jnp.exp(-wide))


def self_project_body(table, x, mod_own, mod_other, weight, normed, raw, q, k, v, own_out, other_out, squares, totals):
    step = pl.program_id(0)
    rows, columns = q.shape
    own = own_image(table, table[FIRST] + step * rows, rows)
    wide = x[...].astype(WIDE)
    low = (
        wide * inverse_size(wide) * (1.0 + pick(own, mod_own, mod_other, 1))
        + pick(own, mod_own, mod_other, 0)
    ).astype(LOW)
    normed[...] = low
    out = dot(low, weight[...])
    raw[...] = out[:, : 2 * columns]
    q[...] = log_exp(out[:, :columns]).astype(LOW)
    keys = log_exp(out[:, columns : 2 * columns]).astype(LOW)
    values = out[:, 2 * columns :].astype(LOW)
    k[...] = keys
    v[...] = values

    @pl.when(step == 0)
    def _():
        squares[...] = jnp.zeros_like(squares)
        totals[...] = jnp.zeros_like(totals)

    ones = jnp.ones((rows, columns), LOW)
    for image in range(2):
        zero = jnp.zeros_like(keys)
        masked = jnp.where(own, keys, zero) if image == 0 else jnp.where(own, zero, keys)
        squares[image] += over_tokens(masked, values)
        totals[image] += over_tokens(masked, ones)

    @pl.when(step == pl.num_programs(0) - 1)
    def _():
        own_out[...] = packed(squares[0], totals[0])
        other_out[...] = packed(squares[1], totals[1])


def self_project(table, x, mod_own, mod_other, weight, columns):
    tokens, width = x.shape
    rows = 128
    row = lambda c: pl.BlockSpec((rows, c), lambda i, t: (i, 0))
    fixed = lambda *s: pl.BlockSpec(s, lambda i, t: (0,) * len(s))
    return call(
        self_project_body,
        "self_project",
        [((tokens, width), LOW), ((tokens, 2 * columns), WIDE)]
        + [((tokens, columns), LOW)] * 3
        + [((columns, LANES), WIDE)] * 2,
        (x, mod_own, mod_other, weight),
        grid=(tokens // rows,),
        in_specs=[row(width), fixed(*mod_own.shape), fixed(*mod_own.shape), fixed(*weight.shape)],
        out_specs=[row(width), row(2 * columns)]
        + [row(columns)] * 3
        + [fixed(columns, LANES)] * 2,
        scratch=[pltpu.VMEM((2, columns, columns), WIDE)] * 2,
        flops=4 * tokens * width * 3 * columns,
        table=table,
    )


def keep_squares(kernels, key_totals, own_fold, other_fold):
    for image, folded in enumerate((own_fold, other_fold)):
        square, total = unpacked(folded[...])
        kernels[image, 0], kernels[image, 1] = split(square)
        key_totals[image, 0], key_totals[image, 1] = split(total)


def self_attend_body(table, q, own_fold, other_fold, attended, wide_out, denominator, kernels, key_totals):
    step = pl.program_id(0)
    rows = q.shape[0]

    @pl.when(step == 0)
    def _():
        keep_squares(kernels, key_totals, own_fold, other_fold)

    own = own_image(table, table[FIRST] + step * rows, rows)
    queries = q[...]

    def both(pair):
        own_part = dot(queries, pair[0, 0]) + dot(queries, pair[0, 1])
        return jnp.where(own, own_part, dot(queries, pair[1, 0]) + dot(queries, pair[1, 1]))

    under = both(key_totals) + 1.0
    out = both(kernels) / under
    attended[...] = out.astype(LOW)
    wide_out[...] = out
    denominator[...] = under


def self_attend(table, q, own_fold, other_fold):
    tokens, columns = q.shape
    rows = 128
    row = pl.BlockSpec((rows, columns), lambda i, t: (i, 0))
    fixed = pl.BlockSpec((columns, LANES), lambda i, t: (0, 0))
    return call(
        self_attend_body,
        "self_attend",
        [((tokens, columns), LOW), ((tokens, columns), WIDE), ((tokens, columns), WIDE)],
        (q, own_fold, other_fold),
        grid=(tokens // rows,),
        in_specs=[row, fixed, fixed],
        out_specs=[row, row, row],
        scratch=[pltpu.VMEM((2, 2, columns, columns), LOW)] * 2,
        flops=16 * tokens * columns * columns,
        table=table,
    )


def self_back_body(table, grad, q, wide_out, denominator, own_fold, other_fold, grad_q, own_out, other_out, kernels, key_totals, squares, totals):
    step = pl.program_id(0)
    rows, columns = q.shape

    @pl.when(step == 0)
    def _():
        keep_squares(kernels, key_totals, own_fold, other_fold)
        squares[...] = jnp.zeros_like(squares)
        totals[...] = jnp.zeros_like(totals)

    place = lax.rem(table[TP_PLACE] + step, pl.num_programs(0))
    own = own_image(table, table[FIRST] + place * rows, rows)
    wide = grad[0].astype(WIDE)
    over = 1.0 / denominator[...]
    numer_high, numer_low = split(wide * over)
    ones = jnp.where(same_head(columns, columns), 1.0, 0.0).astype(LOW)
    high, low = split(wide * wide_out[...])
    denom = -(dot(high, ones) + dot(low, ones)) * over
    denom_high, denom_low = split(denom)

    def back(image):
        square, total = kernels[image, 0], key_totals[image, 0]
        through = (
            times_transposed(numer_high, square)
            + times_transposed(numer_low, square)
            + times_transposed(numer_high, kernels[image, 1])
        )
        totals_part = (
            times_transposed(denom_high, total)
            + times_transposed(denom_low, total)
            + times_transposed(denom_high, key_totals[image, 1])
        )
        return through + totals_part * (1.0 / HEAD)

    grad_q[...] = jnp.where(own, back(0), back(1))
    queries = q[...]
    zero = jnp.zeros_like(queries)
    for image in range(2):
        masked = jnp.where(own, queries, zero) if image == 0 else jnp.where(own, zero, queries)
        squares[image] += over_tokens(masked, numer_high) + over_tokens(masked, numer_low)
        totals[image] += over_tokens(masked, denom_high) + over_tokens(masked, denom_low)

    @pl.when(step == pl.num_programs(0) - 1)
    def _():
        own_out[...] = packed(squares[0], totals[0])
        other_out[...] = packed(squares[1], totals[1])


def self_back(table, grad, q, wide_out, denominator, own_fold, other_fold):
    count, rows, columns = grad.shape
    tokens = q.shape[0]
    turn = lambda i, t: (lax.rem(t[TP_PLACE] + i, count), 0)
    row = pl.BlockSpec((rows, columns), turn)
    fixed = pl.BlockSpec((columns, LANES), lambda i, t: (0, 0))
    return call(
        self_back_body,
        "self_back",
        [((tokens, columns), WIDE)] + [((columns, LANES), WIDE)] * 2,
        (grad, q, wide_out, denominator, own_fold, other_fold),
        grid=(count,),
        in_specs=[pl.BlockSpec((1, rows, columns), lambda i, t: (i, 0, 0)), row, row, row, fixed, fixed],
        out_specs=[row, fixed, fixed],
        scratch=[pltpu.VMEM((2, 2, columns, columns), LOW)] * 2
        + [pltpu.VMEM((2, columns, columns), WIDE)] * 2,
        flops=48 * tokens * columns * columns,
        table=table,
    )


def self_project_back_body(table, grad_q, k, v, raw, own_fold, other_fold, grad_out, kernels, key_totals):
    step = pl.program_id(0)
    rows, columns = k.shape

    @pl.when(step == 0)
    def _():
        keep_squares(kernels, key_totals, own_fold, other_fold)

    own = own_image(table, table[FIRST] + step * rows, rows)
    keys, values = k[...], v[...]
    ones = jnp.ones((16, columns), LOW)

    def grad_k(image):
        total = times_transposed(ones, key_totals[image, 0]) + times_transposed(
            ones, key_totals[image, 1]
        )
        return (
            times_transposed(values, kernels[image, 0])
            + times_transposed(values, kernels[image, 1])
            + total[:1] * (1.0 / HEAD)
        )

    def grad_v(image):
        return dot(keys, kernels[image, 0]) + dot(keys, kernels[image, 1])

    given = raw[...]
    q_part = grad_q[...] * logistic(given[:, :columns])
    k_part = jnp.where(own, grad_k(0), grad_k(1)) * logistic(given[:, columns:])
    v_part = jnp.where(own, grad_v(0), grad_v(1))
    grad_out[...] = jnp.concatenate([q_part, k_part, v_part], axis=1).astype(LOW)


def self_project_back(table, grad_q, k, v, raw, own_fold, other_fold):
    tokens, columns = k.shape
    rows = 128
    row = lambda c: pl.BlockSpec((rows, c), lambda i, t: (i, 0))
    fixed = pl.BlockSpec((columns, LANES), lambda i, t: (0, 0))
    return call(
        self_project_back_body,
        "self_project_back",
        [((tokens, 3 * columns), LOW)],
        (grad_q, k, v, raw, own_fold, other_fold),
        grid=(tokens // rows,),
        in_specs=[row(columns), row(columns), row(columns), row(2 * columns), fixed, fixed],
        out_specs=[row(3 * columns)],
        scratch=[pltpu.VMEM((2, 2, columns, columns), LOW)] * 2,
        flops=16 * tokens * columns * columns,
        table=table,
    )[0]


def live_keys(table, own, keys):
    place = lax.broadcasted_iota(jnp.int32, (1, keys), 1)
    return place < jnp.where(own, table[OWN_LENGTH], table[OTHER_LENGTH])


def shard_of(first, rest, step, offset=0):
    return first[...] if step == 0 else rest[offset + step - 1]


def middle_body(table, att, x, mod_own, mod_other, out_first, query_first, cross_first, rest, kv_own, kv_other, branch, after_low, queries_out, probs_out, text_out, after_cross, normed):
    count, rows, columns = att.shape
    keys = kv_own.shape[1]
    heads = columns // CROSS_HEAD
    own = own_image(table, table[BLOCK_FIRST], rows)
    y1 = jnp.zeros((rows, x.shape[1]), WIDE)
    for step in range(count):
        y1 += times_transposed(att[step], shard_of(out_first, rest, step))
    branch[...] = y1
    x1 = x[...].astype(WIDE) + pick(own, mod_own, mod_other, 2) * y1
    x1_low = x1.astype(LOW)
    after_low[...] = x1_low
    live = live_keys(table, own, keys)
    yc = jnp.zeros_like(x1)
    for step in range(count):
        queries = dot(x1_low, shard_of(query_first, rest, step, count - 1)).astype(LOW)
        queries_out[step] = queries
        mine, theirs = kv_own[step], kv_other[step]
        parts = []
        for head in range(heads):
            lanes = slice(head * CROSS_HEAD, (head + 1) * CROSS_HEAD)
            wide_lanes = slice(columns + head * CROSS_HEAD, columns + (head + 1) * CROSS_HEAD)
            q = queries[:, lanes]
            scores = jnp.where(
                own, times_transposed(q, mine[:, lanes]), times_transposed(q, theirs[:, lanes])
            ) * (1.0 / math.sqrt(CROSS_HEAD))
            scores = jnp.where(live, scores, MASKED_OUT)
            raised = jnp.exp(scores - jnp.max(scores, axis=-1, keepdims=True))
            probs = raised / jnp.sum(raised, axis=-1, keepdims=True)
            probs_out[step * heads + head] = probs
            low = probs.astype(LOW)
            parts.append(
                jnp.where(own, dot(low, mine[:, wide_lanes]), dot(low, theirs[:, wide_lanes]))
            )
        text = jnp.concatenate(parts, axis=1).astype(LOW)
        text_out[step] = text
        yc += times_transposed(text, shard_of(cross_first, rest, step, 2 * count - 2))
    x2 = x1 + yc
    after_cross[...] = x2
    normed[...] = (
        x2 * inverse_size(x2) * (1.0 + pick(own, mod_own, mod_other, 4))
        + pick(own, mod_own, mod_other, 3)
    ).astype(LOW)


def middle_back_body(table, grad_rows, up_weight, grad_1, grad_2, grad_3, x2_in, upstream, branch, mod_own, mod_other, out_first, query_first, cross_first, rest, kv_own, kv_other, probs_in, queries_in, cross_grad, query_grad, attn_grad, attended_grad, after_grad, sums, kv_own_grad, kv_other_grad):
    count, rows, columns = queries_in.shape
    keys = kv_own.shape[1]
    heads = columns // CROSS_HEAD
    scale = 1.0 / math.sqrt(CROSS_HEAD)
    own = own_image(table, table[BLOCK_FIRST], rows)
    grad = (
        times_transposed(grad_rows[...], up_weight[...])
        + grad_1[...].astype(WIDE)
        + grad_2[...].astype(WIDE)
        + grad_3[...].astype(WIDE)
    )
    x2 = x2_in[...]
    inverse = inverse_size(x2)
    xh = x2 * inverse
    sums[0:1], sums[1:2] = both_sums(own, grad)
    sums[2:3], sums[3:4] = both_sums(own, grad * xh)
    e = grad * (1.0 + pick(own, mod_own, mod_other, 4))
    dx2 = upstream[...].astype(WIDE) + inverse * (
        e - xh * jnp.mean(e * xh, axis=-1, keepdims=True)
    )
    dyc = dx2.astype(LOW)
    cross_grad[...] = dyc
    dx1 = dx2
    for step in range(count):
        doc = dot(dyc, shard_of(cross_first, rest, step, 2 * count - 2)).astype(LOW)
        mine, theirs = kv_own[step], kv_other[step]
        queries = queries_in[step]
        query_parts = []
        key_parts = ([], [])
        value_parts = ([], [])
        for head in range(heads):
            lanes = slice(head * CROSS_HEAD, (head + 1) * CROSS_HEAD)
            wide_lanes = slice(columns + head * CROSS_HEAD, columns + (head + 1) * CROSS_HEAD)
            do, q = doc[:, lanes], queries[:, lanes]
            probs = probs_in[step * heads + head]
            dp = jnp.where(
                own,
                times_transposed(do, mine[:, wide_lanes]),
                times_transposed(do, theirs[:, wide_lanes]),
            )
            ds = (probs * (dp - jnp.sum(probs * dp, axis=-1, keepdims=True))).astype(LOW)
            low = probs.astype(LOW)
            zero = jnp.zeros_like(ds)
            query_parts.append(
                jnp.where(own, dot(ds, mine[:, lanes]), dot(ds, theirs[:, lanes])) * scale
            )
            for image in range(2):
                mask = (lambda a: jnp.where(own, a, zero)) if image == 0 else (
                    lambda a: jnp.where(own, zero, a)
                )
                key_parts[image].append(over_tokens(mask(ds), q) * scale)
                value_parts[image].append(over_tokens(mask(low), do))
        dqc = jnp.concatenate(query_parts, axis=1).astype(LOW)
        query_grad[step] = dqc
        kv_own_grad[step] = jnp.concatenate(key_parts[0] + value_parts[0], axis=1).astype(LOW)
        kv_other_grad[step] = jnp.concatenate(key_parts[1] + value_parts[1], axis=1).astype(LOW)
        dx1 = dx1 + times_transposed(dqc, shard_of(query_first, rest, step, count - 1))
    after_grad[...] = dx1
    sums[4:5], sums[5:6] = both_sums(own, dx1 * branch[...])
    sums[6:8] = jnp.zeros((2, sums.shape[1]), WIDE)
    dy1 = (dx1 * pick(own, mod_own, mod_other, 2)).astype(LOW)
    attn_grad[...] = dy1
    for step in range(count):
        attended_grad[step] = dot(dy1, shard_of(out_first, rest, step)).astype(LOW)


def first_norm_back_body(table, grad_rows, weight, grad_1, grad_2, grad_3, after_grad, x, mod_own, mod_other, input_grad, sums):
    rows = x.shape[0]
    own = own_image(table, table[BLOCK_FIRST], rows)
    grad = (
        times_transposed(grad_rows[...], weight[...])
        + grad_1[...].astype(WIDE)
        + grad_2[...].astype(WIDE)
        + grad_3[...].astype(WIDE)
    )
    wide = x[...].astype(WIDE)
    inverse = inverse_size(wide)
    xh = wide * inverse
    sums[0:1], sums[1:2] = both_sums(own, grad)
    sums[2:3], sums[3:4] = both_sums(own, grad * xh)
    sums[4:8] = jnp.zeros((4, sums.shape[1]), WIDE)
    e = grad * (1.0 + pick(own, mod_own, mod_other, 1))
    input_grad[...] = (
        after_grad[...] + inverse * (e - xh * jnp.mean(e * xh, axis=-1, keepdims=True))
    ).astype(LOW)


def output_body(table, hidden_rows, weight, branch_1, branch_2, branch_3, x2, upstream, mod_own, mod_other, output, sums):
    rows = x2.shape[0]
    own = own_image(table, table[BLOCK_FIRST], rows)
    branch = (
        times_transposed(hidden_rows[...], weight[...])
        + branch_1[...].astype(WIDE)
        + branch_2[...].astype(WIDE)
        + branch_3[...].astype(WIDE)
    )
    sums[0:1], sums[1:2] = both_sums(own, upstream[...].astype(WIDE) * branch)
    sums[2:8] = jnp.zeros((6, sums.shape[1]), WIDE)
    output[...] = (x2[...] + pick(own, mod_own, mod_other, 5) * branch).astype(LOW)


def up_body(table, x, weight, wide_out, low_out, ordered):
    block = x[0]
    up = dot(block, weight[...])
    ordered[...] = block
    wide_out[...] = up
    low_out[...] = (up * logistic(up)).astype(LOW)


def up_project(table, blocks, weight):
    count, rows, width = blocks.shape
    columns = weight.shape[1]
    turn = lambda i, t: (lax.rem(t[TP_PLACE] + count - i, count), 0)
    return call(
        up_body,
        "up_project",
        [((count * rows, columns), WIDE), ((count * rows, columns), LOW), ((count * rows, width), LOW)],
        (blocks, weight),
        grid=(count,),
        in_specs=[
            pl.BlockSpec((1, rows, width), lambda i, t: (i, 0, 0)),
            pl.BlockSpec(weight.shape, lambda i, t: (0, 0)),
        ],
        out_specs=[pl.BlockSpec((rows, columns), turn)] * 2 + [pl.BlockSpec((rows, width), turn)],
        flops=2 * count * rows * width * columns,
        table=table,
    )


def fill(padded, block, rim):
    tokens = block.shape[0]
    edge = rim[...].astype(WIDE)
    padded[0:MAXW, :] = edge
    padded[MAXW : MAXW + tokens, :] = block.astype(WIDE)
    padded[MAXW + tokens : 2 * MAXW + tokens, :] = edge


def fill_masks(table, masks):
    tokens = masks.shape[1]
    place = table[FIRST] + lax.broadcasted_iota(jnp.int32, (tokens, LANES), 0)
    width = table[WIDTH]
    cut = table[CUT]
    late = place >= cut
    start = jnp.where(late, cut, 0)
    end = jnp.where(late, table[SEQ_TOKENS], cut)
    column = lax.bitwise_and(place, width - 1)
    one, none = jnp.ones((tokens, LANES), WIDE), jnp.zeros((tokens, LANES), WIDE)
    masks[0] = jnp.where(place - width >= start, one, none)
    masks[1] = jnp.where(place + width < end, one, none)
    masks[2] = jnp.where(column > 0, one, none)
    masks[3] = jnp.where(column < width - 1, one, none)


CHUNK = 64


def three_rows(table, padded, masks, low):
    width = table[WIDTH]
    above = padded[pl.ds(pl.multiple_of(MAXW + low - width, 16), CHUNK), :]
    below = padded[pl.ds(pl.multiple_of(MAXW + low + width, 16), CHUNK), :]
    own = padded[pl.ds(pl.multiple_of(MAXW + low, 16), CHUNK), :]
    rows = pl.ds(pl.multiple_of(low, 16), CHUNK)
    return above * masks[0, rows, :], own, below * masks[1, rows, :]


def nine_taps(rows, taps, left_mask, right_mask):
    mixed = [sum(rows[a] * taps[a][b] for a in range(3)) for b in range(3)]
    return (
        mixed[1]
        + left_mask * pltpu.roll(mixed[0], 1, 0)
        + right_mask * pltpu.roll(mixed[2], CHUNK - 1, 0)
    )


def taps_of(taps, flip):
    read = lambda a, b: taps[3 * a + b : 3 * a + b + 1, :]
    return [[read(2 - a, 2 - b) if flip else read(a, b) for b in range(3)] for a in range(3)]


def mix_body(table, value, gate, value_rim, gate_rim, value_taps, gate_taps, grad_hidden, hidden, grads, value_pad, gate_pad, masks):
    @pl.when(pl.program_id(0) == 0)
    def _():
        fill_masks(table, masks)

    fill(value_pad, value[...], value_rim)
    fill(gate_pad, gate[...], gate_rim)
    value_weights, gate_weights = taps_of(value_taps, False), taps_of(gate_taps, False)

    @pl.loop(0, value.shape[0] // CHUNK)
    def _(index):
        low = index * CHUNK
        rows = pl.ds(pl.multiple_of(low, CHUNK), CHUNK)
        left, right = masks[2, rows, :], masks[3, rows, :]
        mv = nine_taps(three_rows(table, value_pad, masks, low), value_weights, left, right)
        mg = nine_taps(three_rows(table, gate_pad, masks, low), gate_weights, left, right)
        sigma = logistic(mg)
        gated = mg * sigma
        hidden[rows, :] = (mv * gated).astype(LOW)
        dh = grad_hidden[rows, :]
        grads[0, rows, :] = (dh * gated).astype(LOW)
        grads[1, rows, :] = (dh * mv * (sigma * (1.0 + mg * (1.0 - sigma)))).astype(LOW)


def mix(table, activated, rim, taps, grad_hidden):
    tokens, wide = activated.shape
    columns = wide // 2
    tiles = columns // LANES
    block = lambda r, shift: pl.BlockSpec((r, LANES), lambda i, t: (0, i + shift))
    pad = pltpu.VMEM((tokens + 2 * MAXW, LANES), WIDE)
    return call(
        mix_body,
        "mix",
        [((tokens, columns), LOW), ((2, tokens, columns), LOW)],
        (activated, activated, rim, rim, taps, taps, grad_hidden),
        grid=(tiles,),
        in_specs=[
            block(tokens, 0),
            block(tokens, tiles),
            block(MAXW, 0),
            block(MAXW, tiles),
            block(taps.shape[0], 0),
            block(taps.shape[0], tiles),
            block(tokens, 0),
        ],
        out_specs=[
            block(tokens, 0),
            pl.BlockSpec((2, tokens, LANES), lambda i, t: (0, 0, i)),
        ],
        scratch=[pad, pad, pltpu.VMEM((4, tokens, LANES), WIDE)],
        flops=6000 * tokens * columns // 2,
        table=table,
    )


def mix_back_body(table, grads, grads_rim, activated, rim, taps, up, grad_up, tap_grads, grad_pad, act_pad, masks):
    @pl.when(pl.program_id(0) == 0)
    def _():
        fill_masks(table, masks)

    fill(grad_pad, grads[0], grads_rim.at[0])
    fill(act_pad, activated[...], rim)
    weights = taps_of(taps, True)

    def step(index, sums):
        low = index * CHUNK
        rows = pl.ds(pl.multiple_of(low, CHUNK), CHUNK)
        left, right = masks[2, rows, :], masks[3, rows, :]
        mine = three_rows(table, grad_pad, masks, low)
        dact = nine_taps(mine, weights, left, right)
        given = up[rows, :]
        sigma = logistic(given)
        grad_up[rows, :] = (dact * (sigma * (1.0 + given * (1.0 - sigma)))).astype(LOW)
        acts = three_rows(table, act_pad, masks, low)
        turned = (
            right * pltpu.roll(mine[1], CHUNK - 1, 0),
            mine[1],
            left * pltpu.roll(mine[1], 1, 0),
        )
        return tuple(
            sums[3 * a + b]
            + jnp.sum((acts[a] * turned[b]).reshape(CHUNK // 8, 8, LANES), axis=0)
            for a in range(3)
            for b in range(3)
        )

    zero = jnp.zeros((8, LANES), WIDE)
    sums = lax.fori_loop(0, activated.shape[0] // CHUNK, step, (zero,) * 9)
    for tap in range(9):
        tap_grads[tap : tap + 1, :] = jnp.sum(sums[tap], axis=0, keepdims=True)
    tap_grads[9:16, :] = jnp.zeros((7, LANES), WIDE)


def mix_back(table, grads, grads_rim, activated, rim, taps, up):
    tokens, wide = activated.shape
    columns = wide // 2
    tiles = columns // LANES
    block = lambda r: pl.BlockSpec((r, LANES), lambda i, t: (0, i))
    half = lambda r: pl.BlockSpec(
        (1, r, LANES), lambda i, t: (lax.div(i, tiles), 0, lax.rem(i, tiles))
    )
    pad = pltpu.VMEM((tokens + 2 * MAXW, LANES), WIDE)
    return call(
        mix_back_body,
        "mix_back",
        [((tokens, wide), LOW), ((16, wide), WIDE)],
        (grads, grads_rim, activated, rim, taps, up),
        grid=(2 * tiles,),
        in_specs=[half(tokens), half(MAXW), block(tokens), block(MAXW), block(taps.shape[0]), block(tokens)],
        out_specs=[block(tokens), block(16)],
        scratch=[pad, pad, pltpu.VMEM((4, tokens, LANES), WIDE)],
        flops=6000 * tokens * columns,
        table=table,
    )


def eighths_body(table, *refs):
    for place, ref in enumerate(refs[:-1]):
        refs[-1][place] = ref[...]


def order_body(table, *refs):
    pieces, out = refs[:-1], refs[-1]
    units, rows = pieces[0].shape[0], pieces[0].shape[1]
    weights = 3
    for place, piece in enumerate(pieces):
        block = lax.bitwise_xor(table[ROW_PLACE], place)
        for unit in range(units):
            target = (unit % weights) * (units // weights) + unit // weights
            out[target, pl.ds(pl.multiple_of(block * rows, 16), rows), :] = piece[unit]


def after(value, *others):
    return lax.optimization_barrier((value, others))[0]


def fetch_eighths(weights):
    rows, columns = weights[0].shape
    own = rows // 8
    eighth = call(
        eighths_body,
        "eighths",
        [((len(weights), own, columns), weights[0].dtype)],
        weights,
        in_specs=[pl.BlockSpec((own, columns), lambda i, t: (t[0], 0))] * len(weights),
        out_specs=[pl.BlockSpec((len(weights), own, columns), lambda i, t: (0, 0, 0))],
        table=(lax.axis_index("seq") % 8).reshape(1).astype(jnp.int32),
    )[0]
    return [from_behind(eighth, step) for step in range(1, lax.axis_size("tp"))]


def share_eighths(table, fetched, ready):
    count = lax.axis_size("seq")
    far = lambda flip: lax.ppermute(fetched, "seq", [(k, k ^ flip) for k in range(count)])
    even = [fetched] + after([far(2), far(4), far(6)], *ready)
    pieces = []
    for piece in even:
        pieces += [piece, swapped(piece, "seq", 0)]
    units, rows, columns = fetched.shape
    return call(
        order_body, "order", [((units, 8 * rows, columns), fetched.dtype)], pieces, table=table
    )[0]


def token_block(values, place):
    count = lax.axis_size("tp")
    size = values.shape[0] // count
    return lax.dynamic_slice_in_dim(values, (place % count) * size, size, 0)


def placed_blocks(blocks):
    count = len(blocks)
    place = lax.axis_index("tp")
    result = jnp.zeros((count,) + blocks[0].shape, blocks[0].dtype)
    for step in range(count):
        result = lax.dynamic_update_index_in_dim(result, blocks[step], (place - step) % count, 0)
    return result.reshape((count * blocks[0].shape[0],) + blocks[0].shape[1:])


def all_blocks(block):
    return [block] + [from_behind(block, step) for step in range(1, lax.axis_size("tp"))]


def products_body(table, left, right, *outs):
    count = len(outs) + 1
    rows = left.shape[0] // count
    for step, out in enumerate(outs):
        low = lax.rem(table[TP_PLACE] + step + 1, count) * rows
        block = left[pl.ds(pl.multiple_of(low, 16), rows), :]
        out[...] = times_transposed(block, right[...]).astype(LOW)


def products_to_send(table, left, right):
    count = lax.axis_size("tp")
    shape = (left.shape[0] // count, right.shape[0])
    return list(
        call(products_body, "products", [(shape, LOW)] * (count - 1), (left, right), table=table)
    )


def own_rows(left):
    count = lax.axis_size("tp")
    return pl.BlockSpec((left.shape[0] // count, left.shape[1]), lambda i, t: (t[TP_PLACE], 0))


def sent_ahead(products):
    return [from_behind(product, step + 1) for step, product in enumerate(products)]


def same_everywhere(block):
    pair = block + swapped(block, "tp", 0)
    return pair + swapped(pair, "tp", 1)


def sum_rows(grad):
    return lax.optimization_barrier(
        lax.psum_scatter(grad.astype(LOW), "seq", scatter_dimension=0, tiled=True)
    )


def square_body(table, dyc, text, x1, dqc, dy1, att, out):
    parts = [
        over_tokens(left[...], right[0]) for left, right in ((dyc, text), (x1, dqc), (dy1, att))
    ]
    rest = out.shape[1] - sum(part.shape[1] for part in parts)
    if rest:
        parts.append(jnp.zeros((out.shape[0], rest), WIDE))
    out[...] = jnp.concatenate(parts, axis=1).astype(LOW)


def square_parts(table, lefts, rights):
    rows, width = lefts[0].shape
    count, _, columns = rights[0].shape
    block = -(-3 * columns // LANES) * LANES
    whole = pl.BlockSpec((rows, width), lambda i, t: (0, 0))
    one = pl.BlockSpec((1, rows, columns), lambda i, t: (i, 0, 0))
    return call(
        square_body,
        "square_parts",
        [((width, count * block), LOW)],
        [array for pair in zip(lefts, rights) for array in pair],
        grid=(count,),
        in_specs=[whole, one] * 3,
        out_specs=[pl.BlockSpec((width, block), lambda i, t: (0, i))],
        flops=8 * rows * width * count * block,
        table=table,
    )[0]


def ffn_body(table, grad_ffn, hidden, normed, grad_up, out):
    step = pl.program_id(0)

    @pl.when(step == 0)
    def _():
        out[...] = over_tokens(grad_ffn[...], hidden[...]).astype(LOW)

    @pl.when(step > 0)
    def _():
        out[...] = over_tokens(normed[...], grad_up[...]).astype(LOW)


def ffn_parts_of(table, grad_ffn, hidden, normed, grad_up):
    tokens, width = normed.shape
    columns = hidden.shape[1]
    whole = pl.BlockSpec((tokens, width), lambda i, t: (0, 0))
    return call(
        ffn_body,
        "ffn_parts",
        [((width, 3 * columns), LOW)],
        (grad_ffn, hidden, normed, grad_up),
        grid=(3,),
        in_specs=[
            whole,
            pl.BlockSpec((tokens, columns), lambda i, t: (0, 0)),
            whole,
            pl.BlockSpec((tokens, columns), lambda i, t: (0, jnp.maximum(i - 1, 0))),
        ],
        out_specs=[pl.BlockSpec((width, columns), lambda i, t: (0, i))],
        table=table,
    )[0]


def late_body(table, normed, grad_projected, text, kv_grad, out):
    first = over_tokens(normed[...], grad_projected[...]).astype(LOW)
    second = over_tokens(text[...], kv_grad[...]).astype(LOW)
    out[...] = jnp.concatenate([first, second], axis=1)


def shards(
    hidden_in,
    cotangent,
    modulation,
    text_states,
    image_shapes,
    text_lengths,
    qkv_weight,
    attn_out_weight,
    cross_q_weight,
    cross_kv_weight,
    cross_out_weight,
    up_weight,
    conv_weight,
    down_weight,
):
    tokens_here, width = hidden_in.shape
    context = text_states.shape[1]
    keys = -(-context // 16) * 16
    self_cols = qkv_weight.shape[2]
    cross_cols = cross_q_weight.shape[1]
    ffn_cols = up_weight.shape[2]
    ffn_pad = -(-ffn_cols // LANES) * LANES
    count = lax.axis_size("tp")
    tp_index = lax.axis_index("tp")
    block_size = tokens_here // count
    seq_index = lax.axis_index("seq")
    side = seq_index % 2
    first_half = side == 0
    pair = seq_index - side
    pair_shapes = lax.dynamic_slice_in_dim(image_shapes, pair, 2, 0)
    row_width = pair_shapes[0, 1]
    lengths = lax.dynamic_slice_in_dim(text_lengths, pair, 2, 0)
    first_place = side * tokens_here
    table = jnp.stack(
        [
            first_place,
            pair_shapes[0, 0] * row_width,
            side,
            row_width,
            jnp.where(first_half, lengths[0], lengths[1]),
            jnp.where(first_half, lengths[1], lengths[0]),
            first_place + tp_index * block_size,
            jnp.int32(2 * tokens_here),
            tp_index,
            seq_index % 8,
        ]
    ).astype(jnp.int32)

    mod_own = modulation[0]
    mod_other = swapped(mod_own, "seq", 0).astype(WIDE)
    mod_own = mod_own.astype(WIDE)
    fetched = jnp.concatenate(fetch_eighths([attn_out_weight, cross_q_weight, cross_out_weight]))
    qkv_flat = qkv_weight.reshape(width, 3 * self_cols)
    normed_low, raw, q, k, v, part_own, part_other = self_project(
        table, hidden_in, mod_own, mod_other, qkv_flat, self_cols
    )
    theirs = swapped(jnp.stack([part_own, part_other]), "seq", 0)
    fetched = after(fetched, q)
    text_rows = jnp.pad(text_states[0], ((0, keys - context), (0, 0)))
    kv_here = dot(
        after(text_rows, fetched), cross_kv_weight.reshape(width, 2 * cross_cols)
    ).astype(LOW)
    kernel_own, kernel_other = part_own + theirs[1], part_other + theirs[0]
    attended, attended_wide, denominator = self_attend(
        table, after(q, kv_here), kernel_own, kernel_other
    )

    x_block = token_block(hidden_in, tp_index)
    up_block = token_block(cotangent, tp_index)
    up_flat = jnp.pad(after(up_weight, attended), ((0, 0), (0, 0), (0, ffn_pad - ffn_cols))).reshape(
        width, 2 * ffn_pad
    )
    down_flat = jnp.pad(after(down_weight, attended), ((0, 0), (0, ffn_pad - ffn_cols)))
    taps = (
        jnp.pad(conv_weight, ((0, 7), (0, 0), (0, ffn_pad - ffn_cols)))
        .reshape(16, 2 * ffn_pad)
        .astype(WIDE)
    )
    gate_rows = jnp.where(
        (first_place + jnp.arange(tokens_here, dtype=jnp.int32) >= table[CUT])[:, None] == (side == 1),
        mod_own[5:6],
        mod_other[5:6],
    )
    grad_ffn = (cotangent.astype(WIDE) * gate_rows).astype(LOW)
    grad_hidden = dot(grad_ffn, down_flat)
    ready = (up_flat, taps, grad_hidden)
    kv_own = jnp.stack(after(all_blocks(kv_here), *ready))
    kv_other = swapped(kv_own, "seq", 0)
    rest = share_eighths(table, fetched, ready)
    attended_blocks = jnp.stack(
        [token_block(attended, tp_index)]
        + [from_behind(token_block(attended, tp_index + step), step) for step in range(1, count)]
    )
    all_heads = count * cross_cols // CROSS_HEAD
    weights = (attn_out_weight, cross_q_weight, cross_out_weight, rest)
    branch, after_low, queries, probs, text_low, after_cross, normed_two = call(
        middle_body,
        "middle",
        [
            ((block_size, width), WIDE),
            ((block_size, width), LOW),
            ((count, block_size, cross_cols), LOW),
            ((all_heads, block_size, keys), WIDE),
            ((count, block_size, cross_cols), LOW),
            ((block_size, width), WIDE),
            ((block_size, width), LOW),
        ],
        (attended_blocks, x_block, mod_own, mod_other, *weights, kv_own, kv_other),
        flops=60 * block_size * width * width,
        table=table,
    )

    blocks_two = jnp.stack(all_blocks(normed_two))
    up_wide, activated, normed_two_low = up_project(table, blocks_two, up_flat)
    rim = swapped(jnp.where(first_half, activated[-MAXW:], activated[:MAXW]), "seq", 0)
    hidden, grads = mix(table, activated, rim, taps, grad_hidden)
    grads_rim = swapped(jnp.where(first_half, grads[:, -MAXW:], grads[:, :MAXW]), "seq", 0)
    whole = pl.BlockSpec(memory_space=pltpu.VMEM)
    branch_sent = products_to_send(table, hidden, down_flat)
    grad_up, tap_part = mix_back(
        table, grads, grads_rim, activated, rim, taps, after(up_wide, branch_sent)
    )
    branch_parts = sent_ahead(branch_sent)
    norm_two_sent = products_to_send(table, grad_up, up_flat)
    grad_norm_two = sent_ahead(after(norm_two_sent, branch_parts))
    ffn_parts = ffn_parts_of(
        table, grad_ffn, after(hidden, norm_two_sent), normed_two_low, grad_up
    )
    ffn_rows = sum_rows(after(ffn_parts, grad_norm_two))
    output_block, output_sums = call(
        output_body,
        "output",
        [((block_size, width), LOW), ((8, width), WIDE)],
        (
            hidden,
            down_flat,
            *branch_parts,
            after_cross,
            up_block,
            mod_own,
            mod_other,
        ),
        in_specs=[own_rows(hidden)] + [whole] * 8,
        table=table,
    )
    output_blocks = all_blocks(output_block)

    (
        cross_grad,
        query_grad,
        attn_grad,
        attended_grad,
        after_grad,
        middle_sums,
        kv_own_grad,
        kv_other_grad,
    ) = call(
        middle_back_body,
        "middle_back",
        [
            ((block_size, width), LOW),
            ((count, block_size, cross_cols), LOW),
            ((block_size, width), LOW),
            ((count, block_size, self_cols), LOW),
            ((block_size, width), WIDE),
            ((8, width), WIDE),
            ((count, keys, 2 * cross_cols), LOW),
            ((count, keys, 2 * cross_cols), LOW),
        ],
        (
            after(grad_up, ffn_parts, output_block),
            up_flat,
            *grad_norm_two,
            after_cross,
            up_block,
            branch,
            mod_own,
            mod_other,
            *weights,
            kv_own,
            kv_other,
            probs,
            queries,
        ),
        in_specs=[own_rows(grad_up)] + [whole] * 17,
        flops=120 * block_size * width * width,
        table=table,
    )

    grad_blocks = jnp.stack(
        [attended_grad[0]] + [from_ahead(attended_grad[step], step) for step in range(1, count)]
    )
    squares = square_parts(
        table,
        (cross_grad, after_low, attn_grad),
        (text_low, query_grad, after(attended_blocks, attended_grad, output_blocks)),
    )
    square_rows = sum_rows(after(squares, grad_blocks))
    kv_total = kv_own_grad.astype(WIDE) + swapped(kv_other_grad, "seq", 0).astype(WIDE)
    kv_sent = [kv_total[step].astype(LOW) for step in range(1, count)]
    grad_blocks = after(grad_blocks, squares, kv_sent, ffn_rows)
    grad_q, back_own, back_other = self_back(
        table, grad_blocks, q, attended_wide, denominator, kernel_own, kernel_other
    )
    back_theirs = swapped(jnp.stack([back_own, back_other]), "seq", 0)
    kv_grad = kv_total[0]
    for step in range(1, count):
        kv_grad = kv_grad + from_ahead(kv_sent[step - 1], step).astype(WIDE)
    kv_grad = kv_grad.astype(LOW)
    grad_projected = self_project_back(
        table,
        grad_q,
        k,
        v,
        raw,
        back_own + back_theirs[1],
        back_other + back_theirs[0],
    )
    normed_sent = products_to_send(table, grad_projected, qkv_flat)
    grad_normed = sent_ahead(normed_sent)
    grad_projected = after(grad_projected, normed_sent)
    late_parts = call(
        late_body,
        "late_parts",
        [((width, 3 * self_cols + 2 * cross_cols), LOW)],
        (normed_low, grad_projected, text_rows, kv_grad),
        flops=4 * tokens_here * width * 5 * self_cols,
        table=table,
    )[0]
    late_rows = sum_rows(after(late_parts, square_rows, grad_normed))
    def image_total(sums, amount):
        pairs = sums[: 2 * amount].reshape(amount, 2, width)
        return same_everywhere(pairs[:, 0] + swapped(pairs[:, 1], "seq", 0))

    early = image_total(
        after(jnp.concatenate([middle_sums[:6], output_sums[:2]]), normed_sent), 4
    )
    conv_sum = after(tap_part[:9], normed_sent)
    for place in range(lax.axis_size("seq").bit_length() - 1):
        conv_sum = conv_sum + swapped(conv_sum, "seq", place)
    input_block, first_sums = call(
        first_norm_back_body,
        "first_norm_back",
        [((block_size, width), LOW), ((8, width), WIDE)],
        (
            after(grad_projected, late_parts, square_rows, early, conv_sum),
            qkv_flat,
            *grad_normed,
            after_grad,
            x_block,
            mod_own,
            mod_other,
        ),
        in_specs=[own_rows(grad_projected)] + [whole] * 8,
        table=table,
    )
    input_grad = placed_blocks(all_blocks(input_block)).astype(WIDE)
    output = placed_blocks(output_blocks)

    late = image_total(first_sums, 2)
    modulation_grad = jnp.stack([late[0], late[1], early[2], early[0], early[1], early[3]])

    block = square_rows.shape[1] // count
    square_grads = square_rows[:, : 3 * self_cols].astype(WIDE)
    for step in range(1, count):
        piece = square_rows[:, step * block : step * block + 3 * self_cols]
        square_grads = square_grads + from_ahead(piece, step).astype(WIDE)
    late_rows = late_rows.astype(WIDE)

    return (
        output,
        input_grad,
        modulation_grad[None],
        late_rows[:, : 3 * self_cols].reshape(-1, 3, self_cols),
        square_grads[:, 2 * self_cols :],
        square_grads[:, self_cols : 2 * self_cols],
        late_rows[:, 3 * self_cols :].reshape(-1, 2, cross_cols),
        square_grads[:, :self_cols],
        ffn_rows[:, ffn_pad:].astype(WIDE).reshape(-1, 2, ffn_pad)[:, :, :ffn_cols],
        conv_sum.reshape(9, 2, ffn_pad)[:, :, :ffn_cols],
        ffn_rows[:, :ffn_cols].astype(WIDE),
    )


def solution(mesh):
    placed = (
        P("seq", None),
        P("seq", None),
        P("seq", None, None),
        P("seq", None, None),
        P(),
        P(),
        P(None, None, "tp"),
        P(None, "tp"),
        P(None, "tp"),
        P(None, None, "tp"),
        P(None, "tp"),
        P(None, None, "tp"),
        P(None, None, "tp"),
        P(None, "tp"),
    )
    return jax.shard_map(
        shards,
        mesh=mesh,
        in_specs=placed,
        out_specs=(
            P("seq", None),
            P("seq", None),
            P("seq", None, None),
            P("seq", None, "tp"),
            P("seq", "tp"),
            P("seq", "tp"),
            P("seq", None, "tp"),
            P("seq", "tp"),
            P("seq", None, "tp"),
            P(None, None, "tp"),
            P("seq", "tp"),
        ),
        check_vma=False,
    )
```

time: 1180 us -> 516 us (0.44)
  waiting for transfers between devices: 845 us -> 163 us
  Pallas kernels: 0 us -> 181 us
  matrix products: 96.4 us -> 4.3 us
  other arithmetic: 101 us -> 23.2 us
  starting transfers between devices: 3.63 us -> 64.7 us
  blocking collectives: 26.5 us -> 0 us
  local copies, waits for them, and re-layouts: 69.6 us -> 52.2 us
    psum x5 -> x0, waiting for transfers between devices: 509 us -> none  [the longest x1 114 us: shards(): grad_norm_two = lax.psum(times_transposed(grad_up_low, up_flat), 'tp')]
    reduce_scatter x5 -> x3, waiting for transfers between devices: 242 us -> 0.01 us  [sum_rows(): lax.psum_scatter(grad.astype(LOW), 'seq', scatter_dimension=0, tiled=True)]
    pallas_call x0 -> x19, Pallas kernels: none -> 181 us  [call(): pl.pallas_call(body, out_shape=shapes, grid_spec=pltpu.PrefetchScalarGrid...]
    ppermute x0 -> x39, waiting for transfers between devices: none -> 126 us  [the longest x27 105 us: from_behind(): lax.ppermute(block, 'tp', [(k, (k + step) % count) for k in range(count)])]
    unnamed x14 -> x3, waiting for transfers between devices: 93.2 us -> 0.05 us
    dot_general x41 -> x2, matrix products: 96.4 us -> 4.3 us  [dot(): return jnp.dot(left, right, preferred_element_type=WIDE)]
    ppermute x0 -> x39, starting transfers between devices: none -> 53 us  [the longest x27 35.4 us: from_behind(): lax.ppermute(block, 'tp', [(k, (k + step) % count) for k in range(count)])]
    ppermute x9 -> x20, waiting for transfers between devices: 1.2 us -> 36.2 us  [swapped(): return lax.ppermute(block, axis, route)]
  transfers between devices with their start and end apart: 21 -> 62, of which waited for: 13 -> 25; matrix products, arithmetic and copies ran while one was open for 12% -> 12% of each run, Pallas kernels for 0% -> 27%
where the time goes in v2:
time: 516 us; the launch traced here: 507 us
  Pallas kernels  181 us (35%)
  waiting for transfers between devices  163 us (32%)
  starting transfers between devices  64.7 us (13%)
  local copies, waits for them, and re-layouts  52.2 us (10%)
  other arithmetic  23.2 us (4%)
  between operations  18.9 us (4%)
    pallas_call x19, Pallas kernels, call(): pl.pallas_call(body, out_shape=shapes, grid_spec=pltpu.PrefetchScalarGrid...  181 us
    ppermute x27, waiting for transfers between devices, from_behind(): lax.ppermute(block, 'tp', [(k, (k + step) % count) for k in range(count)])  105 us
    ppermute x20, waiting for transfers between devices, swapped(): return lax.ppermute(block, axis, route)  36.2 us
    ppermute x27, starting transfers between devices, from_behind(): lax.ppermute(block, 'tp', [(k, (k + step) % count) for k in range(count)])  35.4 us
    unnamed x103, local copies, waits for them, and re-layouts  15.2 us
    ppermute x9, starting transfers between devices, from_ahead(): lax.ppermute(block, 'tp', [(k, (k - step) % count) for k in range(count)])  14.1 us
    ppermute x9, waiting for transfers between devices, from_ahead(): lax.ppermute(block, 'tp', [(k, (k - step) % count) for k in range(count)])  13.6 us
    ppermute x20, starting transfers between devices, swapped(): return lax.ppermute(block, axis, route)  11.6 us
  transfers between devices with their start and end apart: 62, of which 25 were waited for; matrix products, arithmetic and copies ran while one was open for 12% of the time, Pallas kernels for 27%

profile of v2, /device:TPU:8, one launch (start us, length us, event | category | flops | bytes accessed | tf_op | source)
XLA Modules:
  0.0 506.7 jit_solution(12694001378532928918)
XLA Ops:
  7.3 2.5 copy.43.refs_0_.out_first
  24.1 2.4 copy.42.weight.right
  31.1 10.4 %self_project.1 = (bf16[640,1152]{1,0:T(8,128)(2,1)}, f32[640,576]{1,0:T(8,128)}, bf16[640,288]{1,0:T(8,128)(2,1)}, bf16[640,288]{1,0:T(8,128)(2,1)}, bf16[640,2...) custom-call(s32[10]{0:T(128)} %stack.114.table, bf16[640,1152]{1,0:T(8,128)(2,1)} %x.9, ...), custom_call_target="tpu_custom_call" | custom-call | bytes 78704 | tf_op jit(solution)/shard_map/self_project/pallas_call | solution.py:62
  46.2 2.3 pad_maximum_fusion.2.refs_0_
  57.5 6.8 %self_attend.1 = (bf16[640,288]{1,0:T(8,128)(2,1)}, f32[640,288]{1,0:T(8,128)}, f32[640,288]{1,0:T(8,128)}) custom-call(s32[10]{0:T(128)} %stack.114.table, bf16[640,288]{1,0:T(8,128)(2,1)} %get-tuple-element.89.q, f32[288,128]{1,0:T(8,128)} %get-tuple-element.205.own_fold, f32[288,128]{1,0:T(8,128)} %get-tuple-element.204.other_fold), custom_call_target="tpu_custom_call" | custom-call | bytes 25067 | tf_op jit(solution)/shard_map/self_attend/pallas_call | solution.py:62
  64.3 2.6 copy.47
  68.1 2.7 fusion.12.grad_hidden
  71.1 3.6 copy.61.weight.right.up_weight
  75.2 9.0 %collective-permute-done.16 = bf16[304,576]{1,0:T(8,128)(2,1)} collective-permute-done((bf16[304,576]{1,0:T(8,128)(2,1)}, bf16[304,576]{1,0:T(8,128)(2,1)}, u32[]{:S(2)}, u32[]{:S(2)}) %collective-permute-start.16) | collective-permute-done | bytes 350240 | tf_op jit(solution)/shard_map/ppermute | solution.py:33
  89.4 8.1 %collective-permute-done.10.refs_4_ = bf16[9,144,288]{2,1,0:T(8,128)(2,1)} collective-permute-done((bf16[9,144,288]{2,1,0:T(8,128)(2,1)}, bf16[9,144,288]{2,1,0:T(8,128)(2,1)}, u32[]{:S(2)}, u32[]{:S(2)}) %collective-permute-start.10) | collective-permute-done | bytes 746528 | tf_op jit(solution)/shard_map/ppermute | solution.py:755
  97.4 2.4 collective-permute-start.6
  100.8 5.1 %collective-permute-done.6 = bf16[160,288]{1,0:T(8,128)(2,1)S(1)} collective-permute-done((bf16[160,288]{1,0:T(8,128)(2,1)S(1)}, bf16[160,288]{1,0:T(8,128)(2,1)S(1)}, u32[]{:S(2)}, u32[]{:S(2)}) %collective-permute-start.6) | collective-permute-done | bytes 92192 | tf_op jit(solution)/shard_map/ppermute | solution.py:33
  112.2 7.8 %order.1.rest = bf16[9,1152,288]{2,1,0:T(8,128)(2,1)} custom-call(s32[10]{0:T(128)} %stack.114.table, bf16[9,144,288]{2,1,0:T(8,128)(2,1)} %pad_maximum_fusion.2.refs_0_, bf16[9,144,288]{2,1,0:T(8,128)(2,1)} %copy-done.16, bf16[9,144,288]{2,1,0:T(8,128)(2,1)} %collective-permute-done.9.refs_2_, bf16[9,144,288]{2,1,0:T(8,128)(2,1)} %copy-done.17, ...), custom_call_target="tpu_custom_call" | custom-call | bytes 119439 | tf_op jit(solution)/shard_map/order/pallas_call | solution.py:62
  121.2 19.6 %middle.1 = (f32[160,1152]{1,0:T(8,128)}, bf16[160,1152]{1,0:T(8,128)(2,1)}, bf16[4,160,288]{2,1,0:T(8,128)(2,1)}, f32[16,160,304]{2,1,0:T(8,128)}, bf16[4,160,2...) custom-call(s32[10]{0:T(128)} %stack.114.table, bf16[4,160,288]{2,1,0:T(8,128)(2,1)} %pad_maximum_fusion.3.att, ...), custom_call_target="tpu_custom_call" | custom-call | bytes 176189 | tf_op jit(solution)/shard_map/middle/pallas_call | solution.py:62
  140.8 3.0 collective-permute-start.20
  143.8 2.3 collective-permute-start.21
  146.2 6.2 %collective-permute-done.19 = bf16[160,1152]{1,0:T(8,128)(2,1)S(1)} collective-permute-done((bf16[160,1152]{1,0:T(8,128)(2,1)}, bf16[160,1152]{1,0:T(8,128)(2,1)S(1)}, u32[]{:S(2)}, u32[]{:S(2)}) %collective-permute-start.19) | collective-permute-done | bytes 368672 | tf_op jit(solution)/shard_map/ppermute | solution.py:33
  152.4 21.2 %collective-permute-done.20 = bf16[160,1152]{1,0:T(8,128)(2,1)S(1)} collective-permute-done((bf16[160,1152]{1,0:T(8,128)(2,1)}, bf16[160,1152]{1,0:T(8,128)(2,1)S(1)}, u32[]{:S(2)}, u32[]{:S(2)}) %collective-permute-start.20) | collective-permute-done | bytes 368672 | tf_op jit(solution)/shard_map/ppermute | solution.py:33
  173.6 2.9 collective-permute-done.21
  176.5 2.3 pad_maximum_fusion.1.x
  178.8 8.4 %up_project.1 = (f32[640,1536]{1,0:T(8,128)}, bf16[640,1536]{1,0:T(8,128)(2,1)}, bf16[640,1152]{1,0:T(8,128)(2,1)}) custom-call(s32[10]{0:T(128)} %stack.114.table, bf16[4,160,1152]{2,1,0:T(8,128)(2,1)} %pad_maximum_fusion.1.x, bf16[1152,1536]{1,0:T(8,128)(2,1)} %copy.61.weight.right.up_weight), custom_call_target="tpu_custom_call" | custom-call | bytes 123863 | tf_op jit(solution)/shard_map/up_project/pallas_call | solution.py:62
  190.4 9.6 %mix.1 = (bf16[640,768]{1,0:T(8,128)(2,1)}, bf16[2,640,768]{2,1,0:T(8,128)(2,1)}) custom-call(s32[10]{0:T(128)} %stack.114.table, bf16[640,1536]{1,0:T(8,128)(2,1)} %get-tuple-element.103.value.gate.activated, bf16[640,1536]{1,0:T(8,128)(2,1)} %get-tuple-element.103.value.gate.activated, bf16[32,1536]{1,0:T(8,128)(2,1)} %copy-done.20, ...), custom_call_target="tpu_custom_call" | custom-call | bytes 92405 | tf_op jit(solution)/shard_map/mix/pallas_call | solution.py:62
  200.0 5.0 products.3
  210.4 15.0 %mix_back.1 = (bf16[640,1536]{1,0:T(8,128)(2,1)}, f32[16,1536]{1,0:T(8,128)}) custom-call(s32[10]{0:T(128)} %stack.114.table, bf16[2,640,768]{2,1,0:T(8,128)(2,1)} %get-tuple-element.110.grads, bf16[2,32,768]{2,1,0:T(8,128)(2,1)} %copy-done.36, bf16[640,1536]{1,0:T(8,128)(2,1)} %get-tuple-element.103.value.gate.activated, bf16[32,1536]{1,0:T(8,128)(2,1)} %copy-done.20, ...), custom_call_target="tpu_custom_call" | custom-call | bytes 102236 | tf_op jit(solution)/shard_map/mix_back/pallas_call | solution.py:62
  225.4 7.4 %products.4 = (bf16[160,1152]{1,0:T(8,128)(2,1)}, bf16[160,1152]{1,0:T(8,128)(2,1)}, bf16[160,1152]{1,0:T(8,128)(2,1)}) custom-call(s32[10]{0:T(128)} %stack.114.table, bf16[640,1536]{1,0:T(8,128)(2,1)} %get-tuple-element.119.left.grad_up.grad_rows, bf16[1152,1536]{1,0:T(8,128)(2,1)} %copy.61.weight.right.up_weight), custom_call_target="tpu_custom_call" | custom-call | bytes 66109 | tf_op jit(solution)/shard_map/products/pallas_call | solution.py:62
  232.8 5.0 collective-permute-done.24.branch_2
  238.6 2.6 collective-permute-start.31
  243.1 9.4 %ffn_parts.1 = bf16[1152,2304]{1,0:T(8,128)(2,1)} custom-call(s32[10]{0:T(128)} %stack.114.table, bf16[640,1152]{1,0:T(8,128)(2,1)} %copy-done.6, bf16[640,768]{1,0:T(8,128)(2,1)} %get-tuple-element.117.left.hidden_rows.hidden, bf16[640,1152]{1,0:T(8,128)(2,1)} %get-tuple-element.118.normed, bf16[640,1536]{1,0:T(8,128)(2,1)} %get-tuple-element.119.left.grad_up.grad_rows), custom_call_target="tpu_custom_call" | custom-call | bytes 112066 | tf_op jit(solution)/shard_map/ffn_parts/pallas_call | solution.py:62
  252.6 18.4 %collective-permute-done.31.grad_2 = bf16[160,1152]{1,0:T(8,128)(2,1)S(1)} collective-permute-done((bf16[160,1152]{1,0:T(8,128)(2,1)}, bf16[160,1152]{1,0:T(8,128)(2,1)S(1)}, u32[]{:S(2)}, u32[]{:S(2)}) %collective-permute-start.31) | collective-permute-done | bytes 368672 | tf_op jit(solution)/shard_map/ppermute | solution.py:33
  270.9 2.8 collective-permute-done.32.grad_3
  276.2 4.5 output.1
  283.5 27.1 %middle_back.1 = (bf16[160,1152]{1,0:T(8,128)(2,1)}, bf16[4,160,288]{2,1,0:T(8,128)(2,1)}, bf16[160,1152]{1,0:T(8,128)(2,1)}, bf16[4,160,288]{2,1,0:T(8,128)(2,1...) custom-call(s32[10]{0:T(128)} %stack.114.table, ...), custom_call_target="tpu_custom_call" | custom-call | bytes 278056 | tf_op jit(solution)/shard_map/middle_back/pallas_call | solution.py:62
  314.3 2.8 collective-permute-start.35
  317.1 8.8 %square_parts.1 = bf16[1152,3584]{1,0:T(8,128)(2,1)} custom-call(s32[10]{0:T(128)} %stack.114.table, bf16[160,1152]{1,0:T(8,128)(2,1)} %get-tuple-element.127.dyc, bf16[4,160,288]{2,1,0:T(8,128)(2,1)} %get-tuple-element.128.text, bf16[160,1152]{1,0:T(8,128)(2,1)} %get-tuple-element.129.x1, bf16[4,160,288]{2,1,0:T(8,128)(2,1)} %get-tuple-element.130.dqc, ...), custom_call_target="tpu_custom_call" | custom-call | bytes 104693 | tf_op jit(solution)/shard_map/square_parts/pallas_call | solution.py:62
  333.2 12.1 %self_back.1 = (f32[640,288]{1,0:T(8,128)}, f32[288,128]{1,0:T(8,128)}, f32[288,128]{1,0:T(8,128)}) custom-call(s32[10]{0:T(128)} %stack.114.table, bf16[4,160,288]{2,1,0:T(8,128)(2,1)} %pad_maximum_fusion.4.grad, bf16[640,288]{1,0:T(8,128)(2,1)} %get-tuple-element.89.q, f32[640,288]{1,0:T(8,128)} %get-tuple-element.137.wide_out, ...), custom_call_target="tpu_custom_call" | custom-call | bytes 35389 | tf_op jit(solution)/shard_map/self_back/pallas_call | solution.py:62
  355.0 8.8 %self_project_back.1.left.grad_projected.grad_rows = bf16[640,864]{1,0:T(8,128)(2,1)} custom-call(s32[10]{0:T(128)} %stack.114.table, f32[640,288]{1,0:T(8,128)} %get-tuple-element.139.grad_q, bf16[640,288]{1,0:T(8,128)(2,1)} %get-tuple-element.140.k, bf16[640,288]{1,0:T(8,128)(2,1)} %get-tuple-element.141.v, f32[640,576]{1,0:T(8,128)} %get-tuple-element.142.raw, ...), custom_call_target="tpu_custom_call" | custom-call | bytes 43499 | tf_op jit(solution)/shard_map/self_project_back/pallas_call | solution.py:62
  363.9 5.5 %products.5 = (bf16[160,1152]{1,0:T(8,128)(2,1)}, bf16[160,1152]{1,0:T(8,128)(2,1)}, bf16[160,1152]{1,0:T(8,128)(2,1)}) custom-call(s32[10]{0:T(128)} %stack.114.table, bf16[640,864]{1,0:T(8,128)(2,1)} %self_project_back.1.left.grad_projected.grad_rows, bf16[1152,864]{1,0:T(8,128)(2,1)} %copy.42.weight.right), custom_call_target="tpu_custom_call" | custom-call | bytes 42024 | tf_op jit(solution)/shard_map/products/pallas_call | solution.py:62
  371.4 6.8 %collective-permute-done.38 = bf16[304,576]{1,0:T(8,128)(2,1)} collective-permute-done((bf16[304,576]{1,0:T(8,128)(2,1)}, bf16[304,576]{1,0:T(8,128)(2,1)}, u32[]{:S(2)}, u32[]{:S(2)}) %collective-permute-start.38) | collective-permute-done | bytes 350240 | tf_op jit(solution)/shard_map/ppermute | solution.py:38
  378.2 6.8 %collective-permute-done.40 = bf16[304,576]{1,0:T(8,128)(2,1)} collective-permute-done((bf16[304,576]{1,0:T(8,128)(2,1)S(1)}, bf16[304,576]{1,0:T(8,128)(2,1)}, u32[]{:S(2)}, u32[]{:S(2)}) %collective-permute-start.40) | collective-permute-done | bytes 350240 | tf_op jit(solution)/shard_map/ppermute | solution.py:38
  387.4 2.6 collective-permute-start.47
  398.2 7.5 %late_parts.1 = bf16[1152,1440]{1,0:T(8,128)(2,1)} custom-call(s32[10]{0:T(128)} %stack.114.table, bf16[640,1152]{1,0:T(8,128)(2,1)} %get-tuple-element.149.normed, bf16[640,864]{1,0:T(8,128)(2,1)} %self_project_back.1.left.grad_projected.grad_rows, bf16[304,1152]{1,0:T(8,128)(2,1)} %pad.16.text, bf16[304,576]{1,0:T(8,128)(2,1)} %fusion.3.kv_grad), custom_call_target="tpu_custom_call" | custom-call | bytes 69488 | tf_op jit(solution)/shard_map/late_parts/pallas_call | solution.py:62
  405.7 8.8 %collective-permute-done.42 = f32[4,1152]{1,0:T(4,128)S(1)} collective-permute-done((f32[4,1152]{1,0:T(4,128)S(1)}, f32[4,1152]{1,0:T(4,128)S(1)}, u32[]{:S(2)}, u32[]{:S(2)}) %collective-permute-start.42) | collective-permute-done | bytes 18464 | tf_op jit(solution)/shard_map/ppermute | solution.py:28
  417.5 5.1 collective-permute-done.48.grad_2
  425.6 4.9 first_norm_back.1
  438.5 3.0 collective-permute-start.55
  441.6 25.0 %collective-permute-done.55 = f32[2,1152]{1,0:T(2,128)S(1)} collective-permute-done((f32[2,1152]{1,0:T(2,128)S(1)}, f32[2,1152]{1,0:T(2,128)S(1)}, u32[]{:S(2)}, u32[]{:S(2)}) %collective-permute-start.55) | collective-permute-done | bytes 9248 | tf_op jit(solution)/shard_map/ppermute | solution.py:28
  466.6 3.4 collective-permute-start.51
  471.8 19.1 %collective-permute-done.51 = bf16[160,1152]{1,0:T(8,128)(2,1)S(1)} collective-permute-done((bf16[160,1152]{1,0:T(8,128)(2,1)S(1)}, bf16[160,1152]{1,0:T(8,128)(2,1)S(1)}, u32[]{:S(2)}, u32[]{:S(2)}) %collective-permute-start.51) | collective-permute-done | bytes 368672 | tf_op jit(solution)/shard_map/ppermute | solution.py:33
  (284 shorter events, 118.2 us)
Async XLA Ops:
  7.2 326.0 %reduce-scatter.4.cloned.1.call-start = ((), (), s32[]{:S(2)}) async-start(), calls=%async_computation.3 | async-start | bytes 5971968 | tf_op jit(solution)/shard_map/reduce_scatter | solution.py:818
  14.2 29.2 %collective-permute-start.1 = (bf16[3,144,288]{2,1,0:T(8,128)(2,1)}, bf16[3,144,288]{2,1,0:T(8,128)(2,1)}, u32[]{:S(2)}, u32[]{:S(2)}) collective-permute-start(bf16[3,144,288]{2,1,0:T(8,128)(2,1)} %eighths.1), channel_id=1, source_target_pairs={{0,1},{1,2},{2,3},{3,0},{4,5},{5,6},{6,7},{7,4},{8,9},{9,10},{10,1... | collective-permute-start | bytes 746504 | tf_op jit(solution)/shard_map/ppermute | solution.py:33
  15.7 28.7 %collective-permute-start.2 = (bf16[3,144,288]{2,1,0:T(8,128)(2,1)}, bf16[3,144,288]{2,1,0:T(8,128)(2,1)}, u32[]{:S(2)}, u32[]{:S(2)}) collective-permute-start(bf16[3,144,288]{2,1,0:T(8,128)(2,1)} %eighths.1), channel_id=1, source_target_pairs={{0,2},{1,3},{2,0},{3,1},{4,6},{5,7},{6,4},{7,5},{8,10},{9,11},{10,... | collective-permute-start | bytes 746504 | tf_op jit(solution)/shard_map/ppermute | solution.py:33
  16.8 29.5 %collective-permute-start.3 = (bf16[3,144,288]{2,1,0:T(8,128)(2,1)}, bf16[3,144,288]{2,1,0:T(8,128)(2,1)}, u32[]{:S(2)}, u32[]{:S(2)}) collective-permute-start(bf16[3,144,288]{2,1,0:T(8,128)(2,1)} %eighths.1), channel_id=1, source_target_pairs={{0,3},{1,0},{2,1},{3,2},{4,7},{5,4},{6,5},{7,6},{8,11},{9,8},{10,9... | collective-permute-start | bytes 746504 | tf_op jit(solution)/shard_map/ppermute | solution.py:33
  18.8 11.6 %collective-permute-start = (bf16[6,1152]{1,0:T(8,128)(2,1)S(1)}, bf16[6,1152]{1,0:T(8,128)(2,1)S(1)}, u32[]{:S(2)}, u32[]{:S(2)}) collective-permute-start(bf16[6,1152]{1,0:T(8,128)(2,1)S(1)} %bitcast.144), channel_id=1, source_target_pairs={{0,4},{4,0},{8,12},{12,8},{16,20},{20,16},{24,28},{28,24},{1,5},{5... | collective-permute-start | bytes 41480 | tf_op jit(solution)/shard_map/ppermute | solution.py:28
  42.4 12.8 %collective-permute-start.4 = (f32[2,288,128]{2,1,0:T(8,128)S(1)}, f32[2,288,128]{2,1,0:T(8,128)S(1)}, u32[]{:S(2)}, u32[]{:S(2)}) collective-permute-start(f32[2,288,128]{2,1,0:T(8,128)S(1)} %pad_maximum_fusion.5), channel_id=1, source_target_pairs={{0,4},{4,0},{8,12},{12,8},{16,20},{20,16},{24,28},{28,24},{1,5},{5... | collective-permute-start | bytes 884744 | tf_op jit(solution)/shard_map/ppermute | solution.py:28
  50.1 24.5 %collective-permute-start.15 = (bf16[304,576]{1,0:T(8,128)(2,1)}, bf16[304,576]{1,0:T(8,128)(2,1)}, u32[]{:S(2)}, u32[]{:S(2)}) collective-permute-start(bf16[304,576]{1,0:T(8,128)(2,1)} %convolution_convert_fusion), channel_id=1, source_target_pairs={{0,1},{1,2},{2,3},{3,0},{4,5},{5,6},{6,7},{7,4},{8,9},{9,10},{10,1... | collective-permute-start | bytes 1050632 | tf_op jit(solution)/shard_map/ppermute | solution.py:33
  50.1 34.1 %collective-permute-start.16 = (bf16[304,576]{1,0:T(8,128)(2,1)}, bf16[304,576]{1,0:T(8,128)(2,1)}, u32[]{:S(2)}, u32[]{:S(2)}) collective-permute-start(bf16[304,576]{1,0:T(8,128)(2,1)} %convolution_convert_fusion), channel_id=1, source_target_pairs={{0,2},{1,3},{2,0},{3,1},{4,6},{5,7},{6,4},{7,5},{8,10},{9,11},{10,... | collective-permute-start | bytes 1050632 | tf_op jit(solution)/shard_map/ppermute | solution.py:33
  51.7 34.2 %collective-permute-start.17 = (bf16[304,576]{1,0:T(8,128)(2,1)}, bf16[304,576]{1,0:T(8,128)(2,1)}, u32[]{:S(2)}, u32[]{:S(2)}) collective-permute-start(bf16[304,576]{1,0:T(8,128)(2,1)} %convolution_convert_fusion), channel_id=1, source_target_pairs={{0,3},{1,0},{2,1},{3,2},{4,7},{5,4},{6,5},{7,6},{8,11},{9,8},{10,9... | collective-permute-start | bytes 1050632 | tf_op jit(solution)/shard_map/ppermute | solution.py:33
  53.8 43.7 %collective-permute-start.10 = (bf16[9,144,288]{2,1,0:T(8,128)(2,1)}, bf16[9,144,288]{2,1,0:T(8,128)(2,1)}, u32[]{:S(2)}, u32[]{:S(2)}) collective-permute-start(bf16[9,144,288]{2,1,0:T(8,128)(2,1)} %pad_maximum_fusion.2.refs_0_), channel_id=1, source_target_pairs={{0,16},{4,20},{8,24},{12,28},{16,0},{20,4},{24,8},{28,12},{1,17},{... | collective-permute-start | bytes 2239496 | tf_op jit(solution)/shard_map/ppermute | solution.py:755
  55.3 44.6 %collective-permute-start.11 = (bf16[9,144,288]{2,1,0:T(8,128)(2,1)}, bf16[9,144,288]{2,1,0:T(8,128)(2,1)}, u32[]{:S(2)}, u32[]{:S(2)}) collective-permute-start(bf16[9,144,288]{2,1,0:T(8,128)(2,1)} %pad_maximum_fusion.2.refs_0_), channel_id=1, source_target_pairs={{0,24},{4,28},{8,16},{12,20},{16,8},{20,12},{24,0},{28,4},{1,25},{... | collective-permute-start | bytes 2239496 | tf_op jit(solution)/shard_map/ppermute | solution.py:755
  74.7 25.6 %collective-permute-start.9 = (bf16[9,144,288]{2,1,0:T(8,128)(2,1)}, bf16[9,144,288]{2,1,0:T(8,128)(2,1)}, u32[]{:S(2)}, u32[]{:S(2)}) collective-permute-start(bf16[9,144,288]{2,1,0:T(8,128)(2,1)} %pad_maximum_fusion.2.refs_0_), channel_id=1, source_target_pairs={{0,8},{4,12},{8,0},{12,4},{16,24},{20,28},{24,16},{28,20},{1,9},{5... | collective-permute-start | bytes 2239496 | tf_op jit(solution)/shard_map/ppermute | solution.py:755
  87.6 32.4 %collective-permute-start.18 = (bf16[4,304,576]{2,1,0:T(8,128)(2,1)S(1)}, bf16[4,304,576]{2,1,0:T(8,128)(2,1)S(1)}, u32[]{:S(2)}, u32[]{:S(2)}) collective-permute-start(bf16[4,304,576]{2,1,0:T(8,128)(2,1)S(1)} %pad_maximum_fusion.kv_own), channel_id=1, source_target_pairs={{0,4},{4,0},{8,12},{12,8},{16,20},{20,16},{24,28},{28,24},{1,5},{5... | collective-permute-start | bytes 4202504 | tf_op jit(solution)/shard_map/ppermute | solution.py:28
  89.3 11.0 %collective-permute-start.5 = (bf16[160,288]{1,0:T(8,128)(2,1)S(1)}, bf16[160,288]{1,0:T(8,128)(2,1)S(1)}, u32[]{:S(2)}, u32[]{:S(2)}) collective-permute-start(bf16[160,288]{1,0:T(8,128)(2,1)S(1)} %get-tuple-element.201), channel_id=1, source_target_pairs={{0,1},{1,2},{2,3},{3,0},{4,5},{5,6},{6,7},{7,4},{8,9},{9,10},{10,1... | collective-permute-start | bytes 276488 | tf_op jit(solution)/shard_map/ppermute | solution.py:33
  140.8 11.6 %collective-permute-start.19 = (bf16[160,1152]{1,0:T(8,128)(2,1)}, bf16[160,1152]{1,0:T(8,128)(2,1)S(1)}, u32[]{:S(2)}, u32[]{:S(2)}) collective-permute-start(bf16[160,1152]{1,0:T(8,128)(2,1)} %get-tuple-element.102), channel_id=1, source_target_pairs={{0,1},{1,2},{2,3},{3,0},{4,5},{5,6},{6,7},{7,4},{8,9},{9,10},{10,1... | collective-permute-start | bytes 1105928 | tf_op jit(solution)/shard_map/ppermute | solution.py:33
  140.8 32.8 %collective-permute-start.20 = (bf16[160,1152]{1,0:T(8,128)(2,1)}, bf16[160,1152]{1,0:T(8,128)(2,1)S(1)}, u32[]{:S(2)}, u32[]{:S(2)}) collective-permute-start(bf16[160,1152]{1,0:T(8,128)(2,1)} %get-tuple-element.102), channel_id=1, source_target_pairs={{0,2},{1,3},{2,0},{3,1},{4,6},{5,7},{6,4},{7,5},{8,10},{9,11},{10,... | collective-permute-start | bytes 1105928 | tf_op jit(solution)/shard_map/ppermute | solution.py:33
  143.8 32.7 %collective-permute-start.21 = (bf16[160,1152]{1,0:T(8,128)(2,1)}, bf16[160,1152]{1,0:T(8,128)(2,1)S(1)}, u32[]{:S(2)}, u32[]{:S(2)}) collective-permute-start(bf16[160,1152]{1,0:T(8,128)(2,1)} %get-tuple-element.102), channel_id=1, source_target_pairs={{0,3},{1,0},{2,1},{3,2},{4,7},{5,4},{6,5},{7,6},{8,11},{9,8},{10,9... | collective-permute-start | bytes 1105928 | tf_op jit(solution)/shard_map/ppermute | solution.py:33
  205.0 27.8 %collective-permute-start.23 = (bf16[160,1152]{1,0:T(8,128)(2,1)}, bf16[160,1152]{1,0:T(8,128)(2,1)S(1)}, u32[]{:S(2)}, u32[]{:S(2)}) collective-permute-start(bf16[160,1152]{1,0:T(8,128)(2,1)} %get-tuple-element.105), channel_id=1, source_target_pairs={{0,1},{1,2},{2,3},{3,0},{4,5},{5,6},{6,7},{7,4},{8,9},{9,10},{10,1... | collective-permute-start | bytes 1105928 | tf_op jit(solution)/shard_map/ppermute | solution.py:33
  205.0 32.8 %collective-permute-start.24 = (bf16[160,1152]{1,0:T(8,128)(2,1)}, bf16[160,1152]{1,0:T(8,128)(2,1)S(1)}, u32[]{:S(2)}, u32[]{:S(2)}) collective-permute-start(bf16[160,1152]{1,0:T(8,128)(2,1)} %get-tuple-element.106), channel_id=1, source_target_pairs={{0,2},{1,3},{2,0},{3,1},{4,6},{5,7},{6,4},{7,5},{8,10},{9,11},{10,... | collective-permute-start | bytes 1105928 | tf_op jit(solution)/shard_map/ppermute | solution.py:33
  205.4 33.2 %collective-permute-start.25 = (bf16[160,1152]{1,0:T(8,128)(2,1)}, bf16[160,1152]{1,0:T(8,128)(2,1)S(1)}, u32[]{:S(2)}, u32[]{:S(2)}) collective-permute-start(bf16[160,1152]{1,0:T(8,128)(2,1)} %get-tuple-element.107), channel_id=1, source_target_pairs={{0,3},{1,0},{2,1},{3,2},{4,7},{5,4},{6,5},{7,6},{8,11},{9,8},{10,9... | collective-permute-start | bytes 1105928 | tf_op jit(solution)/shard_map/ppermute | solution.py:33
  238.6 14.0 %collective-permute-start.30 = (bf16[160,1152]{1,0:T(8,128)(2,1)}, bf16[160,1152]{1,0:T(8,128)(2,1)S(1)}, u32[]{:S(2)}, u32[]{:S(2)}) collective-permute-start(bf16[160,1152]{1,0:T(8,128)(2,1)} %get-tuple-element.120), channel_id=1, source_target_pairs={{0,1},{1,2},{2,3},{3,0},{4,5},{5,6},{6,7},{7,4},{8,9},{9,10},{10,1... | collective-permute-start | bytes 1105928 | tf_op jit(solution)/shard_map/ppermute | solution.py:33
  238.6 32.4 %collective-permute-start.31 = (bf16[160,1152]{1,0:T(8,128)(2,1)}, bf16[160,1152]{1,0:T(8,128)(2,1)S(1)}, u32[]{:S(2)}, u32[]{:S(2)}) collective-permute-start(bf16[160,1152]{1,0:T(8,128)(2,1)} %get-tuple-element.121), channel_id=1, source_target_pairs={{0,2},{1,3},{2,0},{3,1},{4,6},{5,7},{6,4},{7,5},{8,10},{9,11},{10,... | collective-permute-start | bytes 1105928 | tf_op jit(solution)/shard_map/ppermute | solution.py:33
  241.2 32.5 %collective-permute-start.32 = (bf16[160,1152]{1,0:T(8,128)(2,1)}, bf16[160,1152]{1,0:T(8,128)(2,1)S(1)}, u32[]{:S(2)}, u32[]{:S(2)}) collective-permute-start(bf16[160,1152]{1,0:T(8,128)(2,1)} %get-tuple-element.122), channel_id=1, source_target_pairs={{0,3},{1,0},{2,1},{3,2},{4,7},{5,4},{6,5},{7,6},{8,11},{9,8},{10,9... | collective-permute-start | bytes 1105928 | tf_op jit(solution)/shard_map/ppermute | solution.py:33
  274.5 143.0 %reduce-scatter.6.cloned.1.call-start = ((), (), s32[]{:S(2)}) async-start(), calls=%async_computation.4 | async-start | bytes 9289728 | tf_op jit(solution)/shard_map/reduce_scatter | solution.py:818
  280.7 33.6 %collective-permute-start.26 = (bf16[160,1152]{1,0:T(8,128)(2,1)}, bf16[160,1152]{1,0:T(8,128)(2,1)S(1)}, u32[]{:S(2)}, u32[]{:S(2)}) collective-permute-start(bf16[160,1152]{1,0:T(8,128)(2,1)} %get-tuple-element.109), channel_id=1, source_target_pairs={{0,1},{1,2},{2,3},{3,0},{4,5},{5,6},{6,7},{7,4},{8,9},{9,10},{10,1... | collective-permute-start | bytes 1105928 | tf_op jit(solution)/shard_map/ppermute | solution.py:33
  280.7 36.4 %collective-permute-start.27 = (bf16[160,1152]{1,0:T(8,128)(2,1)}, bf16[160,1152]{1,0:T(8,128)(2,1)S(1)}, u32[]{:S(2)}, u32[]{:S(2)}) collective-permute-start(bf16[160,1152]{1,0:T(8,128)(2,1)} %get-tuple-element.109), channel_id=1, source_target_pairs={{0,2},{1,3},{2,0},{3,1},{4,6},{5,7},{6,4},{7,5},{8,10},{9,11},{10,... | collective-permute-start | bytes 1105928 | tf_op jit(solution)/shard_map/ppermute | solution.py:33
  281.3 35.7 %collective-permute-start.28 = (bf16[160,1152]{1,0:T(8,128)(2,1)}, bf16[160,1152]{1,0:T(8,128)(2,1)}, u32[]{:S(2)}, u32[]{:S(2)}) collective-permute-start(bf16[160,1152]{1,0:T(8,128)(2,1)} %get-tuple-element.109), channel_id=1, source_target_pairs={{0,3},{1,0},{2,1},{3,2},{4,7},{5,4},{6,5},{7,6},{8,11},{9,8},{10,9... | collective-permute-start | bytes 1105928 | tf_op jit(solution)/shard_map/ppermute | solution.py:33
  311.7 14.1 %collective-permute-start.33 = (bf16[160,288]{1,0:T(8,128)(2,1)S(1)}, bf16[160,288]{1,0:T(8,128)(2,1)S(1)}, u32[]{:S(2)}, u32[]{:S(2)}) collective-permute-start(bf16[160,288]{1,0:T(8,128)(2,1)S(1)} %get-tuple-element.197), channel_id=1, source_target_pairs={{0,3},{1,0},{2,1},{3,2},{4,7},{5,4},{6,5},{7,6},{8,11},{9,8},{10,9... | collective-permute-start | bytes 276488 | tf_op jit(solution)/shard_map/ppermute | solution.py:38
  313.1 12.8 %collective-permute-start.34 = (bf16[160,288]{1,0:T(8,128)(2,1)S(1)}, bf16[160,288]{1,0:T(8,128)(2,1)S(1)}, u32[]{:S(2)}, u32[]{:S(2)}) collective-permute-start(bf16[160,288]{1,0:T(8,128)(2,1)S(1)} %get-tuple-element.196), channel_id=1, source_target_pairs={{0,2},{1,3},{2,0},{3,1},{4,6},{5,7},{6,4},{7,5},{8,10},{9,11},{10,... | collective-permute-start | bytes 276488 | tf_op jit(solution)/shard_map/ppermute | solution.py:38
  314.3 11.6 %collective-permute-start.35 = (bf16[160,288]{1,0:T(8,128)(2,1)S(1)}, bf16[160,288]{1,0:T(8,128)(2,1)S(1)}, u32[]{:S(2)}, u32[]{:S(2)}) collective-permute-start(bf16[160,288]{1,0:T(8,128)(2,1)S(1)} %get-tuple-element.195), channel_id=1, source_target_pairs={{0,1},{1,2},{2,3},{3,0},{4,5},{5,6},{6,7},{7,4},{8,9},{9,10},{10,1... | collective-permute-start | bytes 276488 | tf_op jit(solution)/shard_map/ppermute | solution.py:38
  326.8 168.3 %reduce-scatter.8.cloned.1.call-start = ((), (), s32[]{:S(2)}) async-start(), calls=%async_computation.5 | async-start | bytes 3981312 | tf_op jit(solution)/shard_map/reduce_scatter | solution.py:818
  349.4 28.9 %collective-permute-start.38 = (bf16[304,576]{1,0:T(8,128)(2,1)}, bf16[304,576]{1,0:T(8,128)(2,1)}, u32[]{:S(2)}, u32[]{:S(2)}) collective-permute-start(bf16[304,576]{1,0:T(8,128)(2,1)} %get-tuple-element.187), channel_id=1, source_target_pairs={{0,3},{1,0},{2,1},{3,2},{4,7},{5,4},{6,5},{7,6},{8,11},{9,8},{10,9... | collective-permute-start | bytes 1050632 | tf_op jit(solution)/shard_map/ppermute | solution.py:38
  349.6 28.7 %collective-permute-start.39 = (bf16[304,576]{1,0:T(8,128)(2,1)}, bf16[304,576]{1,0:T(8,128)(2,1)}, u32[]{:S(2)}, u32[]{:S(2)}) collective-permute-start(bf16[304,576]{1,0:T(8,128)(2,1)} %get-tuple-element.186), channel_id=1, source_target_pairs={{0,2},{1,3},{2,0},{3,1},{4,6},{5,7},{6,4},{7,5},{8,10},{9,11},{10,... | collective-permute-start | bytes 1050632 | tf_op jit(solution)/shard_map/ppermute | solution.py:38
  351.7 33.3 %collective-permute-start.40 = (bf16[304,576]{1,0:T(8,128)(2,1)S(1)}, bf16[304,576]{1,0:T(8,128)(2,1)}, u32[]{:S(2)}, u32[]{:S(2)}) collective-permute-start(bf16[304,576]{1,0:T(8,128)(2,1)S(1)} %get-tuple-element.185), channel_id=1, source_target_pairs={{0,1},{1,2},{2,3},{3,0},{4,5},{5,6},{6,7},{7,4},{8,9},{9,10},{10,1... | collective-permute-start | bytes 1050632 | tf_op jit(solution)/shard_map/ppermute | solution.py:38
  371.4 21.1 %collective-permute-start.41 = (f32[4,1152]{1,0:T(4,128)}, f32[4,1152]{1,0:T(4,128)}, u32[]{:S(2)}, u32[]{:S(2)}) collective-permute-start(f32[4,1152]{1,0:T(4,128)} %bitcast.113), channel_id=1, source_target_pairs={{0,4},{4,0},{8,12},{12,8},{16,20},{20,16},{24,28},{28,24},{1,5},{5... | collective-permute-start | bytes 55304 | tf_op jit(solution)/shard_map/ppermute | solution.py:28
  387.4 30.1 %collective-permute-start.47 = (bf16[160,1152]{1,0:T(8,128)(2,1)}, bf16[160,1152]{1,0:T(8,128)(2,1)S(1)}, u32[]{:S(2)}, u32[]{:S(2)}) collective-permute-start(bf16[160,1152]{1,0:T(8,128)(2,1)} %get-tuple-element.145), channel_id=1, source_target_pairs={{0,1},{1,2},{2,3},{3,0},{4,5},{5,6},{6,7},{7,4},{8,9},{9,10},{10,1... | collective-permute-start | bytes 1105928 | tf_op jit(solution)/shard_map/ppermute | solution.py:33
  390.0 32.5 %collective-permute-start.48 = (bf16[160,1152]{1,0:T(8,128)(2,1)S(1)}, bf16[160,1152]{1,0:T(8,128)(2,1)S(1)}, u32[]{:S(2)}, u32[]{:S(2)}) collective-permute-start(bf16[160,1152]{1,0:T(8,128)(2,1)S(1)} %copy-done.46), channel_id=1, source_target_pairs={{0,2},{1,3},{2,0},{3,1},{4,6},{5,7},{6,4},{7,5},{8,10},{9,11},{10,... | collective-permute-start | bytes 1105928 | tf_op jit(solution)/shard_map/ppermute | solution.py:33
  392.0 32.1 %collective-permute-start.49 = (bf16[160,1152]{1,0:T(8,128)(2,1)S(1)}, bf16[160,1152]{1,0:T(8,128)(2,1)S(1)}, u32[]{:S(2)}, u32[]{:S(2)}) collective-permute-start(bf16[160,1152]{1,0:T(8,128)(2,1)S(1)} %copy-done.45), channel_id=1, source_target_pairs={{0,3},{1,0},{2,1},{3,2},{4,7},{5,4},{6,5},{7,6},{8,11},{9,8},{10,9... | collective-permute-start | bytes 1105928 | tf_op jit(solution)/shard_map/ppermute | solution.py:33
  393.3 21.3 %collective-permute-start.42 = (f32[4,1152]{1,0:T(4,128)S(1)}, f32[4,1152]{1,0:T(4,128)S(1)}, u32[]{:S(2)}, u32[]{:S(2)}) collective-permute-start(f32[4,1152]{1,0:T(4,128)S(1)} %fusion.8), channel_id=1, source_target_pairs={{0,1},{1,0},{2,3},{3,2},{4,5},{5,4},{6,7},{7,6},{8,9},{9,8},{10,11... | collective-permute-start | bytes 55304 | tf_op jit(solution)/shard_map/ppermute | solution.py:28
  395.4 20.4 %collective-permute-start.45 = (f32[9,1536]{1,0:T(8,128)S(1)}, f32[9,1536]{1,0:T(8,128)S(1)}, u32[]{:S(2)}, u32[]{:S(2)}) collective-permute-start(f32[9,1536]{1,0:T(8,128)S(1)} %add.205), channel_id=1, source_target_pairs={{0,8},{4,12},{8,0},{12,4},{16,24},{20,28},{24,16},{28,20},{1,9},{5... | collective-permute-start | bytes 165896 | tf_op jit(solution)/shard_map/ppermute | solution.py:28
  414.5 11.0 %collective-permute-start.43 = (f32[4,1152]{1,0:T(4,128)S(1)}, f32[4,1152]{1,0:T(4,128)S(1)}, u32[]{:S(2)}, u32[]{:S(2)}) collective-permute-start(f32[4,1152]{1,0:T(4,128)S(1)} %add.203), channel_id=1, source_target_pairs={{0,2},{1,3},{2,0},{3,1},{4,6},{5,7},{6,4},{7,5},{8,10},{9,11},{10,... | collective-permute-start | bytes 55304 | tf_op jit(solution)/shard_map/ppermute | solution.py:28
  433.0 37.7 %collective-permute-start.56 = (bf16[144,864]{1,0:T(8,128)(2,1)S(1)}, bf16[144,864]{1,0:T(8,128)(2,1)S(1)}, u32[]{:S(2)}, u32[]{:S(2)}) collective-permute-start(bf16[144,864]{1,0:T(8,128)(2,1)S(1)} %get-tuple-element.188), channel_id=1, source_target_pairs={{0,3},{1,0},{2,1},{3,2},{4,7},{5,4},{6,5},{7,6},{8,11},{9,8},{10,9... | collective-permute-start | bytes 746504 | tf_op jit(solution)/shard_map/ppermute | solution.py:38
  434.9 35.7 %collective-permute-start.57 = (bf16[144,864]{1,0:T(8,128)(2,1)S(1)}, bf16[144,864]{1,0:T(8,128)(2,1)S(1)}, u32[]{:S(2)}, u32[]{:S(2)}) collective-permute-start(bf16[144,864]{1,0:T(8,128)(2,1)S(1)} %get-tuple-element.190), channel_id=1, source_target_pairs={{0,2},{1,3},{2,0},{3,1},{4,6},{5,7},{6,4},{7,5},{8,10},{9,11},{10,... | collective-permute-start | bytes 746504 | tf_op jit(solution)/shard_map/ppermute | solution.py:38
  436.9 33.7 %collective-permute-start.58 = (bf16[144,864]{1,0:T(8,128)(2,1)S(1)}, bf16[144,864]{1,0:T(8,128)(2,1)S(1)}, u32[]{:S(2)}, u32[]{:S(2)}) collective-permute-start(bf16[144,864]{1,0:T(8,128)(2,1)S(1)} %get-tuple-element.189), channel_id=1, source_target_pairs={{0,1},{1,2},{2,3},{3,0},{4,5},{5,6},{6,7},{7,4},{8,9},{9,10},{10,1... | collective-permute-start | bytes 746504 | tf_op jit(solution)/shard_map/ppermute | solution.py:38
  437.9 33.9 %collective-permute-start.50 = (bf16[160,1152]{1,0:T(8,128)(2,1)S(1)}, bf16[160,1152]{1,0:T(8,128)(2,1)S(1)}, u32[]{:S(2)}, u32[]{:S(2)}) collective-permute-start(bf16[160,1152]{1,0:T(8,128)(2,1)S(1)} %copy-done.26), channel_id=1, source_target_pairs={{0,1},{1,2},{2,3},{3,0},{4,5},{5,6},{6,7},{7,4},{8,9},{9,10},{10,1... | collective-permute-start | bytes 1105928 | tf_op jit(solution)/shard_map/ppermute | solution.py:33
  438.5 28.2 %collective-permute-start.55 = (f32[2,1152]{1,0:T(2,128)S(1)}, f32[2,1152]{1,0:T(2,128)S(1)}, u32[]{:S(2)}, u32[]{:S(2)}) collective-permute-start(f32[2,1152]{1,0:T(2,128)S(1)} %add.209), channel_id=1, source_target_pairs={{0,2},{1,3},{2,0},{3,1},{4,6},{5,7},{6,4},{7,5},{8,10},{9,11},{10,... | collective-permute-start | bytes 27656 | tf_op jit(solution)/shard_map/ppermute | solution.py:28
  466.6 24.3 %collective-permute-start.51 = (bf16[160,1152]{1,0:T(8,128)(2,1)S(1)}, bf16[160,1152]{1,0:T(8,128)(2,1)S(1)}, u32[]{:S(2)}, u32[]{:S(2)}) collective-permute-start(bf16[160,1152]{1,0:T(8,128)(2,1)S(1)} %copy-done.26), channel_id=1, source_target_pairs={{0,2},{1,3},{2,0},{3,1},{4,6},{5,7},{6,4},{7,5},{8,10},{9,11},{10,... | collective-permute-start | bytes 1105928 | tf_op jit(solution)/shard_map/ppermute | solution.py:33
  470.7 22.5 %collective-permute-start.52 = (bf16[160,1152]{1,0:T(8,128)(2,1)S(1)}, bf16[160,1152]{1,0:T(8,128)(2,1)S(1)}, u32[]{:S(2)}, u32[]{:S(2)}) collective-permute-start(bf16[160,1152]{1,0:T(8,128)(2,1)S(1)} %copy-done.26), channel_id=1, source_target_pairs={{0,3},{1,0},{2,1},{3,2},{4,7},{5,4},{6,5},{7,6},{8,11},{9,8},{10,9... | collective-permute-start | bytes 1105928 | tf_op jit(solution)/shard_map/ppermute | solution.py:33
  (64 other events, 475.9 us)
Sparse Core Ops, SparseCore 0:
  273.9 56.8 reduce-scatter.3
  334.8 72.6 reduce-scatter.5
  424.2 48.7 reduce-scatter.7

commit v3 on v2

--- a/solution.py
+++ b/solution.py
@@ -33,9 +33,8 @@
     return lax.ppermute(block, "tp", [(k, (k + step) % count) for k in range(count)])
 
 
-def from_ahead(block, step):
-    count = lax.axis_size("tp")
-    return lax.ppermute(block, "tp", [(k, (k - step) % count) for k in range(count)])
+def exchanged(blocks):
+    return lax.all_to_all(blocks, "tp", 0, 0, tiled=True)
 
 
 def dot(left, right):
@@ -148,7 +147,7 @@
         + pick(own, mod_own, mod_other, 0)
     ).astype(LOW)
     normed[...] = low
-    out = dot(low, weight[...])
+    out = times_transposed(low, weight[...])
     raw[...] = out[:, : 2 * columns]
     q[...] = log_exp(out[:, :columns]).astype(LOW)
     keys = log_exp(out[:, columns : 2 * columns]).astype(LOW)
@@ -255,8 +254,7 @@
         squares[...] = jnp.zeros_like(squares)
         totals[...] = jnp.zeros_like(totals)
 
-    place = lax.rem(table[TP_PLACE] + step, pl.num_programs(0))
-    own = own_image(table, table[FIRST] + place * rows, rows)
+    own = own_image(table, table[FIRST] + step * rows, rows)
     wide = grad[0].astype(WIDE)
     over = 1.0 / denominator[...]
     numer_high, numer_low = split(wide * over)
@@ -296,8 +294,7 @@
 def self_back(table, grad, q, wide_out, denominator, own_fold, other_fold):
     count, rows, columns = grad.shape
     tokens = q.shape[0]
-    turn = lambda i, t: (lax.rem(t[TP_PLACE] + i, count), 0)
-    row = pl.BlockSpec((rows, columns), turn)
+    row = pl.BlockSpec((rows, columns), lambda i, t: (i, 0))
     fixed = pl.BlockSpec((columns, LANES), lambda i, t: (0, 0))
     return call(
         self_back_body,
@@ -370,18 +367,22 @@
     return place < jnp.where(own, table[OWN_LENGTH], table[OTHER_LENGTH])
 
 
-def shard_of(first, rest, step, offset=0):
-    return first[...] if step == 0 else rest[offset + step - 1]
-
-
-def middle_body(table, att, x, mod_own, mod_other, out_first, query_first, cross_first, rest, kv_own, kv_other, branch, after_low, queries_out, probs_out, text_out, after_cross, normed):
+def shard_of(first, rest, step, which):
+    rows = first.shape[0]
+    return first[...] if step == 0 else rest[step - 1, which * rows : (which + 1) * rows, :]
+
+
+def middle_body(table, att, x, mod_own, mod_other, out_first, query_first, cross_first, *refs):
+    pieces, (kv_own, kv_other) = refs[:8], refs[8:10]
+    branch, after_low, queries_out, probs_out, text_out, after_cross, normed, rest = refs[10:]
+    put_in_order(table, pieces, rest)
     count, rows, columns = att.shape
     keys = kv_own.shape[1]
     heads = columns // CROSS_HEAD
     own = own_image(table, table[BLOCK_FIRST], rows)
     y1 = jnp.zeros((rows, x.shape[1]), WIDE)
     for step in range(count):
-        y1 += times_transposed(att[step], shard_of(out_first, rest, step))
+        y1 += dot(att[turned(table, step, count)], shard_of(out_first, rest, step, 0))
     branch[...] = y1
     x1 = x[...].astype(WIDE) + pick(own, mod_own, mod_other, 2) * y1
     x1_low = x1.astype(LOW)
@@ -389,9 +390,10 @@
     live = live_keys(table, own, keys)
     yc = jnp.zeros_like(x1)
     for step in range(count):
-        queries = dot(x1_low, shard_of(query_first, rest, step, count - 1)).astype(LOW)
+        queries = times_transposed(x1_low, shard_of(query_first, rest, step, 1)).astype(LOW)
         queries_out[step] = queries
-        mine, theirs = kv_own[step], kv_other[step]
+        place = turned(table, step, count)
+        mine, theirs = kv_own[place], kv_other[place]
         parts = []
         for head in range(heads):
             lanes = slice(head * CROSS_HEAD, (head + 1) * CROSS_HEAD)
@@ -410,7 +412,7 @@
             )
         text = jnp.concatenate(parts, axis=1).astype(LOW)
         text_out[step] = text
-        yc += times_transposed(text, shard_of(cross_first, rest, step, 2 * count - 2))
+        yc += dot(text, shard_of(cross_first, rest, step, 2))
     x2 = x1 + yc
     after_cross[...] = x2
     normed[...] = (
@@ -419,18 +421,13 @@
     ).astype(LOW)
 
 
-def middle_back_body(table, grad_rows, up_weight, grad_1, grad_2, grad_3, x2_in, upstream, branch, mod_own, mod_other, out_first, query_first, cross_first, rest, kv_own, kv_other, probs_in, queries_in, cross_grad, query_grad, attn_grad, attended_grad, after_grad, sums, kv_own_grad, kv_other_grad):
+def middle_back_body(table, grads, x2_in, upstream, branch, mod_own, mod_other, out_first, query_first, cross_first, rest, kv_own, kv_other, probs_in, queries_in, cross_grad, query_grad, attn_grad, attended_grad, after_grad, sums, kv_own_grad, kv_other_grad):
     count, rows, columns = queries_in.shape
     keys = kv_own.shape[1]
     heads = columns // CROSS_HEAD
     scale = 1.0 / math.sqrt(CROSS_HEAD)
     own = own_image(table, table[BLOCK_FIRST], rows)
-    grad = (
-        times_transposed(grad_rows[...], up_weight[...])
-        + grad_1[...].astype(WIDE)
-        + grad_2[...].astype(WIDE)
-        + grad_3[...].astype(WIDE)
-    )
+    grad = total(grads)
     x2 = x2_in[...]
     inverse = inverse_size(x2)
     xh = x2 * inverse
@@ -444,8 +441,9 @@
     cross_grad[...] = dyc
     dx1 = dx2
     for step in range(count):
-        doc = dot(dyc, shard_of(cross_first, rest, step, 2 * count - 2)).astype(LOW)
-        mine, theirs = kv_own[step], kv_other[step]
+        doc = times_transposed(dyc, shard_of(cross_first, rest, step, 2)).astype(LOW)
+        place = turned(table, step, count)
+        mine, theirs = kv_own[place], kv_other[place]
         queries = queries_in[step]
         query_parts = []
         key_parts = ([], [])
@@ -474,27 +472,24 @@
                 value_parts[image].append(over_tokens(mask(low), do))
         dqc = jnp.concatenate(query_parts, axis=1).astype(LOW)
         query_grad[step] = dqc
-        kv_own_grad[step] = jnp.concatenate(key_parts[0] + value_parts[0], axis=1).astype(LOW)
-        kv_other_grad[step] = jnp.concatenate(key_parts[1] + value_parts[1], axis=1).astype(LOW)
-        dx1 = dx1 + times_transposed(dqc, shard_of(query_first, rest, step, count - 1))
+        kv_own_grad[place] = jnp.concatenate(key_parts[0] + value_parts[0], axis=1).astype(LOW)
+        kv_other_grad[place] = jnp.concatenate(key_parts[1] + value_parts[1], axis=1).astype(LOW)
+        dx1 = dx1 + dot(dqc, shard_of(query_first, rest, step, 1))
     after_grad[...] = dx1
     sums[4:5], sums[5:6] = both_sums(own, dx1 * branch[...])
     sums[6:8] = jnp.zeros((2, sums.shape[1]), WIDE)
     dy1 = (dx1 * pick(own, mod_own, mod_other, 2)).astype(LOW)
     attn_grad[...] = dy1
     for step in range(count):
-        attended_grad[step] = dot(dy1, shard_of(out_first, rest, step)).astype(LOW)
-
-
-def first_norm_back_body(table, grad_rows, weight, grad_1, grad_2, grad_3, after_grad, x, mod_own, mod_other, input_grad, sums):
+        attended_grad[turned(table, step, count)] = times_transposed(
+            dy1, shard_of(out_first, rest, step, 0)
+        ).astype(LOW)
+
+
+def first_norm_back_body(table, grads, after_grad, x, mod_own, mod_other, input_grad, sums):
     rows = x.shape[0]
     own = own_image(table, table[BLOCK_FIRST], rows)
-    grad = (
-        times_transposed(grad_rows[...], weight[...])
-        + grad_1[...].astype(WIDE)
-        + grad_2[...].astype(WIDE)
-        + grad_3[...].astype(WIDE)
-    )
+    grad = total(grads)
     wide = x[...].astype(WIDE)
     inverse = inverse_size(wide)
     xh = wide * inverse
@@ -507,44 +502,43 @@
     ).astype(LOW)
 
 
-def output_body(table, hidden_rows, weight, branch_1, branch_2, branch_3, x2, upstream, mod_own, mod_other, output, sums):
+def output_body(table, branches, x2, upstream, mod_own, mod_other, output, sums):
     rows = x2.shape[0]
     own = own_image(table, table[BLOCK_FIRST], rows)
-    branch = (
-        times_transposed(hidden_rows[...], weight[...])
-        + branch_1[...].astype(WIDE)
-        + branch_2[...].astype(WIDE)
-        + branch_3[...].astype(WIDE)
-    )
+    branch = total(branches)
     sums[0:1], sums[1:2] = both_sums(own, upstream[...].astype(WIDE) * branch)
     sums[2:8] = jnp.zeros((6, sums.shape[1]), WIDE)
     output[...] = (x2[...] + pick(own, mod_own, mod_other, 5) * branch).astype(LOW)
 
 
-def up_body(table, x, weight, wide_out, low_out, ordered):
-    block = x[0]
-    up = dot(block, weight[...])
-    ordered[...] = block
+def up_body(table, *refs):
+    blocks, weight, (wide_out, low_out, ordered) = refs[:-4], refs[-4], refs[-3:]
+    step = pl.program_id(0)
+    for place, ref in enumerate(blocks):
+
+        @pl.when(step == place)
+        def _():
+            ordered[...] = ref[...]
+
+    up = times_transposed(ordered[...], weight[...])
     wide_out[...] = up
     low_out[...] = (up * logistic(up)).astype(LOW)
 
 
 def up_project(table, blocks, weight):
-    count, rows, width = blocks.shape
-    columns = weight.shape[1]
-    turn = lambda i, t: (lax.rem(t[TP_PLACE] + count - i, count), 0)
+    count = len(blocks)
+    rows, width = blocks[0].shape
+    columns = weight.shape[0]
+    turn = lambda i, t: (turned(t, i, count), 0)
+    whole = lambda a: pl.BlockSpec(a.shape, lambda i, t: (0, 0))
     return call(
         up_body,
         "up_project",
         [((count * rows, columns), WIDE), ((count * rows, columns), LOW), ((count * rows, width), LOW)],
-        (blocks, weight),
+        (*blocks, weight),
         grid=(count,),
-        in_specs=[
-            pl.BlockSpec((1, rows, width), lambda i, t: (i, 0, 0)),
-            pl.BlockSpec(weight.shape, lambda i, t: (0, 0)),
-        ],
+        in_specs=[whole(array) for array in (*blocks, weight)],
         out_specs=[pl.BlockSpec((rows, columns), turn)] * 2 + [pl.BlockSpec((rows, width), turn)],
-        flops=2 * count * rows * width * columns,
         table=table,
     )
 
@@ -715,20 +709,22 @@
     )
 
 
-def eighths_body(table, *refs):
-    for place, ref in enumerate(refs[:-1]):
-        refs[-1][place] = ref[...]
-
-
-def order_body(table, *refs):
-    pieces, out = refs[:-1], refs[-1]
-    units, rows = pieces[0].shape[0], pieces[0].shape[1]
-    weights = 3
+def eighth_body(table, *refs):
+    weights, out, joined = refs[:-2], refs[-2], refs[-1]
+    low = 0
+    for weight in weights:
+        joined[low : low + weight.shape[0], :] = weight[...]
+        low += weight.shape[0]
+    rows = out.shape[0]
+    out[...] = joined[pl.ds(pl.multiple_of(table[0] * rows, 16), rows), :]
+
+
+def put_in_order(table, pieces, out):
+    steps, rows = pieces[0].shape[0], pieces[0].shape[1]
     for place, piece in enumerate(pieces):
         block = lax.bitwise_xor(table[ROW_PLACE], place)
-        for unit in range(units):
-            target = (unit % weights) * (units // weights) + unit // weights
-            out[target, pl.ds(pl.multiple_of(block * rows, 16), rows), :] = piece[unit]
+        for step in range(steps):
+            out[step, pl.ds(pl.multiple_of(block * rows, 16), rows), :] = piece[step]
 
 
 def after(value, *others):
@@ -736,31 +732,26 @@
 
 
 def fetch_eighths(weights):
-    rows, columns = weights[0].shape
-    own = rows // 8
+    columns = weights[0].shape[1]
+    rows = -(-sum(weight.shape[0] for weight in weights) // LANES) * 16
     eighth = call(
-        eighths_body,
-        "eighths",
-        [((len(weights), own, columns), weights[0].dtype)],
+        eighth_body,
+        "eighth",
+        [((rows, columns), weights[0].dtype)],
         weights,
-        in_specs=[pl.BlockSpec((own, columns), lambda i, t: (t[0], 0))] * len(weights),
-        out_specs=[pl.BlockSpec((len(weights), own, columns), lambda i, t: (0, 0, 0))],
+        scratch=[pltpu.VMEM((8 * rows, columns), weights[0].dtype)],
         table=(lax.axis_index("seq") % 8).reshape(1).astype(jnp.int32),
     )[0]
-    return [from_behind(eighth, step) for step in range(1, lax.axis_size("tp"))]
-
-
-def share_eighths(table, fetched, ready):
+    return jnp.stack([from_behind(eighth, step) for step in range(1, lax.axis_size("tp"))])
+
+
+def share_eighths(fetched, ready):
     count = lax.axis_size("seq")
     far = lambda flip: lax.ppermute(fetched, "seq", [(k, k ^ flip) for k in range(count)])
-    even = [fetched] + after([far(2), far(4), far(6)], *ready)
     pieces = []
-    for piece in even:
+    for piece in [fetched] + after([far(2), far(4), far(6)], *ready):
         pieces += [piece, swapped(piece, "seq", 0)]
-    units, rows, columns = fetched.shape
-    return call(
-        order_body, "order", [((units, 8 * rows, columns), fetched.dtype)], pieces, table=table
-    )[0]
+    return pieces
 
 
 def token_block(values, place):
@@ -782,35 +773,43 @@
     return [block] + [from_behind(block, step) for step in range(1, lax.axis_size("tp"))]
 
 
-def products_body(table, left, right, *outs):
-    count = len(outs) + 1
-    rows = left.shape[0] // count
-    for step, out in enumerate(outs):
-        low = lax.rem(table[TP_PLACE] + step + 1, count) * rows
-        block = left[pl.ds(pl.multiple_of(low, 16), rows), :]
-        out[...] = times_transposed(block, right[...]).astype(LOW)
-
-
-def products_to_send(table, left, right):
+def product_body(table, left, right, out):
+    out[0] = dot(left[...], right[...]).astype(LOW)
+
+
+def product(table, left, right):
     count = lax.axis_size("tp")
-    shape = (left.shape[0] // count, right.shape[0])
-    return list(
-        call(products_body, "products", [(shape, LOW)] * (count - 1), (left, right), table=table)
-    )
-
-
-def own_rows(left):
+    rows, columns = left.shape[0] // count, left.shape[1]
+    return call(
+        product_body,
+        "product",
+        [((count, rows, right.shape[1]), LOW)],
+        (left, right),
+        grid=(count,),
+        in_specs=[
+            pl.BlockSpec((rows, columns), lambda i, t: (i, 0)),
+            pl.BlockSpec(right.shape, lambda i, t: (0, 0)),
+        ],
+        out_specs=[pl.BlockSpec((1, rows, right.shape[1]), lambda i, t: (i, 0, 0))],
+        table=table,
+    )[0]
+
+
+def total(parts):
+    result = parts[0].astype(WIDE)
+    for place in range(1, parts.shape[0]):
+        result += parts[place].astype(WIDE)
+    return result
+
+
+def turned(table, step, count):
+    return lax.rem(table[TP_PLACE] + count - step, count)
+
+
+def same_everywhere(block):
     count = lax.axis_size("tp")
-    return pl.BlockSpec((left.shape[0] // count, left.shape[1]), lambda i, t: (t[TP_PLACE], 0))
-
-
-def sent_ahead(products):
-    return [from_behind(product, step + 1) for step, product in enumerate(products)]
-
-
-def same_everywhere(block):
-    pair = block + swapped(block, "tp", 0)
-    return pair + swapped(pair, "tp", 1)
+    flipped = lambda flip: lax.ppermute(block, "tp", [(k, k ^ flip) for k in range(count)])
+    return (block + flipped(1)) + (flipped(2) + flipped(3))
 
 
 def sum_rows(grad):
@@ -834,14 +833,15 @@
     count, _, columns = rights[0].shape
     block = -(-3 * columns // LANES) * LANES
     whole = pl.BlockSpec((rows, width), lambda i, t: (0, 0))
-    one = pl.BlockSpec((1, rows, columns), lambda i, t: (i, 0, 0))
+    one = pl.BlockSpec((1, rows, columns), lambda i, t: (turned(t, i, count), 0, 0))
+    still = pl.BlockSpec((1, rows, columns), lambda i, t: (i, 0, 0))
     return call(
         square_body,
         "square_parts",
         [((width, count * block), LOW)],
         [array for pair in zip(lefts, rights) for array in pair],
         grid=(count,),
-        in_specs=[whole, one] * 3,
+        in_specs=[whole, one, whole, one, whole, still],
         out_specs=[pl.BlockSpec((width, block), lambda i, t: (0, i))],
         flops=8 * rows * width * count * block,
         table=table,
@@ -881,9 +881,9 @@
     )[0]
 
 
-def late_body(table, normed, grad_projected, text, kv_grad, out):
+def late_body(table, normed, grad_projected, text, kv_grads, out):
     first = over_tokens(normed[...], grad_projected[...]).astype(LOW)
-    second = over_tokens(text[...], kv_grad[...]).astype(LOW)
+    second = over_tokens(text[...], total(kv_grads).astype(LOW)).astype(LOW)
     out[...] = jnp.concatenate([first, second], axis=1)
 
 
@@ -939,17 +939,19 @@
     mod_own = modulation[0]
     mod_other = swapped(mod_own, "seq", 0).astype(WIDE)
     mod_own = mod_own.astype(WIDE)
-    fetched = jnp.concatenate(fetch_eighths([attn_out_weight, cross_q_weight, cross_out_weight]))
-    qkv_flat = qkv_weight.reshape(width, 3 * self_cols)
+    weights = [attn_out_weight.T, cross_q_weight.T, cross_out_weight.T]
+    fetched = fetch_eighths(weights)
+    qkv_flat = qkv_weight.transpose(1, 2, 0).reshape(3 * self_cols, width)
+    text_rows = jnp.pad(text_states[0], ((0, keys - context), (0, 0)))
+    kv_here = times_transposed(
+        text_rows, cross_kv_weight.transpose(1, 2, 0).reshape(2 * cross_cols, width)
+    ).astype(LOW)
+    kv_sent_first = jnp.broadcast_to(kv_here[None], (count,) + kv_here.shape)
     normed_low, raw, q, k, v, part_own, part_other = self_project(
-        table, hidden_in, mod_own, mod_other, qkv_flat, self_cols
+        table, after(hidden_in, kv_sent_first), mod_own, mod_other, qkv_flat, self_cols
     )
     theirs = swapped(jnp.stack([part_own, part_other]), "seq", 0)
     fetched = after(fetched, q)
-    text_rows = jnp.pad(text_states[0], ((0, keys - context), (0, 0)))
-    kv_here = dot(
-        after(text_rows, fetched), cross_kv_weight.reshape(width, 2 * cross_cols)
-    ).astype(LOW)
     kernel_own, kernel_other = part_own + theirs[1], part_other + theirs[0]
     attended, attended_wide, denominator = self_attend(
         table, after(q, kv_here), kernel_own, kernel_other
@@ -957,10 +959,10 @@
 
     x_block = token_block(hidden_in, tp_index)
     up_block = token_block(cotangent, tp_index)
-    up_flat = jnp.pad(after(up_weight, attended), ((0, 0), (0, 0), (0, ffn_pad - ffn_cols))).reshape(
-        width, 2 * ffn_pad
-    )
-    down_flat = jnp.pad(after(down_weight, attended), ((0, 0), (0, ffn_pad - ffn_cols)))
+    up_flat = jnp.pad(
+        after(up_weight.transpose(1, 2, 0), attended), ((0, 0), (0, ffn_pad - ffn_cols), (0, 0))
+    ).reshape(2 * ffn_pad, width)
+    down_flat = jnp.pad(after(down_weight.T, attended), ((0, ffn_pad - ffn_cols), (0, 0)))
     taps = (
         jnp.pad(conv_weight, ((0, 7), (0, 0), (0, ffn_pad - ffn_cols)))
         .reshape(16, 2 * ffn_pad)
@@ -972,18 +974,16 @@
         mod_other[5:6],
     )
     grad_ffn = (cotangent.astype(WIDE) * gate_rows).astype(LOW)
-    grad_hidden = dot(grad_ffn, down_flat)
+    grad_hidden = times_transposed(grad_ffn, down_flat)
     ready = (up_flat, taps, grad_hidden)
-    kv_own = jnp.stack(after(all_blocks(kv_here), *ready))
+    split_tokens = lambda values: values.reshape(count, block_size, values.shape[1])
+    kv_own = exchanged(kv_sent_first)
+    attended_blocks = exchanged(after(split_tokens(attended), kv_own))
+    kv_own = after(kv_own, *ready)
     kv_other = swapped(kv_own, "seq", 0)
-    rest = share_eighths(table, fetched, ready)
-    attended_blocks = jnp.stack(
-        [token_block(attended, tp_index)]
-        + [from_behind(token_block(attended, tp_index + step), step) for step in range(1, count)]
-    )
+    pieces = share_eighths(fetched, ready)
     all_heads = count * cross_cols // CROSS_HEAD
-    weights = (attn_out_weight, cross_q_weight, cross_out_weight, rest)
-    branch, after_low, queries, probs, text_low, after_cross, normed_two = call(
+    branch, after_low, queries, probs, text_low, after_cross, normed_two, rest = call(
         middle_body,
         "middle",
         [
@@ -994,25 +994,24 @@
             ((count, block_size, cross_cols), LOW),
             ((block_size, width), WIDE),
             ((block_size, width), LOW),
+            ((count - 1, 8 * fetched.shape[1], width), LOW),
         ],
-        (attended_blocks, x_block, mod_own, mod_other, *weights, kv_own, kv_other),
+        (attended_blocks, x_block, mod_own, mod_other, *weights, *pieces, kv_own, kv_other),
         flops=60 * block_size * width * width,
         table=table,
     )
 
-    blocks_two = jnp.stack(all_blocks(normed_two))
-    up_wide, activated, normed_two_low = up_project(table, blocks_two, up_flat)
+    up_wide, activated, normed_two_low = up_project(table, all_blocks(normed_two), up_flat)
     rim = swapped(jnp.where(first_half, activated[-MAXW:], activated[:MAXW]), "seq", 0)
     hidden, grads = mix(table, activated, rim, taps, grad_hidden)
     grads_rim = swapped(jnp.where(first_half, grads[:, -MAXW:], grads[:, :MAXW]), "seq", 0)
-    whole = pl.BlockSpec(memory_space=pltpu.VMEM)
-    branch_sent = products_to_send(table, hidden, down_flat)
+    branch_sent = product(table, hidden, down_flat)
     grad_up, tap_part = mix_back(
         table, grads, grads_rim, activated, rim, taps, after(up_wide, branch_sent)
     )
-    branch_parts = sent_ahead(branch_sent)
-    norm_two_sent = products_to_send(table, grad_up, up_flat)
-    grad_norm_two = sent_ahead(after(norm_two_sent, branch_parts))
+    branches = exchanged(branch_sent)
+    norm_two_sent = product(table, grad_up, up_flat)
+    grad_norm_two = exchanged(after(norm_two_sent, branches))
     ffn_parts = ffn_parts_of(
         table, grad_ffn, after(hidden, norm_two_sent), normed_two_low, grad_up
     )
@@ -1021,16 +1020,7 @@
         output_body,
         "output",
         [((block_size, width), LOW), ((8, width), WIDE)],
-        (
-            hidden,
-            down_flat,
-            *branch_parts,
-            after_cross,
-            up_block,
-            mod_own,
-            mod_other,
-        ),
-        in_specs=[own_rows(hidden)] + [whole] * 8,
+        (branches, after_cross, up_block, mod_own, mod_other),
         table=table,
     )
     output_blocks = all_blocks(output_block)
@@ -1058,45 +1048,40 @@
             ((count, keys, 2 * cross_cols), LOW),
         ],
         (
-            after(grad_up, ffn_parts, output_block),
-            up_flat,
-            *grad_norm_two,
+            after(grad_norm_two, ffn_parts, output_block),
             after_cross,
             up_block,
             branch,
             mod_own,
             mod_other,
             *weights,
+            rest,
             kv_own,
             kv_other,
             probs,
             queries,
         ),
-        in_specs=[own_rows(grad_up)] + [whole] * 17,
         flops=120 * block_size * width * width,
         table=table,
     )
 
-    grad_blocks = jnp.stack(
-        [attended_grad[0]] + [from_ahead(attended_grad[step], step) for step in range(1, count)]
-    )
+    grad_blocks = exchanged(after(attended_grad, output_blocks))
     squares = square_parts(
         table,
         (cross_grad, after_low, attn_grad),
-        (text_low, query_grad, after(attended_blocks, attended_grad, output_blocks)),
+        (text_low, query_grad, after(attended_blocks, attended_grad)),
     )
     square_rows = sum_rows(after(squares, grad_blocks))
-    kv_total = kv_own_grad.astype(WIDE) + swapped(kv_other_grad, "seq", 0).astype(WIDE)
-    kv_sent = [kv_total[step].astype(LOW) for step in range(1, count)]
+    kv_sent = (
+        kv_own_grad.astype(WIDE) + swapped(kv_other_grad, "seq", 0).astype(WIDE)
+    ).astype(LOW)
+    kv_sent = after(kv_sent, grad_blocks)
+    kv_parts = exchanged(kv_sent)
     grad_blocks = after(grad_blocks, squares, kv_sent, ffn_rows)
     grad_q, back_own, back_other = self_back(
         table, grad_blocks, q, attended_wide, denominator, kernel_own, kernel_other
     )
     back_theirs = swapped(jnp.stack([back_own, back_other]), "seq", 0)
-    kv_grad = kv_total[0]
-    for step in range(1, count):
-        kv_grad = kv_grad + from_ahead(kv_sent[step - 1], step).astype(WIDE)
-    kv_grad = kv_grad.astype(LOW)
     grad_projected = self_project_back(
         table,
         grad_q,
@@ -1106,25 +1091,16 @@
         back_own + back_theirs[1],
         back_other + back_theirs[0],
     )
-    normed_sent = products_to_send(table, grad_projected, qkv_flat)
-    grad_normed = sent_ahead(normed_sent)
-    grad_projected = after(grad_projected, normed_sent)
+    normed_sent = product(table, grad_projected, qkv_flat)
+    grad_normed = exchanged(after(normed_sent, kv_parts))
     late_parts = call(
         late_body,
         "late_parts",
         [((width, 3 * self_cols + 2 * cross_cols), LOW)],
-        (normed_low, grad_projected, text_rows, kv_grad),
-        flops=4 * tokens_here * width * 5 * self_cols,
+        (normed_low, after(grad_projected, normed_sent), text_rows, kv_parts),
         table=table,
     )[0]
     late_rows = sum_rows(after(late_parts, square_rows, grad_normed))
-    def image_total(sums, amount):
-        pairs = sums[: 2 * amount].reshape(amount, 2, width)
-        return same_everywhere(pairs[:, 0] + swapped(pairs[:, 1], "seq", 0))
-
-    early = image_total(
-        after(jnp.concatenate([middle_sums[:6], output_sums[:2]]), normed_sent), 4
-    )
     conv_sum = after(tap_part[:9], normed_sent)
     for place in range(lax.axis_size("seq").bit_length() - 1):
         conv_sum = conv_sum + swapped(conv_sum, "seq", place)
@@ -1133,28 +1109,26 @@
         "first_norm_back",
         [((block_size, width), LOW), ((8, width), WIDE)],
         (
-            after(grad_projected, late_parts, square_rows, early, conv_sum),
-            qkv_flat,
-            *grad_normed,
+            after(grad_normed, late_parts, square_rows),
             after_grad,
             x_block,
             mod_own,
             mod_other,
         ),
-        in_specs=[own_rows(grad_projected)] + [whole] * 8,
-        table=table,
-    )
-    input_grad = placed_blocks(all_blocks(input_block)).astype(WIDE)
+        table=table,
+    )
+    square_sent = square_rows.reshape(square_rows.shape[0], count, -1).transpose(1, 0, 2)
+    square_grads = total(exchanged(after(square_sent, grad_normed)))[:, : 3 * self_cols]
+    input_blocks = all_blocks(input_block)
+    input_grad = placed_blocks(input_blocks).astype(WIDE)
     output = placed_blocks(output_blocks)
 
-    late = image_total(first_sums, 2)
-    modulation_grad = jnp.stack([late[0], late[1], early[2], early[0], early[1], early[3]])
-
-    block = square_rows.shape[1] // count
-    square_grads = square_rows[:, : 3 * self_cols].astype(WIDE)
-    for step in range(1, count):
-        piece = square_rows[:, step * block : step * block + 3 * self_cols]
-        square_grads = square_grads + from_ahead(piece, step).astype(WIDE)
+    pairs = jnp.concatenate([first_sums[:4], middle_sums[4:6], middle_sums[:4], output_sums[:2]])
+    pairs = pairs.reshape(6, 2, width)
+    modulation_grad = same_everywhere(
+        after(pairs[:, 0] + swapped(pairs[:, 1], "seq", 0), input_blocks)
+    )
+
     late_rows = late_rows.astype(WIDE)
 
     return (

time: 516 us -> 498 us (0.965)
  the two profiles are of different devices: /device:TPU:8 before, /device:TPU:0 now
where the time goes in v3:
time: 498 us; the launch traced here: 490 us
  Pallas kernels  175 us (35%)
  waiting for transfers between devices  159 us (32%)
  starting transfers between devices  85.8 us (17%)
  local copies, waits for them, and re-layouts  33.8 us (7%)
  between operations  18.7 us (4%)
  other arithmetic  14.1 us (3%)
    pallas_call x18, Pallas kernels, call(): pl.pallas_call(body, out_shape=shapes, grid_spec=pltpu.PrefetchScalarGrid...  175 us
    all_to_all x8, waiting for transfers between devices, exchanged(): return lax.all_to_all(blocks, 'tp', 0, 0, tiled=True)  75.9 us
    ppermute x12, waiting for transfers between devices, from_behind(): lax.ppermute(block, 'tp', [(k, (k + step) % count) for k in range(count)])  43.3 us
    all_to_all x8, starting transfers between devices, exchanged(): return lax.all_to_all(blocks, 'tp', 0, 0, tiled=True)  39.5 us
    ppermute x3, starting transfers between devices, same_everywhere(): lax.ppermute(block, 'tp', [(k, k ^ flip) for k in range(count)])  19.1 us
    ppermute x12, starting transfers between devices, from_behind(): lax.ppermute(block, 'tp', [(k, (k + step) % count) for k in range(count)])  18.7 us
    unnamed x83, local copies, waits for them, and re-layouts  11.8 us
    ppermute x3, waiting for transfers between devices, share_eighths(): lax.ppermute(fetched, 'seq', [(k, k ^ flip) for k in range(count)])  11.7 us
  transfers between devices with their start and end apart: 44, of which 19 were waited for; matrix products, arithmetic and copies ran while one was open for 7% of the time, Pallas kernels for 26%

profile of v3, /device:TPU:0, one launch (start us, length us, event | category | flops | bytes accessed | tf_op | source)
XLA Modules:
  0.0 490.4 jit_solution(12120654272653885137)
XLA Ops:
  7.2 2.5 eighth.1
  9.7 3.0 collective-permute-start.2
  12.7 2.6 collective-permute-start.3
  18.8 3.7 all-to-all-start
  30.4 11.9 %self_project.1 = (bf16[640,1152]{1,0:T(8,128)(2,1)}, f32[640,576]{1,0:T(8,128)}, bf16[640,288]{1,0:T(8,128)(2,1)}, bf16[640,288]{1,0:T(8,128)(2,1)}, bf16[640,2...) custom-call(s32[10]{0:T(128)} %stack.65.table, bf16[640,1152]{1,0:T(8,128)(2,1)} %x.8, ...), custom_call_target="tpu_custom_call" | custom-call | bytes 78704 | tf_op jit(solution)/shard_map/self_project/pallas_call | solution.py:61
  50.4 6.8 %self_attend.1 = (bf16[640,288]{1,0:T(8,128)(2,1)}, f32[640,288]{1,0:T(8,128)}, f32[640,288]{1,0:T(8,128)}) custom-call(s32[10]{0:T(128)} %stack.65.table, bf16[640,288]{1,0:T(8,128)(2,1)} %get-tuple-element.80.q, f32[288,128]{1,0:T(8,128)} %get-tuple-element.173.own_fold, f32[288,128]{1,0:T(8,128)} %get-tuple-element.172.other_fold), custom_call_target="tpu_custom_call" | custom-call | bytes 25067 | tf_op jit(solution)/shard_map/self_attend/pallas_call | solution.py:61
  57.2 2.8 fusion.7.grad_hidden
  60.1 2.1 pad.17
  62.1 9.1 %all-to-all-done.refs_8_.kv_own = bf16[4,304,576]{2,1,0:T(8,128)(2,1)S(1)} async-done(((bf16[4,304,576]{2,1,0:T(8,128)(2,1)}), bf16[4,304,576]{2,1,0:T(8,128)(2,1)S(1)}, u32[]{:S(2)}, u32[]{:S(2)}) %all-to-all-start) | async-done | bytes 1400864 | tf_op jit(solution)/shard_map/all_to_all | solution.py:37
  71.7 11.7 %collective-permute-done.7.refs_4_ = bf16[3,112,1152]{2,1,0:T(8,128)(2,1)} collective-permute-done((bf16[3,112,1152]{2,1,0:T(8,128)(2,1)}, bf16[3,112,1152]{2,1,0:T(8,128)(2,1)}, u32[]{:S(2)}, u32[]{:S(2)}) %collective-permute-start.7) | collective-permute-done | bytes 774176 | tf_op jit(solution)/shard_map/ppermute | solution.py:750
  84.0 5.3 %all-to-all-start.1 = ((bf16[4,160,288]{2,1,0:T(8,128)(2,1)}), bf16[4,160,288]{2,1,0:T(8,128)(2,1)}, u32[]{:S(2)}, u32[]{:S(2)}) async-start(bf16[4,160,288]{2,1,0:T(8,128)(2,1)} %bitcast.121), calls=%async_computation.1 | async-start | bytes 983040 | tf_op jit(solution)/shard_map/all_to_all | solution.py:37
  91.1 12.7 %all-to-all-done.1.att = bf16[4,160,288]{2,1,0:T(8,128)(2,1)} async-done(((bf16[4,160,288]{2,1,0:T(8,128)(2,1)}), bf16[4,160,288]{2,1,0:T(8,128)(2,1)}, u32[]{:S(2)}, u32[]{:S(2)}) %all-to-all-start.1) | async-done | bytes 368672 | tf_op jit(solution)/shard_map/all_to_all | solution.py:37
  105.0 20.9 %middle.1 = (f32[160,1152]{1,0:T(8,128)}, bf16[160,1152]{1,0:T(8,128)(2,1)}, bf16[4,160,288]{2,1,0:T(8,128)(2,1)}, f32[16,160,304]{2,1,0:T(8,128)}, bf16[4,160,2...) custom-call(s32[10]{0:T(128)} %stack.65.table, ...), custom_call_target="tpu_custom_call" | custom-call | bytes 240332 | tf_op jit(solution)/shard_map/middle/pallas_call | solution.py:61
  129.7 9.8 %collective-permute-done.13.refs_1_ = bf16[160,1152]{1,0:T(8,128)(2,1)S(1)} collective-permute-done((bf16[160,1152]{1,0:T(8,128)(2,1)}, bf16[160,1152]{1,0:T(8,128)(2,1)S(1)}, u32[]{:S(2)}, u32[]{:S(2)}) %collective-permute-start.13) | collective-permute-done | bytes 368672 | tf_op jit(solution)/shard_map/ppermute | solution.py:33
  139.6 14.3 %collective-permute-done.14.refs_2_ = bf16[160,1152]{1,0:T(8,128)(2,1)S(1)} collective-permute-done((bf16[160,1152]{1,0:T(8,128)(2,1)}, bf16[160,1152]{1,0:T(8,128)(2,1)S(1)}, u32[]{:S(2)}, u32[]{:S(2)}) %collective-permute-start.14) | collective-permute-done | bytes 368672 | tf_op jit(solution)/shard_map/ppermute | solution.py:33
  155.3 10.1 %up_project.1 = (f32[640,1536]{1,0:T(8,128)}, bf16[640,1536]{1,0:T(8,128)(2,1)}, bf16[640,1152]{1,0:T(8,128)(2,1)}) custom-call(s32[10]{0:T(128)} %stack.65.table, bf16[160,1152]{1,0:T(8,128)(2,1)} %get-tuple-element.92.refs_0_, bf16[160,1152]{1,0:T(8,128)(2,1)} %copy-done.29, bf16[160,1152]{1,0:T(8,128)(2,1)} %copy-done.30, bf16[160,1152]{1,0:T(8,128)(2,1)} %copy-done.31, ...), custom_call_target="tpu_custom_call" | custom-call | bytes 123863 | tf_op jit(solution)/shard_map/up_project/pallas_call | solution.py:61
  168.4 9.6 %mix.1 = (bf16[640,768]{1,0:T(8,128)(2,1)}, bf16[2,640,768]{2,1,0:T(8,128)(2,1)}) custom-call(s32[10]{0:T(128)} %stack.65.table, bf16[640,1536]{1,0:T(8,128)(2,1)} %get-tuple-element.93.value.gate.activated, bf16[640,1536]{1,0:T(8,128)(2,1)} %get-tuple-element.93.value.gate.activated, bf16[32,1536]{1,0:T(8,128)(2,1)} %copy-done.19, ...), custom_call_target="tpu_custom_call" | custom-call | bytes 92405 | tf_op jit(solution)/shard_map/mix/pallas_call | solution.py:61
  178.0 5.7 %product.3 = bf16[4,160,1152]{2,1,0:T(8,128)(2,1)} custom-call(s32[10]{0:T(128)} %stack.65.table, bf16[640,768]{1,0:T(8,128)(2,1)} %get-tuple-element.102.left.hidden, bf16[768,1152]{1,0:T(8,128)(2,1)} %pad.19.right), custom_call_target="tpu_custom_call" | custom-call | bytes 42270 | tf_op jit(solution)/shard_map/product/pallas_call | solution.py:61
  183.8 8.5 %all-to-all-start.2 = ((bf16[4,160,1152]{2,1,0:T(8,128)(2,1)}), bf16[4,160,1152]{2,1,0:T(8,128)(2,1)S(1)}, u32[]{:S(2)}, u32[]{:S(2)}) async-start(bf16[4,160,1152]{2,1,0:T(8,128)(2,1)} %product.3), calls=%async_computation.2 | async-start | bytes 2949120 | tf_op jit(solution)/shard_map/all_to_all | solution.py:37
  195.3 15.0 %mix_back.1 = (bf16[640,1536]{1,0:T(8,128)(2,1)}, f32[16,1536]{1,0:T(8,128)}) custom-call(s32[10]{0:T(128)} %stack.65.table, bf16[2,640,768]{2,1,0:T(8,128)(2,1)} %get-tuple-element.97.grads, bf16[2,32,768]{2,1,0:T(8,128)(2,1)} %copy-done.32, bf16[640,1536]{1,0:T(8,128)(2,1)} %get-tuple-element.93.value.gate.activated, bf16[32,1536]{1,0:T(8,128)(2,1)} %copy-done.19, ...), custom_call_target="tpu_custom_call" | custom-call | bytes 102236 | tf_op jit(solution)/shard_map/mix_back/pallas_call | solution.py:61
  210.3 7.3 %product.4 = bf16[4,160,1152]{2,1,0:T(8,128)(2,1)} custom-call(s32[10]{0:T(128)} %stack.65.table, bf16[640,1536]{1,0:T(8,128)(2,1)} %get-tuple-element.100.left.grad_up, bf16[1536,1152]{1,0:T(8,128)(2,1)} %bitcast.95), custom_call_target="tpu_custom_call" | custom-call | bytes 69795 | tf_op jit(solution)/shard_map/product/pallas_call | solution.py:61
  217.6 10.2 %all-to-all-done.2.branches = bf16[4,160,1152]{2,1,0:T(8,128)(2,1)S(1)} async-done(((bf16[4,160,1152]{2,1,0:T(8,128)(2,1)}), bf16[4,160,1152]{2,1,0:T(8,128)(2,1)S(1)}, u32[]{:S(2)}, u32[]{:S(2)}) %all-to-all-start.2) | async-done | bytes 1474592 | tf_op jit(solution)/shard_map/all_to_all | solution.py:37
  227.8 3.6 all-to-all-start.3
  231.4 9.4 %ffn_parts.1 = bf16[1152,2304]{1,0:T(8,128)(2,1)} custom-call(s32[10]{0:T(128)} %stack.65.table, bf16[640,1152]{1,0:T(8,128)(2,1)} %copy-done.5, bf16[640,768]{1,0:T(8,128)(2,1)} %get-tuple-element.102.left.hidden, bf16[640,1152]{1,0:T(8,128)(2,1)} %get-tuple-element.103.normed, bf16[640,1536]{1,0:T(8,128)(2,1)} %get-tuple-element.100.left.grad_up), custom_call_target="tpu_custom_call" | custom-call | bytes 112066 | tf_op jit(solution)/shard_map/ffn_parts/pallas_call | solution.py:61
  240.9 25.4 %all-to-all-done.3.grads = bf16[4,160,1152]{2,1,0:T(8,128)(2,1)S(1)} async-done(((bf16[4,160,1152]{2,1,0:T(8,128)(2,1)}), bf16[4,160,1152]{2,1,0:T(8,128)(2,1)S(1)}, u32[]{:S(2)}, u32[]{:S(2)}) %all-to-all-start.3) | async-done | bytes 1474592 | tf_op jit(solution)/shard_map/all_to_all | solution.py:37
  269.1 3.7 output.1
  276.7 24.0 %middle_back.1 = (bf16[160,1152]{1,0:T(8,128)(2,1)}, bf16[4,160,288]{2,1,0:T(8,128)(2,1)}, bf16[160,1152]{1,0:T(8,128)(2,1)}, bf16[4,160,288]{2,1,0:T(8,128)(2,1...) custom-call(s32[10]{0:T(128)} %stack.65.table, ...), custom_call_target="tpu_custom_call" | custom-call | bytes 228904 | tf_op jit(solution)/shard_map/middle_back/pallas_call | solution.py:61
  301.6 7.7 %all-to-all-start.4 = ((bf16[4,160,288]{2,1,0:T(8,128)(2,1)}), bf16[4,160,288]{2,1,0:T(8,128)(2,1)S(1)}, u32[]{:S(2)}, u32[]{:S(2)}) async-start(bf16[4,160,288]{2,1,0:T(8,128)(2,1)} %get-tuple-element.110), calls=%async_computation.4 | async-start | bytes 983040 | tf_op jit(solution)/shard_map/all_to_all | solution.py:37
  309.3 9.1 %square_parts.1 = bf16[1152,3584]{1,0:T(8,128)(2,1)} custom-call(s32[10]{0:T(128)} %stack.65.table, bf16[160,1152]{1,0:T(8,128)(2,1)} %get-tuple-element.111.dyc, bf16[4,160,288]{2,1,0:T(8,128)(2,1)} %get-tuple-element.112.text, bf16[160,1152]{1,0:T(8,128)(2,1)} %get-tuple-element.113.x1, bf16[4,160,288]{2,1,0:T(8,128)(2,1)} %get-tuple-element.114.dqc, ...), custom_call_target="tpu_custom_call" | custom-call | bytes 104693 | tf_op jit(solution)/shard_map/square_parts/pallas_call | solution.py:61
  318.3 3.9 all-to-all-done.4.grad
  323.0 3.6 collective-permute-done.21
  328.2 3.6 all-to-all-start.5
  331.9 12.2 %self_back.1 = (f32[640,288]{1,0:T(8,128)}, f32[288,128]{1,0:T(8,128)}, f32[288,128]{1,0:T(8,128)}) custom-call(s32[10]{0:T(128)} %stack.65.table, bf16[4,160,288]{2,1,0:T(8,128)(2,1)} %copy-done.11, bf16[640,288]{1,0:T(8,128)(2,1)} %get-tuple-element.80.q, f32[640,288]{1,0:T(8,128)} %get-tuple-element.122.wide_out, ...), custom_call_target="tpu_custom_call" | custom-call | bytes 35389 | tf_op jit(solution)/shard_map/self_back/pallas_call | solution.py:61
  348.4 8.6 %self_project_back.1.left.grad_projected = bf16[640,864]{1,0:T(8,128)(2,1)} custom-call(s32[10]{0:T(128)} %stack.65.table, f32[640,288]{1,0:T(8,128)} %get-tuple-element.124.grad_q, bf16[640,288]{1,0:T(8,128)(2,1)} %get-tuple-element.125.k, bf16[640,288]{1,0:T(8,128)(2,1)} %get-tuple-element.126.v, f32[640,576]{1,0:T(8,128)} %get-tuple-element.127.raw, ...), custom_call_target="tpu_custom_call" | custom-call | bytes 43499 | tf_op jit(solution)/shard_map/self_project_back/pallas_call | solution.py:61
  357.1 6.0 %product.5 = bf16[4,160,1152]{2,1,0:T(8,128)(2,1)} custom-call(s32[10]{0:T(128)} %stack.65.table, bf16[640,864]{1,0:T(8,128)(2,1)} %self_project_back.1.left.grad_projected, bf16[864,1152]{1,0:T(8,128)(2,1)} %bitcast.97), custom_call_target="tpu_custom_call" | custom-call | bytes 45711 | tf_op jit(solution)/shard_map/product/pallas_call | solution.py:61
  363.0 5.9 %all-to-all-done.5.kv_grads = bf16[4,304,576]{2,1,0:T(8,128)(2,1)S(1)} async-done(((bf16[4,304,576]{2,1,0:T(8,128)(2,1)}), bf16[4,304,576]{2,1,0:T(8,128)(2,1)S(1)}, u32[]{:S(2)}, u32[]{:S(2)}) %all-to-all-start.5) | async-done | bytes 1400864 | tf_op jit(solution)/shard_map/all_to_all | solution.py:37
  368.9 3.6 all-to-all-start.6
  372.6 2.1 pad.16.text
  377.9 7.8 %late_parts.1 = bf16[1152,1440]{1,0:T(8,128)(2,1)} custom-call(s32[10]{0:T(128)} %stack.65.table, bf16[640,1152]{1,0:T(8,128)(2,1)} %get-tuple-element.131.normed, bf16[640,864]{1,0:T(8,128)(2,1)} %self_project_back.1.left.grad_projected, bf16[304,1152]{1,0:T(8,128)(2,1)} %pad.16.text, bf16[4,304,576]{2,1,0:T(8,128)(2,1)} %copy-done.4), custom_call_target="tpu_custom_call" | custom-call | bytes 79994 | tf_op jit(solution)/shard_map/late_parts/pallas_call | solution.py:61
  386.9 11.5 %reduce-scatter.6.cloned.1.call-done = bf16[144,3584]{1,0:T(8,128)(2,1)} async-done(((bf16[1152,3584]{1,0:T(8,128)(2,1)}), bf16[144,3584]{1,0:T(8,128)(2,1)}) %reduce-scatter.6.cloned.1.call-update) | async-done | bytes 1032208 | tf_op jit(solution)/shard_map/reduce_scatter | solution.py:817
  398.3 8.7 %all-to-all-done.6.grads = bf16[4,160,1152]{2,1,0:T(8,128)(2,1)S(1)} async-done(((bf16[4,160,1152]{2,1,0:T(8,128)(2,1)}), bf16[4,160,1152]{2,1,0:T(8,128)(2,1)S(1)}, u32[]{:S(2)}, u32[]{:S(2)}) %all-to-all-start.6) | async-done | bytes 1474592 | tf_op jit(solution)/shard_map/all_to_all | solution.py:37
  411.7 2.3 collective-permute-done.32
  414.7 4.3 first_norm_back.1
  424.1 3.7 all-to-all-start.7
  429.3 3.6 collective-permute-done.23
  432.9 15.6 %collective-permute-done.24 = bf16[160,1152]{1,0:T(8,128)(2,1)S(1)} collective-permute-done((bf16[160,1152]{1,0:T(8,128)(2,1)}, bf16[160,1152]{1,0:T(8,128)(2,1)S(1)}, u32[]{:S(2)}, u32[]{:S(2)}) %collective-permute-start.24) | collective-permute-done | bytes 368672 | tf_op jit(solution)/shard_map/ppermute | solution.py:33
  448.5 16.8 %collective-permute-start.27 = (f32[6,1152]{1,0:T(8,128)S(1)}, f32[6,1152]{1,0:T(8,128)S(1)}, u32[]{:S(2)}, u32[]{:S(2)}) collective-permute-start(f32[6,1152]{1,0:T(8,128)S(1)} %fusion.4), channel_id=1, source_target_pairs={{0,1},{1,0},{2,3},{3,2},{4,5},{5,4},{6,7},{7,6},{8,9},{9,8},{10,11... | collective-permute-start | bytes 82952 | tf_op jit(solution)/shard_map/ppermute | solution.py:811
  469.6 7.8 %collective-permute-done.28 = f32[6,1152]{1,0:T(8,128)S(1)} collective-permute-done((f32[6,1152]{1,0:T(8,128)S(1)}, f32[6,1152]{1,0:T(8,128)S(1)}, u32[]{:S(2)}, u32[]{:S(2)}) %collective-permute-start.28) | collective-permute-done | bytes 27680 | tf_op jit(solution)/shard_map/ppermute | solution.py:811
  (209 shorter events, 71.6 us)
Async XLA Ops:
  9.7 35.4 %collective-permute-start.2 = (bf16[112,1152]{1,0:T(8,128)(2,1)}, bf16[112,1152]{1,0:T(8,128)(2,1)S(1)}, u32[]{:S(2)}, u32[]{:S(2)}) collective-permute-start(bf16[112,1152]{1,0:T(8,128)(2,1)} %eighth.1), channel_id=1, source_target_pairs={{0,1},{1,2},{2,3},{3,0},{4,5},{5,6},{6,7},{7,4},{8,9},{9,10},{10,1... | collective-permute-start | bytes 774152 | tf_op jit(solution)/shard_map/ppermute | solution.py:33
  12.7 32.4 %collective-permute-start.3 = (bf16[112,1152]{1,0:T(8,128)(2,1)}, bf16[112,1152]{1,0:T(8,128)(2,1)S(1)}, u32[]{:S(2)}, u32[]{:S(2)}) collective-permute-start(bf16[112,1152]{1,0:T(8,128)(2,1)} %eighth.1), channel_id=1, source_target_pairs={{0,2},{1,3},{2,0},{3,1},{4,6},{5,7},{6,4},{7,5},{8,10},{9,11},{10,... | collective-permute-start | bytes 774152 | tf_op jit(solution)/shard_map/ppermute | solution.py:33
  15.3 29.8 %collective-permute-start.4 = (bf16[112,1152]{1,0:T(8,128)(2,1)}, bf16[112,1152]{1,0:T(8,128)(2,1)S(1)}, u32[]{:S(2)}, u32[]{:S(2)}) collective-permute-start(bf16[112,1152]{1,0:T(8,128)(2,1)} %eighth.1), channel_id=1, source_target_pairs={{0,3},{1,0},{2,1},{3,2},{4,7},{5,4},{6,5},{7,6},{8,11},{9,8},{10,9... | collective-permute-start | bytes 774152 | tf_op jit(solution)/shard_map/ppermute | solution.py:33
  16.7 13.1 %collective-permute-start = (bf16[6,1152]{1,0:T(8,128)(2,1)S(1)}, bf16[6,1152]{1,0:T(8,128)(2,1)S(1)}, u32[]{:S(2)}, u32[]{:S(2)}) collective-permute-start(bf16[6,1152]{1,0:T(8,128)(2,1)S(1)} %bitcast.130), channel_id=1, source_target_pairs={{0,4},{4,0},{8,12},{12,8},{16,20},{20,16},{24,28},{28,24},{1,5},{5... | collective-permute-start | bytes 41480 | tf_op jit(solution)/shard_map/ppermute | solution.py:28
  18.8 52.4 %all-to-all-start = ((bf16[4,304,576]{2,1,0:T(8,128)(2,1)}), bf16[4,304,576]{2,1,0:T(8,128)(2,1)S(1)}, u32[]{:S(2)}, u32[]{:S(2)}) async-start(bf16[4,304,576]{2,1,0:T(8,128)(2,1)} %broadcast_in_dim.63), calls=%async_computation | async-start | bytes 3112960 | tf_op jit(solution)/shard_map/all_to_all | solution.py:37
  30.4 14.3 %copy-start.10 = (bf16[640,1152]{1,0:T(8,128)(2,1)S(1)}, bf16[640,1152]{1,0:T(8,128)(2,1)}, u32[]{:S(2)}) copy-start(bf16[640,1152]{1,0:T(8,128)(2,1)} %param.15) | copy-start | bytes 4423684
  43.3 6.3 %collective-permute-start.1 = (f32[2,288,128]{2,1,0:T(8,128)S(1)}, f32[2,288,128]{2,1,0:T(8,128)S(1)}, u32[]{:S(2)}, u32[]{:S(2)}) collective-permute-start(f32[2,288,128]{2,1,0:T(8,128)S(1)} %pad_maximum_fusion.1), channel_id=1, source_target_pairs={{0,4},{4,0},{8,12},{12,8},{16,20},{20,16},{24,28},{28,24},{1,5},{5... | collective-permute-start | bytes 884744 | tf_op jit(solution)/shard_map/ppermute | solution.py:28
  46.1 25.6 %collective-permute-start.6 = (bf16[3,112,1152]{2,1,0:T(8,128)(2,1)}, bf16[3,112,1152]{2,1,0:T(8,128)(2,1)}, u32[]{:S(2)}, u32[]{:S(2)}) collective-permute-start(bf16[3,112,1152]{2,1,0:T(8,128)(2,1)} %pad_maximum_fusion.refs_0_), channel_id=1, source_target_pairs={{0,8},{4,12},{8,0},{12,4},{16,24},{20,28},{24,16},{28,20},{1,9},{5... | collective-permute-start | bytes 2322440 | tf_op jit(solution)/shard_map/ppermute | solution.py:750
  47.6 35.8 %collective-permute-start.7 = (bf16[3,112,1152]{2,1,0:T(8,128)(2,1)}, bf16[3,112,1152]{2,1,0:T(8,128)(2,1)}, u32[]{:S(2)}, u32[]{:S(2)}) collective-permute-start(bf16[3,112,1152]{2,1,0:T(8,128)(2,1)} %pad_maximum_fusion.refs_0_), channel_id=1, source_target_pairs={{0,16},{4,20},{8,24},{12,28},{16,0},{20,4},{24,8},{28,12},{1,17},{... | collective-permute-start | bytes 2322440 | tf_op jit(solution)/shard_map/ppermute | solution.py:750
  49.2 34.3 %collective-permute-start.8 = (bf16[3,112,1152]{2,1,0:T(8,128)(2,1)}, bf16[3,112,1152]{2,1,0:T(8,128)(2,1)}, u32[]{:S(2)}, u32[]{:S(2)}) collective-permute-start(bf16[3,112,1152]{2,1,0:T(8,128)(2,1)} %pad_maximum_fusion.refs_0_), channel_id=1, source_target_pairs={{0,24},{4,28},{8,16},{12,20},{16,8},{20,12},{24,0},{28,4},{1,25},{... | collective-permute-start | bytes 2322440 | tf_op jit(solution)/shard_map/ppermute | solution.py:750
  71.2 32.6 %copy-start.2 = (bf16[4,304,576]{2,1,0:T(8,128)(2,1)}, bf16[4,304,576]{2,1,0:T(8,128)(2,1)S(1)}, u32[]{:S(2)}) copy-start(bf16[4,304,576]{2,1,0:T(8,128)(2,1)S(1)} %all-to-all-done.refs_8_.kv_own) | copy-start | bytes 4202500
  71.2 32.6 %collective-permute-start.12 = (bf16[4,304,576]{2,1,0:T(8,128)(2,1)S(1)}, bf16[4,304,576]{2,1,0:T(8,128)(2,1)S(1)}, u32[]{:S(2)}, u32[]{:S(2)}) collective-permute-start(bf16[4,304,576]{2,1,0:T(8,128)(2,1)S(1)} %all-to-all-done.refs_8_.kv_own), channel_id=1, source_target_pairs={{0,4},{4,0},{8,12},{12,8},{16,20},{20,16},{24,28},{28,24},{1,5},{5... | collective-permute-start | bytes 4202504 | tf_op jit(solution)/shard_map/ppermute | solution.py:28
  71.3 19.7 %collective-permute-start.5 = (bf16[3,112,1152]{2,1,0:T(8,128)(2,1)}, bf16[3,112,1152]{2,1,0:T(8,128)(2,1)}, u32[]{:S(2)}, u32[]{:S(2)}) collective-permute-start(bf16[3,112,1152]{2,1,0:T(8,128)(2,1)} %pad_maximum_fusion.refs_0_), channel_id=1, source_target_pairs={{0,4},{4,0},{8,12},{12,8},{16,20},{20,16},{24,28},{28,24},{1,5},{5... | collective-permute-start | bytes 2322440 | tf_op jit(solution)/shard_map/ppermute | solution.py:28
  83.5 7.6 %collective-permute-start.10 = (bf16[3,112,1152]{2,1,0:T(8,128)(2,1)}, bf16[3,112,1152]{2,1,0:T(8,128)(2,1)}, u32[]{:S(2)}, u32[]{:S(2)}) collective-permute-start(bf16[3,112,1152]{2,1,0:T(8,128)(2,1)} %collective-permute-done.7.refs_4_), channel_id=1, source_target_pairs={{0,4},{4,0},{8,12},{12,8},{16,20},{20,16},{24,28},{28,24},{1,5},{5... | collective-permute-start | bytes 2322440 | tf_op jit(solution)/shard_map/ppermute | solution.py:28
  83.5 7.6 %collective-permute-start.11 = (bf16[3,112,1152]{2,1,0:T(8,128)(2,1)}, bf16[3,112,1152]{2,1,0:T(8,128)(2,1)}, u32[]{:S(2)}, u32[]{:S(2)}) collective-permute-start(bf16[3,112,1152]{2,1,0:T(8,128)(2,1)} %collective-permute-done.8.refs_6_), channel_id=1, source_target_pairs={{0,4},{4,0},{8,12},{12,8},{16,20},{20,16},{24,28},{28,24},{1,5},{5... | collective-permute-start | bytes 2322440 | tf_op jit(solution)/shard_map/ppermute | solution.py:28
  84.0 7.1 %collective-permute-start.9 = (bf16[3,112,1152]{2,1,0:T(8,128)(2,1)}, bf16[3,112,1152]{2,1,0:T(8,128)(2,1)}, u32[]{:S(2)}, u32[]{:S(2)}) collective-permute-start(bf16[3,112,1152]{2,1,0:T(8,128)(2,1)} %collective-permute-done.6.refs_2_), channel_id=1, source_target_pairs={{0,4},{4,0},{8,12},{12,8},{16,20},{20,16},{24,28},{28,24},{1,5},{5... | collective-permute-start | bytes 2322440 | tf_op jit(solution)/shard_map/ppermute | solution.py:28
  84.0 19.8 %all-to-all-start.1 = ((bf16[4,160,288]{2,1,0:T(8,128)(2,1)}), bf16[4,160,288]{2,1,0:T(8,128)(2,1)}, u32[]{:S(2)}, u32[]{:S(2)}) async-start(bf16[4,160,288]{2,1,0:T(8,128)(2,1)} %bitcast.121), calls=%async_computation.1 | async-start | bytes 983040 | tf_op jit(solution)/shard_map/all_to_all | solution.py:37
  125.9 40.5 %copy-start.14 = (bf16[1152,720]{0,1:T(8,128)(2,1)S(1)}, bf16[1152,720]{0,1:T(8,128)(2,1)}, u32[]{:S(2)}) copy-start(bf16[1152,720]{0,1:T(8,128)(2,1)} %param.27) | copy-start | bytes 4976644
  125.9 13.7 %collective-permute-start.13 = (bf16[160,1152]{1,0:T(8,128)(2,1)}, bf16[160,1152]{1,0:T(8,128)(2,1)S(1)}, u32[]{:S(2)}, u32[]{:S(2)}) collective-permute-start(bf16[160,1152]{1,0:T(8,128)(2,1)} %get-tuple-element.92.refs_0_), channel_id=1, source_target_pairs={{0,1},{1,2},{2,3},{3,0},{4,5},{5,6},{6,7},{7,4},{8,9},{9,10},{10,1... | collective-permute-start | bytes 1105928 | tf_op jit(solution)/shard_map/ppermute | solution.py:33
  125.9 27.9 %collective-permute-start.14 = (bf16[160,1152]{1,0:T(8,128)(2,1)}, bf16[160,1152]{1,0:T(8,128)(2,1)S(1)}, u32[]{:S(2)}, u32[]{:S(2)}) collective-permute-start(bf16[160,1152]{1,0:T(8,128)(2,1)} %get-tuple-element.92.refs_0_), channel_id=1, source_target_pairs={{0,2},{1,3},{2,0},{3,1},{4,6},{5,7},{6,4},{7,5},{8,10},{9,11},{10,... | collective-permute-start | bytes 1105928 | tf_op jit(solution)/shard_map/ppermute | solution.py:33
  127.9 25.9 %collective-permute-start.15 = (bf16[160,1152]{1,0:T(8,128)(2,1)}, bf16[160,1152]{1,0:T(8,128)(2,1)S(1)}, u32[]{:S(2)}, u32[]{:S(2)}) collective-permute-start(bf16[160,1152]{1,0:T(8,128)(2,1)} %get-tuple-element.92.refs_0_), channel_id=1, source_target_pairs={{0,3},{1,0},{2,1},{3,2},{4,7},{5,4},{6,5},{7,6},{8,11},{9,8},{10,9... | collective-permute-start | bytes 1105928 | tf_op jit(solution)/shard_map/ppermute | solution.py:33
  139.6 14.3 %copy-start.29 = (bf16[160,1152]{1,0:T(8,128)(2,1)}, bf16[160,1152]{1,0:T(8,128)(2,1)S(1)}, u32[]{:S(2)}) copy-start(bf16[160,1152]{1,0:T(8,128)(2,1)S(1)} %collective-permute-done.13.refs_1_) | copy-start | bytes 1105924
  166.3 1.5 collective-permute-start.16
  183.8 44.0 %all-to-all-start.2 = ((bf16[4,160,1152]{2,1,0:T(8,128)(2,1)}), bf16[4,160,1152]{2,1,0:T(8,128)(2,1)S(1)}, u32[]{:S(2)}, u32[]{:S(2)}) async-start(bf16[4,160,1152]{2,1,0:T(8,128)(2,1)} %product.3), calls=%async_computation.2 | async-start | bytes 2949120 | tf_op jit(solution)/shard_map/all_to_all | solution.py:37
  193.3 1.4 collective-permute-start.20
  227.8 38.5 %all-to-all-start.3 = ((bf16[4,160,1152]{2,1,0:T(8,128)(2,1)}), bf16[4,160,1152]{2,1,0:T(8,128)(2,1)S(1)}, u32[]{:S(2)}, u32[]{:S(2)}) async-start(bf16[4,160,1152]{2,1,0:T(8,128)(2,1)} %product.4), calls=%async_computation.3 | async-start | bytes 2949120 | tf_op jit(solution)/shard_map/all_to_all | solution.py:37
  231.3 100.5 %reduce-scatter.4.cloned.1.call-start = ((), (), s32[]{:S(2)}) async-start(), calls=%async_computation.11 | async-start | bytes 5971968 | tf_op jit(solution)/shard_map/reduce_scatter | solution.py:817
  272.8 27.9 %collective-permute-start.17 = (bf16[160,1152]{1,0:T(8,128)(2,1)}, bf16[160,1152]{1,0:T(8,128)(2,1)S(1)}, u32[]{:S(2)}, u32[]{:S(2)}) collective-permute-start(bf16[160,1152]{1,0:T(8,128)(2,1)} %get-tuple-element.96), channel_id=1, source_target_pairs={{0,1},{1,2},{2,3},{3,0},{4,5},{5,6},{6,7},{7,4},{8,9},{9,10},{10,1... | collective-permute-start | bytes 1105928 | tf_op jit(solution)/shard_map/ppermute | solution.py:33
  272.8 27.9 %collective-permute-start.18 = (bf16[160,1152]{1,0:T(8,128)(2,1)}, bf16[160,1152]{1,0:T(8,128)(2,1)S(1)}, u32[]{:S(2)}, u32[]{:S(2)}) collective-permute-start(bf16[160,1152]{1,0:T(8,128)(2,1)} %get-tuple-element.96), channel_id=1, source_target_pairs={{0,2},{1,3},{2,0},{3,1},{4,6},{5,7},{6,4},{7,5},{8,10},{9,11},{10,... | collective-permute-start | bytes 1105928 | tf_op jit(solution)/shard_map/ppermute | solution.py:33
  274.8 26.0 %collective-permute-start.19 = (bf16[160,1152]{1,0:T(8,128)(2,1)}, bf16[160,1152]{1,0:T(8,128)(2,1)S(1)}, u32[]{:S(2)}, u32[]{:S(2)}) collective-permute-start(bf16[160,1152]{1,0:T(8,128)(2,1)} %get-tuple-element.96), channel_id=1, source_target_pairs={{0,3},{1,0},{2,1},{3,2},{4,7},{5,4},{6,5},{7,6},{8,11},{9,8},{10,9... | collective-permute-start | bytes 1105928 | tf_op jit(solution)/shard_map/ppermute | solution.py:33
  301.6 20.7 %all-to-all-start.4 = ((bf16[4,160,288]{2,1,0:T(8,128)(2,1)}), bf16[4,160,288]{2,1,0:T(8,128)(2,1)S(1)}, u32[]{:S(2)}, u32[]{:S(2)}) async-start(bf16[4,160,288]{2,1,0:T(8,128)(2,1)} %get-tuple-element.110), calls=%async_computation.4 | async-start | bytes 983040 | tf_op jit(solution)/shard_map/all_to_all | solution.py:37
  309.3 89.1 %reduce-scatter.6.cloned.1.call-start = ((), (), s32[]{:S(2)}) async-start(), calls=%async_computation.12 | async-start | bytes 9289728 | tf_op jit(solution)/shard_map/reduce_scatter | solution.py:817
  323.0 3.6 collective-permute-start.21
  328.2 40.7 %all-to-all-start.5 = ((bf16[4,304,576]{2,1,0:T(8,128)(2,1)}), bf16[4,304,576]{2,1,0:T(8,128)(2,1)S(1)}, u32[]{:S(2)}, u32[]{:S(2)}) async-start(bf16[4,304,576]{2,1,0:T(8,128)(2,1)} %add_convert_fusion), calls=%async_computation.6 | async-start | bytes 3112960 | tf_op jit(solution)/shard_map/all_to_all | solution.py:37
  345.1 1.6 collective-permute-start.22
  368.9 38.1 %all-to-all-start.6 = ((bf16[4,160,1152]{2,1,0:T(8,128)(2,1)}), bf16[4,160,1152]{2,1,0:T(8,128)(2,1)S(1)}, u32[]{:S(2)}, u32[]{:S(2)}) async-start(bf16[4,160,1152]{2,1,0:T(8,128)(2,1)} %product.5), calls=%async_computation.7 | async-start | bytes 2949120 | tf_op jit(solution)/shard_map/all_to_all | solution.py:37
  372.5 106.7 %reduce-scatter.8.cloned.1.call-start = ((), (), s32[]{:S(2)}) async-start(), calls=%async_computation.13 | async-start | bytes 3981312 | tf_op jit(solution)/shard_map/reduce_scatter | solution.py:817
  376.6 9.2 %collective-permute-start.30 = (f32[9,1536]{1,0:T(8,128)S(1)}, f32[9,1536]{1,0:T(8,128)S(1)}, u32[]{:S(2)}, u32[]{:S(2)}) collective-permute-start(f32[9,1536]{1,0:T(8,128)S(1)} %bitcast.126), channel_id=1, source_target_pairs={{0,4},{4,0},{8,12},{12,8},{16,20},{20,16},{24,28},{28,24},{1,5},{5... | collective-permute-start | bytes 165896 | tf_op jit(solution)/shard_map/ppermute | solution.py:28
  385.7 23.6 %collective-permute-start.31 = (f32[9,1536]{1,0:T(8,128)S(1)}, f32[9,1536]{1,0:T(8,128)S(1)}, u32[]{:S(2)}, u32[]{:S(2)}) collective-permute-start(f32[9,1536]{1,0:T(8,128)S(1)} %add.159), channel_id=1, source_target_pairs={{0,8},{4,12},{8,0},{12,4},{16,24},{20,28},{24,16},{28,20},{1,9},{5... | collective-permute-start | bytes 165896 | tf_op jit(solution)/shard_map/ppermute | solution.py:28
  409.4 4.7 collective-permute-start.32
  419.0 13.8 %collective-permute-start.23 = (bf16[160,1152]{1,0:T(8,128)(2,1)}, bf16[160,1152]{1,0:T(8,128)(2,1)S(1)}, u32[]{:S(2)}, u32[]{:S(2)}) collective-permute-start(bf16[160,1152]{1,0:T(8,128)(2,1)} %get-tuple-element.136), channel_id=1, source_target_pairs={{0,1},{1,2},{2,3},{3,0},{4,5},{5,6},{6,7},{7,4},{8,9},{9,10},{10,1... | collective-permute-start | bytes 1105928 | tf_op jit(solution)/shard_map/ppermute | solution.py:33
  419.3 29.2 %collective-permute-start.24 = (bf16[160,1152]{1,0:T(8,128)(2,1)}, bf16[160,1152]{1,0:T(8,128)(2,1)S(1)}, u32[]{:S(2)}, u32[]{:S(2)}) collective-permute-start(bf16[160,1152]{1,0:T(8,128)(2,1)} %get-tuple-element.136), channel_id=1, source_target_pairs={{0,2},{1,3},{2,0},{3,1},{4,6},{5,7},{6,4},{7,5},{8,10},{9,11},{10,... | collective-permute-start | bytes 1105928 | tf_op jit(solution)/shard_map/ppermute | solution.py:33
  421.2 27.2 %collective-permute-start.25 = (bf16[160,1152]{1,0:T(8,128)(2,1)}, bf16[160,1152]{1,0:T(8,128)(2,1)S(1)}, u32[]{:S(2)}, u32[]{:S(2)}) collective-permute-start(bf16[160,1152]{1,0:T(8,128)(2,1)} %get-tuple-element.136), channel_id=1, source_target_pairs={{0,3},{1,0},{2,1},{3,2},{4,7},{5,4},{6,5},{7,6},{8,11},{9,8},{10,9... | collective-permute-start | bytes 1105928 | tf_op jit(solution)/shard_map/ppermute | solution.py:33
  424.1 54.0 %all-to-all-start.7 = ((bf16[4,144,896]{2,1,0:T(8,128)(2,1)}), bf16[4,144,896]{2,1,0:T(8,128)(2,1)S(1)}, u32[]{:S(2)}, u32[]{:S(2)}) async-start(bf16[4,144,896]{2,1,0:T(8,128)(2,1)} %bitcast.89), calls=%async_computation.10 | async-start | bytes 2064384 | tf_op jit(solution)/shard_map/all_to_all | solution.py:37
  428.0 1.3 collective-permute-start.26
  448.5 21.2 %collective-permute-start.27 = (f32[6,1152]{1,0:T(8,128)S(1)}, f32[6,1152]{1,0:T(8,128)S(1)}, u32[]{:S(2)}, u32[]{:S(2)}) collective-permute-start(f32[6,1152]{1,0:T(8,128)S(1)} %fusion.4), channel_id=1, source_target_pairs={{0,1},{1,0},{2,3},{3,2},{4,5},{5,4},{6,7},{7,6},{8,9},{9,8},{10,11... | collective-permute-start | bytes 82952 | tf_op jit(solution)/shard_map/ppermute | solution.py:811
  465.2 12.3 %collective-permute-start.28 = (f32[6,1152]{1,0:T(8,128)S(1)}, f32[6,1152]{1,0:T(8,128)S(1)}, u32[]{:S(2)}, u32[]{:S(2)}) collective-permute-start(f32[6,1152]{1,0:T(8,128)S(1)} %fusion.4), channel_id=1, source_target_pairs={{0,2},{1,3},{2,0},{3,1},{4,6},{5,7},{6,4},{7,5},{8,10},{9,11},{10,... | collective-permute-start | bytes 82952 | tf_op jit(solution)/shard_map/ppermute | solution.py:811
  466.9 10.6 %collective-permute-start.29 = (f32[6,1152]{1,0:T(8,128)S(1)}, f32[6,1152]{1,0:T(8,128)S(1)}, u32[]{:S(2)}, u32[]{:S(2)}) collective-permute-start(f32[6,1152]{1,0:T(8,128)S(1)} %fusion.4), channel_id=1, source_target_pairs={{0,3},{1,2},{2,1},{3,0},{4,7},{5,6},{6,5},{7,4},{8,11},{9,10},{10,... | collective-permute-start | bytes 82952 | tf_op jit(solution)/shard_map/ppermute | solution.py:811
  (37 other events, 141.7 us)
Sparse Core Ops, SparseCore 0:
  266.4 55.1 reduce-scatter.3
  325.7 72.5 reduce-scatter.5
  407.2 46.2 reduce-scatter.7

commit v4 on v3

--- a/solution.py
+++ b/solution.py
@@ -134,7 +134,7 @@
 
 
 def logistic(wide):
-    return 1.0 / (1.0 + jnp.exp(-wide))
+    return 0.5 + 0.5 * jnp.tanh(0.5 * wide)
 
 
 def self_project_body(table, x, mod_own, mod_other, weight, normed, raw, q, k, v, own_out, other_out, squares, totals):
@@ -421,13 +421,13 @@
     ).astype(LOW)
 
 
-def middle_back_body(table, grads, x2_in, upstream, branch, mod_own, mod_other, out_first, query_first, cross_first, rest, kv_own, kv_other, probs_in, queries_in, cross_grad, query_grad, attn_grad, attended_grad, after_grad, sums, kv_own_grad, kv_other_grad):
+def middle_back_body(table, grad_own, grad_1, grad_2, grad_3, x2_in, upstream, branch, mod_own, mod_other, out_first, query_first, cross_first, rest, kv_own, kv_other, probs_in, queries_in, cross_grad, query_grad, attn_grad, attended_grad, after_grad, sums, kv_own_grad, kv_other_grad):
     count, rows, columns = queries_in.shape
     keys = kv_own.shape[1]
     heads = columns // CROSS_HEAD
     scale = 1.0 / math.sqrt(CROSS_HEAD)
     own = own_image(table, table[BLOCK_FIRST], rows)
-    grad = total(grads)
+    grad = with_own(grad_own, grad_1, grad_2, grad_3)
     x2 = x2_in[...]
     inverse = inverse_size(x2)
     xh = x2 * inverse
@@ -486,10 +486,10 @@
         ).astype(LOW)
 
 
-def first_norm_back_body(table, grads, after_grad, x, mod_own, mod_other, input_grad, sums):
+def first_norm_back_body(table, grad_own, grad_1, grad_2, grad_3, after_grad, x, mod_own, mod_other, input_grad, sums):
     rows = x.shape[0]
     own = own_image(table, table[BLOCK_FIRST], rows)
-    grad = total(grads)
+    grad = with_own(grad_own, grad_1, grad_2, grad_3)
     wide = x[...].astype(WIDE)
     inverse = inverse_size(wide)
     xh = wide * inverse
@@ -513,12 +513,13 @@
 
 def up_body(table, *refs):
     blocks, weight, (wide_out, low_out, ordered) = refs[:-4], refs[-4], refs[-3:]
-    step = pl.program_id(0)
-    for place, ref in enumerate(blocks):
-
-        @pl.when(step == place)
-        def _():
-            ordered[...] = ref[...]
+    rows = blocks[0].shape[0]
+
+    @pl.when(pl.program_id(0) == 0)
+    def _():
+        for step, block in enumerate(blocks):
+            low = turned(table, step, len(blocks)) * rows
+            ordered[pl.ds(pl.multiple_of(low, 16), rows), :] = block[...]
 
     up = times_transposed(ordered[...], weight[...])
     wide_out[...] = up
@@ -526,19 +527,20 @@
 
 
 def up_project(table, blocks, weight):
-    count = len(blocks)
     rows, width = blocks[0].shape
-    columns = weight.shape[0]
-    turn = lambda i, t: (turned(t, i, count), 0)
-    whole = lambda a: pl.BlockSpec(a.shape, lambda i, t: (0, 0))
+    tokens = len(blocks) * rows
+    columns = 3 * LANES
+    whole = lambda *shape: pl.BlockSpec(shape, lambda i, t: (0, 0))
+    column = pl.BlockSpec((tokens, columns), lambda i, t: (0, i))
     return call(
         up_body,
         "up_project",
-        [((count * rows, columns), WIDE), ((count * rows, columns), LOW), ((count * rows, width), LOW)],
+        [((tokens, weight.shape[0]), WIDE), ((tokens, weight.shape[0]), LOW), ((tokens, width), LOW)],
         (*blocks, weight),
-        grid=(count,),
-        in_specs=[whole(array) for array in (*blocks, weight)],
-        out_specs=[pl.BlockSpec((rows, columns), turn)] * 2 + [pl.BlockSpec((rows, width), turn)],
+        grid=(weight.shape[0] // columns,),
+        in_specs=[whole(rows, width)] * len(blocks)
+        + [pl.BlockSpec((columns, width), lambda i, t: (i, 0))],
+        out_specs=[column, column, whole(tokens, width)],
         table=table,
     )
 
@@ -760,6 +762,11 @@
     return lax.dynamic_slice_in_dim(values, (place % count) * size, size, 0)
 
 
+def own_rows(values):
+    rows = values.shape[0] // lax.axis_size("tp")
+    return pl.BlockSpec((rows, values.shape[1]), lambda i, t: (t[TP_PLACE], 0))
+
+
 def placed_blocks(blocks):
     count = len(blocks)
     place = lax.axis_index("tp")
@@ -773,26 +780,31 @@
     return [block] + [from_behind(block, step) for step in range(1, lax.axis_size("tp"))]
 
 
-def product_body(table, left, right, out):
-    out[0] = dot(left[...], right[...]).astype(LOW)
-
-
-def product(table, left, right):
+def product(left, right):
     count = lax.axis_size("tp")
-    rows, columns = left.shape[0] // count, left.shape[1]
-    return call(
-        product_body,
-        "product",
-        [((count, rows, right.shape[1]), LOW)],
-        (left, right),
-        grid=(count,),
-        in_specs=[
-            pl.BlockSpec((rows, columns), lambda i, t: (i, 0)),
-            pl.BlockSpec(right.shape, lambda i, t: (0, 0)),
-        ],
-        out_specs=[pl.BlockSpec((1, rows, right.shape[1]), lambda i, t: (i, 0, 0))],
-        table=table,
-    )[0]
+    return dot(left, right).astype(LOW).reshape(count, left.shape[0] // count, right.shape[1])
+
+
+def spread(blocks):
+    count = lax.axis_size("tp")
+    place = lax.axis_index("tp")
+    return [
+        from_behind(
+            lax.dynamic_index_in_dim(blocks, (place + step) % count, 0, keepdims=False), step
+        )
+        for step in range(1, count)
+    ]
+
+
+def own_block(blocks):
+    return pl.BlockSpec((1,) + blocks.shape[1:], lambda i, t: (t[TP_PLACE], 0, 0))
+
+
+def with_own(own, *others):
+    result = own[0].astype(WIDE)
+    for other in others:
+        result += other[...].astype(WIDE)
+    return result
 
 
 def total(parts):
@@ -818,7 +830,8 @@
     )
 
 
-def square_body(table, dyc, text, x1, dqc, dy1, att, out):
+def square_body(table, dyc, text, x1, dqc, dy1, att, kv_mine, kv_theirs, out, kv_out):
+    kv_out[...] = (kv_mine[...].astype(WIDE) + kv_theirs[...].astype(WIDE)).astype(LOW)
     parts = [
         over_tokens(left[...], right[0]) for left, right in ((dyc, text), (x1, dqc), (dy1, att))
     ]
@@ -828,24 +841,24 @@
     out[...] = jnp.concatenate(parts, axis=1).astype(LOW)
 
 
-def square_parts(table, lefts, rights):
+def square_parts(table, lefts, rights, kv_mine, kv_theirs):
     rows, width = lefts[0].shape
     count, _, columns = rights[0].shape
     block = -(-3 * columns // LANES) * LANES
     whole = pl.BlockSpec((rows, width), lambda i, t: (0, 0))
     one = pl.BlockSpec((1, rows, columns), lambda i, t: (turned(t, i, count), 0, 0))
     still = pl.BlockSpec((1, rows, columns), lambda i, t: (i, 0, 0))
+    kv = pl.BlockSpec((1,) + kv_mine.shape[1:], lambda i, t: (i, 0, 0))
     return call(
         square_body,
         "square_parts",
-        [((width, count * block), LOW)],
-        [array for pair in zip(lefts, rights) for array in pair],
+        [((width, count * block), LOW), (kv_mine.shape, LOW)],
+        [array for pair in zip(lefts, rights) for array in pair] + [kv_mine, kv_theirs],
         grid=(count,),
-        in_specs=[whole, one, whole, one, whole, still],
-        out_specs=[pl.BlockSpec((width, block), lambda i, t: (0, i))],
-        flops=8 * rows * width * count * block,
-        table=table,
-    )[0]
+        in_specs=[whole, one, whole, one, whole, still, kv, kv],
+        out_specs=[pl.BlockSpec((width, block), lambda i, t: (0, i)), kv],
+        table=table,
+    )
 
 
 def ffn_body(table, grad_ffn, hidden, normed, grad_up, out):
@@ -957,8 +970,8 @@
         table, after(q, kv_here), kernel_own, kernel_other
     )
 
-    x_block = token_block(hidden_in, tp_index)
-    up_block = token_block(cotangent, tp_index)
+    whole = pl.BlockSpec(memory_space=pltpu.VMEM)
+    x_rows, upstream_rows = own_rows(hidden_in), own_rows(cotangent)
     up_flat = jnp.pad(
         after(up_weight.transpose(1, 2, 0), attended), ((0, 0), (0, ffn_pad - ffn_cols), (0, 0))
     ).reshape(2 * ffn_pad, width)
@@ -975,13 +988,13 @@
     )
     grad_ffn = (cotangent.astype(WIDE) * gate_rows).astype(LOW)
     grad_hidden = times_transposed(grad_ffn, down_flat)
-    ready = (up_flat, taps, grad_hidden)
+    ready = (up_flat, down_flat, taps, grad_hidden)
     split_tokens = lambda values: values.reshape(count, block_size, values.shape[1])
     kv_own = exchanged(kv_sent_first)
     attended_blocks = exchanged(after(split_tokens(attended), kv_own))
     kv_own = after(kv_own, *ready)
     kv_other = swapped(kv_own, "seq", 0)
-    pieces = share_eighths(fetched, ready)
+    pieces = share_eighths(fetched, (*ready, attended_blocks))
     all_heads = count * cross_cols // CROSS_HEAD
     branch, after_low, queries, probs, text_low, after_cross, normed_two, rest = call(
         middle_body,
@@ -996,7 +1009,8 @@
             ((block_size, width), LOW),
             ((count - 1, 8 * fetched.shape[1], width), LOW),
         ],
-        (attended_blocks, x_block, mod_own, mod_other, *weights, *pieces, kv_own, kv_other),
+        (attended_blocks, hidden_in, mod_own, mod_other, *weights, *pieces, kv_own, kv_other),
+        in_specs=[whole, x_rows] + [whole] * 15,
         flops=60 * block_size * width * width,
         table=table,
     )
@@ -1005,25 +1019,26 @@
     rim = swapped(jnp.where(first_half, activated[-MAXW:], activated[:MAXW]), "seq", 0)
     hidden, grads = mix(table, activated, rim, taps, grad_hidden)
     grads_rim = swapped(jnp.where(first_half, grads[:, -MAXW:], grads[:, :MAXW]), "seq", 0)
-    branch_sent = product(table, hidden, down_flat)
+    branch_sent = product(hidden, down_flat)
     grad_up, tap_part = mix_back(
         table, grads, grads_rim, activated, rim, taps, after(up_wide, branch_sent)
     )
     branches = exchanged(branch_sent)
-    norm_two_sent = product(table, grad_up, up_flat)
-    grad_norm_two = exchanged(after(norm_two_sent, branches))
-    ffn_parts = ffn_parts_of(
-        table, grad_ffn, after(hidden, norm_two_sent), normed_two_low, grad_up
-    )
-    ffn_rows = sum_rows(after(ffn_parts, grad_norm_two))
+    norm_two_sent = product(grad_up, up_flat)
+    grad_norm_two = spread(norm_two_sent)
     output_block, output_sums = call(
         output_body,
         "output",
         [((block_size, width), LOW), ((8, width), WIDE)],
-        (branches, after_cross, up_block, mod_own, mod_other),
-        table=table,
-    )
-    output_blocks = all_blocks(output_block)
+        (branches, after_cross, cotangent, mod_own, mod_other),
+        in_specs=[whole, whole, upstream_rows, whole, whole],
+        table=table,
+    )
+    ffn_parts = ffn_parts_of(
+        table, grad_ffn, after(hidden, norm_two_sent, output_block), normed_two_low, grad_up
+    )
+    ffn_rows = sum_rows(after(ffn_parts, grad_norm_two))
+    output_blocks = all_blocks(after(output_block, grad_norm_two))
 
     (
         cross_grad,
@@ -1048,9 +1063,10 @@
             ((count, keys, 2 * cross_cols), LOW),
         ],
         (
-            after(grad_norm_two, ffn_parts, output_block),
+            after(norm_two_sent, ffn_parts, output_block),
+            *grad_norm_two,
             after_cross,
-            up_block,
+            cotangent,
             branch,
             mod_own,
             mod_other,
@@ -1061,20 +1077,21 @@
             probs,
             queries,
         ),
+        in_specs=[own_block(norm_two_sent)] + [whole] * 4 + [upstream_rows] + [whole] * 11,
         flops=120 * block_size * width * width,
         table=table,
     )
 
     grad_blocks = exchanged(after(attended_grad, output_blocks))
-    squares = square_parts(
+    kv_theirs = swapped(after(kv_other_grad, output_blocks), "seq", 0)
+    squares, kv_sent = square_parts(
         table,
         (cross_grad, after_low, attn_grad),
         (text_low, query_grad, after(attended_blocks, attended_grad)),
+        kv_own_grad,
+        kv_theirs,
     )
     square_rows = sum_rows(after(squares, grad_blocks))
-    kv_sent = (
-        kv_own_grad.astype(WIDE) + swapped(kv_other_grad, "seq", 0).astype(WIDE)
-    ).astype(LOW)
     kv_sent = after(kv_sent, grad_blocks)
     kv_parts = exchanged(kv_sent)
     grad_blocks = after(grad_blocks, squares, kv_sent, ffn_rows)
@@ -1091,8 +1108,8 @@
         back_own + back_theirs[1],
         back_other + back_theirs[0],
     )
-    normed_sent = product(table, grad_projected, qkv_flat)
-    grad_normed = exchanged(after(normed_sent, kv_parts))
+    normed_sent = product(grad_projected, qkv_flat)
+    grad_normed = spread(normed_sent)
     late_parts = call(
         late_body,
         "late_parts",
@@ -1104,41 +1121,44 @@
     conv_sum = after(tap_part[:9], normed_sent)
     for place in range(lax.axis_size("seq").bit_length() - 1):
         conv_sum = conv_sum + swapped(conv_sum, "seq", place)
+    square_sent = square_rows.reshape(square_rows.shape[0], count, -1).transpose(1, 0, 2)
     input_block, first_sums = call(
         first_norm_back_body,
         "first_norm_back",
         [((block_size, width), LOW), ((8, width), WIDE)],
         (
-            after(grad_normed, late_parts, square_rows),
+            after(normed_sent, late_parts, square_sent),
+            *grad_normed,
             after_grad,
-            x_block,
+            hidden_in,
             mod_own,
             mod_other,
         ),
-        table=table,
-    )
-    square_sent = square_rows.reshape(square_rows.shape[0], count, -1).transpose(1, 0, 2)
-    square_grads = total(exchanged(after(square_sent, grad_normed)))[:, : 3 * self_cols]
-    input_blocks = all_blocks(input_block)
-    input_grad = placed_blocks(input_blocks).astype(WIDE)
-    output = placed_blocks(output_blocks)
-
+        in_specs=[own_block(normed_sent)] + [whole] * 4 + [x_rows, whole, whole],
+        table=table,
+    )
+    square_parts_here = exchanged(square_sent)
+    square_grads = total(square_parts_here)[:, : 3 * self_cols]
     pairs = jnp.concatenate([first_sums[:4], middle_sums[4:6], middle_sums[:4], output_sums[:2]])
     pairs = pairs.reshape(6, 2, width)
-    modulation_grad = same_everywhere(
-        after(pairs[:, 0] + swapped(pairs[:, 1], "seq", 0), input_blocks)
-    )
-
+    pairs = pairs[:, 0] + swapped(pairs[:, 1], "seq", 0)
+    input_block = after(input_block, square_parts_here)
     late_rows = late_rows.astype(WIDE)
+    qkv_grad = late_rows[:, : 3 * self_cols].reshape(-1, 3, self_cols)
+    ckv_grad = late_rows[:, 3 * self_cols :].reshape(-1, 2, cross_cols)
+    output = placed_blocks(output_blocks)
+    input_blocks = after(all_blocks(input_block), qkv_grad, ckv_grad, square_grads, output)
+    modulation_grad = same_everywhere(after(pairs, input_blocks))
+    input_grad = placed_blocks(input_blocks).astype(WIDE)
 
     return (
         output,
         input_grad,
         modulation_grad[None],
-        late_rows[:, : 3 * self_cols].reshape(-1, 3, self_cols),
+        qkv_grad,
         square_grads[:, 2 * self_cols :],
         square_grads[:, self_cols : 2 * self_cols],
-        late_rows[:, 3 * self_cols :].reshape(-1, 2, cross_cols),
+        ckv_grad,
         square_grads[:, :self_cols],
         ffn_rows[:, ffn_pad:].astype(WIDE).reshape(-1, 2, ffn_pad)[:, :, :ffn_cols],
         conv_sum.reshape(9, 2, ffn_pad)[:, :, :ffn_cols],

time: 498 us -> 472 us (0.948)
  the two profiles are of different devices: /device:TPU:0 before, /device:TPU:8 now
where the time goes in v4:
time: 472 us; the launch traced here: 463 us
  Pallas kernels  157 us (33%)
  waiting for transfers between devices  154 us (33%)
  starting transfers between devices  71.2 us (15%)
  local copies, waits for them, and re-layouts  32.4 us (7%)
  between operations  18.7 us (4%)
  matrix products  14.8 us (3%)
  other arithmetic  14.4 us (3%)
    pallas_call x15, Pallas kernels, call(): pl.pallas_call(body, out_shape=shapes, grid_spec=pltpu.PrefetchScalarGrid...  157 us
    ppermute x18, waiting for transfers between devices, from_behind(): lax.ppermute(block, 'tp', [(k, (k + step) % count) for k in range(count)])  68.5 us
    reduce_scatter x3, waiting for transfers between devices, sum_rows(): lax.psum_scatter(grad.astype(LOW), 'seq', scatter_dimension=0, tiled=True)  42.1 us
    all_to_all x6, starting transfers between devices, exchanged(): return lax.all_to_all(blocks, 'tp', 0, 0, tiled=True)  31.4 us
    ppermute x18, starting transfers between devices, from_behind(): lax.ppermute(block, 'tp', [(k, (k + step) % count) for k in range(count)])  29.1 us
    all_to_all x6, waiting for transfers between devices, exchanged(): return lax.all_to_all(blocks, 'tp', 0, 0, tiled=True)  26.7 us
    unnamed x101, local copies, waits for them, and re-layouts  12.5 us
    dot_general x3, matrix products, dot(): return jnp.dot(left, right, preferred_element_type=WIDE)  11.2 us
  transfers between devices with their start and end apart: 48, of which 26 were waited for; matrix products, arithmetic and copies ran while one was open for 10% of the time, Pallas kernels for 25%

profile of v4, /device:TPU:8, one launch (start us, length us, event | category | flops | bytes accessed | tf_op | source)
XLA Modules:
  0.0 463.3 jit_solution(1599587504936072020)
XLA Ops:
  7.2 2.5 eighth.1
  12.3 2.0 collective-permute-start.4
  16.4 5.0 %all-to-all-start = ((bf16[4,304,576]{2,1,0:T(8,128)(2,1)}), bf16[4,304,576]{2,1,0:T(8,128)(2,1)S(1)}, u32[]{:S(2)}, u32[]{:S(2)}) async-start(bf16[4,304,576]{2,1,0:T(8,128)(2,1)} %broadcast_in_dim.63), calls=%async_computation | async-start | bytes 3112960 | tf_op jit(solution)/shard_map/all_to_all | solution.py:37
  29.3 11.9 %self_project.1 = (bf16[640,1152]{1,0:T(8,128)(2,1)}, f32[640,576]{1,0:T(8,128)}, bf16[640,288]{1,0:T(8,128)(2,1)}, bf16[640,288]{1,0:T(8,128)(2,1)}, bf16[640,2...) custom-call(s32[10]{0:T(128)} %stack.65.table, bf16[640,1152]{1,0:T(8,128)(2,1)} %x.12, ...), custom_call_target="tpu_custom_call" | custom-call | bytes 78704 | tf_op jit(solution)/shard_map/self_project/pallas_call | solution.py:61
  44.0 2.5 pad_maximum_fusion.refs_0_
  50.7 6.8 %self_attend.1 = (bf16[640,288]{1,0:T(8,128)(2,1)}, f32[640,288]{1,0:T(8,128)}, f32[640,288]{1,0:T(8,128)}) custom-call(s32[10]{0:T(128)} %stack.65.table, bf16[640,288]{1,0:T(8,128)(2,1)} %get-tuple-element.86.q, f32[288,128]{1,0:T(8,128)} %get-tuple-element.191.own_fold, f32[288,128]{1,0:T(8,128)} %get-tuple-element.190.other_fold), custom_call_target="tpu_custom_call" | custom-call | bytes 25067 | tf_op jit(solution)/shard_map/self_attend/pallas_call | solution.py:61
  57.6 2.9 fusion.8.grad_hidden
  60.5 2.1 pad.17
  62.6 4.5 all-to-all-done.refs_8_.kv_own
  67.1 7.9 %all-to-all-start.1 = ((bf16[4,160,288]{2,1,0:T(8,128)(2,1)}), bf16[4,160,288]{2,1,0:T(8,128)(2,1)}, u32[]{:S(2)}, u32[]{:S(2)}) async-start(bf16[4,160,288]{2,1,0:T(8,128)(2,1)} %bitcast.143), calls=%async_computation.1 | async-start | bytes 983040 | tf_op jit(solution)/shard_map/all_to_all | solution.py:37
  75.2 8.9 %collective-permute-done.7.refs_4_ = bf16[3,112,1152]{2,1,0:T(8,128)(2,1)} collective-permute-done((bf16[3,112,1152]{2,1,0:T(8,128)(2,1)}, bf16[3,112,1152]{2,1,0:T(8,128)(2,1)}, u32[]{:S(2)}, u32[]{:S(2)}) %collective-permute-start.7) | collective-permute-done | bytes 774176 | tf_op jit(solution)/shard_map/ppermute | solution.py:752
  84.1 2.5 all-to-all-done.1.att
  93.4 20.9 %middle.1 = (f32[160,1152]{1,0:T(8,128)}, bf16[160,1152]{1,0:T(8,128)(2,1)}, bf16[4,160,288]{2,1,0:T(8,128)(2,1)}, f32[16,160,304]{2,1,0:T(8,128)}, bf16[4,160,2...) custom-call(s32[10]{0:T(128)} %stack.65.table, ...), custom_call_target="tpu_custom_call" | custom-call | bytes 251392 | tf_op jit(solution)/shard_map/middle/pallas_call | solution.py:61
  115.6 4.2 collective-permute-start.14
  120.0 7.1 %collective-permute-done.13.refs_1_ = bf16[160,1152]{1,0:T(8,128)(2,1)S(1)} collective-permute-done((bf16[160,1152]{1,0:T(8,128)(2,1)}, bf16[160,1152]{1,0:T(8,128)(2,1)S(1)}, u32[]{:S(2)}, u32[]{:S(2)}) %collective-permute-start.13) | collective-permute-done | bytes 368672 | tf_op jit(solution)/shard_map/ppermute | solution.py:33
  127.0 20.7 %collective-permute-done.14.refs_2_ = bf16[160,1152]{1,0:T(8,128)(2,1)S(1)} collective-permute-done((bf16[160,1152]{1,0:T(8,128)(2,1)}, bf16[160,1152]{1,0:T(8,128)(2,1)S(1)}, u32[]{:S(2)}, u32[]{:S(2)}) %collective-permute-start.14) | collective-permute-done | bytes 368672 | tf_op jit(solution)/shard_map/ppermute | solution.py:33
  147.7 3.8 collective-permute-done.15.refs_3_
  152.3 8.5 %up_project.1 = (f32[640,1536]{1,0:T(8,128)}, bf16[640,1536]{1,0:T(8,128)(2,1)}, bf16[640,1152]{1,0:T(8,128)(2,1)}) custom-call(s32[10]{0:T(128)} %stack.65.table, bf16[160,1152]{1,0:T(8,128)(2,1)} %get-tuple-element.98.refs_0_, bf16[160,1152]{1,0:T(8,128)(2,1)} %copy-done.37, bf16[160,1152]{1,0:T(8,128)(2,1)} %copy-done.38, bf16[160,1152]{1,0:T(8,128)(2,1)} %copy-done.39, ...), custom_call_target="tpu_custom_call" | custom-call | bytes 123863 | tf_op jit(solution)/shard_map/up_project/pallas_call | solution.py:61
  163.8 9.4 %mix.1 = (bf16[640,768]{1,0:T(8,128)(2,1)}, bf16[2,640,768]{2,1,0:T(8,128)(2,1)}) custom-call(s32[10]{0:T(128)} %stack.65.table, bf16[640,1536]{1,0:T(8,128)(2,1)} %get-tuple-element.99.value.gate.activated, bf16[640,1536]{1,0:T(8,128)(2,1)} %get-tuple-element.99.value.gate.activated, bf16[32,1536]{1,0:T(8,128)(2,1)} %copy-done.19, ...), custom_call_target="tpu_custom_call" | custom-call | bytes 92405 | tf_op jit(solution)/shard_map/mix/pallas_call | solution.py:61
  173.1 3.8 convolution_convert_fusion.2
  176.9 3.5 all-to-all-start.2
  183.5 14.8 %mix_back.1 = (bf16[640,1536]{1,0:T(8,128)(2,1)}, f32[16,1536]{1,0:T(8,128)}) custom-call(s32[10]{0:T(128)} %stack.65.table, bf16[2,640,768]{2,1,0:T(8,128)(2,1)} %get-tuple-element.103.grads, bf16[2,32,768]{2,1,0:T(8,128)(2,1)} %copy-done.40, bf16[640,1536]{1,0:T(8,128)(2,1)} %get-tuple-element.99.value.gate.activated, bf16[32,1536]{1,0:T(8,128)(2,1)} %copy-done.19, ...), custom_call_target="tpu_custom_call" | custom-call | bytes 102236 | tf_op jit(solution)/shard_map/mix_back/pallas_call | solution.py:61
  198.3 4.2 convolution_convert_fusion.1
  205.7 2.0 collective-permute-start.20
  207.7 5.9 %all-to-all-done.2.branches = bf16[4,160,1152]{2,1,0:T(8,128)(2,1)S(1)} async-done(((bf16[4,160,1152]{2,1,0:T(8,128)(2,1)}), bf16[4,160,1152]{2,1,0:T(8,128)(2,1)S(1)}, u32[]{:S(2)}, u32[]{:S(2)}) %all-to-all-start.2) | async-done | bytes 1474592 | tf_op jit(solution)/shard_map/all_to_all | solution.py:37
  214.7 3.7 output.1
  218.4 9.4 %ffn_parts.1 = bf16[1152,2304]{1,0:T(8,128)(2,1)} custom-call(s32[10]{0:T(128)} %stack.65.table, bf16[640,1152]{1,0:T(8,128)(2,1)} %copy-done.7, bf16[640,768]{1,0:T(8,128)(2,1)} %get-tuple-element.108.hidden, bf16[640,1152]{1,0:T(8,128)(2,1)} %get-tuple-element.109.normed, bf16[640,1536]{1,0:T(8,128)(2,1)} %get-tuple-element.106.grad_up), custom_call_target="tpu_custom_call" | custom-call | bytes 112066 | tf_op jit(solution)/shard_map/ffn_parts/pallas_call | solution.py:61
  227.8 9.4 %collective-permute-done.18.grad_1 = bf16[160,1152]{1,0:T(8,128)(2,1)S(1)} collective-permute-done((bf16[160,1152]{1,0:T(8,128)(2,1)}, bf16[160,1152]{1,0:T(8,128)(2,1)S(1)}, u32[]{:S(2)}, u32[]{:S(2)}) %collective-permute-start.18) | collective-permute-done | bytes 368672 | tf_op jit(solution)/shard_map/ppermute | solution.py:33
  237.1 7.4 %collective-permute-done.19.grad_2 = bf16[160,1152]{1,0:T(8,128)(2,1)} collective-permute-done((bf16[160,1152]{1,0:T(8,128)(2,1)}, bf16[160,1152]{1,0:T(8,128)(2,1)}, u32[]{:S(2)}, u32[]{:S(2)}) %collective-permute-start.19) | collective-permute-done | bytes 368672 | tf_op jit(solution)/shard_map/ppermute | solution.py:33
  245.8 4.1 collective-permute-start.22
  250.3 25.9 %middle_back.1 = (bf16[160,1152]{1,0:T(8,128)(2,1)}, bf16[4,160,288]{2,1,0:T(8,128)(2,1)}, bf16[160,1152]{1,0:T(8,128)(2,1)}, bf16[4,160,288]{2,1,0:T(8,128)(2,1...) custom-call(s32[10]{0:T(128)} %stack.65.table, ...), custom_call_target="tpu_custom_call" | custom-call | bytes 251023 | tf_op jit(solution)/shard_map/middle_back/pallas_call | solution.py:61
  276.9 3.3 collective-permute-done.23
  281.1 3.5 all-to-all-start.3
  285.8 10.1 %square_parts.1 = (bf16[1152,3584]{1,0:T(8,128)(2,1)}, bf16[4,304,576]{2,1,0:T(8,128)(2,1)}) custom-call(s32[10]{0:T(128)} %stack.65.table, bf16[160,1152]{1,0:T(8,128)(2,1)} %get-tuple-element.117.dyc, bf16[4,160,288]{2,1,0:T(8,128)(2,1)} %get-tuple-element.118.text, bf16[160,1152]{1,0:T(8,128)(2,1)} %get-tuple-element.119.x1, ...), custom_call_target="tpu_custom_call" | custom-call | bytes 146718 | tf_op jit(solution)/shard_map/square_parts/pallas_call | solution.py:61
  297.0 6.1 %all-to-all-start.4 = ((bf16[4,304,576]{2,1,0:T(8,128)(2,1)}), bf16[4,304,576]{2,1,0:T(8,128)(2,1)S(1)}, u32[]{:S(2)}, u32[]{:S(2)}) async-start(bf16[4,304,576]{2,1,0:T(8,128)(2,1)} %get-tuple-element.128), calls=%async_computation.5 | async-start | bytes 3112960 | tf_op jit(solution)/shard_map/all_to_all | solution.py:37
  303.6 11.9 %self_back.1 = (f32[640,288]{1,0:T(8,128)}, f32[288,128]{1,0:T(8,128)}, f32[288,128]{1,0:T(8,128)}) custom-call(s32[10]{0:T(128)} %stack.65.table, bf16[4,160,288]{2,1,0:T(8,128)(2,1)} %copy-done.13, bf16[640,288]{1,0:T(8,128)(2,1)} %get-tuple-element.86.q, f32[640,288]{1,0:T(8,128)} %get-tuple-element.131.wide_out, ...), custom_call_target="tpu_custom_call" | custom-call | bytes 35389 | tf_op jit(solution)/shard_map/self_back/pallas_call | solution.py:61
  320.1 9.2 %self_project_back.1.grad_projected = bf16[640,864]{1,0:T(8,128)(2,1)} custom-call(s32[10]{0:T(128)} %stack.65.table, f32[640,288]{1,0:T(8,128)} %get-tuple-element.133.grad_q, bf16[640,288]{1,0:T(8,128)(2,1)} %get-tuple-element.134.k, bf16[640,288]{1,0:T(8,128)(2,1)} %get-tuple-element.135.v, f32[640,576]{1,0:T(8,128)} %get-tuple-element.136.raw, ...), custom_call_target="tpu_custom_call" | custom-call | bytes 43499 | tf_op jit(solution)/shard_map/self_project_back/pallas_call | solution.py:61
  329.3 3.1 convolution_convert_fusion
  340.0 8.0 %late_parts.1 = bf16[1152,1440]{1,0:T(8,128)(2,1)} custom-call(s32[10]{0:T(128)} %stack.65.table, bf16[640,1152]{1,0:T(8,128)(2,1)} %get-tuple-element.139.normed, bf16[640,864]{1,0:T(8,128)(2,1)} %self_project_back.1.grad_projected, bf16[304,1152]{1,0:T(8,128)(2,1)} %pad.16.text, bf16[4,304,576]{2,1,0:T(8,128)(2,1)} %copy-done.6), custom_call_target="tpu_custom_call" | custom-call | bytes 79994 | tf_op jit(solution)/shard_map/late_parts/pallas_call | solution.py:61
  348.0 30.4 %reduce-scatter.6.cloned.1.call-done = bf16[144,3584]{1,0:T(8,128)(2,1)} async-done(((bf16[1152,3584]{1,0:T(8,128)(2,1)}), bf16[144,3584]{1,0:T(8,128)(2,1)}) %reduce-scatter.6.cloned.1.call-update) | async-done | bytes 1032208 | tf_op jit(solution)/shard_map/reduce_scatter | solution.py:829
  384.4 5.3 %all-to-all-start.5 = ((bf16[4,144,896]{2,1,0:T(8,128)(2,1)}), bf16[4,144,896]{2,1,0:T(8,128)(2,1)S(1)}, u32[]{:S(2)}, u32[]{:S(2)}) async-start(bf16[4,144,896]{2,1,0:T(8,128)(2,1)} %bitcast.109), calls=%async_computation.7 | async-start | bytes 2064384 | tf_op jit(solution)/shard_map/all_to_all | solution.py:37
  391.6 4.4 first_norm_back.1
  398.6 13.6 %all-to-all-done.5 = bf16[4,144,896]{2,1,0:T(8,128)(2,1)S(1)} async-done(((bf16[4,144,896]{2,1,0:T(8,128)(2,1)}), bf16[4,144,896]{2,1,0:T(8,128)(2,1)S(1)}, u32[]{:S(2)}, u32[]{:S(2)}) %all-to-all-start.5) | async-done | bytes 1032224 | tf_op jit(solution)/shard_map/all_to_all | solution.py:37
  413.6 4.2 collective-permute-start.30
  418.9 11.1 %reduce-scatter.8.cloned.1.call-done = bf16[144,1440]{1,0:T(8,128)(2,1)} async-done(((bf16[1152,1440]{1,0:T(8,128)(2,1)}), bf16[144,1440]{1,0:T(8,128)(2,1)}) %reduce-scatter.8.cloned.1.call-update) | async-done | bytes 414736 | tf_op jit(solution)/shard_map/reduce_scatter | solution.py:829
  433.6 10.9 %collective-permute-done.30 = bf16[160,1152]{1,0:T(8,128)(2,1)S(1)} collective-permute-done((bf16[160,1152]{1,0:T(8,128)(2,1)S(1)}, bf16[160,1152]{1,0:T(8,128)(2,1)S(1)}, u32[]{:S(2)}, u32[]{:S(2)}) %collective-permute-start.30) | collective-permute-done | bytes 368672 | tf_op jit(solution)/shard_map/ppermute | solution.py:33
  444.4 3.9 collective-permute-done.31
  449.2 2.6 collective-permute-start.35
  (233 shorter events, 74.7 us)
Async XLA Ops:
  9.7 34.1 %collective-permute-start.2 = (bf16[112,1152]{1,0:T(8,128)(2,1)}, bf16[112,1152]{1,0:T(8,128)(2,1)S(1)}, u32[]{:S(2)}, u32[]{:S(2)}) collective-permute-start(bf16[112,1152]{1,0:T(8,128)(2,1)} %eighth.1), channel_id=1, source_target_pairs={{0,1},{1,2},{2,3},{3,0},{4,5},{5,6},{6,7},{7,4},{8,9},{9,10},{10,1... | collective-permute-start | bytes 774152 | tf_op jit(solution)/shard_map/ppermute | solution.py:33
  11.3 32.5 %collective-permute-start.3 = (bf16[112,1152]{1,0:T(8,128)(2,1)}, bf16[112,1152]{1,0:T(8,128)(2,1)}, u32[]{:S(2)}, u32[]{:S(2)}) collective-permute-start(bf16[112,1152]{1,0:T(8,128)(2,1)} %eighth.1), channel_id=1, source_target_pairs={{0,2},{1,3},{2,0},{3,1},{4,6},{5,7},{6,4},{7,5},{8,10},{9,11},{10,... | collective-permute-start | bytes 774152 | tf_op jit(solution)/shard_map/ppermute | solution.py:33
  12.3 31.6 %collective-permute-start.4 = (bf16[112,1152]{1,0:T(8,128)(2,1)}, bf16[112,1152]{1,0:T(8,128)(2,1)}, u32[]{:S(2)}, u32[]{:S(2)}) collective-permute-start(bf16[112,1152]{1,0:T(8,128)(2,1)} %eighth.1), channel_id=1, source_target_pairs={{0,3},{1,0},{2,1},{3,2},{4,7},{5,4},{6,5},{7,6},{8,11},{9,8},{10,9... | collective-permute-start | bytes 774152 | tf_op jit(solution)/shard_map/ppermute | solution.py:33
  14.3 14.4 %collective-permute-start = (bf16[6,1152]{1,0:T(8,128)(2,1)S(1)}, bf16[6,1152]{1,0:T(8,128)(2,1)S(1)}, u32[]{:S(2)}, u32[]{:S(2)}) collective-permute-start(bf16[6,1152]{1,0:T(8,128)(2,1)S(1)} %bitcast.150), channel_id=1, source_target_pairs={{0,4},{4,0},{8,12},{12,8},{16,20},{20,16},{24,28},{28,24},{1,5},{5... | collective-permute-start | bytes 41480 | tf_op jit(solution)/shard_map/ppermute | solution.py:28
  16.4 50.6 %all-to-all-start = ((bf16[4,304,576]{2,1,0:T(8,128)(2,1)}), bf16[4,304,576]{2,1,0:T(8,128)(2,1)S(1)}, u32[]{:S(2)}, u32[]{:S(2)}) async-start(bf16[4,304,576]{2,1,0:T(8,128)(2,1)} %broadcast_in_dim.63), calls=%async_computation | async-start | bytes 3112960 | tf_op jit(solution)/shard_map/all_to_all | solution.py:37
  42.3 7.7 %collective-permute-start.1 = (f32[2,288,128]{2,1,0:T(8,128)S(1)}, f32[2,288,128]{2,1,0:T(8,128)S(1)}, u32[]{:S(2)}, u32[]{:S(2)}) collective-permute-start(f32[2,288,128]{2,1,0:T(8,128)S(1)} %pad_maximum_fusion.1), channel_id=1, source_target_pairs={{0,4},{4,0},{8,12},{12,8},{16,20},{20,16},{24,28},{28,24},{1,5},{5... | collective-permute-start | bytes 884744 | tf_op jit(solution)/shard_map/ppermute | solution.py:28
  46.5 28.7 %collective-permute-start.6 = (bf16[3,112,1152]{2,1,0:T(8,128)(2,1)}, bf16[3,112,1152]{2,1,0:T(8,128)(2,1)}, u32[]{:S(2)}, u32[]{:S(2)}) collective-permute-start(bf16[3,112,1152]{2,1,0:T(8,128)(2,1)} %pad_maximum_fusion.refs_0_), channel_id=1, source_target_pairs={{0,8},{4,12},{8,0},{12,4},{16,24},{20,28},{24,16},{28,20},{1,9},{5... | collective-permute-start | bytes 2322440 | tf_op jit(solution)/shard_map/ppermute | solution.py:752
  48.0 36.1 %collective-permute-start.7 = (bf16[3,112,1152]{2,1,0:T(8,128)(2,1)}, bf16[3,112,1152]{2,1,0:T(8,128)(2,1)}, u32[]{:S(2)}, u32[]{:S(2)}) collective-permute-start(bf16[3,112,1152]{2,1,0:T(8,128)(2,1)} %pad_maximum_fusion.refs_0_), channel_id=1, source_target_pairs={{0,16},{4,20},{8,24},{12,28},{16,0},{20,4},{24,8},{28,12},{1,17},{... | collective-permute-start | bytes 2322440 | tf_op jit(solution)/shard_map/ppermute | solution.py:752
  49.5 34.6 %collective-permute-start.8 = (bf16[3,112,1152]{2,1,0:T(8,128)(2,1)}, bf16[3,112,1152]{2,1,0:T(8,128)(2,1)}, u32[]{:S(2)}, u32[]{:S(2)}) collective-permute-start(bf16[3,112,1152]{2,1,0:T(8,128)(2,1)} %pad_maximum_fusion.refs_0_), channel_id=1, source_target_pairs={{0,24},{4,28},{8,16},{12,20},{16,8},{20,12},{24,0},{28,4},{1,25},{... | collective-permute-start | bytes 2322440 | tf_op jit(solution)/shard_map/ppermute | solution.py:752
  67.1 24.3 %collective-permute-start.12 = (bf16[4,304,576]{2,1,0:T(8,128)(2,1)S(1)}, bf16[4,304,576]{2,1,0:T(8,128)(2,1)S(1)}, u32[]{:S(2)}, u32[]{:S(2)}) collective-permute-start(bf16[4,304,576]{2,1,0:T(8,128)(2,1)S(1)} %all-to-all-done.refs_8_.kv_own), channel_id=1, source_target_pairs={{0,4},{4,0},{8,12},{12,8},{16,20},{20,16},{24,28},{28,24},{1,5},{5... | collective-permute-start | bytes 4202504 | tf_op jit(solution)/shard_map/ppermute | solution.py:28
  67.1 19.6 %all-to-all-start.1 = ((bf16[4,160,288]{2,1,0:T(8,128)(2,1)}), bf16[4,160,288]{2,1,0:T(8,128)(2,1)}, u32[]{:S(2)}, u32[]{:S(2)}) async-start(bf16[4,160,288]{2,1,0:T(8,128)(2,1)} %bitcast.143), calls=%async_computation.1 | async-start | bytes 983040 | tf_op jit(solution)/shard_map/all_to_all | solution.py:37
  75.0 12.1 %collective-permute-start.5 = (bf16[3,112,1152]{2,1,0:T(8,128)(2,1)}, bf16[3,112,1152]{2,1,0:T(8,128)(2,1)}, u32[]{:S(2)}, u32[]{:S(2)}) collective-permute-start(bf16[3,112,1152]{2,1,0:T(8,128)(2,1)} %pad_maximum_fusion.refs_0_), channel_id=1, source_target_pairs={{0,4},{4,0},{8,12},{12,8},{16,20},{20,16},{24,28},{28,24},{1,5},{5... | collective-permute-start | bytes 2322440 | tf_op jit(solution)/shard_map/ppermute | solution.py:28
  86.6 2.5 collective-permute-start.10
  86.6 3.6 collective-permute-start.11
  87.1 4.2 collective-permute-start.9
  114.3 12.7 %collective-permute-start.13 = (bf16[160,1152]{1,0:T(8,128)(2,1)}, bf16[160,1152]{1,0:T(8,128)(2,1)S(1)}, u32[]{:S(2)}, u32[]{:S(2)}) collective-permute-start(bf16[160,1152]{1,0:T(8,128)(2,1)} %get-tuple-element.98.refs_0_), channel_id=1, source_target_pairs={{0,1},{1,2},{2,3},{3,0},{4,5},{5,6},{6,7},{7,4},{8,9},{9,10},{10,1... | collective-permute-start | bytes 1105928 | tf_op jit(solution)/shard_map/ppermute | solution.py:33
  115.6 32.2 %collective-permute-start.14 = (bf16[160,1152]{1,0:T(8,128)(2,1)}, bf16[160,1152]{1,0:T(8,128)(2,1)S(1)}, u32[]{:S(2)}, u32[]{:S(2)}) collective-permute-start(bf16[160,1152]{1,0:T(8,128)(2,1)} %get-tuple-element.98.refs_0_), channel_id=1, source_target_pairs={{0,2},{1,3},{2,0},{3,1},{4,6},{5,7},{6,4},{7,5},{8,10},{9,11},{10,... | collective-permute-start | bytes 1105928 | tf_op jit(solution)/shard_map/ppermute | solution.py:33
  119.8 31.7 %collective-permute-start.15 = (bf16[160,1152]{1,0:T(8,128)(2,1)}, bf16[160,1152]{1,0:T(8,128)(2,1)S(1)}, u32[]{:S(2)}, u32[]{:S(2)}) collective-permute-start(bf16[160,1152]{1,0:T(8,128)(2,1)} %get-tuple-element.98.refs_0_), channel_id=1, source_target_pairs={{0,3},{1,0},{2,1},{3,2},{4,7},{5,4},{6,5},{7,6},{8,11},{9,8},{10,9... | collective-permute-start | bytes 1105928 | tf_op jit(solution)/shard_map/ppermute | solution.py:33
  161.8 1.4 collective-permute-start.16
  176.9 36.6 %all-to-all-start.2 = ((bf16[4,160,1152]{2,1,0:T(8,128)(2,1)}), bf16[4,160,1152]{2,1,0:T(8,128)(2,1)S(1)}, u32[]{:S(2)}, u32[]{:S(2)}) async-start(bf16[4,160,1152]{2,1,0:T(8,128)(2,1)} %bitcast.32), calls=%async_computation.2 | async-start | bytes 2949120 | tf_op jit(solution)/shard_map/all_to_all | solution.py:37
  180.5 123.1 %reduce-scatter.4.cloned.1.call-start = ((), (), s32[]{:S(2)}) async-start(), calls=%async_computation.9 | async-start | bytes 5971968 | tf_op jit(solution)/shard_map/reduce_scatter | solution.py:829
  181.5 1.4 collective-permute-start.17
  203.6 33.5 %collective-permute-start.18 = (bf16[160,1152]{1,0:T(8,128)(2,1)}, bf16[160,1152]{1,0:T(8,128)(2,1)S(1)}, u32[]{:S(2)}, u32[]{:S(2)}) collective-permute-start(bf16[160,1152]{1,0:T(8,128)(2,1)} %get-tuple-element.184), channel_id=1, source_target_pairs={{0,1},{1,2},{2,3},{3,0},{4,5},{5,6},{6,7},{7,4},{8,9},{9,10},{10,1... | collective-permute-start | bytes 1105928 | tf_op jit(solution)/shard_map/ppermute | solution.py:33
  204.8 39.8 %collective-permute-start.19 = (bf16[160,1152]{1,0:T(8,128)(2,1)}, bf16[160,1152]{1,0:T(8,128)(2,1)}, u32[]{:S(2)}, u32[]{:S(2)}) collective-permute-start(bf16[160,1152]{1,0:T(8,128)(2,1)} %get-tuple-element.183), channel_id=1, source_target_pairs={{0,2},{1,3},{2,0},{3,1},{4,6},{5,7},{6,4},{7,5},{8,10},{9,11},{10,... | collective-permute-start | bytes 1105928 | tf_op jit(solution)/shard_map/ppermute | solution.py:33
  205.7 40.0 %collective-permute-start.20 = (bf16[160,1152]{1,0:T(8,128)(2,1)}, bf16[160,1152]{1,0:T(8,128)(2,1)}, u32[]{:S(2)}, u32[]{:S(2)}) collective-permute-start(bf16[160,1152]{1,0:T(8,128)(2,1)} %get-tuple-element.182), channel_id=1, source_target_pairs={{0,3},{1,0},{2,1},{3,2},{4,7},{5,4},{6,5},{7,6},{8,11},{9,8},{10,9... | collective-permute-start | bytes 1105928 | tf_op jit(solution)/shard_map/ppermute | solution.py:33
  245.7 30.4 %collective-permute-start.21 = (bf16[160,1152]{1,0:T(8,128)(2,1)S(1)}, bf16[160,1152]{1,0:T(8,128)(2,1)S(1)}, u32[]{:S(2)}, u32[]{:S(2)}) collective-permute-start(bf16[160,1152]{1,0:T(8,128)(2,1)S(1)} %copy-done.28), channel_id=1, source_target_pairs={{0,1},{1,2},{2,3},{3,0},{4,5},{5,6},{6,7},{7,4},{8,9},{9,10},{10,1... | collective-permute-start | bytes 1105928 | tf_op jit(solution)/shard_map/ppermute | solution.py:33
  245.8 31.1 %collective-permute-start.22 = (bf16[160,1152]{1,0:T(8,128)(2,1)S(1)}, bf16[160,1152]{1,0:T(8,128)(2,1)S(1)}, u32[]{:S(2)}, u32[]{:S(2)}) collective-permute-start(bf16[160,1152]{1,0:T(8,128)(2,1)S(1)} %copy-done.28), channel_id=1, source_target_pairs={{0,2},{1,3},{2,0},{3,1},{4,6},{5,7},{6,4},{7,5},{8,10},{9,11},{10,... | collective-permute-start | bytes 1105928 | tf_op jit(solution)/shard_map/ppermute | solution.py:33
  249.9 30.3 %collective-permute-start.23 = (bf16[160,1152]{1,0:T(8,128)(2,1)S(1)}, bf16[160,1152]{1,0:T(8,128)(2,1)S(1)}, u32[]{:S(2)}, u32[]{:S(2)}) collective-permute-start(bf16[160,1152]{1,0:T(8,128)(2,1)S(1)} %copy-done.28), channel_id=1, source_target_pairs={{0,3},{1,0},{2,1},{3,2},{4,7},{5,4},{6,5},{7,6},{8,11},{9,8},{10,9... | collective-permute-start | bytes 1105928 | tf_op jit(solution)/shard_map/ppermute | solution.py:33
  281.0 3.6 collective-permute-start.24
  281.1 15.1 %all-to-all-start.3 = ((bf16[4,160,288]{2,1,0:T(8,128)(2,1)}), bf16[4,160,288]{2,1,0:T(8,128)(2,1)S(1)}, u32[]{:S(2)}, u32[]{:S(2)}) async-start(bf16[4,160,288]{2,1,0:T(8,128)(2,1)} %get-tuple-element.116), calls=%async_computation.3 | async-start | bytes 983040 | tf_op jit(solution)/shard_map/all_to_all | solution.py:37
  284.6 93.8 %reduce-scatter.6.cloned.1.call-start = ((), (), s32[]{:S(2)}) async-start(), calls=%async_computation.10 | async-start | bytes 9289728 | tf_op jit(solution)/shard_map/reduce_scatter | solution.py:829
  297.0 41.8 %all-to-all-start.4 = ((bf16[4,304,576]{2,1,0:T(8,128)(2,1)}), bf16[4,304,576]{2,1,0:T(8,128)(2,1)S(1)}, u32[]{:S(2)}, u32[]{:S(2)}) async-start(bf16[4,304,576]{2,1,0:T(8,128)(2,1)} %get-tuple-element.128), calls=%async_computation.5 | async-start | bytes 3112960 | tf_op jit(solution)/shard_map/all_to_all | solution.py:37
  303.1 126.9 %reduce-scatter.8.cloned.1.call-start = ((), (), s32[]{:S(2)}) async-start(), calls=%async_computation.11 | async-start | bytes 3981312 | tf_op jit(solution)/shard_map/reduce_scatter | solution.py:829
  316.6 1.7 collective-permute-start.25
  333.4 45.0 %collective-permute-start.26 = (bf16[160,1152]{1,0:T(8,128)(2,1)}, bf16[160,1152]{1,0:T(8,128)(2,1)}, u32[]{:S(2)}, u32[]{:S(2)}) collective-permute-start(bf16[160,1152]{1,0:T(8,128)(2,1)} %get-tuple-element.181), channel_id=1, source_target_pairs={{0,1},{1,2},{2,3},{3,0},{4,5},{5,6},{6,7},{7,4},{8,9},{9,10},{10,1... | collective-permute-start | bytes 1105928 | tf_op jit(solution)/shard_map/ppermute | solution.py:33
  334.8 43.6 %collective-permute-start.27 = (bf16[160,1152]{1,0:T(8,128)(2,1)}, bf16[160,1152]{1,0:T(8,128)(2,1)}, u32[]{:S(2)}, u32[]{:S(2)}) collective-permute-start(bf16[160,1152]{1,0:T(8,128)(2,1)} %get-tuple-element.180), channel_id=1, source_target_pairs={{0,2},{1,3},{2,0},{3,1},{4,6},{5,7},{6,4},{7,5},{8,10},{9,11},{10,... | collective-permute-start | bytes 1105928 | tf_op jit(solution)/shard_map/ppermute | solution.py:33
  336.3 42.1 %collective-permute-start.28 = (bf16[160,1152]{1,0:T(8,128)(2,1)S(1)}, bf16[160,1152]{1,0:T(8,128)(2,1)}, u32[]{:S(2)}, u32[]{:S(2)}) collective-permute-start(bf16[160,1152]{1,0:T(8,128)(2,1)S(1)} %get-tuple-element.179), channel_id=1, source_target_pairs={{0,3},{1,0},{2,1},{3,2},{4,7},{5,4},{6,5},{7,6},{8,11},{9,8},{10,9... | collective-permute-start | bytes 1105928 | tf_op jit(solution)/shard_map/ppermute | solution.py:33
  380.5 1.4 collective-permute-start.36
  381.9 9.0 %collective-permute-start.37 = (f32[9,1536]{1,0:T(8,128)S(1)}, f32[9,1536]{1,0:T(8,128)S(1)}, u32[]{:S(2)}, u32[]{:S(2)}) collective-permute-start(f32[9,1536]{1,0:T(8,128)S(1)} %add.194), channel_id=1, source_target_pairs={{0,8},{4,12},{8,0},{12,4},{16,24},{20,28},{24,16},{28,20},{1,9},{5... | collective-permute-start | bytes 165896 | tf_op jit(solution)/shard_map/ppermute | solution.py:28
  384.4 27.8 %all-to-all-start.5 = ((bf16[4,144,896]{2,1,0:T(8,128)(2,1)}), bf16[4,144,896]{2,1,0:T(8,128)(2,1)S(1)}, u32[]{:S(2)}, u32[]{:S(2)}) async-start(bf16[4,144,896]{2,1,0:T(8,128)(2,1)} %bitcast.109), calls=%async_computation.7 | async-start | bytes 2064384 | tf_op jit(solution)/shard_map/all_to_all | solution.py:37
  390.9 7.0 %collective-permute-start.38 = (f32[9,1536]{1,0:T(8,128)S(1)}, f32[9,1536]{1,0:T(8,128)S(1)}, u32[]{:S(2)}, u32[]{:S(2)}) collective-permute-start(f32[9,1536]{1,0:T(8,128)S(1)} %add.195), channel_id=1, source_target_pairs={{0,16},{4,20},{8,24},{12,28},{16,0},{20,4},{24,8},{28,12},{1,17},{... | collective-permute-start | bytes 165896 | tf_op jit(solution)/shard_map/ppermute | solution.py:28
  397.0 1.6 collective-permute-start.32
  412.1 21.4 %collective-permute-start.29 = (bf16[160,1152]{1,0:T(8,128)(2,1)S(1)}, bf16[160,1152]{1,0:T(8,128)(2,1)S(1)}, u32[]{:S(2)}, u32[]{:S(2)}) collective-permute-start(bf16[160,1152]{1,0:T(8,128)(2,1)S(1)} %copy-done.36), channel_id=1, source_target_pairs={{0,1},{1,2},{2,3},{3,0},{4,5},{5,6},{6,7},{7,4},{8,9},{9,10},{10,1... | collective-permute-start | bytes 1105928 | tf_op jit(solution)/shard_map/ppermute | solution.py:33
  413.6 30.8 %collective-permute-start.30 = (bf16[160,1152]{1,0:T(8,128)(2,1)S(1)}, bf16[160,1152]{1,0:T(8,128)(2,1)S(1)}, u32[]{:S(2)}, u32[]{:S(2)}) collective-permute-start(bf16[160,1152]{1,0:T(8,128)(2,1)S(1)} %copy-done.36), channel_id=1, source_target_pairs={{0,2},{1,3},{2,0},{3,1},{4,6},{5,7},{6,4},{7,5},{8,10},{9,11},{10,... | collective-permute-start | bytes 1105928 | tf_op jit(solution)/shard_map/ppermute | solution.py:33
  417.8 30.5 %collective-permute-start.31 = (bf16[160,1152]{1,0:T(8,128)(2,1)S(1)}, bf16[160,1152]{1,0:T(8,128)(2,1)}, u32[]{:S(2)}, u32[]{:S(2)}) collective-permute-start(bf16[160,1152]{1,0:T(8,128)(2,1)S(1)} %copy-done.36), channel_id=1, source_target_pairs={{0,3},{1,0},{2,1},{3,2},{4,7},{5,4},{6,5},{7,6},{8,11},{9,8},{10,9... | collective-permute-start | bytes 1105928 | tf_op jit(solution)/shard_map/ppermute | solution.py:33
  448.3 7.6 %collective-permute-start.33 = (f32[6,1152]{1,0:T(8,128)S(1)}, f32[6,1152]{1,0:T(8,128)S(1)}, u32[]{:S(2)}, u32[]{:S(2)}) collective-permute-start(f32[6,1152]{1,0:T(8,128)S(1)} %fusion.4), channel_id=1, source_target_pairs={{0,1},{1,0},{2,3},{3,2},{4,5},{5,4},{6,7},{7,6},{8,9},{9,8},{10,11... | collective-permute-start | bytes 82952 | tf_op jit(solution)/shard_map/ppermute | solution.py:823
  448.3 7.6 %collective-permute-start.34 = (f32[6,1152]{1,0:T(8,128)S(1)}, f32[6,1152]{1,0:T(8,128)S(1)}, u32[]{:S(2)}, u32[]{:S(2)}) collective-permute-start(f32[6,1152]{1,0:T(8,128)S(1)} %fusion.4), channel_id=1, source_target_pairs={{0,2},{1,3},{2,0},{3,1},{4,6},{5,7},{6,4},{7,5},{8,10},{9,11},{10,... | collective-permute-start | bytes 82952 | tf_op jit(solution)/shard_map/ppermute | solution.py:823
  449.2 6.7 %collective-permute-start.35 = (f32[6,1152]{1,0:T(8,128)S(1)}, f32[6,1152]{1,0:T(8,128)S(1)}, u32[]{:S(2)}, u32[]{:S(2)}) collective-permute-start(f32[6,1152]{1,0:T(8,128)S(1)} %fusion.4), channel_id=1, source_target_pairs={{0,3},{1,2},{2,1},{3,0},{4,7},{5,6},{6,5},{7,4},{8,11},{9,10},{10,... | collective-permute-start | bytes 82952 | tf_op jit(solution)/shard_map/ppermute | solution.py:823
  (50 other events, 335.5 us)
Sparse Core Ops, SparseCore 0:
  245.8 57.7 reduce-scatter.3
  307.7 70.6 reduce-scatter.5
  381.9 48.0 reduce-scatter.7

commit v5 on v4

--- a/solution.py
+++ b/solution.py
@@ -1142,13 +1142,13 @@
     pairs = jnp.concatenate([first_sums[:4], middle_sums[4:6], middle_sums[:4], output_sums[:2]])
     pairs = pairs.reshape(6, 2, width)
     pairs = pairs[:, 0] + swapped(pairs[:, 1], "seq", 0)
-    input_block = after(input_block, square_parts_here)
+    modulation_grad = same_everywhere(pairs)
+    input_block = after(input_block, square_parts_here, modulation_grad)
     late_rows = late_rows.astype(WIDE)
     qkv_grad = late_rows[:, : 3 * self_cols].reshape(-1, 3, self_cols)
     ckv_grad = late_rows[:, 3 * self_cols :].reshape(-1, 2, cross_cols)
     output = placed_blocks(output_blocks)
     input_blocks = after(all_blocks(input_block), qkv_grad, ckv_grad, square_grads, output)
-    modulation_grad = same_everywhere(after(pairs, input_blocks))
     input_grad = placed_blocks(input_blocks).astype(WIDE)
 
     return (

time: 472 us -> 468 us (level)
    ppermute x3, waiting for transfers between devices: 0.01 us -> 14.9 us  [same_everywhere(): lax.ppermute(block, 'tp', [(k, k ^ flip) for k in range(count)])]
    all_to_all x6, waiting for transfers between devices: 26.7 us -> 13.1 us  [exchanged(): return lax.all_to_all(blocks, 'tp', 0, 0, tiled=True)]
  transfers between devices with their start and end apart: 48 -> 48, of which waited for: 26 -> 30; matrix products, arithmetic and copies ran while one was open for 10% -> 9% of each run, Pallas kernels for 25% -> 25%
where the time goes in v5:
time: 468 us; the launch traced here: 461 us
  Pallas kernels  157 us (34%)
  waiting for transfers between devices  156 us (33%)
  starting transfers between devices  68.9 us (15%)
  local copies, waits for them, and re-layouts  31.5 us (7%)
  between operations  18.7 us (4%)
  matrix products  14.8 us (3%)
  other arithmetic  14.3 us (3%)
    pallas_call x15, Pallas kernels, call(): pl.pallas_call(body, out_shape=shapes, grid_spec=pltpu.PrefetchScalarGrid...  157 us
    ppermute x18, waiting for transfers between devices, from_behind(): lax.ppermute(block, 'tp', [(k, (k + step) % count) for k in range(count)])  71.3 us
    reduce_scatter x3, waiting for transfers between devices, sum_rows(): lax.psum_scatter(grad.astype(LOW), 'seq', scatter_dimension=0, tiled=True)  38.9 us
    all_to_all x6, starting transfers between devices, exchanged(): return lax.all_to_all(blocks, 'tp', 0, 0, tiled=True)  31.3 us
    ppermute x18, starting transfers between devices, from_behind(): lax.ppermute(block, 'tp', [(k, (k + step) % count) for k in range(count)])  26.7 us
    ppermute x3, waiting for transfers between devices, same_everywhere(): lax.ppermute(block, 'tp', [(k, k ^ flip) for k in range(count)])  14.9 us
    all_to_all x6, waiting for transfers between devices, exchanged(): return lax.all_to_all(blocks, 'tp', 0, 0, tiled=True)  13.1 us
    unnamed x101, local copies, waits for them, and re-layouts  12.5 us
  transfers between devices with their start and end apart: 48, of which 30 were waited for; matrix products, arithmetic and copies ran while one was open for 9% of the time, Pallas kernels for 25%

profile of v5, /device:TPU:8, one launch (start us, length us, event | category | flops | bytes accessed | tf_op | source)
XLA Modules:
  0.0 461.1 jit_solution(16445230400228450597)
XLA Ops:
  7.2 2.5 eighth.1
  16.4 5.0 %all-to-all-start = ((bf16[4,304,576]{2,1,0:T(8,128)(2,1)}), bf16[4,304,576]{2,1,0:T(8,128)(2,1)S(1)}, u32[]{:S(2)}, u32[]{:S(2)}) async-start(bf16[4,304,576]{2,1,0:T(8,128)(2,1)} %broadcast_in_dim.63), calls=%async_computation | async-start | bytes 3112960 | tf_op jit(solution)/shard_map/all_to_all | solution.py:37
  29.3 11.9 %self_project.1 = (bf16[640,1152]{1,0:T(8,128)(2,1)}, f32[640,576]{1,0:T(8,128)}, bf16[640,288]{1,0:T(8,128)(2,1)}, bf16[640,288]{1,0:T(8,128)(2,1)}, bf16[640,2...) custom-call(s32[10]{0:T(128)} %stack.65.table, bf16[640,1152]{1,0:T(8,128)(2,1)} %x.12, ...), custom_call_target="tpu_custom_call" | custom-call | bytes 78704 | tf_op jit(solution)/shard_map/self_project/pallas_call | solution.py:61
  44.0 2.5 pad_maximum_fusion.refs_0_
  50.7 6.8 %self_attend.1 = (bf16[640,288]{1,0:T(8,128)(2,1)}, f32[640,288]{1,0:T(8,128)}, f32[640,288]{1,0:T(8,128)}) custom-call(s32[10]{0:T(128)} %stack.65.table, bf16[640,288]{1,0:T(8,128)(2,1)} %get-tuple-element.85.q, f32[288,128]{1,0:T(8,128)} %get-tuple-element.189.own_fold, f32[288,128]{1,0:T(8,128)} %get-tuple-element.188.other_fold), custom_call_target="tpu_custom_call" | custom-call | bytes 25067 | tf_op jit(solution)/shard_map/self_attend/pallas_call | solution.py:61
  57.6 2.8 fusion.8.grad_hidden
  62.6 4.5 all-to-all-done.refs_8_.kv_own
  67.1 7.9 %all-to-all-start.1 = ((bf16[4,160,288]{2,1,0:T(8,128)(2,1)}), bf16[4,160,288]{2,1,0:T(8,128)(2,1)}, u32[]{:S(2)}, u32[]{:S(2)}) async-start(bf16[4,160,288]{2,1,0:T(8,128)(2,1)} %bitcast.143), calls=%async_computation.1 | async-start | bytes 983040 | tf_op jit(solution)/shard_map/all_to_all | solution.py:37
  75.2 8.9 %collective-permute-done.7.refs_4_ = bf16[3,112,1152]{2,1,0:T(8,128)(2,1)} collective-permute-done((bf16[3,112,1152]{2,1,0:T(8,128)(2,1)}, bf16[3,112,1152]{2,1,0:T(8,128)(2,1)}, u32[]{:S(2)}, u32[]{:S(2)}) %collective-permute-start.7) | collective-permute-done | bytes 774176 | tf_op jit(solution)/shard_map/ppermute | solution.py:752
  84.1 2.5 all-to-all-done.1.att
  93.4 20.9 %middle.1 = (f32[160,1152]{1,0:T(8,128)}, bf16[160,1152]{1,0:T(8,128)(2,1)}, bf16[4,160,288]{2,1,0:T(8,128)(2,1)}, f32[16,160,304]{2,1,0:T(8,128)}, bf16[4,160,2...) custom-call(s32[10]{0:T(128)} %stack.65.table, ...), custom_call_target="tpu_custom_call" | custom-call | bytes 251392 | tf_op jit(solution)/shard_map/middle/pallas_call | solution.py:61
  115.6 4.2 collective-permute-start.14
  120.0 7.1 %collective-permute-done.13.refs_1_ = bf16[160,1152]{1,0:T(8,128)(2,1)S(1)} collective-permute-done((bf16[160,1152]{1,0:T(8,128)(2,1)}, bf16[160,1152]{1,0:T(8,128)(2,1)S(1)}, u32[]{:S(2)}, u32[]{:S(2)}) %collective-permute-start.13) | collective-permute-done | bytes 368672 | tf_op jit(solution)/shard_map/ppermute | solution.py:33
  127.0 20.7 %collective-permute-done.14.refs_2_ = bf16[160,1152]{1,0:T(8,128)(2,1)S(1)} collective-permute-done((bf16[160,1152]{1,0:T(8,128)(2,1)}, bf16[160,1152]{1,0:T(8,128)(2,1)S(1)}, u32[]{:S(2)}, u32[]{:S(2)}) %collective-permute-start.14) | collective-permute-done | bytes 368672 | tf_op jit(solution)/shard_map/ppermute | solution.py:33
  147.7 3.8 collective-permute-done.15.refs_3_
  152.3 8.5 %up_project.1 = (f32[640,1536]{1,0:T(8,128)}, bf16[640,1536]{1,0:T(8,128)(2,1)}, bf16[640,1152]{1,0:T(8,128)(2,1)}) custom-call(s32[10]{0:T(128)} %stack.65.table, bf16[160,1152]{1,0:T(8,128)(2,1)} %get-tuple-element.97.refs_0_, bf16[160,1152]{1,0:T(8,128)(2,1)} %copy-done.37, bf16[160,1152]{1,0:T(8,128)(2,1)} %copy-done.38, bf16[160,1152]{1,0:T(8,128)(2,1)} %copy-done.39, ...), custom_call_target="tpu_custom_call" | custom-call | bytes 123863 | tf_op jit(solution)/shard_map/up_project/pallas_call | solution.py:61
  163.8 9.4 %mix.1 = (bf16[640,768]{1,0:T(8,128)(2,1)}, bf16[2,640,768]{2,1,0:T(8,128)(2,1)}) custom-call(s32[10]{0:T(128)} %stack.65.table, bf16[640,1536]{1,0:T(8,128)(2,1)} %get-tuple-element.98.value.gate.activated, bf16[640,1536]{1,0:T(8,128)(2,1)} %get-tuple-element.98.value.gate.activated, bf16[32,1536]{1,0:T(8,128)(2,1)} %copy-done.19, ...), custom_call_target="tpu_custom_call" | custom-call | bytes 92405 | tf_op jit(solution)/shard_map/mix/pallas_call | solution.py:61
  173.1 3.8 convolution_convert_fusion.2
  177.0 3.5 all-to-all-start.2
  183.5 14.8 %mix_back.1 = (bf16[640,1536]{1,0:T(8,128)(2,1)}, f32[16,1536]{1,0:T(8,128)}) custom-call(s32[10]{0:T(128)} %stack.65.table, bf16[2,640,768]{2,1,0:T(8,128)(2,1)} %get-tuple-element.102.grads, bf16[2,32,768]{2,1,0:T(8,128)(2,1)} %copy-done.40, bf16[640,1536]{1,0:T(8,128)(2,1)} %get-tuple-element.98.value.gate.activated, bf16[32,1536]{1,0:T(8,128)(2,1)} %copy-done.19, ...), custom_call_target="tpu_custom_call" | custom-call | bytes 102236 | tf_op jit(solution)/shard_map/mix_back/pallas_call | solution.py:61
  198.3 4.2 convolution_convert_fusion.1
  207.8 5.8 %all-to-all-done.2.branches = bf16[4,160,1152]{2,1,0:T(8,128)(2,1)S(1)} async-done(((bf16[4,160,1152]{2,1,0:T(8,128)(2,1)}), bf16[4,160,1152]{2,1,0:T(8,128)(2,1)S(1)}, u32[]{:S(2)}, u32[]{:S(2)}) %all-to-all-start.2) | async-done | bytes 1474592 | tf_op jit(solution)/shard_map/all_to_all | solution.py:37
  214.7 3.7 output.1
  218.4 9.4 %ffn_parts.1 = bf16[1152,2304]{1,0:T(8,128)(2,1)} custom-call(s32[10]{0:T(128)} %stack.65.table, bf16[640,1152]{1,0:T(8,128)(2,1)} %copy-done.7, bf16[640,768]{1,0:T(8,128)(2,1)} %get-tuple-element.107.hidden, bf16[640,1152]{1,0:T(8,128)(2,1)} %get-tuple-element.108.normed, bf16[640,1536]{1,0:T(8,128)(2,1)} %get-tuple-element.105.grad_up), custom_call_target="tpu_custom_call" | custom-call | bytes 112066 | tf_op jit(solution)/shard_map/ffn_parts/pallas_call | solution.py:61
  227.8 9.4 %collective-permute-done.18.grad_1 = bf16[160,1152]{1,0:T(8,128)(2,1)S(1)} collective-permute-done((bf16[160,1152]{1,0:T(8,128)(2,1)}, bf16[160,1152]{1,0:T(8,128)(2,1)S(1)}, u32[]{:S(2)}, u32[]{:S(2)}) %collective-permute-start.18) | collective-permute-done | bytes 368672 | tf_op jit(solution)/shard_map/ppermute | solution.py:33
  237.2 7.4 %collective-permute-done.19.grad_2 = bf16[160,1152]{1,0:T(8,128)(2,1)} collective-permute-done((bf16[160,1152]{1,0:T(8,128)(2,1)}, bf16[160,1152]{1,0:T(8,128)(2,1)}, u32[]{:S(2)}, u32[]{:S(2)}) %collective-permute-start.19) | collective-permute-done | bytes 368672 | tf_op jit(solution)/shard_map/ppermute | solution.py:33
  245.8 4.1 collective-permute-start.22
  250.3 25.8 %middle_back.1 = (bf16[160,1152]{1,0:T(8,128)(2,1)}, bf16[4,160,288]{2,1,0:T(8,128)(2,1)}, bf16[160,1152]{1,0:T(8,128)(2,1)}, bf16[4,160,288]{2,1,0:T(8,128)(2,1...) custom-call(s32[10]{0:T(128)} %stack.65.table, ...), custom_call_target="tpu_custom_call" | custom-call | bytes 251023 | tf_op jit(solution)/shard_map/middle_back/pallas_call | solution.py:61
  276.9 3.3 collective-permute-done.23
  281.1 3.5 all-to-all-start.3
  285.8 10.2 %square_parts.1 = (bf16[1152,3584]{1,0:T(8,128)(2,1)}, bf16[4,304,576]{2,1,0:T(8,128)(2,1)}) custom-call(s32[10]{0:T(128)} %stack.65.table, bf16[160,1152]{1,0:T(8,128)(2,1)} %get-tuple-element.116.dyc, bf16[4,160,288]{2,1,0:T(8,128)(2,1)} %get-tuple-element.117.text, bf16[160,1152]{1,0:T(8,128)(2,1)} %get-tuple-element.118.x1, ...), custom_call_target="tpu_custom_call" | custom-call | bytes 146718 | tf_op jit(solution)/shard_map/square_parts/pallas_call | solution.py:61
  297.0 6.1 %all-to-all-start.4 = ((bf16[4,304,576]{2,1,0:T(8,128)(2,1)}), bf16[4,304,576]{2,1,0:T(8,128)(2,1)S(1)}, u32[]{:S(2)}, u32[]{:S(2)}) async-start(bf16[4,304,576]{2,1,0:T(8,128)(2,1)} %get-tuple-element.127), calls=%async_computation.5 | async-start | bytes 3112960 | tf_op jit(solution)/shard_map/all_to_all | solution.py:37
  303.7 11.9 %self_back.1 = (f32[640,288]{1,0:T(8,128)}, f32[288,128]{1,0:T(8,128)}, f32[288,128]{1,0:T(8,128)}) custom-call(s32[10]{0:T(128)} %stack.65.table, bf16[4,160,288]{2,1,0:T(8,128)(2,1)} %copy-done.13, bf16[640,288]{1,0:T(8,128)(2,1)} %get-tuple-element.85.q, f32[640,288]{1,0:T(8,128)} %get-tuple-element.130.wide_out, ...), custom_call_target="tpu_custom_call" | custom-call | bytes 35389 | tf_op jit(solution)/shard_map/self_back/pallas_call | solution.py:61
  320.2 9.2 %self_project_back.1.grad_projected = bf16[640,864]{1,0:T(8,128)(2,1)} custom-call(s32[10]{0:T(128)} %stack.65.table, f32[640,288]{1,0:T(8,128)} %get-tuple-element.132.grad_q, bf16[640,288]{1,0:T(8,128)(2,1)} %get-tuple-element.133.k, bf16[640,288]{1,0:T(8,128)(2,1)} %get-tuple-element.134.v, f32[640,576]{1,0:T(8,128)} %get-tuple-element.135.raw, ...), custom_call_target="tpu_custom_call" | custom-call | bytes 43499 | tf_op jit(solution)/shard_map/self_project_back/pallas_call | solution.py:61
  329.4 3.1 convolution_convert_fusion
  340.0 8.0 %late_parts.1 = bf16[1152,1440]{1,0:T(8,128)(2,1)} custom-call(s32[10]{0:T(128)} %stack.65.table, bf16[640,1152]{1,0:T(8,128)(2,1)} %get-tuple-element.138.normed, bf16[640,864]{1,0:T(8,128)(2,1)} %self_project_back.1.grad_projected, bf16[304,1152]{1,0:T(8,128)(2,1)} %pad.16.text, bf16[4,304,576]{2,1,0:T(8,128)(2,1)} %copy-done.6), custom_call_target="tpu_custom_call" | custom-call | bytes 79994 | tf_op jit(solution)/shard_map/late_parts/pallas_call | solution.py:61
  348.0 30.5 %reduce-scatter.6.cloned.1.call-done = bf16[144,3584]{1,0:T(8,128)(2,1)} async-done(((bf16[1152,3584]{1,0:T(8,128)(2,1)}), bf16[144,3584]{1,0:T(8,128)(2,1)}) %reduce-scatter.6.cloned.1.call-update) | async-done | bytes 1032208 | tf_op jit(solution)/shard_map/reduce_scatter | solution.py:829
  384.5 5.3 %all-to-all-start.5 = ((bf16[4,144,896]{2,1,0:T(8,128)(2,1)}), bf16[4,144,896]{2,1,0:T(8,128)(2,1)S(1)}, u32[]{:S(2)}, u32[]{:S(2)}) async-start(bf16[4,144,896]{2,1,0:T(8,128)(2,1)} %bitcast.109), calls=%async_computation.7 | async-start | bytes 2064384 | tf_op jit(solution)/shard_map/all_to_all | solution.py:37
  389.8 4.3 first_norm_back.1
  397.3 2.8 collective-permute-start.31
  402.3 6.6 %collective-permute-done.30 = f32[6,1152]{1,0:T(8,128)S(1)} collective-permute-done((f32[6,1152]{1,0:T(8,128)S(1)}, f32[6,1152]{1,0:T(8,128)S(1)}, u32[]{:S(2)}, u32[]{:S(2)}) %collective-permute-start.30) | collective-permute-done | bytes 27680 | tf_op jit(solution)/shard_map/ppermute | solution.py:823
  408.9 6.0 %collective-permute-done.31 = f32[6,1152]{1,0:T(8,128)S(1)} collective-permute-done((f32[6,1152]{1,0:T(8,128)S(1)}, f32[6,1152]{1,0:T(8,128)S(1)}, u32[]{:S(2)}, u32[]{:S(2)}) %collective-permute-start.31) | collective-permute-done | bytes 27680 | tf_op jit(solution)/shard_map/ppermute | solution.py:823
  414.9 2.3 collective-permute-done.32
  418.4 2.9 collective-permute-start.34
  422.4 7.7 %reduce-scatter.8.cloned.1.call-done = bf16[144,1440]{1,0:T(8,128)(2,1)} async-done(((bf16[1152,1440]{1,0:T(8,128)(2,1)}), bf16[144,1440]{1,0:T(8,128)(2,1)}) %reduce-scatter.8.cloned.1.call-update) | async-done | bytes 414736 | tf_op jit(solution)/shard_map/reduce_scatter | solution.py:829
  434.6 8.7 %collective-permute-done.33 = bf16[160,1152]{1,0:T(8,128)(2,1)S(1)} collective-permute-done((bf16[160,1152]{1,0:T(8,128)(2,1)S(1)}, bf16[160,1152]{1,0:T(8,128)(2,1)S(1)}, u32[]{:S(2)}, u32[]{:S(2)}) %collective-permute-start.33) | collective-permute-done | bytes 368672 | tf_op jit(solution)/shard_map/ppermute | solution.py:33
  443.3 6.0 %collective-permute-done.34 = bf16[160,1152]{1,0:T(8,128)(2,1)S(1)} collective-permute-done((bf16[160,1152]{1,0:T(8,128)(2,1)S(1)}, bf16[160,1152]{1,0:T(8,128)(2,1)S(1)}, u32[]{:S(2)}, u32[]{:S(2)}) %collective-permute-start.34) | collective-permute-done | bytes 368672 | tf_op jit(solution)/shard_map/ppermute | solution.py:33
  449.3 2.8 collective-permute-done.35
  (233 shorter events, 79.0 us)
Async XLA Ops:
  9.7 34.1 %collective-permute-start.2 = (bf16[112,1152]{1,0:T(8,128)(2,1)}, bf16[112,1152]{1,0:T(8,128)(2,1)S(1)}, u32[]{:S(2)}, u32[]{:S(2)}) collective-permute-start(bf16[112,1152]{1,0:T(8,128)(2,1)} %eighth.1), channel_id=1, source_target_pairs={{0,1},{1,2},{2,3},{3,0},{4,5},{5,6},{6,7},{7,4},{8,9},{9,10},{10,1... | collective-permute-start | bytes 774152 | tf_op jit(solution)/shard_map/ppermute | solution.py:33
  11.3 32.5 %collective-permute-start.3 = (bf16[112,1152]{1,0:T(8,128)(2,1)}, bf16[112,1152]{1,0:T(8,128)(2,1)}, u32[]{:S(2)}, u32[]{:S(2)}) collective-permute-start(bf16[112,1152]{1,0:T(8,128)(2,1)} %eighth.1), channel_id=1, source_target_pairs={{0,2},{1,3},{2,0},{3,1},{4,6},{5,7},{6,4},{7,5},{8,10},{9,11},{10,... | collective-permute-start | bytes 774152 | tf_op jit(solution)/shard_map/ppermute | solution.py:33
  12.3 31.6 %collective-permute-start.4 = (bf16[112,1152]{1,0:T(8,128)(2,1)}, bf16[112,1152]{1,0:T(8,128)(2,1)}, u32[]{:S(2)}, u32[]{:S(2)}) collective-permute-start(bf16[112,1152]{1,0:T(8,128)(2,1)} %eighth.1), channel_id=1, source_target_pairs={{0,3},{1,0},{2,1},{3,2},{4,7},{5,4},{6,5},{7,6},{8,11},{9,8},{10,9... | collective-permute-start | bytes 774152 | tf_op jit(solution)/shard_map/ppermute | solution.py:33
  14.3 14.4 %collective-permute-start = (bf16[6,1152]{1,0:T(8,128)(2,1)S(1)}, bf16[6,1152]{1,0:T(8,128)(2,1)S(1)}, u32[]{:S(2)}, u32[]{:S(2)}) collective-permute-start(bf16[6,1152]{1,0:T(8,128)(2,1)S(1)} %bitcast.150), channel_id=1, source_target_pairs={{0,4},{4,0},{8,12},{12,8},{16,20},{20,16},{24,28},{28,24},{1,5},{5... | collective-permute-start | bytes 41480 | tf_op jit(solution)/shard_map/ppermute | solution.py:28
  16.4 50.6 %all-to-all-start = ((bf16[4,304,576]{2,1,0:T(8,128)(2,1)}), bf16[4,304,576]{2,1,0:T(8,128)(2,1)S(1)}, u32[]{:S(2)}, u32[]{:S(2)}) async-start(bf16[4,304,576]{2,1,0:T(8,128)(2,1)} %broadcast_in_dim.63), calls=%async_computation | async-start | bytes 3112960 | tf_op jit(solution)/shard_map/all_to_all | solution.py:37
  42.3 7.7 %collective-permute-start.1 = (f32[2,288,128]{2,1,0:T(8,128)S(1)}, f32[2,288,128]{2,1,0:T(8,128)S(1)}, u32[]{:S(2)}, u32[]{:S(2)}) collective-permute-start(f32[2,288,128]{2,1,0:T(8,128)S(1)} %pad_maximum_fusion.1), channel_id=1, source_target_pairs={{0,4},{4,0},{8,12},{12,8},{16,20},{20,16},{24,28},{28,24},{1,5},{5... | collective-permute-start | bytes 884744 | tf_op jit(solution)/shard_map/ppermute | solution.py:28
  46.5 28.7 %collective-permute-start.6 = (bf16[3,112,1152]{2,1,0:T(8,128)(2,1)}, bf16[3,112,1152]{2,1,0:T(8,128)(2,1)}, u32[]{:S(2)}, u32[]{:S(2)}) collective-permute-start(bf16[3,112,1152]{2,1,0:T(8,128)(2,1)} %pad_maximum_fusion.refs_0_), channel_id=1, source_target_pairs={{0,8},{4,12},{8,0},{12,4},{16,24},{20,28},{24,16},{28,20},{1,9},{5... | collective-permute-start | bytes 2322440 | tf_op jit(solution)/shard_map/ppermute | solution.py:752
  48.0 36.1 %collective-permute-start.7 = (bf16[3,112,1152]{2,1,0:T(8,128)(2,1)}, bf16[3,112,1152]{2,1,0:T(8,128)(2,1)}, u32[]{:S(2)}, u32[]{:S(2)}) collective-permute-start(bf16[3,112,1152]{2,1,0:T(8,128)(2,1)} %pad_maximum_fusion.refs_0_), channel_id=1, source_target_pairs={{0,16},{4,20},{8,24},{12,28},{16,0},{20,4},{24,8},{28,12},{1,17},{... | collective-permute-start | bytes 2322440 | tf_op jit(solution)/shard_map/ppermute | solution.py:752
  49.5 34.6 %collective-permute-start.8 = (bf16[3,112,1152]{2,1,0:T(8,128)(2,1)}, bf16[3,112,1152]{2,1,0:T(8,128)(2,1)}, u32[]{:S(2)}, u32[]{:S(2)}) collective-permute-start(bf16[3,112,1152]{2,1,0:T(8,128)(2,1)} %pad_maximum_fusion.refs_0_), channel_id=1, source_target_pairs={{0,24},{4,28},{8,16},{12,20},{16,8},{20,12},{24,0},{28,4},{1,25},{... | collective-permute-start | bytes 2322440 | tf_op jit(solution)/shard_map/ppermute | solution.py:752
  67.1 24.3 %collective-permute-start.12 = (bf16[4,304,576]{2,1,0:T(8,128)(2,1)S(1)}, bf16[4,304,576]{2,1,0:T(8,128)(2,1)S(1)}, u32[]{:S(2)}, u32[]{:S(2)}) collective-permute-start(bf16[4,304,576]{2,1,0:T(8,128)(2,1)S(1)} %all-to-all-done.refs_8_.kv_own), channel_id=1, source_target_pairs={{0,4},{4,0},{8,12},{12,8},{16,20},{20,16},{24,28},{28,24},{1,5},{5... | collective-permute-start | bytes 4202504 | tf_op jit(solution)/shard_map/ppermute | solution.py:28
  67.1 19.6 %all-to-all-start.1 = ((bf16[4,160,288]{2,1,0:T(8,128)(2,1)}), bf16[4,160,288]{2,1,0:T(8,128)(2,1)}, u32[]{:S(2)}, u32[]{:S(2)}) async-start(bf16[4,160,288]{2,1,0:T(8,128)(2,1)} %bitcast.143), calls=%async_computation.1 | async-start | bytes 983040 | tf_op jit(solution)/shard_map/all_to_all | solution.py:37
  75.0 12.1 %collective-permute-start.5 = (bf16[3,112,1152]{2,1,0:T(8,128)(2,1)}, bf16[3,112,1152]{2,1,0:T(8,128)(2,1)}, u32[]{:S(2)}, u32[]{:S(2)}) collective-permute-start(bf16[3,112,1152]{2,1,0:T(8,128)(2,1)} %pad_maximum_fusion.refs_0_), channel_id=1, source_target_pairs={{0,4},{4,0},{8,12},{12,8},{16,20},{20,16},{24,28},{28,24},{1,5},{5... | collective-permute-start | bytes 2322440 | tf_op jit(solution)/shard_map/ppermute | solution.py:28
  86.6 2.5 collective-permute-start.10
  86.6 3.6 collective-permute-start.11
  87.1 4.2 collective-permute-start.9
  114.3 12.7 %collective-permute-start.13 = (bf16[160,1152]{1,0:T(8,128)(2,1)}, bf16[160,1152]{1,0:T(8,128)(2,1)S(1)}, u32[]{:S(2)}, u32[]{:S(2)}) collective-permute-start(bf16[160,1152]{1,0:T(8,128)(2,1)} %get-tuple-element.97.refs_0_), channel_id=1, source_target_pairs={{0,1},{1,2},{2,3},{3,0},{4,5},{5,6},{6,7},{7,4},{8,9},{9,10},{10,1... | collective-permute-start | bytes 1105928 | tf_op jit(solution)/shard_map/ppermute | solution.py:33
  115.6 32.2 %collective-permute-start.14 = (bf16[160,1152]{1,0:T(8,128)(2,1)}, bf16[160,1152]{1,0:T(8,128)(2,1)S(1)}, u32[]{:S(2)}, u32[]{:S(2)}) collective-permute-start(bf16[160,1152]{1,0:T(8,128)(2,1)} %get-tuple-element.97.refs_0_), channel_id=1, source_target_pairs={{0,2},{1,3},{2,0},{3,1},{4,6},{5,7},{6,4},{7,5},{8,10},{9,11},{10,... | collective-permute-start | bytes 1105928 | tf_op jit(solution)/shard_map/ppermute | solution.py:33
  119.8 31.7 %collective-permute-start.15 = (bf16[160,1152]{1,0:T(8,128)(2,1)}, bf16[160,1152]{1,0:T(8,128)(2,1)S(1)}, u32[]{:S(2)}, u32[]{:S(2)}) collective-permute-start(bf16[160,1152]{1,0:T(8,128)(2,1)} %get-tuple-element.97.refs_0_), channel_id=1, source_target_pairs={{0,3},{1,0},{2,1},{3,2},{4,7},{5,4},{6,5},{7,6},{8,11},{9,8},{10,9... | collective-permute-start | bytes 1105928 | tf_op jit(solution)/shard_map/ppermute | solution.py:33
  161.8 1.4 collective-permute-start.16
  177.0 36.6 %all-to-all-start.2 = ((bf16[4,160,1152]{2,1,0:T(8,128)(2,1)}), bf16[4,160,1152]{2,1,0:T(8,128)(2,1)S(1)}, u32[]{:S(2)}, u32[]{:S(2)}) async-start(bf16[4,160,1152]{2,1,0:T(8,128)(2,1)} %bitcast.32), calls=%async_computation.2 | async-start | bytes 2949120 | tf_op jit(solution)/shard_map/all_to_all | solution.py:37
  180.5 123.2 %reduce-scatter.4.cloned.1.call-start = ((), (), s32[]{:S(2)}) async-start(), calls=%async_computation.9 | async-start | bytes 5971968 | tf_op jit(solution)/shard_map/reduce_scatter | solution.py:829
  181.5 1.4 collective-permute-start.17
  203.7 33.5 %collective-permute-start.18 = (bf16[160,1152]{1,0:T(8,128)(2,1)}, bf16[160,1152]{1,0:T(8,128)(2,1)S(1)}, u32[]{:S(2)}, u32[]{:S(2)}) collective-permute-start(bf16[160,1152]{1,0:T(8,128)(2,1)} %get-tuple-element.182), channel_id=1, source_target_pairs={{0,1},{1,2},{2,3},{3,0},{4,5},{5,6},{6,7},{7,4},{8,9},{9,10},{10,1... | collective-permute-start | bytes 1105928 | tf_op jit(solution)/shard_map/ppermute | solution.py:33
  204.8 39.8 %collective-permute-start.19 = (bf16[160,1152]{1,0:T(8,128)(2,1)}, bf16[160,1152]{1,0:T(8,128)(2,1)}, u32[]{:S(2)}, u32[]{:S(2)}) collective-permute-start(bf16[160,1152]{1,0:T(8,128)(2,1)} %get-tuple-element.181), channel_id=1, source_target_pairs={{0,2},{1,3},{2,0},{3,1},{4,6},{5,7},{6,4},{7,5},{8,10},{9,11},{10,... | collective-permute-start | bytes 1105928 | tf_op jit(solution)/shard_map/ppermute | solution.py:33
  205.7 40.0 %collective-permute-start.20 = (bf16[160,1152]{1,0:T(8,128)(2,1)}, bf16[160,1152]{1,0:T(8,128)(2,1)}, u32[]{:S(2)}, u32[]{:S(2)}) collective-permute-start(bf16[160,1152]{1,0:T(8,128)(2,1)} %get-tuple-element.180), channel_id=1, source_target_pairs={{0,3},{1,0},{2,1},{3,2},{4,7},{5,4},{6,5},{7,6},{8,11},{9,8},{10,9... | collective-permute-start | bytes 1105928 | tf_op jit(solution)/shard_map/ppermute | solution.py:33
  245.8 30.3 %collective-permute-start.21 = (bf16[160,1152]{1,0:T(8,128)(2,1)S(1)}, bf16[160,1152]{1,0:T(8,128)(2,1)S(1)}, u32[]{:S(2)}, u32[]{:S(2)}) collective-permute-start(bf16[160,1152]{1,0:T(8,128)(2,1)S(1)} %copy-done.28), channel_id=1, source_target_pairs={{0,1},{1,2},{2,3},{3,0},{4,5},{5,6},{6,7},{7,4},{8,9},{9,10},{10,1... | collective-permute-start | bytes 1105928 | tf_op jit(solution)/shard_map/ppermute | solution.py:33
  245.8 31.1 %collective-permute-start.22 = (bf16[160,1152]{1,0:T(8,128)(2,1)S(1)}, bf16[160,1152]{1,0:T(8,128)(2,1)S(1)}, u32[]{:S(2)}, u32[]{:S(2)}) collective-permute-start(bf16[160,1152]{1,0:T(8,128)(2,1)S(1)} %copy-done.28), channel_id=1, source_target_pairs={{0,2},{1,3},{2,0},{3,1},{4,6},{5,7},{6,4},{7,5},{8,10},{9,11},{10,... | collective-permute-start | bytes 1105928 | tf_op jit(solution)/shard_map/ppermute | solution.py:33
  249.9 30.3 %collective-permute-start.23 = (bf16[160,1152]{1,0:T(8,128)(2,1)S(1)}, bf16[160,1152]{1,0:T(8,128)(2,1)S(1)}, u32[]{:S(2)}, u32[]{:S(2)}) collective-permute-start(bf16[160,1152]{1,0:T(8,128)(2,1)S(1)} %copy-done.28), channel_id=1, source_target_pairs={{0,3},{1,0},{2,1},{3,2},{4,7},{5,4},{6,5},{7,6},{8,11},{9,8},{10,9... | collective-permute-start | bytes 1105928 | tf_op jit(solution)/shard_map/ppermute | solution.py:33
  281.0 3.6 collective-permute-start.24
  281.1 15.1 %all-to-all-start.3 = ((bf16[4,160,288]{2,1,0:T(8,128)(2,1)}), bf16[4,160,288]{2,1,0:T(8,128)(2,1)S(1)}, u32[]{:S(2)}, u32[]{:S(2)}) async-start(bf16[4,160,288]{2,1,0:T(8,128)(2,1)} %get-tuple-element.115), calls=%async_computation.3 | async-start | bytes 983040 | tf_op jit(solution)/shard_map/all_to_all | solution.py:37
  284.6 93.9 %reduce-scatter.6.cloned.1.call-start = ((), (), s32[]{:S(2)}) async-start(), calls=%async_computation.10 | async-start | bytes 9289728 | tf_op jit(solution)/shard_map/reduce_scatter | solution.py:829
  297.0 41.8 %all-to-all-start.4 = ((bf16[4,304,576]{2,1,0:T(8,128)(2,1)}), bf16[4,304,576]{2,1,0:T(8,128)(2,1)S(1)}, u32[]{:S(2)}, u32[]{:S(2)}) async-start(bf16[4,304,576]{2,1,0:T(8,128)(2,1)} %get-tuple-element.127), calls=%async_computation.5 | async-start | bytes 3112960 | tf_op jit(solution)/shard_map/all_to_all | solution.py:37
  303.1 127.0 %reduce-scatter.8.cloned.1.call-start = ((), (), s32[]{:S(2)}) async-start(), calls=%async_computation.11 | async-start | bytes 3981312 | tf_op jit(solution)/shard_map/reduce_scatter | solution.py:829
  316.7 1.6 collective-permute-start.25
  333.4 45.1 %collective-permute-start.26 = (bf16[160,1152]{1,0:T(8,128)(2,1)}, bf16[160,1152]{1,0:T(8,128)(2,1)}, u32[]{:S(2)}, u32[]{:S(2)}) collective-permute-start(bf16[160,1152]{1,0:T(8,128)(2,1)} %get-tuple-element.179), channel_id=1, source_target_pairs={{0,1},{1,2},{2,3},{3,0},{4,5},{5,6},{6,7},{7,4},{8,9},{9,10},{10,1... | collective-permute-start | bytes 1105928 | tf_op jit(solution)/shard_map/ppermute | solution.py:33
  335.0 43.5 %collective-permute-start.27 = (bf16[160,1152]{1,0:T(8,128)(2,1)}, bf16[160,1152]{1,0:T(8,128)(2,1)}, u32[]{:S(2)}, u32[]{:S(2)}) collective-permute-start(bf16[160,1152]{1,0:T(8,128)(2,1)} %get-tuple-element.178), channel_id=1, source_target_pairs={{0,2},{1,3},{2,0},{3,1},{4,6},{5,7},{6,4},{7,5},{8,10},{9,11},{10,... | collective-permute-start | bytes 1105928 | tf_op jit(solution)/shard_map/ppermute | solution.py:33
  336.5 42.0 %collective-permute-start.28 = (bf16[160,1152]{1,0:T(8,128)(2,1)S(1)}, bf16[160,1152]{1,0:T(8,128)(2,1)}, u32[]{:S(2)}, u32[]{:S(2)}) collective-permute-start(bf16[160,1152]{1,0:T(8,128)(2,1)S(1)} %get-tuple-element.177), channel_id=1, source_target_pairs={{0,3},{1,0},{2,1},{3,2},{4,7},{5,4},{6,5},{7,6},{8,11},{9,8},{10,9... | collective-permute-start | bytes 1105928 | tf_op jit(solution)/shard_map/ppermute | solution.py:33
  380.6 1.4 collective-permute-start.36
  382.0 14.4 %collective-permute-start.37 = (f32[9,1536]{1,0:T(8,128)S(1)}, f32[9,1536]{1,0:T(8,128)S(1)}, u32[]{:S(2)}, u32[]{:S(2)}) collective-permute-start(f32[9,1536]{1,0:T(8,128)S(1)} %add.194), channel_id=1, source_target_pairs={{0,8},{4,12},{8,0},{12,4},{16,24},{20,28},{24,16},{28,20},{1,9},{5... | collective-permute-start | bytes 165896 | tf_op jit(solution)/shard_map/ppermute | solution.py:28
  384.5 33.4 %all-to-all-start.5 = ((bf16[4,144,896]{2,1,0:T(8,128)(2,1)}), bf16[4,144,896]{2,1,0:T(8,128)(2,1)S(1)}, u32[]{:S(2)}, u32[]{:S(2)}) async-start(bf16[4,144,896]{2,1,0:T(8,128)(2,1)} %bitcast.109), calls=%async_computation.7 | async-start | bytes 2064384 | tf_op jit(solution)/shard_map/all_to_all | solution.py:37
  395.1 2.0 collective-permute-start.29
  396.4 5.3 %collective-permute-start.38 = (f32[9,1536]{1,0:T(8,128)S(1)}, f32[9,1536]{1,0:T(8,128)S(1)}, u32[]{:S(2)}, u32[]{:S(2)}) collective-permute-start(f32[9,1536]{1,0:T(8,128)S(1)} %add.195), channel_id=1, source_target_pairs={{0,16},{4,20},{8,24},{12,28},{16,0},{20,4},{24,8},{28,12},{1,17},{... | collective-permute-start | bytes 165896 | tf_op jit(solution)/shard_map/ppermute | solution.py:28
  397.1 11.8 %collective-permute-start.30 = (f32[6,1152]{1,0:T(8,128)S(1)}, f32[6,1152]{1,0:T(8,128)S(1)}, u32[]{:S(2)}, u32[]{:S(2)}) collective-permute-start(f32[6,1152]{1,0:T(8,128)S(1)} %fusion.4), channel_id=1, source_target_pairs={{0,1},{1,0},{2,3},{3,2},{4,5},{5,4},{6,7},{7,6},{8,9},{9,8},{10,11... | collective-permute-start | bytes 82952 | tf_op jit(solution)/shard_map/ppermute | solution.py:823
  397.3 17.6 %collective-permute-start.31 = (f32[6,1152]{1,0:T(8,128)S(1)}, f32[6,1152]{1,0:T(8,128)S(1)}, u32[]{:S(2)}, u32[]{:S(2)}) collective-permute-start(f32[6,1152]{1,0:T(8,128)S(1)} %fusion.4), channel_id=1, source_target_pairs={{0,2},{1,3},{2,0},{3,1},{4,6},{5,7},{6,4},{7,5},{8,10},{9,11},{10,... | collective-permute-start | bytes 82952 | tf_op jit(solution)/shard_map/ppermute | solution.py:823
  400.1 17.1 %collective-permute-start.32 = (f32[6,1152]{1,0:T(8,128)S(1)}, f32[6,1152]{1,0:T(8,128)S(1)}, u32[]{:S(2)}, u32[]{:S(2)}) collective-permute-start(f32[6,1152]{1,0:T(8,128)S(1)} %fusion.4), channel_id=1, source_target_pairs={{0,3},{1,2},{2,1},{3,0},{4,7},{5,6},{6,5},{7,4},{8,11},{9,10},{10,... | collective-permute-start | bytes 82952 | tf_op jit(solution)/shard_map/ppermute | solution.py:823
  417.9 25.4 %collective-permute-start.33 = (bf16[160,1152]{1,0:T(8,128)(2,1)S(1)}, bf16[160,1152]{1,0:T(8,128)(2,1)S(1)}, u32[]{:S(2)}, u32[]{:S(2)}) collective-permute-start(bf16[160,1152]{1,0:T(8,128)(2,1)S(1)} %copy-done.36), channel_id=1, source_target_pairs={{0,1},{1,2},{2,3},{3,0},{4,5},{5,6},{6,7},{7,4},{8,9},{9,10},{10,1... | collective-permute-start | bytes 1105928 | tf_op jit(solution)/shard_map/ppermute | solution.py:33
  418.4 30.9 %collective-permute-start.34 = (bf16[160,1152]{1,0:T(8,128)(2,1)S(1)}, bf16[160,1152]{1,0:T(8,128)(2,1)S(1)}, u32[]{:S(2)}, u32[]{:S(2)}) collective-permute-start(bf16[160,1152]{1,0:T(8,128)(2,1)S(1)} %copy-done.36), channel_id=1, source_target_pairs={{0,2},{1,3},{2,0},{3,1},{4,6},{5,7},{6,4},{7,5},{8,10},{9,11},{10,... | collective-permute-start | bytes 1105928 | tf_op jit(solution)/shard_map/ppermute | solution.py:33
  421.3 30.8 %collective-permute-start.35 = (bf16[160,1152]{1,0:T(8,128)(2,1)S(1)}, bf16[160,1152]{1,0:T(8,128)(2,1)S(1)}, u32[]{:S(2)}, u32[]{:S(2)}) collective-permute-start(bf16[160,1152]{1,0:T(8,128)(2,1)S(1)} %copy-done.36), channel_id=1, source_target_pairs={{0,3},{1,0},{2,1},{3,2},{4,7},{5,4},{6,5},{7,6},{8,11},{9,8},{10,9... | collective-permute-start | bytes 1105928 | tf_op jit(solution)/shard_map/ppermute | solution.py:33
  (50 other events, 341.7 us)
Sparse Core Ops, SparseCore 0:
  245.9 57.8 reduce-scatter.3
  307.8 70.6 reduce-scatter.5
  382.0 48.0 reduce-scatter.7

commit v6 on v5

--- a/solution.py
+++ b/solution.py
@@ -175,7 +175,7 @@
 
 def self_project(table, x, mod_own, mod_other, weight, columns):
     tokens, width = x.shape
-    rows = 128
+    rows = tokens // 2
     row = lambda c: pl.BlockSpec((rows, c), lambda i, t: (i, 0))
     fixed = lambda *s: pl.BlockSpec(s, lambda i, t: (0,) * len(s))
     return call(
@@ -227,7 +227,7 @@
 
 def self_attend(table, q, own_fold, other_fold):
     tokens, columns = q.shape
-    rows = 128
+    rows = tokens // 2
     row = pl.BlockSpec((rows, columns), lambda i, t: (i, 0))
     fixed = pl.BlockSpec((columns, LANES), lambda i, t: (0, 0))
     return call(
@@ -345,7 +345,7 @@
 
 def self_project_back(table, grad_q, k, v, raw, own_fold, other_fold):
     tokens, columns = k.shape
-    rows = 128
+    rows = tokens // 2
     row = lambda c: pl.BlockSpec((rows, c), lambda i, t: (i, 0))
     fixed = pl.BlockSpec((columns, LANES), lambda i, t: (0, 0))
     return call(

time: 468 us -> 469 us (level)
  Pallas kernels: 157 us -> 152 us
    pallas_call x15, Pallas kernels: 157 us -> 152 us  [call(): pl.pallas_call(body, out_shape=shapes, grid_spec=pltpu.PrefetchScalarGrid...]
  transfers between devices with their start and end apart: 48 -> 48, of which waited for: 30 -> 31; matrix products, arithmetic and copies ran while one was open for 9% -> 9% of each run, Pallas kernels for 25% -> 24%
where the time goes in v6:
time: 469 us; the launch traced here: 461 us
  waiting for transfers between devices  160 us (34%)
  Pallas kernels  152 us (32%)
  starting transfers between devices  69.1 us (15%)
  local copies, waits for them, and re-layouts  31.5 us (7%)
  between operations  18.9 us (4%)
  matrix products  14.8 us (3%)
  other arithmetic  14 us (3%)
    pallas_call x15, Pallas kernels, call(): pl.pallas_call(body, out_shape=shapes, grid_spec=pltpu.PrefetchScalarGrid...  152 us
    ppermute x18, waiting for transfers between devices, from_behind(): lax.ppermute(block, 'tp', [(k, (k + step) % count) for k in range(count)])  73.6 us
    reduce_scatter x3, waiting for transfers between devices, sum_rows(): lax.psum_scatter(grad.astype(LOW), 'seq', scatter_dimension=0, tiled=True)  40 us
    all_to_all x6, starting transfers between devices, exchanged(): return lax.all_to_all(blocks, 'tp', 0, 0, tiled=True)  30.9 us
    ppermute x18, starting transfers between devices, from_behind(): lax.ppermute(block, 'tp', [(k, (k + step) % count) for k in range(count)])  27.4 us
    ppermute x3, waiting for transfers between devices, same_everywhere(): lax.ppermute(block, 'tp', [(k, k ^ flip) for k in range(count)])  15 us
    all_to_all x6, waiting for transfers between devices, exchanged(): return lax.all_to_all(blocks, 'tp', 0, 0, tiled=True)  14.9 us
    unnamed x101, local copies, waits for them, and re-layouts  12.5 us
  transfers between devices with their start and end apart: 48, of which 31 were waited for; matrix products, arithmetic and copies ran while one was open for 9% of the time, Pallas kernels for 24%

profile of v6, /device:TPU:8, one launch (start us, length us, event | category | flops | bytes accessed | tf_op | source)
XLA Modules:
  0.0 460.8 jit_solution(1748443292936336569)
XLA Ops:
  7.2 2.5 eighth.1
  16.4 5.0 %all-to-all-start = ((bf16[4,304,576]{2,1,0:T(8,128)(2,1)}), bf16[4,304,576]{2,1,0:T(8,128)(2,1)S(1)}, u32[]{:S(2)}, u32[]{:S(2)}) async-start(bf16[4,304,576]{2,1,0:T(8,128)(2,1)} %broadcast_in_dim.63), calls=%async_computation | async-start | bytes 3112960 | tf_op jit(solution)/shard_map/all_to_all | solution.py:37
  29.3 9.5 %self_project.1 = (bf16[640,1152]{1,0:T(8,128)(2,1)}, f32[640,576]{1,0:T(8,128)}, bf16[640,288]{1,0:T(8,128)(2,1)}, bf16[640,288]{1,0:T(8,128)(2,1)}, bf16[640,2...) custom-call(s32[10]{0:T(128)} %stack.65.table, bf16[640,1152]{1,0:T(8,128)(2,1)} %x.12, ...), custom_call_target="tpu_custom_call" | custom-call | bytes 78704 | tf_op jit(solution)/shard_map/self_project/pallas_call | solution.py:61
  41.3 2.6 collective-permute-done.4
  50.4 5.9 %self_attend.1 = (bf16[640,288]{1,0:T(8,128)(2,1)}, f32[640,288]{1,0:T(8,128)}, f32[640,288]{1,0:T(8,128)}) custom-call(s32[10]{0:T(128)} %stack.65.table, bf16[640,288]{1,0:T(8,128)(2,1)} %get-tuple-element.85.q, f32[288,128]{1,0:T(8,128)} %get-tuple-element.189.own_fold, f32[288,128]{1,0:T(8,128)} %get-tuple-element.188.other_fold), custom_call_target="tpu_custom_call" | custom-call | bytes 25067 | tf_op jit(solution)/shard_map/self_attend/pallas_call | solution.py:61
  56.3 2.8 fusion.8.grad_hidden
  61.2 5.8 %all-to-all-done.refs_8_.kv_own = bf16[4,304,576]{2,1,0:T(8,128)(2,1)S(1)} async-done(((bf16[4,304,576]{2,1,0:T(8,128)(2,1)}), bf16[4,304,576]{2,1,0:T(8,128)(2,1)S(1)}, u32[]{:S(2)}, u32[]{:S(2)}) %all-to-all-start) | async-done | bytes 1400864 | tf_op jit(solution)/shard_map/all_to_all | solution.py:37
  67.1 7.6 %all-to-all-start.1 = ((bf16[4,160,288]{2,1,0:T(8,128)(2,1)}), bf16[4,160,288]{2,1,0:T(8,128)(2,1)}, u32[]{:S(2)}, u32[]{:S(2)}) async-start(bf16[4,160,288]{2,1,0:T(8,128)(2,1)} %bitcast.143), calls=%async_computation.1 | async-start | bytes 983040 | tf_op jit(solution)/shard_map/all_to_all | solution.py:37
  74.8 8.5 %collective-permute-done.7.refs_4_ = bf16[3,112,1152]{2,1,0:T(8,128)(2,1)} collective-permute-done((bf16[3,112,1152]{2,1,0:T(8,128)(2,1)}, bf16[3,112,1152]{2,1,0:T(8,128)(2,1)}, u32[]{:S(2)}, u32[]{:S(2)}) %collective-permute-start.7) | collective-permute-done | bytes 774176 | tf_op jit(solution)/shard_map/ppermute | solution.py:752
  83.3 3.0 all-to-all-done.1.att
  93.1 20.9 %middle.1 = (f32[160,1152]{1,0:T(8,128)}, bf16[160,1152]{1,0:T(8,128)(2,1)}, bf16[4,160,288]{2,1,0:T(8,128)(2,1)}, f32[16,160,304]{2,1,0:T(8,128)}, bf16[4,160,2...) custom-call(s32[10]{0:T(128)} %stack.65.table, ...), custom_call_target="tpu_custom_call" | custom-call | bytes 251392 | tf_op jit(solution)/shard_map/middle/pallas_call | solution.py:61
  115.3 4.2 collective-permute-start.14
  119.9 6.8 %collective-permute-done.13.refs_1_ = bf16[160,1152]{1,0:T(8,128)(2,1)S(1)} collective-permute-done((bf16[160,1152]{1,0:T(8,128)(2,1)}, bf16[160,1152]{1,0:T(8,128)(2,1)S(1)}, u32[]{:S(2)}, u32[]{:S(2)}) %collective-permute-start.13) | collective-permute-done | bytes 368672 | tf_op jit(solution)/shard_map/ppermute | solution.py:33
  126.7 20.7 %collective-permute-done.14.refs_2_ = bf16[160,1152]{1,0:T(8,128)(2,1)S(1)} collective-permute-done((bf16[160,1152]{1,0:T(8,128)(2,1)}, bf16[160,1152]{1,0:T(8,128)(2,1)S(1)}, u32[]{:S(2)}, u32[]{:S(2)}) %collective-permute-start.14) | collective-permute-done | bytes 368672 | tf_op jit(solution)/shard_map/ppermute | solution.py:33
  147.4 3.8 collective-permute-done.15.refs_3_
  152.0 8.5 %up_project.1 = (f32[640,1536]{1,0:T(8,128)}, bf16[640,1536]{1,0:T(8,128)(2,1)}, bf16[640,1152]{1,0:T(8,128)(2,1)}) custom-call(s32[10]{0:T(128)} %stack.65.table, bf16[160,1152]{1,0:T(8,128)(2,1)} %get-tuple-element.97.refs_0_, bf16[160,1152]{1,0:T(8,128)(2,1)} %copy-done.37, bf16[160,1152]{1,0:T(8,128)(2,1)} %copy-done.38, bf16[160,1152]{1,0:T(8,128)(2,1)} %copy-done.39, ...), custom_call_target="tpu_custom_call" | custom-call | bytes 123863 | tf_op jit(solution)/shard_map/up_project/pallas_call | solution.py:61
  163.5 9.4 %mix.1 = (bf16[640,768]{1,0:T(8,128)(2,1)}, bf16[2,640,768]{2,1,0:T(8,128)(2,1)}) custom-call(s32[10]{0:T(128)} %stack.65.table, bf16[640,1536]{1,0:T(8,128)(2,1)} %get-tuple-element.98.value.gate.activated, bf16[640,1536]{1,0:T(8,128)(2,1)} %get-tuple-element.98.value.gate.activated, bf16[32,1536]{1,0:T(8,128)(2,1)} %copy-done.19, ...), custom_call_target="tpu_custom_call" | custom-call | bytes 92405 | tf_op jit(solution)/shard_map/mix/pallas_call | solution.py:61
  172.8 3.8 convolution_convert_fusion.2
  176.6 3.5 all-to-all-start.2
  183.2 14.8 %mix_back.1 = (bf16[640,1536]{1,0:T(8,128)(2,1)}, f32[16,1536]{1,0:T(8,128)}) custom-call(s32[10]{0:T(128)} %stack.65.table, bf16[2,640,768]{2,1,0:T(8,128)(2,1)} %get-tuple-element.102.grads, bf16[2,32,768]{2,1,0:T(8,128)(2,1)} %copy-done.40, bf16[640,1536]{1,0:T(8,128)(2,1)} %get-tuple-element.98.value.gate.activated, bf16[32,1536]{1,0:T(8,128)(2,1)} %copy-done.19, ...), custom_call_target="tpu_custom_call" | custom-call | bytes 102236 | tf_op jit(solution)/shard_map/mix_back/pallas_call | solution.py:61
  198.0 4.2 convolution_convert_fusion.1
  207.4 5.8 %all-to-all-done.2.branches = bf16[4,160,1152]{2,1,0:T(8,128)(2,1)S(1)} async-done(((bf16[4,160,1152]{2,1,0:T(8,128)(2,1)}), bf16[4,160,1152]{2,1,0:T(8,128)(2,1)S(1)}, u32[]{:S(2)}, u32[]{:S(2)}) %all-to-all-start.2) | async-done | bytes 1474592 | tf_op jit(solution)/shard_map/all_to_all | solution.py:37
  214.4 3.7 output.1
  218.1 9.4 %ffn_parts.1 = bf16[1152,2304]{1,0:T(8,128)(2,1)} custom-call(s32[10]{0:T(128)} %stack.65.table, bf16[640,1152]{1,0:T(8,128)(2,1)} %copy-done.7, bf16[640,768]{1,0:T(8,128)(2,1)} %get-tuple-element.107.hidden, bf16[640,1152]{1,0:T(8,128)(2,1)} %get-tuple-element.108.normed, bf16[640,1536]{1,0:T(8,128)(2,1)} %get-tuple-element.105.grad_up), custom_call_target="tpu_custom_call" | custom-call | bytes 112066 | tf_op jit(solution)/shard_map/ffn_parts/pallas_call | solution.py:61
  227.5 9.4 %collective-permute-done.18.grad_1 = bf16[160,1152]{1,0:T(8,128)(2,1)S(1)} collective-permute-done((bf16[160,1152]{1,0:T(8,128)(2,1)}, bf16[160,1152]{1,0:T(8,128)(2,1)S(1)}, u32[]{:S(2)}, u32[]{:S(2)}) %collective-permute-start.18) | collective-permute-done | bytes 368672 | tf_op jit(solution)/shard_map/ppermute | solution.py:33
  236.8 7.4 %collective-permute-done.19.grad_2 = bf16[160,1152]{1,0:T(8,128)(2,1)} collective-permute-done((bf16[160,1152]{1,0:T(8,128)(2,1)}, bf16[160,1152]{1,0:T(8,128)(2,1)}, u32[]{:S(2)}, u32[]{:S(2)}) %collective-permute-start.19) | collective-permute-done | bytes 368672 | tf_op jit(solution)/shard_map/ppermute | solution.py:33
  245.5 4.1 collective-permute-start.22
  249.9 25.7 %middle_back.1 = (bf16[160,1152]{1,0:T(8,128)(2,1)}, bf16[4,160,288]{2,1,0:T(8,128)(2,1)}, bf16[160,1152]{1,0:T(8,128)(2,1)}, bf16[4,160,288]{2,1,0:T(8,128)(2,1...) custom-call(s32[10]{0:T(128)} %stack.65.table, ...), custom_call_target="tpu_custom_call" | custom-call | bytes 251023 | tf_op jit(solution)/shard_map/middle_back/pallas_call | solution.py:61
  276.6 3.3 collective-permute-done.23
  280.8 3.5 all-to-all-start.3
  285.5 10.2 %square_parts.1 = (bf16[1152,3584]{1,0:T(8,128)(2,1)}, bf16[4,304,576]{2,1,0:T(8,128)(2,1)}) custom-call(s32[10]{0:T(128)} %stack.65.table, bf16[160,1152]{1,0:T(8,128)(2,1)} %get-tuple-element.116.dyc, bf16[4,160,288]{2,1,0:T(8,128)(2,1)} %get-tuple-element.117.text, bf16[160,1152]{1,0:T(8,128)(2,1)} %get-tuple-element.118.x1, ...), custom_call_target="tpu_custom_call" | custom-call | bytes 146718 | tf_op jit(solution)/shard_map/square_parts/pallas_call | solution.py:61
  296.7 6.1 %all-to-all-start.4 = ((bf16[4,304,576]{2,1,0:T(8,128)(2,1)}), bf16[4,304,576]{2,1,0:T(8,128)(2,1)S(1)}, u32[]{:S(2)}, u32[]{:S(2)}) async-start(bf16[4,304,576]{2,1,0:T(8,128)(2,1)} %get-tuple-element.127), calls=%async_computation.5 | async-start | bytes 3112960 | tf_op jit(solution)/shard_map/all_to_all | solution.py:37
  303.3 11.9 %self_back.1 = (f32[640,288]{1,0:T(8,128)}, f32[288,128]{1,0:T(8,128)}, f32[288,128]{1,0:T(8,128)}) custom-call(s32[10]{0:T(128)} %stack.65.table, bf16[4,160,288]{2,1,0:T(8,128)(2,1)} %copy-done.13, bf16[640,288]{1,0:T(8,128)(2,1)} %get-tuple-element.85.q, f32[640,288]{1,0:T(8,128)} %get-tuple-element.130.wide_out, ...), custom_call_target="tpu_custom_call" | custom-call | bytes 35389 | tf_op jit(solution)/shard_map/self_back/pallas_call | solution.py:61
  319.8 7.8 %self_project_back.1.grad_projected = bf16[640,864]{1,0:T(8,128)(2,1)} custom-call(s32[10]{0:T(128)} %stack.65.table, f32[640,288]{1,0:T(8,128)} %get-tuple-element.132.grad_q, bf16[640,288]{1,0:T(8,128)(2,1)} %get-tuple-element.133.k, bf16[640,288]{1,0:T(8,128)(2,1)} %get-tuple-element.134.v, f32[640,576]{1,0:T(8,128)} %get-tuple-element.135.raw, ...), custom_call_target="tpu_custom_call" | custom-call | bytes 43499 | tf_op jit(solution)/shard_map/self_project_back/pallas_call | solution.py:61
  327.6 3.1 convolution_convert_fusion
  338.7 7.8 %late_parts.1 = bf16[1152,1440]{1,0:T(8,128)(2,1)} custom-call(s32[10]{0:T(128)} %stack.65.table, bf16[640,1152]{1,0:T(8,128)(2,1)} %get-tuple-element.138.normed, bf16[640,864]{1,0:T(8,128)(2,1)} %self_project_back.1.grad_projected, bf16[304,1152]{1,0:T(8,128)(2,1)} %pad.16.text, bf16[4,304,576]{2,1,0:T(8,128)(2,1)} %copy-done.6), custom_call_target="tpu_custom_call" | custom-call | bytes 79994 | tf_op jit(solution)/shard_map/late_parts/pallas_call | solution.py:61
  346.5 31.6 %reduce-scatter.6.cloned.1.call-done = bf16[144,3584]{1,0:T(8,128)(2,1)} async-done(((bf16[1152,3584]{1,0:T(8,128)(2,1)}), bf16[144,3584]{1,0:T(8,128)(2,1)}) %reduce-scatter.6.cloned.1.call-update) | async-done | bytes 1032208 | tf_op jit(solution)/shard_map/reduce_scatter | solution.py:829
  384.1 5.2 %all-to-all-start.5 = ((bf16[4,144,896]{2,1,0:T(8,128)(2,1)}), bf16[4,144,896]{2,1,0:T(8,128)(2,1)S(1)}, u32[]{:S(2)}, u32[]{:S(2)}) async-start(bf16[4,144,896]{2,1,0:T(8,128)(2,1)} %bitcast.109), calls=%async_computation.7 | async-start | bytes 2064384 | tf_op jit(solution)/shard_map/all_to_all | solution.py:37
  389.2 4.2 first_norm_back.1
  396.6 2.9 collective-permute-start.31
  401.7 6.7 %collective-permute-done.30 = f32[6,1152]{1,0:T(8,128)S(1)} collective-permute-done((f32[6,1152]{1,0:T(8,128)S(1)}, f32[6,1152]{1,0:T(8,128)S(1)}, u32[]{:S(2)}, u32[]{:S(2)}) %collective-permute-start.30) | collective-permute-done | bytes 27680 | tf_op jit(solution)/shard_map/ppermute | solution.py:823
  408.4 6.0 %collective-permute-done.31 = f32[6,1152]{1,0:T(8,128)S(1)} collective-permute-done((f32[6,1152]{1,0:T(8,128)S(1)}, f32[6,1152]{1,0:T(8,128)S(1)}, u32[]{:S(2)}, u32[]{:S(2)}) %collective-permute-start.31) | collective-permute-done | bytes 27680 | tf_op jit(solution)/shard_map/ppermute | solution.py:823
  414.3 2.3 collective-permute-done.32
  417.9 2.9 collective-permute-start.34
  421.8 7.9 %reduce-scatter.8.cloned.1.call-done = bf16[144,1440]{1,0:T(8,128)(2,1)} async-done(((bf16[1152,1440]{1,0:T(8,128)(2,1)}), bf16[144,1440]{1,0:T(8,128)(2,1)}) %reduce-scatter.8.cloned.1.call-update) | async-done | bytes 414736 | tf_op jit(solution)/shard_map/reduce_scatter | solution.py:829
  434.2 8.6 %collective-permute-done.33 = bf16[160,1152]{1,0:T(8,128)(2,1)S(1)} collective-permute-done((bf16[160,1152]{1,0:T(8,128)(2,1)S(1)}, bf16[160,1152]{1,0:T(8,128)(2,1)S(1)}, u32[]{:S(2)}, u32[]{:S(2)}) %collective-permute-start.33) | collective-permute-done | bytes 368672 | tf_op jit(solution)/shard_map/ppermute | solution.py:33
  442.7 6.0 %collective-permute-done.34 = bf16[160,1152]{1,0:T(8,128)(2,1)S(1)} collective-permute-done((bf16[160,1152]{1,0:T(8,128)(2,1)S(1)}, bf16[160,1152]{1,0:T(8,128)(2,1)S(1)}, u32[]{:S(2)}, u32[]{:S(2)}) %collective-permute-start.34) | collective-permute-done | bytes 368672 | tf_op jit(solution)/shard_map/ppermute | solution.py:33
  448.7 2.8 collective-permute-done.35
  (233 shorter events, 81.8 us)
Async XLA Ops:
  9.7 31.6 %collective-permute-start.2 = (bf16[112,1152]{1,0:T(8,128)(2,1)}, bf16[112,1152]{1,0:T(8,128)(2,1)S(1)}, u32[]{:S(2)}, u32[]{:S(2)}) collective-permute-start(bf16[112,1152]{1,0:T(8,128)(2,1)} %eighth.1), channel_id=1, source_target_pairs={{0,1},{1,2},{2,3},{3,0},{4,5},{5,6},{6,7},{7,4},{8,9},{9,10},{10,1... | collective-permute-start | bytes 774152 | tf_op jit(solution)/shard_map/ppermute | solution.py:33
  11.3 30.0 %collective-permute-start.3 = (bf16[112,1152]{1,0:T(8,128)(2,1)}, bf16[112,1152]{1,0:T(8,128)(2,1)}, u32[]{:S(2)}, u32[]{:S(2)}) collective-permute-start(bf16[112,1152]{1,0:T(8,128)(2,1)} %eighth.1), channel_id=1, source_target_pairs={{0,2},{1,3},{2,0},{3,1},{4,6},{5,7},{6,4},{7,5},{8,10},{9,11},{10,... | collective-permute-start | bytes 774152 | tf_op jit(solution)/shard_map/ppermute | solution.py:33
  12.3 31.6 %collective-permute-start.4 = (bf16[112,1152]{1,0:T(8,128)(2,1)}, bf16[112,1152]{1,0:T(8,128)(2,1)}, u32[]{:S(2)}, u32[]{:S(2)}) collective-permute-start(bf16[112,1152]{1,0:T(8,128)(2,1)} %eighth.1), channel_id=1, source_target_pairs={{0,3},{1,0},{2,1},{3,2},{4,7},{5,4},{6,5},{7,6},{8,11},{9,8},{10,9... | collective-permute-start | bytes 774152 | tf_op jit(solution)/shard_map/ppermute | solution.py:33
  14.3 14.3 %collective-permute-start = (bf16[6,1152]{1,0:T(8,128)(2,1)S(1)}, bf16[6,1152]{1,0:T(8,128)(2,1)S(1)}, u32[]{:S(2)}, u32[]{:S(2)}) collective-permute-start(bf16[6,1152]{1,0:T(8,128)(2,1)S(1)} %bitcast.150), channel_id=1, source_target_pairs={{0,4},{4,0},{8,12},{12,8},{16,20},{20,16},{24,28},{28,24},{1,5},{5... | collective-permute-start | bytes 41480 | tf_op jit(solution)/shard_map/ppermute | solution.py:28
  16.4 50.6 %all-to-all-start = ((bf16[4,304,576]{2,1,0:T(8,128)(2,1)}), bf16[4,304,576]{2,1,0:T(8,128)(2,1)S(1)}, u32[]{:S(2)}, u32[]{:S(2)}) async-start(bf16[4,304,576]{2,1,0:T(8,128)(2,1)} %broadcast_in_dim.63), calls=%async_computation | async-start | bytes 3112960 | tf_op jit(solution)/shard_map/all_to_all | solution.py:37
  39.8 9.8 %collective-permute-start.1 = (f32[2,288,128]{2,1,0:T(8,128)S(1)}, f32[2,288,128]{2,1,0:T(8,128)S(1)}, u32[]{:S(2)}, u32[]{:S(2)}) collective-permute-start(f32[2,288,128]{2,1,0:T(8,128)S(1)} %pad_maximum_fusion.1), channel_id=1, source_target_pairs={{0,4},{4,0},{8,12},{12,8},{16,20},{20,16},{24,28},{28,24},{1,5},{5... | collective-permute-start | bytes 884744 | tf_op jit(solution)/shard_map/ppermute | solution.py:28
  46.1 28.7 %collective-permute-start.6 = (bf16[3,112,1152]{2,1,0:T(8,128)(2,1)}, bf16[3,112,1152]{2,1,0:T(8,128)(2,1)}, u32[]{:S(2)}, u32[]{:S(2)}) collective-permute-start(bf16[3,112,1152]{2,1,0:T(8,128)(2,1)} %pad_maximum_fusion.refs_0_), channel_id=1, source_target_pairs={{0,8},{4,12},{8,0},{12,4},{16,24},{20,28},{24,16},{28,20},{1,9},{5... | collective-permute-start | bytes 2322440 | tf_op jit(solution)/shard_map/ppermute | solution.py:752
  47.6 35.7 %collective-permute-start.7 = (bf16[3,112,1152]{2,1,0:T(8,128)(2,1)}, bf16[3,112,1152]{2,1,0:T(8,128)(2,1)}, u32[]{:S(2)}, u32[]{:S(2)}) collective-permute-start(bf16[3,112,1152]{2,1,0:T(8,128)(2,1)} %pad_maximum_fusion.refs_0_), channel_id=1, source_target_pairs={{0,16},{4,20},{8,24},{12,28},{16,0},{20,4},{24,8},{28,12},{1,17},{... | collective-permute-start | bytes 2322440 | tf_op jit(solution)/shard_map/ppermute | solution.py:752
  49.1 34.2 %collective-permute-start.8 = (bf16[3,112,1152]{2,1,0:T(8,128)(2,1)}, bf16[3,112,1152]{2,1,0:T(8,128)(2,1)}, u32[]{:S(2)}, u32[]{:S(2)}) collective-permute-start(bf16[3,112,1152]{2,1,0:T(8,128)(2,1)} %pad_maximum_fusion.refs_0_), channel_id=1, source_target_pairs={{0,24},{4,28},{8,16},{12,20},{16,8},{20,12},{24,0},{28,4},{1,25},{... | collective-permute-start | bytes 2322440 | tf_op jit(solution)/shard_map/ppermute | solution.py:752
  67.1 23.9 %collective-permute-start.12 = (bf16[4,304,576]{2,1,0:T(8,128)(2,1)S(1)}, bf16[4,304,576]{2,1,0:T(8,128)(2,1)S(1)}, u32[]{:S(2)}, u32[]{:S(2)}) collective-permute-start(bf16[4,304,576]{2,1,0:T(8,128)(2,1)S(1)} %all-to-all-done.refs_8_.kv_own), channel_id=1, source_target_pairs={{0,4},{4,0},{8,12},{12,8},{16,20},{20,16},{24,28},{28,24},{1,5},{5... | collective-permute-start | bytes 4202504 | tf_op jit(solution)/shard_map/ppermute | solution.py:28
  67.1 19.2 %all-to-all-start.1 = ((bf16[4,160,288]{2,1,0:T(8,128)(2,1)}), bf16[4,160,288]{2,1,0:T(8,128)(2,1)}, u32[]{:S(2)}, u32[]{:S(2)}) async-start(bf16[4,160,288]{2,1,0:T(8,128)(2,1)} %bitcast.143), calls=%async_computation.1 | async-start | bytes 983040 | tf_op jit(solution)/shard_map/all_to_all | solution.py:37
  74.7 12.1 %collective-permute-start.5 = (bf16[3,112,1152]{2,1,0:T(8,128)(2,1)}, bf16[3,112,1152]{2,1,0:T(8,128)(2,1)}, u32[]{:S(2)}, u32[]{:S(2)}) collective-permute-start(bf16[3,112,1152]{2,1,0:T(8,128)(2,1)} %pad_maximum_fusion.refs_0_), channel_id=1, source_target_pairs={{0,4},{4,0},{8,12},{12,8},{16,20},{20,16},{24,28},{28,24},{1,5},{5... | collective-permute-start | bytes 2322440 | tf_op jit(solution)/shard_map/ppermute | solution.py:28
  86.3 2.5 collective-permute-start.10
  86.3 3.6 collective-permute-start.11
  86.8 4.2 collective-permute-start.9
  114.0 12.7 %collective-permute-start.13 = (bf16[160,1152]{1,0:T(8,128)(2,1)}, bf16[160,1152]{1,0:T(8,128)(2,1)S(1)}, u32[]{:S(2)}, u32[]{:S(2)}) collective-permute-start(bf16[160,1152]{1,0:T(8,128)(2,1)} %get-tuple-element.97.refs_0_), channel_id=1, source_target_pairs={{0,1},{1,2},{2,3},{3,0},{4,5},{5,6},{6,7},{7,4},{8,9},{9,10},{10,1... | collective-permute-start | bytes 1105928 | tf_op jit(solution)/shard_map/ppermute | solution.py:33
  115.3 32.2 %collective-permute-start.14 = (bf16[160,1152]{1,0:T(8,128)(2,1)}, bf16[160,1152]{1,0:T(8,128)(2,1)S(1)}, u32[]{:S(2)}, u32[]{:S(2)}) collective-permute-start(bf16[160,1152]{1,0:T(8,128)(2,1)} %get-tuple-element.97.refs_0_), channel_id=1, source_target_pairs={{0,2},{1,3},{2,0},{3,1},{4,6},{5,7},{6,4},{7,5},{8,10},{9,11},{10,... | collective-permute-start | bytes 1105928 | tf_op jit(solution)/shard_map/ppermute | solution.py:33
  119.5 31.7 %collective-permute-start.15 = (bf16[160,1152]{1,0:T(8,128)(2,1)}, bf16[160,1152]{1,0:T(8,128)(2,1)S(1)}, u32[]{:S(2)}, u32[]{:S(2)}) collective-permute-start(bf16[160,1152]{1,0:T(8,128)(2,1)} %get-tuple-element.97.refs_0_), channel_id=1, source_target_pairs={{0,3},{1,0},{2,1},{3,2},{4,7},{5,4},{6,5},{7,6},{8,11},{9,8},{10,9... | collective-permute-start | bytes 1105928 | tf_op jit(solution)/shard_map/ppermute | solution.py:33
  161.5 1.4 collective-permute-start.16
  176.6 36.6 %all-to-all-start.2 = ((bf16[4,160,1152]{2,1,0:T(8,128)(2,1)}), bf16[4,160,1152]{2,1,0:T(8,128)(2,1)S(1)}, u32[]{:S(2)}, u32[]{:S(2)}) async-start(bf16[4,160,1152]{2,1,0:T(8,128)(2,1)} %bitcast.32), calls=%async_computation.2 | async-start | bytes 2949120 | tf_op jit(solution)/shard_map/all_to_all | solution.py:37
  180.2 123.1 %reduce-scatter.4.cloned.1.call-start = ((), (), s32[]{:S(2)}) async-start(), calls=%async_computation.9 | async-start | bytes 5971968 | tf_op jit(solution)/shard_map/reduce_scatter | solution.py:829
  181.2 1.4 collective-permute-start.17
  203.4 33.5 %collective-permute-start.18 = (bf16[160,1152]{1,0:T(8,128)(2,1)}, bf16[160,1152]{1,0:T(8,128)(2,1)S(1)}, u32[]{:S(2)}, u32[]{:S(2)}) collective-permute-start(bf16[160,1152]{1,0:T(8,128)(2,1)} %get-tuple-element.182), channel_id=1, source_target_pairs={{0,1},{1,2},{2,3},{3,0},{4,5},{5,6},{6,7},{7,4},{8,9},{9,10},{10,1... | collective-permute-start | bytes 1105928 | tf_op jit(solution)/shard_map/ppermute | solution.py:33
  204.5 39.8 %collective-permute-start.19 = (bf16[160,1152]{1,0:T(8,128)(2,1)}, bf16[160,1152]{1,0:T(8,128)(2,1)}, u32[]{:S(2)}, u32[]{:S(2)}) collective-permute-start(bf16[160,1152]{1,0:T(8,128)(2,1)} %get-tuple-element.181), channel_id=1, source_target_pairs={{0,2},{1,3},{2,0},{3,1},{4,6},{5,7},{6,4},{7,5},{8,10},{9,11},{10,... | collective-permute-start | bytes 1105928 | tf_op jit(solution)/shard_map/ppermute | solution.py:33
  205.4 40.0 %collective-permute-start.20 = (bf16[160,1152]{1,0:T(8,128)(2,1)}, bf16[160,1152]{1,0:T(8,128)(2,1)}, u32[]{:S(2)}, u32[]{:S(2)}) collective-permute-start(bf16[160,1152]{1,0:T(8,128)(2,1)} %get-tuple-element.180), channel_id=1, source_target_pairs={{0,3},{1,0},{2,1},{3,2},{4,7},{5,4},{6,5},{7,6},{8,11},{9,8},{10,9... | collective-permute-start | bytes 1105928 | tf_op jit(solution)/shard_map/ppermute | solution.py:33
  245.4 30.2 %collective-permute-start.21 = (bf16[160,1152]{1,0:T(8,128)(2,1)S(1)}, bf16[160,1152]{1,0:T(8,128)(2,1)S(1)}, u32[]{:S(2)}, u32[]{:S(2)}) collective-permute-start(bf16[160,1152]{1,0:T(8,128)(2,1)S(1)} %copy-done.28), channel_id=1, source_target_pairs={{0,1},{1,2},{2,3},{3,0},{4,5},{5,6},{6,7},{7,4},{8,9},{9,10},{10,1... | collective-permute-start | bytes 1105928 | tf_op jit(solution)/shard_map/ppermute | solution.py:33
  245.5 31.1 %collective-permute-start.22 = (bf16[160,1152]{1,0:T(8,128)(2,1)S(1)}, bf16[160,1152]{1,0:T(8,128)(2,1)S(1)}, u32[]{:S(2)}, u32[]{:S(2)}) collective-permute-start(bf16[160,1152]{1,0:T(8,128)(2,1)S(1)} %copy-done.28), channel_id=1, source_target_pairs={{0,2},{1,3},{2,0},{3,1},{4,6},{5,7},{6,4},{7,5},{8,10},{9,11},{10,... | collective-permute-start | bytes 1105928 | tf_op jit(solution)/shard_map/ppermute | solution.py:33
  249.6 30.3 %collective-permute-start.23 = (bf16[160,1152]{1,0:T(8,128)(2,1)S(1)}, bf16[160,1152]{1,0:T(8,128)(2,1)S(1)}, u32[]{:S(2)}, u32[]{:S(2)}) collective-permute-start(bf16[160,1152]{1,0:T(8,128)(2,1)S(1)} %copy-done.28), channel_id=1, source_target_pairs={{0,3},{1,0},{2,1},{3,2},{4,7},{5,4},{6,5},{7,6},{8,11},{9,8},{10,9... | collective-permute-start | bytes 1105928 | tf_op jit(solution)/shard_map/ppermute | solution.py:33
  280.7 3.6 collective-permute-start.24
  280.8 15.1 %all-to-all-start.3 = ((bf16[4,160,288]{2,1,0:T(8,128)(2,1)}), bf16[4,160,288]{2,1,0:T(8,128)(2,1)S(1)}, u32[]{:S(2)}, u32[]{:S(2)}) async-start(bf16[4,160,288]{2,1,0:T(8,128)(2,1)} %get-tuple-element.115), calls=%async_computation.3 | async-start | bytes 983040 | tf_op jit(solution)/shard_map/all_to_all | solution.py:37
  284.3 93.8 %reduce-scatter.6.cloned.1.call-start = ((), (), s32[]{:S(2)}) async-start(), calls=%async_computation.10 | async-start | bytes 9289728 | tf_op jit(solution)/shard_map/reduce_scatter | solution.py:829
  296.7 40.9 %all-to-all-start.4 = ((bf16[4,304,576]{2,1,0:T(8,128)(2,1)}), bf16[4,304,576]{2,1,0:T(8,128)(2,1)S(1)}, u32[]{:S(2)}, u32[]{:S(2)}) async-start(bf16[4,304,576]{2,1,0:T(8,128)(2,1)} %get-tuple-element.127), calls=%async_computation.5 | async-start | bytes 3112960 | tf_op jit(solution)/shard_map/all_to_all | solution.py:37
  302.8 126.9 %reduce-scatter.8.cloned.1.call-start = ((), (), s32[]{:S(2)}) async-start(), calls=%async_computation.11 | async-start | bytes 3981312 | tf_op jit(solution)/shard_map/reduce_scatter | solution.py:829
  316.3 1.6 collective-permute-start.25
  331.7 46.4 %collective-permute-start.26 = (bf16[160,1152]{1,0:T(8,128)(2,1)}, bf16[160,1152]{1,0:T(8,128)(2,1)}, u32[]{:S(2)}, u32[]{:S(2)}) collective-permute-start(bf16[160,1152]{1,0:T(8,128)(2,1)} %get-tuple-element.179), channel_id=1, source_target_pairs={{0,1},{1,2},{2,3},{3,0},{4,5},{5,6},{6,7},{7,4},{8,9},{9,10},{10,1... | collective-permute-start | bytes 1105928 | tf_op jit(solution)/shard_map/ppermute | solution.py:33
  333.1 45.0 %collective-permute-start.27 = (bf16[160,1152]{1,0:T(8,128)(2,1)}, bf16[160,1152]{1,0:T(8,128)(2,1)}, u32[]{:S(2)}, u32[]{:S(2)}) collective-permute-start(bf16[160,1152]{1,0:T(8,128)(2,1)} %get-tuple-element.178), channel_id=1, source_target_pairs={{0,2},{1,3},{2,0},{3,1},{4,6},{5,7},{6,4},{7,5},{8,10},{9,11},{10,... | collective-permute-start | bytes 1105928 | tf_op jit(solution)/shard_map/ppermute | solution.py:33
  334.6 43.5 %collective-permute-start.28 = (bf16[160,1152]{1,0:T(8,128)(2,1)S(1)}, bf16[160,1152]{1,0:T(8,128)(2,1)}, u32[]{:S(2)}, u32[]{:S(2)}) collective-permute-start(bf16[160,1152]{1,0:T(8,128)(2,1)S(1)} %get-tuple-element.177), channel_id=1, source_target_pairs={{0,3},{1,0},{2,1},{3,2},{4,7},{5,4},{6,5},{7,6},{8,11},{9,8},{10,9... | collective-permute-start | bytes 1105928 | tf_op jit(solution)/shard_map/ppermute | solution.py:33
  380.2 1.4 collective-permute-start.36
  381.6 14.2 %collective-permute-start.37 = (f32[9,1536]{1,0:T(8,128)S(1)}, f32[9,1536]{1,0:T(8,128)S(1)}, u32[]{:S(2)}, u32[]{:S(2)}) collective-permute-start(f32[9,1536]{1,0:T(8,128)S(1)} %add.194), channel_id=1, source_target_pairs={{0,8},{4,12},{8,0},{12,4},{16,24},{20,28},{24,16},{28,20},{1,9},{5... | collective-permute-start | bytes 165896 | tf_op jit(solution)/shard_map/ppermute | solution.py:28
  384.1 33.2 %all-to-all-start.5 = ((bf16[4,144,896]{2,1,0:T(8,128)(2,1)}), bf16[4,144,896]{2,1,0:T(8,128)(2,1)S(1)}, u32[]{:S(2)}, u32[]{:S(2)}) async-start(bf16[4,144,896]{2,1,0:T(8,128)(2,1)} %bitcast.109), calls=%async_computation.7 | async-start | bytes 2064384 | tf_op jit(solution)/shard_map/all_to_all | solution.py:37
  394.4 2.1 collective-permute-start.29
  395.8 5.3 %collective-permute-start.38 = (f32[9,1536]{1,0:T(8,128)S(1)}, f32[9,1536]{1,0:T(8,128)S(1)}, u32[]{:S(2)}, u32[]{:S(2)}) collective-permute-start(f32[9,1536]{1,0:T(8,128)S(1)} %add.195), channel_id=1, source_target_pairs={{0,16},{4,20},{8,24},{12,28},{16,0},{20,4},{24,8},{28,12},{1,17},{... | collective-permute-start | bytes 165896 | tf_op jit(solution)/shard_map/ppermute | solution.py:28
  396.5 11.8 %collective-permute-start.30 = (f32[6,1152]{1,0:T(8,128)S(1)}, f32[6,1152]{1,0:T(8,128)S(1)}, u32[]{:S(2)}, u32[]{:S(2)}) collective-permute-start(f32[6,1152]{1,0:T(8,128)S(1)} %fusion.4), channel_id=1, source_target_pairs={{0,1},{1,0},{2,3},{3,2},{4,5},{5,4},{6,7},{7,6},{8,9},{9,8},{10,11... | collective-permute-start | bytes 82952 | tf_op jit(solution)/shard_map/ppermute | solution.py:823
  396.6 17.7 %collective-permute-start.31 = (f32[6,1152]{1,0:T(8,128)S(1)}, f32[6,1152]{1,0:T(8,128)S(1)}, u32[]{:S(2)}, u32[]{:S(2)}) collective-permute-start(f32[6,1152]{1,0:T(8,128)S(1)} %fusion.4), channel_id=1, source_target_pairs={{0,2},{1,3},{2,0},{3,1},{4,6},{5,7},{6,4},{7,5},{8,10},{9,11},{10,... | collective-permute-start | bytes 82952 | tf_op jit(solution)/shard_map/ppermute | solution.py:823
  399.5 17.2 %collective-permute-start.32 = (f32[6,1152]{1,0:T(8,128)S(1)}, f32[6,1152]{1,0:T(8,128)S(1)}, u32[]{:S(2)}, u32[]{:S(2)}) collective-permute-start(f32[6,1152]{1,0:T(8,128)S(1)} %fusion.4), channel_id=1, source_target_pairs={{0,3},{1,2},{2,1},{3,0},{4,7},{5,6},{6,5},{7,4},{8,11},{9,10},{10,... | collective-permute-start | bytes 82952 | tf_op jit(solution)/shard_map/ppermute | solution.py:823
  417.3 25.4 %collective-permute-start.33 = (bf16[160,1152]{1,0:T(8,128)(2,1)S(1)}, bf16[160,1152]{1,0:T(8,128)(2,1)S(1)}, u32[]{:S(2)}, u32[]{:S(2)}) collective-permute-start(bf16[160,1152]{1,0:T(8,128)(2,1)S(1)} %copy-done.36), channel_id=1, source_target_pairs={{0,1},{1,2},{2,3},{3,0},{4,5},{5,6},{6,7},{7,4},{8,9},{9,10},{10,1... | collective-permute-start | bytes 1105928 | tf_op jit(solution)/shard_map/ppermute | solution.py:33
  417.9 30.9 %collective-permute-start.34 = (bf16[160,1152]{1,0:T(8,128)(2,1)S(1)}, bf16[160,1152]{1,0:T(8,128)(2,1)S(1)}, u32[]{:S(2)}, u32[]{:S(2)}) collective-permute-start(bf16[160,1152]{1,0:T(8,128)(2,1)S(1)} %copy-done.36), channel_id=1, source_target_pairs={{0,2},{1,3},{2,0},{3,1},{4,6},{5,7},{6,4},{7,5},{8,10},{9,11},{10,... | collective-permute-start | bytes 1105928 | tf_op jit(solution)/shard_map/ppermute | solution.py:33
  420.7 30.8 %collective-permute-start.35 = (bf16[160,1152]{1,0:T(8,128)(2,1)S(1)}, bf16[160,1152]{1,0:T(8,128)(2,1)S(1)}, u32[]{:S(2)}, u32[]{:S(2)}) collective-permute-start(bf16[160,1152]{1,0:T(8,128)(2,1)S(1)} %copy-done.36), channel_id=1, source_target_pairs={{0,3},{1,0},{2,1},{3,2},{4,7},{5,4},{6,5},{7,6},{8,11},{9,8},{10,9... | collective-permute-start | bytes 1105928 | tf_op jit(solution)/shard_map/ppermute | solution.py:33
  (50 other events, 343.7 us)
Sparse Core Ops, SparseCore 0:
  245.5 57.7 reduce-scatter.3
  307.4 70.6 reduce-scatter.5
  381.6 48.0 reduce-scatter.7

commit v7 on v5

--- a/solution.py
+++ b/solution.py
@@ -1118,9 +1118,6 @@
         table=table,
     )[0]
     late_rows = sum_rows(after(late_parts, square_rows, grad_normed))
-    conv_sum = after(tap_part[:9], normed_sent)
-    for place in range(lax.axis_size("seq").bit_length() - 1):
-        conv_sum = conv_sum + swapped(conv_sum, "seq", place)
     square_sent = square_rows.reshape(square_rows.shape[0], count, -1).transpose(1, 0, 2)
     input_block, first_sums = call(
         first_norm_back_body,
@@ -1144,6 +1141,9 @@
     pairs = pairs[:, 0] + swapped(pairs[:, 1], "seq", 0)
     modulation_grad = same_everywhere(pairs)
     input_block = after(input_block, square_parts_here, modulation_grad)
+    conv_sum = after(tap_part[:9], input_block)
+    for place in range(lax.axis_size("seq").bit_length() - 1):
+        conv_sum = conv_sum + swapped(conv_sum, "seq", place)
     late_rows = late_rows.astype(WIDE)
     qkv_grad = late_rows[:, : 3 * self_cols].reshape(-1, 3, self_cols)
     ckv_grad = late_rows[:, 3 * self_cols :].reshape(-1, 2, cross_cols)

time: 468 us -> 470 us (level)
    ppermute x15, waiting for transfers between devices: 8.37 us -> 16.4 us  [swapped(): return lax.ppermute(block, axis, route)]
    reduce_scatter x3, waiting for transfers between devices: 38.9 us -> 31 us  [sum_rows(): lax.psum_scatter(grad.astype(LOW), 'seq', scatter_dimension=0, tiled=True)]
    unnamed x101 -> x99, local copies, waits for them, and re-layouts: 12.5 us -> 10.6 us
  transfers between devices with their start and end apart: 48 -> 48, of which waited for: 30 -> 30; matrix products, arithmetic and copies ran while one was open for 9% -> 10% of each run, Pallas kernels for 25% -> 25%
where the time goes in v7:
time: 470 us; the launch traced here: 463 us
  Pallas kernels  158 us (34%)
  waiting for transfers between devices  154 us (33%)
  starting transfers between devices  69.5 us (15%)
  local copies, waits for them, and re-layouts  33.7 us (7%)
  between operations  18.6 us (4%)
  matrix products  14.8 us (3%)
  other arithmetic  14.3 us (3%)
    pallas_call x15, Pallas kernels, call(): pl.pallas_call(body, out_shape=shapes, grid_spec=pltpu.PrefetchScalarGrid...  158 us
    ppermute x18, waiting for transfers between devices, from_behind(): lax.ppermute(block, 'tp', [(k, (k + step) % count) for k in range(count)])  69.2 us
    all_to_all x6, starting transfers between devices, exchanged(): return lax.all_to_all(blocks, 'tp', 0, 0, tiled=True)  31.3 us
    reduce_scatter x3, waiting for transfers between devices, sum_rows(): lax.psum_scatter(grad.astype(LOW), 'seq', scatter_dimension=0, tiled=True)  31 us
    ppermute x18, starting transfers between devices, from_behind(): lax.ppermute(block, 'tp', [(k, (k + step) % count) for k in range(count)])  26.7 us
    ppermute x15, waiting for transfers between devices, swapped(): return lax.ppermute(block, axis, route)  16.4 us
    ppermute x3, waiting for transfers between devices, same_everywhere(): lax.ppermute(block, 'tp', [(k, k ^ flip) for k in range(count)])  15.6 us
    all_to_all x6, waiting for transfers between devices, exchanged(): return lax.all_to_all(blocks, 'tp', 0, 0, tiled=True)  13.1 us
  transfers between devices with their start and end apart: 48, of which 30 were waited for; matrix products, arithmetic and copies ran while one was open for 10% of the time, Pallas kernels for 25%

profile of v7, /device:TPU:8, one launch (start us, length us, event | category | flops | bytes accessed | tf_op | source)
XLA Modules:
  0.0 462.9 jit_solution(16352746346165940334)
XLA Ops:
  7.2 2.5 eighth.1
  16.4 5.0 %all-to-all-start = ((bf16[4,304,576]{2,1,0:T(8,128)(2,1)}), bf16[4,304,576]{2,1,0:T(8,128)(2,1)S(1)}, u32[]{:S(2)}, u32[]{:S(2)}) async-start(bf16[4,304,576]{2,1,0:T(8,128)(2,1)} %broadcast_in_dim.63), calls=%async_computation | async-start | bytes 3112960 | tf_op jit(solution)/shard_map/all_to_all | solution.py:37
  29.3 11.9 %self_project.1 = (bf16[640,1152]{1,0:T(8,128)(2,1)}, f32[640,576]{1,0:T(8,128)}, bf16[640,288]{1,0:T(8,128)(2,1)}, bf16[640,288]{1,0:T(8,128)(2,1)}, bf16[640,2...) custom-call(s32[10]{0:T(128)} %stack.65.table, bf16[640,1152]{1,0:T(8,128)(2,1)} %x.12, ...), custom_call_target="tpu_custom_call" | custom-call | bytes 78704 | tf_op jit(solution)/shard_map/self_project/pallas_call | solution.py:61
  44.0 2.5 pad_maximum_fusion.refs_0_
  50.7 6.9 %self_attend.1 = (bf16[640,288]{1,0:T(8,128)(2,1)}, f32[640,288]{1,0:T(8,128)}, f32[640,288]{1,0:T(8,128)}) custom-call(s32[10]{0:T(128)} %stack.65.table, bf16[640,288]{1,0:T(8,128)(2,1)} %get-tuple-element.85.q, f32[288,128]{1,0:T(8,128)} %get-tuple-element.189.own_fold, f32[288,128]{1,0:T(8,128)} %get-tuple-element.188.other_fold), custom_call_target="tpu_custom_call" | custom-call | bytes 25067 | tf_op jit(solution)/shard_map/self_attend/pallas_call | solution.py:61
  57.6 2.9 fusion.8.grad_hidden
  62.6 4.5 all-to-all-done.refs_8_.kv_own
  67.1 7.9 %all-to-all-start.1 = ((bf16[4,160,288]{2,1,0:T(8,128)(2,1)}), bf16[4,160,288]{2,1,0:T(8,128)(2,1)}, u32[]{:S(2)}, u32[]{:S(2)}) async-start(bf16[4,160,288]{2,1,0:T(8,128)(2,1)} %bitcast.142), calls=%async_computation.1 | async-start | bytes 983040 | tf_op jit(solution)/shard_map/all_to_all | solution.py:37
  75.2 8.9 %collective-permute-done.7.refs_4_ = bf16[3,112,1152]{2,1,0:T(8,128)(2,1)} collective-permute-done((bf16[3,112,1152]{2,1,0:T(8,128)(2,1)}, bf16[3,112,1152]{2,1,0:T(8,128)(2,1)}, u32[]{:S(2)}, u32[]{:S(2)}) %collective-permute-start.7) | collective-permute-done | bytes 774176 | tf_op jit(solution)/shard_map/ppermute | solution.py:752
  84.1 2.6 all-to-all-done.1.att
  93.4 20.9 %middle.1 = (f32[160,1152]{1,0:T(8,128)}, bf16[160,1152]{1,0:T(8,128)(2,1)}, bf16[4,160,288]{2,1,0:T(8,128)(2,1)}, f32[16,160,304]{2,1,0:T(8,128)}, bf16[4,160,2...) custom-call(s32[10]{0:T(128)} %stack.65.table, ...), custom_call_target="tpu_custom_call" | custom-call | bytes 251392 | tf_op jit(solution)/shard_map/middle/pallas_call | solution.py:61
  115.6 4.2 collective-permute-start.14
  120.0 7.1 %collective-permute-done.13.refs_1_ = bf16[160,1152]{1,0:T(8,128)(2,1)S(1)} collective-permute-done((bf16[160,1152]{1,0:T(8,128)(2,1)}, bf16[160,1152]{1,0:T(8,128)(2,1)S(1)}, u32[]{:S(2)}, u32[]{:S(2)}) %collective-permute-start.13) | collective-permute-done | bytes 368672 | tf_op jit(solution)/shard_map/ppermute | solution.py:33
  127.0 20.7 %collective-permute-done.14.refs_2_ = bf16[160,1152]{1,0:T(8,128)(2,1)S(1)} collective-permute-done((bf16[160,1152]{1,0:T(8,128)(2,1)}, bf16[160,1152]{1,0:T(8,128)(2,1)S(1)}, u32[]{:S(2)}, u32[]{:S(2)}) %collective-permute-start.14) | collective-permute-done | bytes 368672 | tf_op jit(solution)/shard_map/ppermute | solution.py:33
  147.7 3.8 collective-permute-done.15.refs_3_
  152.3 8.5 %up_project.1 = (f32[640,1536]{1,0:T(8,128)}, bf16[640,1536]{1,0:T(8,128)(2,1)}, bf16[640,1152]{1,0:T(8,128)(2,1)}) custom-call(s32[10]{0:T(128)} %stack.65.table, bf16[160,1152]{1,0:T(8,128)(2,1)} %get-tuple-element.97.refs_0_, bf16[160,1152]{1,0:T(8,128)(2,1)} %copy-done.36, bf16[160,1152]{1,0:T(8,128)(2,1)} %copy-done.37, bf16[160,1152]{1,0:T(8,128)(2,1)} %copy-done.38, ...), custom_call_target="tpu_custom_call" | custom-call | bytes 123863 | tf_op jit(solution)/shard_map/up_project/pallas_call | solution.py:61
  163.8 9.4 %mix.1 = (bf16[640,768]{1,0:T(8,128)(2,1)}, bf16[2,640,768]{2,1,0:T(8,128)(2,1)}) custom-call(s32[10]{0:T(128)} %stack.65.table, bf16[640,1536]{1,0:T(8,128)(2,1)} %get-tuple-element.98.value.gate.activated, bf16[640,1536]{1,0:T(8,128)(2,1)} %get-tuple-element.98.value.gate.activated, bf16[32,1536]{1,0:T(8,128)(2,1)} %copy-done.18, ...), custom_call_target="tpu_custom_call" | custom-call | bytes 92405 | tf_op jit(solution)/shard_map/mix/pallas_call | solution.py:61
  173.1 3.8 convolution_convert_fusion.2
  177.0 3.5 all-to-all-start.2
  183.5 14.8 %mix_back.1 = (bf16[640,1536]{1,0:T(8,128)(2,1)}, f32[16,1536]{1,0:T(8,128)}) custom-call(s32[10]{0:T(128)} %stack.65.table, bf16[2,640,768]{2,1,0:T(8,128)(2,1)} %get-tuple-element.102.grads, bf16[2,32,768]{2,1,0:T(8,128)(2,1)} %copy-done.39, bf16[640,1536]{1,0:T(8,128)(2,1)} %get-tuple-element.98.value.gate.activated, bf16[32,1536]{1,0:T(8,128)(2,1)} %copy-done.18, ...), custom_call_target="tpu_custom_call" | custom-call | bytes 102236 | tf_op jit(solution)/shard_map/mix_back/pallas_call | solution.py:61
  198.3 4.2 convolution_convert_fusion.1
  207.8 5.9 %all-to-all-done.2.branches = bf16[4,160,1152]{2,1,0:T(8,128)(2,1)S(1)} async-done(((bf16[4,160,1152]{2,1,0:T(8,128)(2,1)}), bf16[4,160,1152]{2,1,0:T(8,128)(2,1)S(1)}, u32[]{:S(2)}, u32[]{:S(2)}) %all-to-all-start.2) | async-done | bytes 1474592 | tf_op jit(solution)/shard_map/all_to_all | solution.py:37
  214.7 3.7 output.1
  218.4 9.4 %ffn_parts.1 = bf16[1152,2304]{1,0:T(8,128)(2,1)} custom-call(s32[10]{0:T(128)} %stack.65.table, bf16[640,1152]{1,0:T(8,128)(2,1)} %copy-done.7, bf16[640,768]{1,0:T(8,128)(2,1)} %get-tuple-element.107.hidden, bf16[640,1152]{1,0:T(8,128)(2,1)} %get-tuple-element.108.normed, bf16[640,1536]{1,0:T(8,128)(2,1)} %get-tuple-element.105.grad_up), custom_call_target="tpu_custom_call" | custom-call | bytes 112066 | tf_op jit(solution)/shard_map/ffn_parts/pallas_call | solution.py:61
  227.8 9.3 %collective-permute-done.18.grad_1 = bf16[160,1152]{1,0:T(8,128)(2,1)S(1)} collective-permute-done((bf16[160,1152]{1,0:T(8,128)(2,1)}, bf16[160,1152]{1,0:T(8,128)(2,1)S(1)}, u32[]{:S(2)}, u32[]{:S(2)}) %collective-permute-start.18) | collective-permute-done | bytes 368672 | tf_op jit(solution)/shard_map/ppermute | solution.py:33
  237.2 7.4 %collective-permute-done.19.grad_2 = bf16[160,1152]{1,0:T(8,128)(2,1)} collective-permute-done((bf16[160,1152]{1,0:T(8,128)(2,1)}, bf16[160,1152]{1,0:T(8,128)(2,1)}, u32[]{:S(2)}, u32[]{:S(2)}) %collective-permute-start.19) | collective-permute-done | bytes 368672 | tf_op jit(solution)/shard_map/ppermute | solution.py:33
  245.8 4.1 collective-permute-start.22
  250.3 25.9 %middle_back.1 = (bf16[160,1152]{1,0:T(8,128)(2,1)}, bf16[4,160,288]{2,1,0:T(8,128)(2,1)}, bf16[160,1152]{1,0:T(8,128)(2,1)}, bf16[4,160,288]{2,1,0:T(8,128)(2,1...) custom-call(s32[10]{0:T(128)} %stack.65.table, ...), custom_call_target="tpu_custom_call" | custom-call | bytes 251023 | tf_op jit(solution)/shard_map/middle_back/pallas_call | solution.py:61
  276.9 3.4 collective-permute-done.23
  281.2 3.5 all-to-all-start.3
  285.9 10.2 %square_parts.1 = (bf16[1152,3584]{1,0:T(8,128)(2,1)}, bf16[4,304,576]{2,1,0:T(8,128)(2,1)}) custom-call(s32[10]{0:T(128)} %stack.65.table, bf16[160,1152]{1,0:T(8,128)(2,1)} %get-tuple-element.116.dyc, bf16[4,160,288]{2,1,0:T(8,128)(2,1)} %get-tuple-element.117.text, bf16[160,1152]{1,0:T(8,128)(2,1)} %get-tuple-element.118.x1, ...), custom_call_target="tpu_custom_call" | custom-call | bytes 146718 | tf_op jit(solution)/shard_map/square_parts/pallas_call | solution.py:61
  297.1 6.1 %all-to-all-start.4 = ((bf16[4,304,576]{2,1,0:T(8,128)(2,1)}), bf16[4,304,576]{2,1,0:T(8,128)(2,1)S(1)}, u32[]{:S(2)}, u32[]{:S(2)}) async-start(bf16[4,304,576]{2,1,0:T(8,128)(2,1)} %get-tuple-element.127), calls=%async_computation.5 | async-start | bytes 3112960 | tf_op jit(solution)/shard_map/all_to_all | solution.py:37
  303.7 11.9 %self_back.1 = (f32[640,288]{1,0:T(8,128)}, f32[288,128]{1,0:T(8,128)}, f32[288,128]{1,0:T(8,128)}) custom-call(s32[10]{0:T(128)} %stack.65.table, bf16[4,160,288]{2,1,0:T(8,128)(2,1)} %copy-done.13, bf16[640,288]{1,0:T(8,128)(2,1)} %get-tuple-element.85.q, f32[640,288]{1,0:T(8,128)} %get-tuple-element.130.wide_out, ...), custom_call_target="tpu_custom_call" | custom-call | bytes 35389 | tf_op jit(solution)/shard_map/self_back/pallas_call | solution.py:61
  320.1 9.2 %self_project_back.1.grad_projected = bf16[640,864]{1,0:T(8,128)(2,1)} custom-call(s32[10]{0:T(128)} %stack.65.table, f32[640,288]{1,0:T(8,128)} %get-tuple-element.132.grad_q, bf16[640,288]{1,0:T(8,128)(2,1)} %get-tuple-element.133.k, bf16[640,288]{1,0:T(8,128)(2,1)} %get-tuple-element.134.v, f32[640,576]{1,0:T(8,128)} %get-tuple-element.135.raw, ...), custom_call_target="tpu_custom_call" | custom-call | bytes 43499 | tf_op jit(solution)/shard_map/self_project_back/pallas_call | solution.py:61
  329.4 3.1 convolution_convert_fusion
  340.0 8.0 %late_parts.1 = bf16[1152,1440]{1,0:T(8,128)(2,1)} custom-call(s32[10]{0:T(128)} %stack.65.table, bf16[640,1152]{1,0:T(8,128)(2,1)} %get-tuple-element.138.normed, bf16[640,864]{1,0:T(8,128)(2,1)} %self_project_back.1.grad_projected, bf16[304,1152]{1,0:T(8,128)(2,1)} %pad.16.text, bf16[4,304,576]{2,1,0:T(8,128)(2,1)} %copy-done.6), custom_call_target="tpu_custom_call" | custom-call | bytes 79994 | tf_op jit(solution)/shard_map/late_parts/pallas_call | solution.py:61
  348.0 30.5 %reduce-scatter.6.cloned.1.call-done = bf16[144,3584]{1,0:T(8,128)(2,1)} async-done(((bf16[1152,3584]{1,0:T(8,128)(2,1)}), bf16[144,3584]{1,0:T(8,128)(2,1)}) %reduce-scatter.6.cloned.1.call-update) | async-done | bytes 1032208 | tf_op jit(solution)/shard_map/reduce_scatter | solution.py:829
  384.1 5.3 %all-to-all-start.5 = ((bf16[4,144,896]{2,1,0:T(8,128)(2,1)}), bf16[4,144,896]{2,1,0:T(8,128)(2,1)S(1)}, u32[]{:S(2)}, u32[]{:S(2)}) async-start(bf16[4,144,896]{2,1,0:T(8,128)(2,1)} %bitcast.109), calls=%async_computation.7 | async-start | bytes 2064384 | tf_op jit(solution)/shard_map/all_to_all | solution.py:37
  389.4 4.4 first_norm_back.1
  396.1 2.9 collective-permute-start.31
  400.8 7.4 %collective-permute-done.30 = f32[6,1152]{1,0:T(8,128)S(1)} collective-permute-done((f32[6,1152]{1,0:T(8,128)S(1)}, f32[6,1152]{1,0:T(8,128)S(1)}, u32[]{:S(2)}, u32[]{:S(2)}) %collective-permute-start.30) | collective-permute-done | bytes 27680 | tf_op jit(solution)/shard_map/ppermute | solution.py:823
  408.2 5.9 %collective-permute-done.31 = f32[6,1152]{1,0:T(8,128)S(1)} collective-permute-done((f32[6,1152]{1,0:T(8,128)S(1)}, f32[6,1152]{1,0:T(8,128)S(1)}, u32[]{:S(2)}, u32[]{:S(2)}) %collective-permute-start.31) | collective-permute-done | bytes 27680 | tf_op jit(solution)/shard_map/ppermute | solution.py:823
  414.1 2.3 collective-permute-done.32
  418.5 2.9 collective-permute-start.34
  423.0 5.5 %collective-permute-done.37 = f32[9,1536]{1,0:T(8,128)S(1)} collective-permute-done((f32[9,1536]{1,0:T(8,128)S(1)}, f32[9,1536]{1,0:T(8,128)S(1)}, u32[]{:S(2)}, u32[]{:S(2)}) %collective-permute-start.37) | collective-permute-done | bytes 55328 | tf_op jit(solution)/shard_map/ppermute | solution.py:28
  430.8 2.4 collective-permute-done.38
  438.3 12.4 %collective-permute-done.34 = bf16[160,1152]{1,0:T(8,128)(2,1)S(1)} collective-permute-done((bf16[160,1152]{1,0:T(8,128)(2,1)S(1)}, bf16[160,1152]{1,0:T(8,128)(2,1)S(1)}, u32[]{:S(2)}, u32[]{:S(2)}) %collective-permute-start.34) | collective-permute-done | bytes 368672 | tf_op jit(solution)/shard_map/ppermute | solution.py:33
  450.7 3.2 collective-permute-done.35
  (231 shorter events, 81.6 us)
Async XLA Ops:
  9.7 34.1 %collective-permute-start.2 = (bf16[112,1152]{1,0:T(8,128)(2,1)}, bf16[112,1152]{1,0:T(8,128)(2,1)S(1)}, u32[]{:S(2)}, u32[]{:S(2)}) collective-permute-start(bf16[112,1152]{1,0:T(8,128)(2,1)} %eighth.1), channel_id=1, source_target_pairs={{0,1},{1,2},{2,3},{3,0},{4,5},{5,6},{6,7},{7,4},{8,9},{9,10},{10,1... | collective-permute-start | bytes 774152 | tf_op jit(solution)/shard_map/ppermute | solution.py:33
  11.3 32.5 %collective-permute-start.3 = (bf16[112,1152]{1,0:T(8,128)(2,1)}, bf16[112,1152]{1,0:T(8,128)(2,1)}, u32[]{:S(2)}, u32[]{:S(2)}) collective-permute-start(bf16[112,1152]{1,0:T(8,128)(2,1)} %eighth.1), channel_id=1, source_target_pairs={{0,2},{1,3},{2,0},{3,1},{4,6},{5,7},{6,4},{7,5},{8,10},{9,11},{10,... | collective-permute-start | bytes 774152 | tf_op jit(solution)/shard_map/ppermute | solution.py:33
  12.3 31.6 %collective-permute-start.4 = (bf16[112,1152]{1,0:T(8,128)(2,1)}, bf16[112,1152]{1,0:T(8,128)(2,1)}, u32[]{:S(2)}, u32[]{:S(2)}) collective-permute-start(bf16[112,1152]{1,0:T(8,128)(2,1)} %eighth.1), channel_id=1, source_target_pairs={{0,3},{1,0},{2,1},{3,2},{4,7},{5,4},{6,5},{7,6},{8,11},{9,8},{10,9... | collective-permute-start | bytes 774152 | tf_op jit(solution)/shard_map/ppermute | solution.py:33
  14.3 14.4 %collective-permute-start = (bf16[6,1152]{1,0:T(8,128)(2,1)S(1)}, bf16[6,1152]{1,0:T(8,128)(2,1)S(1)}, u32[]{:S(2)}, u32[]{:S(2)}) collective-permute-start(bf16[6,1152]{1,0:T(8,128)(2,1)S(1)} %bitcast.149), channel_id=1, source_target_pairs={{0,4},{4,0},{8,12},{12,8},{16,20},{20,16},{24,28},{28,24},{1,5},{5... | collective-permute-start | bytes 41480 | tf_op jit(solution)/shard_map/ppermute | solution.py:28
  16.4 50.6 %all-to-all-start = ((bf16[4,304,576]{2,1,0:T(8,128)(2,1)}), bf16[4,304,576]{2,1,0:T(8,128)(2,1)S(1)}, u32[]{:S(2)}, u32[]{:S(2)}) async-start(bf16[4,304,576]{2,1,0:T(8,128)(2,1)} %broadcast_in_dim.63), calls=%async_computation | async-start | bytes 3112960 | tf_op jit(solution)/shard_map/all_to_all | solution.py:37
  42.2 7.7 %collective-permute-start.1 = (f32[2,288,128]{2,1,0:T(8,128)S(1)}, f32[2,288,128]{2,1,0:T(8,128)S(1)}, u32[]{:S(2)}, u32[]{:S(2)}) collective-permute-start(f32[2,288,128]{2,1,0:T(8,128)S(1)} %pad_maximum_fusion.1), channel_id=1, source_target_pairs={{0,4},{4,0},{8,12},{12,8},{16,20},{20,16},{24,28},{28,24},{1,5},{5... | collective-permute-start | bytes 884744 | tf_op jit(solution)/shard_map/ppermute | solution.py:28
  46.5 28.7 %collective-permute-start.6 = (bf16[3,112,1152]{2,1,0:T(8,128)(2,1)}, bf16[3,112,1152]{2,1,0:T(8,128)(2,1)}, u32[]{:S(2)}, u32[]{:S(2)}) collective-permute-start(bf16[3,112,1152]{2,1,0:T(8,128)(2,1)} %pad_maximum_fusion.refs_0_), channel_id=1, source_target_pairs={{0,8},{4,12},{8,0},{12,4},{16,24},{20,28},{24,16},{28,20},{1,9},{5... | collective-permute-start | bytes 2322440 | tf_op jit(solution)/shard_map/ppermute | solution.py:752
  48.0 36.1 %collective-permute-start.7 = (bf16[3,112,1152]{2,1,0:T(8,128)(2,1)}, bf16[3,112,1152]{2,1,0:T(8,128)(2,1)}, u32[]{:S(2)}, u32[]{:S(2)}) collective-permute-start(bf16[3,112,1152]{2,1,0:T(8,128)(2,1)} %pad_maximum_fusion.refs_0_), channel_id=1, source_target_pairs={{0,16},{4,20},{8,24},{12,28},{16,0},{20,4},{24,8},{28,12},{1,17},{... | collective-permute-start | bytes 2322440 | tf_op jit(solution)/shard_map/ppermute | solution.py:752
  49.5 34.6 %collective-permute-start.8 = (bf16[3,112,1152]{2,1,0:T(8,128)(2,1)}, bf16[3,112,1152]{2,1,0:T(8,128)(2,1)}, u32[]{:S(2)}, u32[]{:S(2)}) collective-permute-start(bf16[3,112,1152]{2,1,0:T(8,128)(2,1)} %pad_maximum_fusion.refs_0_), channel_id=1, source_target_pairs={{0,24},{4,28},{8,16},{12,20},{16,8},{20,12},{24,0},{28,4},{1,25},{... | collective-permute-start | bytes 2322440 | tf_op jit(solution)/shard_map/ppermute | solution.py:752
  67.1 24.3 %collective-permute-start.12 = (bf16[4,304,576]{2,1,0:T(8,128)(2,1)S(1)}, bf16[4,304,576]{2,1,0:T(8,128)(2,1)S(1)}, u32[]{:S(2)}, u32[]{:S(2)}) collective-permute-start(bf16[4,304,576]{2,1,0:T(8,128)(2,1)S(1)} %all-to-all-done.refs_8_.kv_own), channel_id=1, source_target_pairs={{0,4},{4,0},{8,12},{12,8},{16,20},{20,16},{24,28},{28,24},{1,5},{5... | collective-permute-start | bytes 4202504 | tf_op jit(solution)/shard_map/ppermute | solution.py:28
  67.1 19.6 %all-to-all-start.1 = ((bf16[4,160,288]{2,1,0:T(8,128)(2,1)}), bf16[4,160,288]{2,1,0:T(8,128)(2,1)}, u32[]{:S(2)}, u32[]{:S(2)}) async-start(bf16[4,160,288]{2,1,0:T(8,128)(2,1)} %bitcast.142), calls=%async_computation.1 | async-start | bytes 983040 | tf_op jit(solution)/shard_map/all_to_all | solution.py:37
  75.0 12.1 %collective-permute-start.5 = (bf16[3,112,1152]{2,1,0:T(8,128)(2,1)}, bf16[3,112,1152]{2,1,0:T(8,128)(2,1)}, u32[]{:S(2)}, u32[]{:S(2)}) collective-permute-start(bf16[3,112,1152]{2,1,0:T(8,128)(2,1)} %pad_maximum_fusion.refs_0_), channel_id=1, source_target_pairs={{0,4},{4,0},{8,12},{12,8},{16,20},{20,16},{24,28},{28,24},{1,5},{5... | collective-permute-start | bytes 2322440 | tf_op jit(solution)/shard_map/ppermute | solution.py:28
  86.7 2.5 collective-permute-start.10
  86.7 3.6 collective-permute-start.11
  87.2 4.2 collective-permute-start.9
  114.3 12.7 %collective-permute-start.13 = (bf16[160,1152]{1,0:T(8,128)(2,1)}, bf16[160,1152]{1,0:T(8,128)(2,1)S(1)}, u32[]{:S(2)}, u32[]{:S(2)}) collective-permute-start(bf16[160,1152]{1,0:T(8,128)(2,1)} %get-tuple-element.97.refs_0_), channel_id=1, source_target_pairs={{0,1},{1,2},{2,3},{3,0},{4,5},{5,6},{6,7},{7,4},{8,9},{9,10},{10,1... | collective-permute-start | bytes 1105928 | tf_op jit(solution)/shard_map/ppermute | solution.py:33
  115.6 32.2 %collective-permute-start.14 = (bf16[160,1152]{1,0:T(8,128)(2,1)}, bf16[160,1152]{1,0:T(8,128)(2,1)S(1)}, u32[]{:S(2)}, u32[]{:S(2)}) collective-permute-start(bf16[160,1152]{1,0:T(8,128)(2,1)} %get-tuple-element.97.refs_0_), channel_id=1, source_target_pairs={{0,2},{1,3},{2,0},{3,1},{4,6},{5,7},{6,4},{7,5},{8,10},{9,11},{10,... | collective-permute-start | bytes 1105928 | tf_op jit(solution)/shard_map/ppermute | solution.py:33
  119.8 31.7 %collective-permute-start.15 = (bf16[160,1152]{1,0:T(8,128)(2,1)}, bf16[160,1152]{1,0:T(8,128)(2,1)S(1)}, u32[]{:S(2)}, u32[]{:S(2)}) collective-permute-start(bf16[160,1152]{1,0:T(8,128)(2,1)} %get-tuple-element.97.refs_0_), channel_id=1, source_target_pairs={{0,3},{1,0},{2,1},{3,2},{4,7},{5,4},{6,5},{7,6},{8,11},{9,8},{10,9... | collective-permute-start | bytes 1105928 | tf_op jit(solution)/shard_map/ppermute | solution.py:33
  161.8 1.4 collective-permute-start.16
  177.0 36.6 %all-to-all-start.2 = ((bf16[4,160,1152]{2,1,0:T(8,128)(2,1)}), bf16[4,160,1152]{2,1,0:T(8,128)(2,1)S(1)}, u32[]{:S(2)}, u32[]{:S(2)}) async-start(bf16[4,160,1152]{2,1,0:T(8,128)(2,1)} %bitcast.32), calls=%async_computation.2 | async-start | bytes 2949120 | tf_op jit(solution)/shard_map/all_to_all | solution.py:37
  180.5 123.2 %reduce-scatter.4.cloned.1.call-start = ((), (), s32[]{:S(2)}) async-start(), calls=%async_computation.9 | async-start | bytes 5971968 | tf_op jit(solution)/shard_map/reduce_scatter | solution.py:829
  181.5 1.4 collective-permute-start.17
  203.7 33.5 %collective-permute-start.18 = (bf16[160,1152]{1,0:T(8,128)(2,1)}, bf16[160,1152]{1,0:T(8,128)(2,1)S(1)}, u32[]{:S(2)}, u32[]{:S(2)}) collective-permute-start(bf16[160,1152]{1,0:T(8,128)(2,1)} %get-tuple-element.182), channel_id=1, source_target_pairs={{0,1},{1,2},{2,3},{3,0},{4,5},{5,6},{6,7},{7,4},{8,9},{9,10},{10,1... | collective-permute-start | bytes 1105928 | tf_op jit(solution)/shard_map/ppermute | solution.py:33
  204.8 39.8 %collective-permute-start.19 = (bf16[160,1152]{1,0:T(8,128)(2,1)}, bf16[160,1152]{1,0:T(8,128)(2,1)}, u32[]{:S(2)}, u32[]{:S(2)}) collective-permute-start(bf16[160,1152]{1,0:T(8,128)(2,1)} %get-tuple-element.181), channel_id=1, source_target_pairs={{0,2},{1,3},{2,0},{3,1},{4,6},{5,7},{6,4},{7,5},{8,10},{9,11},{10,... | collective-permute-start | bytes 1105928 | tf_op jit(solution)/shard_map/ppermute | solution.py:33
  205.7 40.0 %collective-permute-start.20 = (bf16[160,1152]{1,0:T(8,128)(2,1)}, bf16[160,1152]{1,0:T(8,128)(2,1)}, u32[]{:S(2)}, u32[]{:S(2)}) collective-permute-start(bf16[160,1152]{1,0:T(8,128)(2,1)} %get-tuple-element.180), channel_id=1, source_target_pairs={{0,3},{1,0},{2,1},{3,2},{4,7},{5,4},{6,5},{7,6},{8,11},{9,8},{10,9... | collective-permute-start | bytes 1105928 | tf_op jit(solution)/shard_map/ppermute | solution.py:33
  245.8 30.4 %collective-permute-start.21 = (bf16[160,1152]{1,0:T(8,128)(2,1)S(1)}, bf16[160,1152]{1,0:T(8,128)(2,1)S(1)}, u32[]{:S(2)}, u32[]{:S(2)}) collective-permute-start(bf16[160,1152]{1,0:T(8,128)(2,1)S(1)} %copy-done.29), channel_id=1, source_target_pairs={{0,1},{1,2},{2,3},{3,0},{4,5},{5,6},{6,7},{7,4},{8,9},{9,10},{10,1... | collective-permute-start | bytes 1105928 | tf_op jit(solution)/shard_map/ppermute | solution.py:33
  245.8 31.1 %collective-permute-start.22 = (bf16[160,1152]{1,0:T(8,128)(2,1)S(1)}, bf16[160,1152]{1,0:T(8,128)(2,1)S(1)}, u32[]{:S(2)}, u32[]{:S(2)}) collective-permute-start(bf16[160,1152]{1,0:T(8,128)(2,1)S(1)} %copy-done.29), channel_id=1, source_target_pairs={{0,2},{1,3},{2,0},{3,1},{4,6},{5,7},{6,4},{7,5},{8,10},{9,11},{10,... | collective-permute-start | bytes 1105928 | tf_op jit(solution)/shard_map/ppermute | solution.py:33
  250.0 30.3 %collective-permute-start.23 = (bf16[160,1152]{1,0:T(8,128)(2,1)S(1)}, bf16[160,1152]{1,0:T(8,128)(2,1)S(1)}, u32[]{:S(2)}, u32[]{:S(2)}) collective-permute-start(bf16[160,1152]{1,0:T(8,128)(2,1)S(1)} %copy-done.29), channel_id=1, source_target_pairs={{0,3},{1,0},{2,1},{3,2},{4,7},{5,4},{6,5},{7,6},{8,11},{9,8},{10,9... | collective-permute-start | bytes 1105928 | tf_op jit(solution)/shard_map/ppermute | solution.py:33
  281.1 3.6 collective-permute-start.24
  281.2 15.1 %all-to-all-start.3 = ((bf16[4,160,288]{2,1,0:T(8,128)(2,1)}), bf16[4,160,288]{2,1,0:T(8,128)(2,1)S(1)}, u32[]{:S(2)}, u32[]{:S(2)}) async-start(bf16[4,160,288]{2,1,0:T(8,128)(2,1)} %get-tuple-element.115), calls=%async_computation.3 | async-start | bytes 983040 | tf_op jit(solution)/shard_map/all_to_all | solution.py:37
  284.7 93.8 %reduce-scatter.6.cloned.1.call-start = ((), (), s32[]{:S(2)}) async-start(), calls=%async_computation.10 | async-start | bytes 9289728 | tf_op jit(solution)/shard_map/reduce_scatter | solution.py:829
  297.1 41.7 %all-to-all-start.4 = ((bf16[4,304,576]{2,1,0:T(8,128)(2,1)}), bf16[4,304,576]{2,1,0:T(8,128)(2,1)S(1)}, u32[]{:S(2)}, u32[]{:S(2)}) async-start(bf16[4,304,576]{2,1,0:T(8,128)(2,1)} %get-tuple-element.127), calls=%async_computation.5 | async-start | bytes 3112960 | tf_op jit(solution)/shard_map/all_to_all | solution.py:37
  303.2 130.7 %reduce-scatter.8.cloned.1.call-start = ((), (), s32[]{:S(2)}) async-start(), calls=%async_computation.11 | async-start | bytes 3981312 | tf_op jit(solution)/shard_map/reduce_scatter | solution.py:829
  316.6 1.6 collective-permute-start.25
  333.4 45.1 %collective-permute-start.26 = (bf16[160,1152]{1,0:T(8,128)(2,1)}, bf16[160,1152]{1,0:T(8,128)(2,1)}, u32[]{:S(2)}, u32[]{:S(2)}) collective-permute-start(bf16[160,1152]{1,0:T(8,128)(2,1)} %get-tuple-element.179), channel_id=1, source_target_pairs={{0,1},{1,2},{2,3},{3,0},{4,5},{5,6},{6,7},{7,4},{8,9},{9,10},{10,1... | collective-permute-start | bytes 1105928 | tf_op jit(solution)/shard_map/ppermute | solution.py:33
  334.9 43.6 %collective-permute-start.27 = (bf16[160,1152]{1,0:T(8,128)(2,1)}, bf16[160,1152]{1,0:T(8,128)(2,1)}, u32[]{:S(2)}, u32[]{:S(2)}) collective-permute-start(bf16[160,1152]{1,0:T(8,128)(2,1)} %get-tuple-element.178), channel_id=1, source_target_pairs={{0,2},{1,3},{2,0},{3,1},{4,6},{5,7},{6,4},{7,5},{8,10},{9,11},{10,... | collective-permute-start | bytes 1105928 | tf_op jit(solution)/shard_map/ppermute | solution.py:33
  336.4 42.0 %collective-permute-start.28 = (bf16[160,1152]{1,0:T(8,128)(2,1)S(1)}, bf16[160,1152]{1,0:T(8,128)(2,1)}, u32[]{:S(2)}, u32[]{:S(2)}) collective-permute-start(bf16[160,1152]{1,0:T(8,128)(2,1)S(1)} %get-tuple-element.177), channel_id=1, source_target_pairs={{0,3},{1,0},{2,1},{3,2},{4,7},{5,4},{6,5},{7,6},{8,11},{9,8},{10,9... | collective-permute-start | bytes 1105928 | tf_op jit(solution)/shard_map/ppermute | solution.py:33
  384.1 32.4 %all-to-all-start.5 = ((bf16[4,144,896]{2,1,0:T(8,128)(2,1)}), bf16[4,144,896]{2,1,0:T(8,128)(2,1)S(1)}, u32[]{:S(2)}, u32[]{:S(2)}) async-start(bf16[4,144,896]{2,1,0:T(8,128)(2,1)} %bitcast.109), calls=%async_computation.7 | async-start | bytes 2064384 | tf_op jit(solution)/shard_map/all_to_all | solution.py:37
  394.7 1.3 collective-permute-start.29
  396.0 12.2 %collective-permute-start.30 = (f32[6,1152]{1,0:T(8,128)S(1)}, f32[6,1152]{1,0:T(8,128)S(1)}, u32[]{:S(2)}, u32[]{:S(2)}) collective-permute-start(f32[6,1152]{1,0:T(8,128)S(1)} %fusion.4), channel_id=1, source_target_pairs={{0,1},{1,0},{2,3},{3,2},{4,5},{5,4},{6,7},{7,6},{8,9},{9,8},{10,11... | collective-permute-start | bytes 82952 | tf_op jit(solution)/shard_map/ppermute | solution.py:823
  396.1 18.0 %collective-permute-start.31 = (f32[6,1152]{1,0:T(8,128)S(1)}, f32[6,1152]{1,0:T(8,128)S(1)}, u32[]{:S(2)}, u32[]{:S(2)}) collective-permute-start(f32[6,1152]{1,0:T(8,128)S(1)} %fusion.4), channel_id=1, source_target_pairs={{0,2},{1,3},{2,0},{3,1},{4,6},{5,7},{6,4},{7,5},{8,10},{9,11},{10,... | collective-permute-start | bytes 82952 | tf_op jit(solution)/shard_map/ppermute | solution.py:823
  399.0 17.4 %collective-permute-start.32 = (f32[6,1152]{1,0:T(8,128)S(1)}, f32[6,1152]{1,0:T(8,128)S(1)}, u32[]{:S(2)}, u32[]{:S(2)}) collective-permute-start(f32[6,1152]{1,0:T(8,128)S(1)} %fusion.4), channel_id=1, source_target_pairs={{0,3},{1,2},{2,1},{3,0},{4,7},{5,6},{6,5},{7,4},{8,11},{9,10},{10,... | collective-permute-start | bytes 82952 | tf_op jit(solution)/shard_map/ppermute | solution.py:823
  416.5 5.0 %collective-permute-start.36 = (f32[9,1536]{1,0:T(8,128)S(1)}, f32[9,1536]{1,0:T(8,128)S(1)}, u32[]{:S(2)}, u32[]{:S(2)}) collective-permute-start(f32[9,1536]{1,0:T(8,128)S(1)} %bitcast.145), channel_id=1, source_target_pairs={{0,4},{4,0},{8,12},{12,8},{16,20},{20,16},{24,28},{28,24},{1,5},{5... | collective-permute-start | bytes 165896 | tf_op jit(solution)/shard_map/ppermute | solution.py:28
  418.0 20.4 %collective-permute-start.33 = (bf16[160,1152]{1,0:T(8,128)(2,1)S(1)}, bf16[160,1152]{1,0:T(8,128)(2,1)S(1)}, u32[]{:S(2)}, u32[]{:S(2)}) collective-permute-start(bf16[160,1152]{1,0:T(8,128)(2,1)S(1)} %copy-done.35), channel_id=1, source_target_pairs={{0,1},{1,2},{2,3},{3,0},{4,5},{5,6},{6,7},{7,4},{8,9},{9,10},{10,1... | collective-permute-start | bytes 1105928 | tf_op jit(solution)/shard_map/ppermute | solution.py:33
  418.5 32.2 %collective-permute-start.34 = (bf16[160,1152]{1,0:T(8,128)(2,1)S(1)}, bf16[160,1152]{1,0:T(8,128)(2,1)S(1)}, u32[]{:S(2)}, u32[]{:S(2)}) collective-permute-start(bf16[160,1152]{1,0:T(8,128)(2,1)S(1)} %copy-done.35), channel_id=1, source_target_pairs={{0,2},{1,3},{2,0},{3,1},{4,6},{5,7},{6,4},{7,5},{8,10},{9,11},{10,... | collective-permute-start | bytes 1105928 | tf_op jit(solution)/shard_map/ppermute | solution.py:33
  421.4 32.5 %collective-permute-start.35 = (bf16[160,1152]{1,0:T(8,128)(2,1)S(1)}, bf16[160,1152]{1,0:T(8,128)(2,1)S(1)}, u32[]{:S(2)}, u32[]{:S(2)}) collective-permute-start(bf16[160,1152]{1,0:T(8,128)(2,1)S(1)} %copy-done.35), channel_id=1, source_target_pairs={{0,3},{1,0},{2,1},{3,2},{4,7},{5,4},{6,5},{7,6},{8,11},{9,8},{10,9... | collective-permute-start | bytes 1105928 | tf_op jit(solution)/shard_map/ppermute | solution.py:33
  421.4 7.1 %collective-permute-start.37 = (f32[9,1536]{1,0:T(8,128)S(1)}, f32[9,1536]{1,0:T(8,128)S(1)}, u32[]{:S(2)}, u32[]{:S(2)}) collective-permute-start(f32[9,1536]{1,0:T(8,128)S(1)} %add.194), channel_id=1, source_target_pairs={{0,8},{4,12},{8,0},{12,4},{16,24},{20,28},{24,16},{28,20},{1,9},{5... | collective-permute-start | bytes 165896 | tf_op jit(solution)/shard_map/ppermute | solution.py:28
  428.5 4.7 %collective-permute-start.38 = (f32[9,1536]{1,0:T(8,128)S(1)}, f32[9,1536]{1,0:T(8,128)S(1)}, u32[]{:S(2)}, u32[]{:S(2)}) collective-permute-start(f32[9,1536]{1,0:T(8,128)S(1)} %add.195), channel_id=1, source_target_pairs={{0,16},{4,20},{8,24},{12,28},{16,0},{20,4},{24,8},{28,12},{1,17},{... | collective-permute-start | bytes 165896 | tf_op jit(solution)/shard_map/ppermute | solution.py:28
  (49 other events, 382.8 us)
Sparse Core Ops, SparseCore 0:
  245.9 57.7 reduce-scatter.3
  307.8 70.6 reduce-scatter.5
  382.0 49.9 reduce-scatter.7
